TPU v7x, 32 devices: a whole 2x2x4 slice. The times are simulated.
32 devices in a mesh: gx: 8 (over z, y), gy: 4 (over x, core).
Axes of the slice: x: 2, y: 2, z: 4, core: 2. Of those that a mesh axis runs over, the one named last changes fastest.
Arguments:
- ref_image: bfloat16 [8, 512, 512], P(None, 'gx', 'gy'), may hold values from -6 to 6
- def_image: bfloat16 [8, 512, 512], P(None, 'gx', 'gy'), may hold values from -6 to 6
- shift_xy: int32 [2, 4096], P(None, ('gx', 'gy')), may hold values from -64 to 63, as said below
- shift_z: int32 [4096], P(('gx', 'gy')), may hold values from -2 to 1, as said below
- frac: float32 [3, 4096], P(None, ('gx', 'gy')), may hold values from 0 to 1
- connectivity: int32 [8, 4096], P(None, ('gx', 'gy')), may hold values from 0 to 305, as said below
Outputs:
- residual: bfloat16 [8, 512, 512], P(None, 'gx', 'gy')
- step_disp: float32 [3, 2, 64, 64], P(None, None, 'gx', 'gy')
- gn_product: float32 [3, 2, 64, 64], P(None, None, 'gx', 'gy')
- misfit: float32 [], replicated
Inputs may be any that keep to these rules, and one draw needn't show every extreme that they name: `connectivity`: each device's elements appear in a shuffled order; corner c = 4 cz + 2 cx + cy of an element with lower-corner node (a, b, c0) is node ((a + cz) (64/8+1) + b + cx) (128/8+1) + c0 + cy of the device's node grid, and every element of the device's brick is listed once. `shift_xy`: the in-plane shifts follow a continuous displacement field over the slab: elements side by side differ by a few voxels. `shift_z`: the plane shifts follow a continuous field over the slab.
All inputs are finite; a program needn't handle non-finite values.
Results may differ from a plain program's by a relative error of at most 0.0004.
Values may be sent and summed in bfloat16 or wider, within the bound.
No kernel may reach another device: no remote copies, remote signals or barrier semaphores. Data moves between devices by JAX's collectives and lax.ppermute only.
A program may use at most 64 MiB of HBM per device.

v0:
```python
import jax
import jax.numpy as jnp
from jax import lax
from jax.sharding import PartitionSpec as P

HALO = 64


def padded_2(x, sides, width):
    for axis, dim in sides:
        peers, length = (lax.axis_size(axis), x.shape[dim])
        up = [(i, (i + 1) % peers) for i in range(peers - 1)]
        down = [(j, i) for i, j in up]
        last = lax.slice_in_dim(x, length - width, length, axis=dim)
        initial = lax.slice_in_dim(x, 0, width, axis=dim)
        before = lax.ppermute(last, axis, up)
        after = lax.ppermute(initial, axis, down)
        x = jnp.concatenate([before, x, after], axis=dim)
    return x


def basis():
    lane = jnp.arange(512, dtype=jnp.int32)
    coords = [
        (lane // 64 % 8).astype(jnp.float32),
        (lane // 8 % 8).astype(jnp.float32),
        (lane % 8).astype(jnp.float32),
    ]
    coords = [(v + 0.5) / 8.0 for v in coords]
    rows = []
    for corner in range(8):
        bits = [corner // 4 % 2, corner // 2 % 2, corner % 2]
        prod = jnp.ones((512,), jnp.float32)
        for bit, pos in zip(bits, coords):
            prod = prod * (pos if bit == 1 else 1.0 - pos)
        rows.append(prod)
    return jnp.stack(rows)


def interpolate(tile, frac):
    wz, wx, wy = (frac[0], frac[1], frac[2])
    low_z = tile[:8] * (1.0 - wz) + tile[1:] * wz
    dif_z = tile[1:] - tile[:8]

    def along_x(a):
        return a[:, :8] * (1.0 - wx) + a[:, 1:] * wx

    def along_y(a):
        return a[:, :, :8] * (1.0 - wy) + a[:, :, 1:] * wy

    low_zx = along_x(low_z)
    dif_zx = along_x(dif_z)
    dif_xl = low_z[:, 1:] - low_z[:, :8]
    value = along_y(low_zx)
    slope_z = along_y(dif_zx)
    slope_x = along_y(dif_xl)
    slope_y = low_zx[:, :, 1:] - low_zx[:, :, :8]
    count = tile.shape[-1]
    return (
        value.reshape(512, count),
        jnp.stack([slope_z, slope_x, slope_y]).reshape(3, 512, count),
    )


def assemble(terms, connectivity, grid):
    node_total = grid[0] * grid[1] * grid[2]
    acc = (
        jnp.zeros((3, node_total), jnp.float32)
        .at[:, connectivity.reshape(-1)]
        .add(terms.reshape(3, -1))
    )
    acc = acc.reshape(3, grid[0], grid[1], grid[2])
    side_x = padded_2(acc, (("gx", 2),), 1)
    acc = acc.at[:, :, 0].add(side_x[:, :, 0]).at[:, :, -1].add(side_x[:, :, -1])
    side_y = padded_2(acc, (("gy", 3),), 1)
    acc = acc.at[:, :, :, 0].add(side_y[:, :, :, 0]).at[:, :, :, -1].add(side_y[:, :, :, -1])
    last_x = lax.axis_index("gx") == lax.axis_size("gx") - 1
    last_y = lax.axis_index("gy") == lax.axis_size("gy") - 1
    keep_x = jnp.where((jnp.arange(grid[1]) == grid[1] - 1) & last_x, 0.0, 1.0).astype(jnp.float32)
    keep_y = jnp.where((jnp.arange(grid[2]) == grid[2] - 1) & last_y, 0.0, 1.0).astype(jnp.float32)
    return acc * keep_x[None, None, :, None] * keep_y[None, None, None, :]


def on_device(ref_image, def_image, shift_xy, shift_z, frac, connectivity):
    planes, width_x, width_y = ref_image.shape
    ez_n = planes // 8
    ex_n = width_x // 8
    ey_n = width_y // 8
    count = ez_n * ex_n * ey_n
    nx_n = ex_n + 1
    ny_n = ey_n + 1
    grid = (ez_n + 1, nx_n, ny_n)
    high = lax.Precision.HIGHEST
    ghost = padded_2(def_image, (("gx", 1), ("gy", 2)), HALO)
    padded = jnp.pad(ghost, ((2, 2), (0, 0), (0, 0)))
    span_x = width_x + 2 * HALO
    span_y = width_y + 2 * HALO
    first = connectivity[0]
    layer_z = first // (nx_n * ny_n)
    col_x = first // ny_n % nx_n
    col_y = first % ny_n
    start_z = 8 * layer_z + shift_z + 2
    start_x = 8 * col_x + shift_xy[0] + HALO
    start_y = 8 * col_y + shift_xy[1] + HALO
    anchor = (start_z * span_x + start_x) * span_y + start_y
    lane = jnp.arange(729, dtype=jnp.int32)
    offsets = (lane // 81 * span_x + lane // 9 % 9) * span_y + lane % 9
    index = offsets[:, None] + anchor[None, :]
    tile = jnp.take(padded.reshape(-1), index).astype(jnp.float32).reshape(9, 9, 9, count)
    value, slopes = interpolate(tile, frac)
    struct_id = (layer_z * ex_n + col_x) * ey_n + col_y
    ref_struct = (
        ref_image.reshape(ez_n, 8, ex_n, 8, ey_n, 8).transpose(1, 3, 5, 0, 2, 4).reshape(512, count)
    )
    ref_elem = jnp.take(ref_struct, struct_id, axis=1).astype(jnp.float32)
    misfit_el = ref_elem - value
    inverse = jnp.zeros((count,), jnp.int32).at[struct_id].set(jnp.arange(count, dtype=jnp.int32))
    brick = jnp.take(misfit_el, inverse, axis=1).astype(jnp.bfloat16)
    residual = (
        brick.reshape(8, 8, 8, ez_n, ex_n, ey_n)
        .transpose(3, 0, 4, 1, 5, 2)
        .reshape(planes, width_x, width_y)
    )
    shape_tab = basis()
    weighted = slopes * misfit_el[None] * (1.0 / 512.0)
    terms = jnp.einsum("cv,kve->kce", shape_tab, weighted, precision=high)
    grad_nodes = assemble(terms, connectivity, grid)
    corner_vals = jnp.take(grad_nodes.reshape(3, -1), connectivity.reshape(-1), axis=1).reshape(
        3, 8, count
    )
    moved = jnp.einsum("cv,kce->kve", shape_tab, corner_vals, precision=high)
    along = jnp.sum(slopes * moved, axis=0)
    terms_two = jnp.einsum(
        "cv,kve->kce", shape_tab, slopes * along[None] * (1.0 / 512.0), precision=high
    )
    hess_nodes = assemble(terms_two, connectivity, grid)
    own_grad = grad_nodes[:, :, :ex_n, :ey_n]
    own_hess = hess_nodes[:, :, :ex_n, :ey_n]
    square_sum = jnp.sum(misfit_el * misfit_el)
    grad_sum = jnp.sum(own_grad * own_grad)
    curve_sum = jnp.sum(own_grad * own_hess)
    totals = lax.psum((square_sum, grad_sum, curve_sum), ("gx", "gy"))
    alpha = totals[1] / totals[2]
    voxel_total = planes * width_x * width_y * lax.axis_size("gx") * lax.axis_size("gy")
    misfit = totals[0] / voxel_total
    return (residual, alpha * own_grad, own_hess, misfit)


def solution(mesh):
    in_specs = (
        P(None, "gx", "gy"),
        P(None, "gx", "gy"),
        P(None, ("gx", "gy")),
        P(("gx", "gy")),
        P(None, ("gx", "gy")),
        P(None, ("gx", "gy")),
    )
    out_specs = (P(None, "gx", "gy"), P(None, None, "gx", "gy"), P(None, None, "gx", "gy"), P())
    return jax.shard_map(
        on_device, mesh=mesh, in_specs=in_specs, out_specs=out_specs, check_vma=False
    )
```

profile of v0, /device:TPU:0, one launch (start us, length us, event | category | flops | bytes accessed | tf_op | source)
XLA Modules:
  0.0 683.5 jit_solution(858974843317153411)
XLA Ops:
  0.6 4.9 collective-permute-start
  5.5 1.3 collective-permute-start.1
  7.0 3.5 reshape.917
  10.4 1.1 copy.25
  11.5 0.7 reshape.918
  12.4 1.0 scatter_custom_fusion
  13.4 0.8 gather_fusion
  15.1 1.3 collective-permute-start.3
  16.4 3.1 collective-permute-start.2
  19.5 1.3 collective-permute-done.2
  20.8 0.5 fusion.7
  21.2 1.2 copy.40
  22.5 542.2 %gather_fusion.1 = bf16[93312]{0:T(1024)(128)(2,1)S(1)} fusion(bf16[589824]{0:T(1024)(128)(2,1)S(1)} %bitcast.159, s32[94208]{0:T(1024)S(1)} %pad_clamp_fusion), kind=kCustom, calls=%fused_computation.1 | custom fusion | bytes 746496 | tf_op jit(solution)/shard_map/jit(_take)/gather | solution.py:109
  565.1 0.2 slice_subtract_fusion
  565.3 0.8 multiply_reduce_fusion
  566.4 0.5 convolution_bitcast_fusion.2
  567.0 0.2 copy.38
  567.2 6.1 scatter_custom_fusion.1
  573.5 4.5 collective-permute-start.4
  578.1 1.3 collective-permute-done.4
  579.4 1.3 collective-permute-start.5
  580.8 4.5 collective-permute-done.5
  585.4 4.7 collective-permute-start.6
  590.1 0.9 collective-permute-done.6
  590.9 1.3 collective-permute-start.7
  592.4 5.7 collective-permute-done.7
  598.1 0.7 scatter-add.46
  599.1 2.8 gather_fusion.3
  602.3 0.9 fusion.5
  603.2 0.5 convolution_bitcast_fusion.1
  603.8 0.2 copy.39
  604.0 6.1 scatter_custom_fusion.2
  610.3 5.1 collective-permute-start.8
  615.4 1.3 collective-permute-done.8
  616.7 1.3 collective-permute-start.9
  618.1 0.8 gather_fusion.2
  619.0 0.7 gather.25
  619.7 2.7 collective-permute-done.9
  622.6 3.3 collective-permute-start.10
  625.9 0.3 fusion.8
  626.2 0.5 collective-permute-done.10
  626.8 1.3 collective-permute-start.11
  628.1 1.1 copy.29
  629.2 2.8 reshape.921
  632.2 0.5 scatter-add.63
  632.7 1.3 multiply_reduce_fusion.1
  634.0 45.8 %all-reduce.1 = (f32[]{:T(128)}, f32[]{:T(128)}, f32[]{:T(128)}) all-reduce(f32[]{:T(128)} %get-tuple-element.101, f32[]{:T(128)} %get-tuple-element.100, f32[]{:T(128)} %get-tuple-element.105), channel_id=1, replica_groups=mesh['gx'=8,'gy'=4] {'gx','gy'}, use_global_device_ids=true, to_apply=%region_3.4 | all-reduce | flops 3 | bytes 24 | tf_op jit(solution)/shard_map/psum | solution.py:142
  681.1 0.6 slice_multiply_fusion.7
  (79 shorter events, 3.8 us)
Async XLA Ops:
  0.6 14.2 %collective-permute-start = (bf16[8,64,128]{2,1,0:T(8,128)(2,1)}, bf16[8,64,128]{2,1,0:T(8,128)(2,1)S(1)}, u32[]{:S(2)}, u32[]{:S(2)}) collective-permute-start(bf16[8,64,128]{2,1,0:T(8,128)(2,1)} %param.23), channel_id=1, source_target_pairs={{0,4},{4,8},{8,12},{12,16},{16,20},{20,24},{24,28},{1,5},{5,9},{9,... | collective-permute-start | bytes 393224 | tf_op jit(solution)/shard_map/ppermute | solution.py:16
  5.5 9.3 %collective-permute-start.1 = (bf16[8,64,128]{2,1,0:T(8,128)(2,1)}, bf16[8,64,128]{2,1,0:T(8,128)(2,1)S(1)}, u32[]{:S(2)}, u32[]{:S(2)}) collective-permute-start(bf16[8,64,128]{2,1,0:T(8,128)(2,1)} %param.23), channel_id=1, source_target_pairs={{4,0},{8,4},{12,8},{16,12},{20,16},{24,20},{28,24},{5,1},{9,5},{13... | collective-permute-start | bytes 393224 | tf_op jit(solution)/shard_map/ppermute | solution.py:17
  10.4 1.9 copy-start.1
  11.5 2.9 copy-start.3
  11.5 2.9 copy-start.4
  11.5 3.3 copy-start.2
  11.5 3.3 copy-start
  15.1 4.4 collective-permute-start.3
  16.4 4.4 collective-permute-start.2
  573.5 5.9 collective-permute-start.4
  579.4 5.9 collective-permute-start.5
  585.4 5.5 collective-permute-start.6
  590.9 7.1 %collective-permute-start.7 = (f32[3,2,9,1]{3,2,1,0:T(8,128)S(1)}, f32[3,2,9,1]{3,2,1,0:T(8,128)S(1)}, u32[]{:S(2)}, u32[]{:S(2)}) collective-permute-start(f32[3,2,9,1]{3,2,1,0:T(8,128)S(1)} %get-tuple-element.126), channel_id=1, source_target_pairs={{1,0},{2,1},{3,2},{5,4},{6,5},{7,6},{9,8},{10,9},{11,10},{13,12},{... | collective-permute-start | bytes 656 | tf_op jit(solution)/shard_map/ppermute | solution.py:17
  610.3 6.4 collective-permute-start.8
  616.7 5.7 collective-permute-start.9
  622.6 4.2 collective-permute-start.10
  626.8 5.3 collective-permute-start.11
where the time goes:
time: 684 us; the launch traced here: 683 us
  local copies, waits for them, and re-layouts  563 us (82%)
  blocking collectives  45.8 us (7%)
  starting transfers between devices  33.3 us (5%)
  waiting for transfers between devices  18.2 us (3%)
  other arithmetic  17.2 us (3%)
    gather x1, local copies, waits for them, and re-layouts, on_device(): jnp.take(padded.reshape(-1), index).astype(jnp.float32)  542 us
    psum x1, blocking collectives, on_device(): totals = lax.psum((square_sum, grad_sum, curve_sum), ('gx', 'gy'))  45.8 us
    ppermute x6, starting transfers between devices, padded_2(): before = lax.ppermute(last, axis, up)  25.5 us
  transfers between devices with their start and end apart: 12, of which 8 were waited for; matrix products, arithmetic and copies ran while one was open for 2% of the time, Pallas kernels for 0%

commit v1 on v0

v1 whole, which is shorter than its diff:
```python
import jax
import jax.numpy as jnp
import numpy as np
from jax import lax
from jax.experimental import pallas as pl
from jax.experimental.pallas import tpu as pltpu
from jax.sharding import PartitionSpec as P

HALO = 64
F32 = jnp.float32
BF16 = jnp.bfloat16
SPAN = 192
TILE_ROWS = 12 * SPAN
VMEM = pl.BlockSpec(memory_space=pltpu.VMEM)
SMEM = pl.BlockSpec(memory_space=pltpu.SMEM)
PARAMS = pltpu.CompilerParams(vmem_limit_bytes=40 * 1024 * 1024)


def node_weights(count):
    w = np.zeros((count + 1, 8 * count), np.float32)
    for v in range(8 * count):
        s = (v % 8 + 0.5) / 8.0
        w[v // 8, v] = 1.0 - s
        w[v // 8 + 1, v] = s
    return w


def tables():
    wx = node_weights(8)
    left = np.zeros((64, 6, 64), np.float32)
    for kc in range(6):
        left[kc * 8 : kc * 8 + 8, kc] = wx[:8]
        left[48 + kc, kc] = wx[8]
        left[56 + kc, kc] = wx[0]
    left = left.reshape(64, 384)
    expand = left.T.copy()
    expand[:, 56:] = 0.0
    wy = np.zeros((128, 128), np.float32)
    wy[:, :17] = node_weights(16).T
    as_bf = lambda a: jnp.asarray(a, BF16)
    return as_bf(left / 512.0), as_bf(wy), as_bf(expand), as_bf(wy.T)


def split(x):
    hi = x.astype(BF16)
    return hi, (x - hi.astype(F32)).astype(BF16)


def dot(a, b):
    return jnp.dot(a, b, preferred_element_type=F32)


def dot_right(w, x):
    hi, lo = split(x)
    return dot(w, hi) + dot(w, lo)


def dot_left(x, w):
    hi, lo = split(x)
    return dot(hi, w) + dot(lo, w)


def pack_kernel(up_ref, own_ref, down_ref, right_ref, left_ref):
    left = lax.broadcasted_iota(jnp.int32, (64, 128), 1) < 64
    for p in range(4):
        for s, ref in enumerate((up_ref, own_ref, down_ref)):
            a = ref[p].astype(F32)
            c = ref[p + 4].astype(F32)
            ra = pltpu.roll(a, 64, 1)
            rc = pltpu.roll(c, 64, 1)
            rows = pl.ds(s * 64, 64)
            right_ref[p, rows] = jnp.where(left, ra, c).astype(BF16)
            left_ref[p, rows] = jnp.where(left, a, rc).astype(BF16)


def column_block(rows, face, lane_from):
    lane = lax.broadcasted_iota(jnp.int32, (8, 128), 1)
    out = jnp.where(lane == 8, jnp.broadcast_to(face[:, lane_from : lane_from + 1], (8, 128)), 0.0)
    for kc in range(6):
        col = rows[kc][:, lane_from : lane_from + 1]
        out = jnp.where(lane == kc, jnp.broadcast_to(col, (8, 128)), out)
    return out


def sample_kernel(
    nx, ny, idx_ref, frac_ref, up_ref, own_ref, down_ref, lo_ref, hi_ref, ref_ref, left_ref, wy_ref,
    res_ref, slope_ref, node_ref, send_ref, sq_ref, img, arr, wgt, rsc, gsc,
):
    half = lax.broadcasted_iota(jnp.int32, (64, 128), 1) < 64
    zero = jnp.zeros((2 * SPAN, 128), F32)
    for k in range(3):
        img[pl.ds(k * TILE_ROWS, 2 * SPAN)] = zero
        img[pl.ds(k * TILE_ROWS + 10 * SPAN, 2 * SPAN)] = zero
    for p in range(4):
        for s, ref in enumerate((up_ref, own_ref, down_ref)):
            a = ref[p].astype(F32)
            c = ref[p + 4].astype(F32)
            ra = pltpu.roll(a, 64, 1)
            rc = pltpu.roll(c, 64, 1)
            rows = pl.ds(s * 64, 64)
            lo = lo_ref[p, rows].astype(F32)
            hi = hi_ref[p, rows].astype(F32)
            rlo = pltpu.roll(lo, 64, 1)
            rhi = pltpu.roll(hi, 64, 1)
            at = lambda k, q: pl.ds(k * TILE_ROWS + (q + 2) * SPAN + s * 64, 64)
            img[at(0, p)] = jnp.where(half, lo, ra)
            img[at(1, p)] = a
            img[at(2, p)] = jnp.where(half, ra, rhi)
            img[at(0, p + 4)] = jnp.where(half, rlo, rc)
            img[at(1, p + 4)] = c
            img[at(2, p + 4)] = jnp.where(half, rc, hi)
    for z in range(8):
        rsc[z] = ref_ref[z].astype(F32).reshape(8, 8, 128)

    lane = lax.broadcasted_iota(jnp.int32, (8, 128), 1)

    def element(e, carry):
        base = idx_ref[0, e]
        shift = idx_ref[1, e]
        place = idx_ref[2, e]
        first = idx_ref[3, e]
        where_to = (lane - first) & 127
        mask = where_to < 9
        for z in range(9):
            for q in range(2):
                v = img[pl.ds(base + (z * SPAN + q), 8), :]
                v = pltpu.roll(v, shift, 1)
                pltpu.store(arr.at[place, z * 2 + q], v, mask=mask)
        mask = where_to < 8
        row = place & 7
        for c in range(3):
            pltpu.store(wgt.at[c, row], jnp.full((8, 128), frac_ref[c, e], F32), mask=mask)
        return carry

    lax.fori_loop(0, 128, element, 0, unroll=4)

    phase = lane & 15
    even = phase < 8
    even_next = (phase >= 1) & (phase <= 8)

    def interpolate(cx, square):
        wz, wx, wy = wgt[0, cx], wgt[1, cx], wgt[2, cx]

        def pair(z, q):
            ev = arr[cx, z * 2 + q]
            od = arr[cx + 8, z * 2 + q]
            near = jnp.where(even, ev, od)
            far = pltpu.roll(jnp.where(even_next, ev, od), 127, 1)
            return near, far

        total = [None] * 3
        upper = [None] * 3
        prev = [pair(0, 0), pair(0, 1)]
        for z in range(8):
            cur = [pair(z + 1, 0), pair(z + 1, 1)]
            low, dzx, dx = [], [], []
            for y in range(2):
                d0 = cur[0][y] - prev[0][y]
                d1 = cur[1][y] - prev[1][y]
                l0 = prev[0][y] + wz * d0
                l1 = prev[1][y] + wz * d1
                dx.append(l1 - l0)
                low.append(l0 + wx * dx[y])
                dzx.append(d0 + wx * (d1 - d0))
            prev = cur
            slope_y = low[1] - low[0]
            value = low[0] + wy * slope_y
            slope_z = dzx[0] + wy * (dzx[1] - dzx[0])
            slope_x = dx[0] + wy * (dx[1] - dx[0])
            r = rsc[z, cx] - value
            rsc[z, cx] = r
            square = square + r * r
            for k, s in enumerate((slope_z, slope_x, slope_y)):
                slope_ref[k, z, cx] = s
                w = s * r
                u = w * ((z + 0.5) / 8.0)
                total[k] = w if z == 0 else total[k] + w
                upper[k] = u if z == 0 else upper[k] + u
        for k in range(3):
            gsc[2 * k, cx] = total[k] - upper[k]
            gsc[2 * k + 1, cx] = upper[k]
        return square

    sq_ref[...] = lax.fori_loop(0, 8, interpolate, jnp.zeros((8, 128), F32))
    res_ref[...] = rsc[...].reshape(8, 64, 128).astype(BF16)
    nodes = dot_left(dot_right(left_ref[...], gsc[...].reshape(384, 128)), wy_ref[...])
    node_ref[...] = nodes
    rows = [nodes[kc * 8 : kc * 8 + 8] for kc in range(6)]
    high, low = nodes[48:56], nodes[56:64]
    col_high = column_block(rows, high, 16)
    col_low = column_block(rows, high, 0)
    gx, gy = lax.axis_index("gx"), lax.axis_index("gy")
    send_ref[...] = jnp.zeros(send_ref.shape, F32)
    for dx in (-1, 0, 1):
        for dy in (-1, 0, 1):
            if dx == 0 and dy == 0:
                continue
            block = high if dx == 1 else low if dx == -1 else col_high if dy == 1 else col_low
            px, py = gx + dx, gy + dy

            @pl.when((px >= 0) & (px < nx) & (py >= 0) & (py < ny))
            def _():
                send_ref[px * ny + py] = block


def product_kernel(
    nx, ny, recv_ref, node_ref, slope_ref, sq_ref, expand_ref, wyt_ref, left_ref, wy_ref,
    grad_ref, hess_ref, send_ref, msc, gsc,
):
    gx, gy = lax.axis_index("gx"), lax.axis_index("gy")
    own = gx * ny + gy
    lane = lax.broadcasted_iota(jnp.int32, (8, 128), 1)
    sub = lax.broadcasted_iota(jnp.int32, (8, 128), 0)

    def block(dx, dy):
        px, py = gx + dx, gy + dy
        there = (px >= 0) & (px < nx) & (py >= 0) & (py < ny)
        return recv_ref[jnp.where(there, px * ny + py, own)]

    def column(x, at):
        return jnp.broadcast_to(x[:, at : at + 1], (8, 128))

    def with_corners(dx):
        mid = block(dx, 0)
        mid = mid + jnp.where(lane == 0, column(block(dx, -1), 16), 0.0)
        return mid + jnp.where(lane == 16, column(block(dx, 1), 0), 0.0)

    keep_x = jnp.where(gx == nx - 1, 0.0, 1.0).astype(F32)
    keep_y = jnp.where(gy == ny - 1, 0.0, 1.0).astype(F32)
    keep_lane = jnp.where(lane == 16, keep_y, 1.0)
    row_low = with_corners(-1)
    row_high = with_corners(1)
    col_low = block(0, -1)
    col_high = block(0, 1)
    grads = []
    square = jnp.zeros((8, 128), F32)
    for kc in range(6):
        g = node_ref[kc * 8 : kc * 8 + 8]
        g = g + jnp.where(sub == 0, jnp.broadcast_to(row_low[kc : kc + 1], (8, 128)), 0.0)
        g = g + jnp.where(lane == 0, column(col_low, kc), 0.0)
        g = g + jnp.where(lane == 16, column(col_high, kc), 0.0)
        g = g * keep_lane
        grads.append(g)
        grad_ref[kc] = g
        own_g = jnp.where(lane < 16, g, 0.0)
        square = square + own_g * own_g
    face = node_ref[48:56] + row_high
    face = face + jnp.where(lane == 0, column(col_low, 8), 0.0)
    face = face + jnp.where(lane == 16, column(col_high, 8), 0.0)
    face = jnp.where(sub < 6, face * keep_lane * keep_x, 0.0)
    full = jnp.concatenate(grads + [face, jnp.zeros((8, 128), F32)], axis=0)
    moved = dot_right(expand_ref[...], dot_left(full, wyt_ref[...]))
    msc[...] = moved.reshape(6, 8, 8, 128)

    def apply(cx, curve):
        m0 = [msc[2 * k, cx] for k in range(3)]
        dm = [msc[2 * k + 1, cx] - m0[k] for k in range(3)]
        total = [None] * 3
        upper = [None] * 3
        for z in range(8):
            sz = (z + 0.5) / 8.0
            s = [slope_ref[k, z, cx] for k in range(3)]
            along = s[0] * (m0[0] + sz * dm[0])
            for k in (1, 2):
                along = along + s[k] * (m0[k] + sz * dm[k])
            curve = curve + along * along
            for k in range(3):
                w = s[k] * along
                u = w * sz
                total[k] = w if z == 0 else total[k] + w
                upper[k] = u if z == 0 else upper[k] + u
        for k in range(3):
            gsc[2 * k, cx] = total[k] - upper[k]
            gsc[2 * k + 1, cx] = upper[k]
        return curve

    curve = lax.fori_loop(0, 8, apply, jnp.zeros((8, 128), F32))
    nodes = dot_left(dot_right(left_ref[...], gsc[...].reshape(384, 128)), wy_ref[...])
    rows = [nodes[kc * 8 : kc * 8 + 8] for kc in range(6)]
    for kc in range(6):
        hess_ref[kc] = rows[kc]
    high = nodes[48:56]
    col_high = column_block(rows, high, 16)
    sums = jnp.where(lane == 32, jnp.sum(sq_ref[...]), 0.0)
    sums = jnp.where(lane == 33, jnp.sum(square), sums)
    sums = jnp.where(lane == 34, jnp.sum(curve) * (1.0 / 512.0), sums)
    tail = lane >= 32
    send_ref[...] = jnp.broadcast_to(sums[None], send_ref.shape)
    for dx, dy, data in ((1, 0, high), (1, 1, high), (0, 1, col_high)):
        px, py = gx + dx, gy + dy

        @pl.when((px < nx) & (py < ny))
        def _():
            send_ref[px * ny + py] = jnp.where(tail, sums, data)


def finish_kernel(nx, ny, voxels, recv_ref, grad_ref, hess_ref, step_ref, prod_ref, misfit_ref):
    gx, gy = lax.axis_index("gx"), lax.axis_index("gy")
    own = gx * ny + gy
    lane = lax.broadcasted_iota(jnp.int32, (8, 128), 1)
    sub = lax.broadcasted_iota(jnp.int32, (8, 128), 0)

    def block(dx, dy):
        px, py = gx + dx, gy + dy
        there = (px >= 0) & (py >= 0)
        data = recv_ref[jnp.where(there, px * ny + py, own)]
        return jnp.where(there, data, 0.0)

    def column(x, at):
        return jnp.broadcast_to(x[:, at : at + 1], (8, 128))

    total = jnp.sum(recv_ref[...], axis=0)
    misfit_ref[...] = total[0:1, 32:33] * (1.0 / voxels)
    alpha = column(total, 33) / column(total, 34)
    row_low = block(-1, 0) + jnp.where(lane == 0, column(block(-1, -1), 16), 0.0)
    col_low = block(0, -1)
    for kc in range(6):
        h = hess_ref[kc]
        h = h + jnp.where(sub == 0, jnp.broadcast_to(row_low[kc : kc + 1], (8, 128)), 0.0)
        h = h + jnp.where(lane == 0, column(col_low, kc), 0.0)
        prod_ref[kc // 2, kc % 2] = h[:, :16]
        step_ref[kc // 2, kc % 2] = (alpha * grad_ref[kc])[:, :16]


def on_device(ref_image, def_image, shift_xy, shift_z, frac, connectivity):
    nx, ny = lax.axis_size("gx"), lax.axis_size("gy")
    peers = nx * ny
    sds = jax.ShapeDtypeStruct
    up = [(i, i + 1) for i in range(nx - 1)]
    below = lax.ppermute(def_image, "gx", up)
    above = lax.ppermute(def_image, "gx", [(j, i) for i, j in up])
    to_right, to_left = pl.pallas_call(
        pack_kernel,
        out_shape=(sds((4, SPAN, 128), BF16), sds((4, SPAN, 128), BF16)),
        in_specs=[VMEM] * 3,
        out_specs=(VMEM, VMEM),
        compiler_params=PARAMS,
        name="pack_halo",
    )(below, def_image, above)
    up = [(i, i + 1) for i in range(ny - 1)]
    lo = lax.ppermute(to_right, "gy", up)
    hi = lax.ppermute(to_left, "gy", [(j, i) for i, j in up])

    first = connectivity[0]
    col_x = first // 17 % 9
    col_y = first % 17
    start_x = 8 * col_x + shift_xy[0] + HALO
    start_y = 8 * col_y + shift_xy[1] + HALO
    tile = jnp.minimum(start_y // 64, 2)
    base = tile * TILE_ROWS + (shift_z + 2) * SPAN + start_x
    shift = (8 * col_y - (start_y - 64 * tile)) & 127
    place = (col_y & 1) * 8 + col_x
    idx = jnp.stack([base, shift, place, 8 * col_y])

    left, wy, expand, wyt = tables()
    residual, slopes, nodes, send, square = pl.pallas_call(
        lambda *refs: sample_kernel(nx, ny, *refs),
        out_shape=(
            sds((8, 64, 128), BF16),
            sds((3, 8, 8, 8, 128), F32),
            sds((64, 128), F32),
            sds((peers, 8, 128), F32),
            sds((8, 128), F32),
        ),
        in_specs=[SMEM, SMEM] + [VMEM] * 8,
        out_specs=(VMEM,) * 5,
        scratch_shapes=[
            pltpu.VMEM((3 * TILE_ROWS, 128), F32),
            pltpu.VMEM((16, 18, 8, 128), F32),
            pltpu.VMEM((3, 8, 8, 128), F32),
            pltpu.VMEM((8, 8, 8, 128), F32),
            pltpu.VMEM((6, 8, 8, 128), F32),
        ],
        compiler_params=PARAMS,
        name="sample_and_gradient",
    )(idx, frac, below, def_image, above, lo, hi, ref_image, left, wy)
    recv = lax.all_to_all(send, ("gx", "gy"), 0, 0, tiled=True)
    grads, hess, send = pl.pallas_call(
        lambda *refs: product_kernel(nx, ny, *refs),
        out_shape=(sds((6, 8, 128), F32), sds((6, 8, 128), F32), sds((peers, 8, 128), F32)),
        in_specs=[VMEM] * 8,
        out_specs=(VMEM,) * 3,
        scratch_shapes=[pltpu.VMEM((6, 8, 8, 128), F32), pltpu.VMEM((6, 8, 8, 128), F32)],
        compiler_params=PARAMS,
        name="gauss_newton_product",
    )(recv, nodes, slopes, square, expand, wyt, left, wy)
    recv = lax.all_to_all(send, ("gx", "gy"), 0, 0, tiled=True)
    voxels = 8 * 64 * 128 * peers
    step, product, misfit = pl.pallas_call(
        lambda *refs: finish_kernel(nx, ny, voxels, *refs),
        out_shape=(sds((3, 2, 8, 16), F32), sds((3, 2, 8, 16), F32), sds((1, 1), F32)),
        in_specs=[VMEM] * 3,
        out_specs=(VMEM,) * 3,
        compiler_params=PARAMS,
        name="finish",
    )(recv, grads, hess)
    return (residual, step, product, misfit[0, 0])


def solution(mesh):
    in_specs = (
        P(None, "gx", "gy"),
        P(None, "gx", "gy"),
        P(None, ("gx", "gy")),
        P(("gx", "gy")),
        P(None, ("gx", "gy")),
        P(None, ("gx", "gy")),
    )
    out_specs = (P(None, "gx", "gy"), P(None, None, "gx", "gy"), P(None, None, "gx", "gy"), P())
    return jax.shard_map(
        on_device, mesh=mesh, in_specs=in_specs, out_specs=out_specs, check_vma=False
    )
```

time: 684 us -> 56.6 us (0.08)
  local copies, waits for them, and re-layouts: 563 us -> 0.93 us
  starting transfers between devices: 33.3 us -> 10.2 us
  blocking collectives: 45.8 us -> 26.9 us
  other arithmetic: 17.2 us -> 2.17 us
  waiting for transfers between devices: 18.2 us -> 5.73 us
  Pallas kernels: 0 us -> 9.65 us
    gather x7 -> x0, local copies, waits for them, and re-layouts: 547 us -> none  [the longest x1 542 us: on_device(): jnp.take(padded.reshape(-1), index).astype(jnp.float32)]
    psum x1 -> x0, blocking collectives: 45.8 us -> none  [on_device(): totals = lax.psum((square_sum, grad_sum, curve_sum), ('gx', 'gy'))]
    all_to_all x0 -> x2, blocking collectives: none -> 26.9 us  [on_device(): recv = lax.all_to_all(send, ('gx', 'gy'), 0, 0, tiled=True)]
    ppermute x12 -> x4, starting transfers between devices: 33.3 us -> 10.2 us  [the longest x1 5.51 us: on_device(): below = lax.ppermute(def_image, 'gx', up)]
    ppermute x12 -> x4, waiting for transfers between devices: 18.2 us -> 5.73 us  [the longest x1 3.06 us: on_device(): below = lax.ppermute(def_image, 'gx', up)]
    scatter-add x2 -> x0, other arithmetic: 12.1 us -> none  [assemble(): acc = jnp.zeros((3, node_total), jnp.float32).at[:, connectivity.reshape(...]
    pallas_call x0 -> x4, Pallas kernels: none -> 9.65 us  [the longest x1 7.59 us: on_device(): pl.pallas_call(lambda *refs: sample_kernel(nx, ny, *refs), out_shape=(sds...]
    reshape x11 -> x0, local copies, waits for them, and re-layouts: 8.15 us -> none  [the longest x3 4.25 us: on_device(): ref_image.reshape(ez_n, 8, ex_n, 8, ey_n, 8).transpose(1, 3, 5, 0, 2, 4)]
  transfers between devices with their start and end apart: 12 -> 4, of which waited for: 8 -> 3; matrix products, arithmetic and copies ran while one was open for 2% -> 4% of each run, Pallas kernels for 0% -> 0%
where the time goes in v1:
time: 56.6 us; the launch traced here: 56.3 us
  blocking collectives  26.9 us (48%)
  starting transfers between devices  10.2 us (18%)
  Pallas kernels  9.65 us (17%)
  waiting for transfers between devices  5.73 us (10%)
  other arithmetic  2.17 us (4%)
  local copies, waits for them, and re-layouts  0.93 us (2%)
  between operations  0.74 us (1%)
    all_to_all x2, blocking collectives, on_device(): recv = lax.all_to_all(send, ('gx', 'gy'), 0, 0, tiled=True)  26.9 us
    pallas_call x1, Pallas kernels, on_device(): pl.pallas_call(lambda *refs: sample_kernel(nx, ny, *refs), out_shape=(sds...  7.59 us
    ppermute x1, starting transfers between devices, on_device(): below = lax.ppermute(def_image, 'gx', up)  5.51 us
    ppermute x1, waiting for transfers between devices, on_device(): below = lax.ppermute(def_image, 'gx', up)  3.06 us
    ppermute x1, waiting for transfers between devices, on_device(): hi = lax.ppermute(to_left, 'gy', [(j, i) for i, j in up])  2.37 us
    ppermute x1, starting transfers between devices, on_device(): lo = lax.ppermute(to_right, 'gy', up)  1.93 us
    ppermute x1, starting transfers between devices, on_device(): above = lax.ppermute(def_image, 'gx', [(j, i) for i, j in up])  1.42 us
    ppermute x1, starting transfers between devices, on_device(): hi = lax.ppermute(to_left, 'gy', [(j, i) for i, j in up])  1.29 us
  transfers between devices with their start and end apart: 4, of which 3 were waited for; matrix products, arithmetic and copies ran while one was open for 4% of the time, Pallas kernels for 0%

profile of v1, /device:TPU:0, one launch (start us, length us, event | category | flops | bytes accessed | tf_op | source)
XLA Modules:
  0.0 56.3 jit_solution(6728355980144250799)
XLA Ops:
  0.6 0.0 copy-start.7
  0.6 0.0 copy-start.8
  0.7 1.4 %collective-permute-start.1 = (bf16[8,64,128]{2,1,0:T(8,128)(2,1)}, bf16[8,64,128]{2,1,0:T(8,128)(2,1)S(1)}, u32[]{:S(2)}, u32[]{:S(2)}) collective-permute-start(bf16[8,64,128]{2,1,0:T(8,128)(2,1)} %refs_3_.1), channel_id=1, source_target_pairs={{4,0},{8,4},{12,8},{16,12},{20,16},{24,20},{28,24},{5,1},{9,5},{13... | collective-permute-start | bytes 393224 | tf_op jit(solution)/shard_map/ppermute | solution.py:331
  2.1 5.5 %collective-permute-start = (bf16[8,64,128]{2,1,0:T(8,128)(2,1)}, bf16[8,64,128]{2,1,0:T(8,128)(2,1)S(1)}, u32[]{:S(2)}, u32[]{:S(2)}) collective-permute-start(bf16[8,64,128]{2,1,0:T(8,128)(2,1)} %refs_3_.1), channel_id=1, source_target_pairs={{0,4},{4,8},{8,12},{12,16},{16,20},{20,24},{24,28},{1,5},{5,9},{9,... | collective-permute-start | bytes 393224 | tf_op jit(solution)/shard_map/ppermute | solution.py:330
  7.6 0.7 %subtract_and_fusion = (s32[1,128]{1,0:T(1,128)S(1)}, s32[1,128]{1,0:T(1,128)S(1)}) fusion(s32[2,128]{1,0:T(2,128)} %param.12, s32[8,128]{1,0:T(8,128)} %param.15), kind=kLoop, calls=%fused_computation.21 | loop fusion | flops 3712 | bytes 2048 | tf_op jit(solution)/shard_map/and | solution.py:351
  8.3 0.0 copy-done.7
  8.3 0.0 copy-done.8
  8.4 0.7 %add_bitcast_fusion = s32[1,128]{1,0:T(1,128)S(1)} fusion(s32[2,128]{1,0:T(2,128)S(1)} %copy-done.7, s32[128]{0:T(128)S(1)} %copy-done.8, s32[8,128]{1,0:T(8,128)} %param.15), kind=kLoop, calls=%fused_computation.22 | loop fusion | flops 5760 | bytes 2560 | tf_op jit(solution)/shard_map/stack | solution.py:353
  9.1 0.3 collective-permute-done.1.down_ref.refs_4_
  9.4 3.1 %collective-permute-done.up_ref.refs_2_ = bf16[8,64,128]{2,1,0:T(8,128)(2,1)S(1)} collective-permute-done((bf16[8,64,128]{2,1,0:T(8,128)(2,1)}, bf16[8,64,128]{2,1,0:T(8,128)(2,1)S(1)}, u32[]{:S(2)}, u32[]{:S(2)}) %collective-permute-start) | collective-permute-done | bytes 131104 | tf_op jit(solution)/shard_map/ppermute | solution.py:330
  12.4 0.0 copy-start
  12.4 0.9 %copy-done = bf16[8,64,128]{2,1,0:T(8,128)(2,1)S(1)} copy-done((bf16[8,64,128]{2,1,0:T(8,128)(2,1)S(1)}, bf16[8,64,128]{2,1,0:T(8,128)(2,1)}, u32[]{:S(2)}) %copy-start) | copy-done | bytes 131096
  13.3 0.0 copy-start.1
  13.3 0.0 copy-start.2
  13.3 0.0 copy-start.3
  13.3 0.2 pack_halo.1
  13.5 1.9 %collective-permute-start.2 = (bf16[4,192,128]{2,1,0:T(8,128)(2,1)S(1)}, bf16[4,192,128]{2,1,0:T(8,128)(2,1)S(1)}, u32[]{:S(2)}, u32[]{:S(2)}) collective-permute-start(bf16[4,192,128]{2,1,0:T(8,128)(2,1)S(1)} %get-tuple-element.17), channel_id=1, source_target_pairs={{0,1},{1,2},{2,3},{4,5},{5,6},{6,7},{8,9},{9,10},{10,11},{12,13},{... | collective-permute-start | bytes 589832 | tf_op jit(solution)/shard_map/ppermute | solution.py:341
  15.5 1.3 %collective-permute-start.3 = (bf16[4,192,128]{2,1,0:T(8,128)(2,1)S(1)}, bf16[4,192,128]{2,1,0:T(8,128)(2,1)S(1)}, u32[]{:S(2)}, u32[]{:S(2)}) collective-permute-start(bf16[4,192,128]{2,1,0:T(8,128)(2,1)S(1)} %get-tuple-element.18), channel_id=1, source_target_pairs={{1,0},{2,1},{3,2},{5,4},{6,5},{7,6},{9,8},{10,9},{11,10},{13,12},{... | collective-permute-start | bytes 589832 | tf_op jit(solution)/shard_map/ppermute | solution.py:342
  16.8 0.7 %fusion.1 = (s32[1,128]{1,0:T(1,128)S(1)}, s32[1,128]{1,0:T(1,128)S(1)}) fusion(s32[1,128]{1,0:T(1,128)S(1)} %get-tuple-element.31, s32[8,128]{1,0:T(8,128)} %param.15), kind=kLoop, calls=%fused_computation.16 | loop fusion | flops 2304 | bytes 2048 | tf_op jit(solution)/shard_map/add | solution.py:352
  17.5 0.0 copy-start.6
  17.5 0.0 collective-permute-done.2.refs_5_
  17.5 2.4 %collective-permute-done.3.refs_6_ = bf16[4,192,128]{2,1,0:T(8,128)(2,1)S(1)} collective-permute-done((bf16[4,192,128]{2,1,0:T(8,128)(2,1)S(1)}, bf16[4,192,128]{2,1,0:T(8,128)(2,1)S(1)}, u32[]{:S(2)}, u32[]{:S(2)}) %collective-permute-start.3) | collective-permute-done | bytes 196640 | tf_op jit(solution)/shard_map/ppermute | solution.py:342
  19.9 0.0 copy-done.1
  19.9 0.0 copy-done.2
  19.9 0.0 copy-done.3
  19.9 0.0 copy-done.6
  19.9 7.6 %sample_and_gradient.1 = (bf16[8,64,128]{2,1,0:T(8,128)(2,1)}, f32[3,8,8,8,128]{4,3,2,1,0:T(8,128)S(1)}, f32[64,128]{1,0:T(8,128)S(1)}, f32[32,8,128]{2,1,0:T(8,128)S(1)}, f32[8,128]{1,0:T(8,128)S(1)}) custom-call(s32[4,128]{1,0:T(4,128)S(1)} %pad_add_fusion.refs_0_, f32[3,128]{1,0:T(4,128)S(1)} %copy-done.6, ...), custom_call_target="tpu_custom_call" | custom-call | tf_op jit(solution)/shard_map/sample_and_gradient/pallas_call | solution.py:356
  27.5 0.0 copy-start.4
  27.5 0.0 copy-start.5
  27.5 16.9 %all_to_all.10.refs_0_ = f32[32,8,128]{2,1,0:T(8,128)S(1)} all-to-all(f32[32,8,128]{2,1,0:T(8,128)S(1)} %get-tuple-element.20), channel_id=1, replica_groups=mesh['gx'=8,'gy'=4] {'gx','gy'}, dimensions={0} | all-to-all | bytes 262144 | tf_op jit(solution)/shard_map/all_to_all | solution.py:377
  44.4 0.0 copy-done.4
  44.4 0.0 copy-done.5
  44.4 1.2 %gauss_newton_product.1 = (f32[6,8,128]{2,1,0:T(8,128)S(1)}, f32[6,8,128]{2,1,0:T(8,128)S(1)}, f32[32,8,128]{2,1,0:T(8,128)S(1)}) custom-call(f32[32,8,128]{2,1,0:T(8,128)S(1)} %all_to_all.10.refs_0_, f32[64,128]{1,0:T(8,128)S(1)} %get-tuple-element.21.refs_1_, f32[3,8,8,8,128]{4,3,2,1,0:T(8,128)S(1)} %get-tuple-element.22.refs_2_, ...), custom_call_target="tpu_custom_call" | custom-call | tf_op jit(solution)/shard_map/gauss_newton_product/pallas_call | solution.py:378
  45.5 10.0 %all_to_all.11.refs_0_ = f32[32,8,128]{2,1,0:T(8,128)S(1)} all-to-all(f32[32,8,128]{2,1,0:T(8,128)S(1)} %get-tuple-element.24), channel_id=1, replica_groups=mesh['gx'=8,'gy'=4] {'gx','gy'}, dimensions={0} | all-to-all | bytes 262144 | tf_op jit(solution)/shard_map/all_to_all | solution.py:387
  55.5 0.7 %finish.1 = (f32[3,2,8,16]{3,2,1,0:T(8,128)}, f32[3,2,8,16]{3,2,1,0:T(8,128)}, f32[1,1]{1,0:T(1,128)}) custom-call(f32[32,8,128]{2,1,0:T(8,128)S(1)} %all_to_all.11.refs_0_, f32[6,8,128]{2,1,0:T(8,128)S(1)} %get-tuple-element.25.refs_1_, f32[6,8,128]{2,1,0:T(8,128)S(1)} %get-tuple-element.26.refs_2_), custom_call_target="tpu_custom_call" | custom-call | tf_op jit(solution)/shard_map/finish/pallas_call | solution.py:389
  (1 shorter events, 0.0 us)
Async XLA Ops:
  0.6 7.7 %copy-start.7 = (s32[2,128]{1,0:T(2,128)S(1)}, s32[2,128]{1,0:T(2,128)}, u32[]{:S(2)}) copy-start(s32[2,128]{1,0:T(2,128)} %param.12) | copy-start | bytes 3076
  0.6 7.7 %copy-start.8 = (s32[128]{0:T(128)S(1)}, s32[128]{0:T(128)}, u32[]{:S(2)}) copy-start(s32[128]{0:T(128)} %param.13) | copy-start | bytes 1540
  0.7 8.7 %collective-permute-start.1 = (bf16[8,64,128]{2,1,0:T(8,128)(2,1)}, bf16[8,64,128]{2,1,0:T(8,128)(2,1)S(1)}, u32[]{:S(2)}, u32[]{:S(2)}) collective-permute-start(bf16[8,64,128]{2,1,0:T(8,128)(2,1)} %refs_3_.1), channel_id=1, source_target_pairs={{4,0},{8,4},{12,8},{16,12},{20,16},{24,20},{28,24},{5,1},{9,5},{13... | collective-permute-start | bytes 393224 | tf_op jit(solution)/shard_map/ppermute | solution.py:331
  2.1 10.3 %collective-permute-start = (bf16[8,64,128]{2,1,0:T(8,128)(2,1)}, bf16[8,64,128]{2,1,0:T(8,128)(2,1)S(1)}, u32[]{:S(2)}, u32[]{:S(2)}) collective-permute-start(bf16[8,64,128]{2,1,0:T(8,128)(2,1)} %refs_3_.1), channel_id=1, source_target_pairs={{0,4},{4,8},{8,12},{12,16},{16,20},{20,24},{24,28},{1,5},{5,9},{9,... | collective-permute-start | bytes 393224 | tf_op jit(solution)/shard_map/ppermute | solution.py:330
  12.4 0.9 %copy-start = (bf16[8,64,128]{2,1,0:T(8,128)(2,1)S(1)}, bf16[8,64,128]{2,1,0:T(8,128)(2,1)}, u32[]{:S(2)}) copy-start(bf16[8,64,128]{2,1,0:T(8,128)(2,1)} %refs_3_.1) | copy-start | bytes 393220
  13.3 6.6 %copy-start.1 = (bf16[64,384]{1,0:T(8,128)(2,1)S(1)}, bf16[64,384]{1,0:T(8,128)(2,1)}, u32[]{:S(2)}) copy-start(bf16[64,384]{1,0:T(8,128)(2,1)} %constant.60.clone.refs_8_.refs_6_) | copy-start | bytes 147460
  13.3 6.6 %copy-start.2 = (bf16[8,64,128]{2,1,0:T(8,128)(2,1)S(1)}, bf16[8,64,128]{2,1,0:T(8,128)(2,1)}, u32[]{:S(2)}) copy-start(bf16[8,64,128]{2,1,0:T(8,128)(2,1)} %refs_7_.2) | copy-start | bytes 393220
  13.3 6.6 %copy-start.3 = (bf16[128,128]{1,0:T(8,128)(2,1)S(1)}, bf16[128,128]{1,0:T(8,128)(2,1)}, u32[]{:S(2)}) copy-start(bf16[128,128]{1,0:T(8,128)(2,1)} %constant.61.clone.refs_9_.refs_7_) | copy-start | bytes 98308
  13.5 4.0 %collective-permute-start.2 = (bf16[4,192,128]{2,1,0:T(8,128)(2,1)S(1)}, bf16[4,192,128]{2,1,0:T(8,128)(2,1)S(1)}, u32[]{:S(2)}, u32[]{:S(2)}) collective-permute-start(bf16[4,192,128]{2,1,0:T(8,128)(2,1)S(1)} %get-tuple-element.17), channel_id=1, source_target_pairs={{0,1},{1,2},{2,3},{4,5},{5,6},{6,7},{8,9},{9,10},{10,11},{12,13},{... | collective-permute-start | bytes 589832 | tf_op jit(solution)/shard_map/ppermute | solution.py:341
  15.5 4.4 %collective-permute-start.3 = (bf16[4,192,128]{2,1,0:T(8,128)(2,1)S(1)}, bf16[4,192,128]{2,1,0:T(8,128)(2,1)S(1)}, u32[]{:S(2)}, u32[]{:S(2)}) collective-permute-start(bf16[4,192,128]{2,1,0:T(8,128)(2,1)S(1)} %get-tuple-element.18), channel_id=1, source_target_pairs={{1,0},{2,1},{3,2},{5,4},{6,5},{7,6},{9,8},{10,9},{11,10},{13,12},{... | collective-permute-start | bytes 589832 | tf_op jit(solution)/shard_map/ppermute | solution.py:342
  17.5 2.4 %copy-start.6 = (f32[3,128]{1,0:T(4,128)S(1)}, f32[3,128]{1,0:T(4,128)}, u32[]{:S(2)}) copy-start(f32[3,128]{1,0:T(4,128)} %refs_1_.1) | copy-start | bytes 4612
  27.5 16.9 %copy-start.4 = (bf16[384,64]{1,0:T(8,128)(2,1)S(1)}, bf16[384,64]{1,0:T(8,128)(2,1)}, u32[]{:S(2)}) copy-start(bf16[384,64]{1,0:T(8,128)(2,1)} %constant.62.clone.refs_4_) | copy-start | bytes 147460
  27.5 16.9 %copy-start.5 = (bf16[128,128]{1,0:T(8,128)(2,1)S(1)}, bf16[128,128]{1,0:T(8,128)(2,1)}, u32[]{:S(2)}) copy-start(bf16[128,128]{1,0:T(8,128)(2,1)} %constant.63.clone.refs_5_) | copy-start | bytes 98308

commit v2 on v1

--- a/solution.py
+++ b/solution.py
@@ -73,13 +73,41 @@
             left_ref[p, rows] = jnp.where(left, a, rc).astype(BF16)
 
 
-def column_block(rows, face, lane_from):
-    lane = lax.broadcasted_iota(jnp.int32, (8, 128), 1)
-    out = jnp.where(lane == 8, jnp.broadcast_to(face[:, lane_from : lane_from + 1], (8, 128)), 0.0)
+def over_sublanes(x):
+    return jnp.sum(x, axis=0, keepdims=True)
+
+
+def lanes_of(x, idx):
+    return jnp.take_along_axis(x, idx & 127, axis=1, mode="promise_in_bounds")
+
+
+def face_row(face):
+    return over_sublanes(pltpu.roll(face, 0, 1, stride=17, stride_axis=0))
+
+
+def face_of(row):
+    lane = lax.broadcasted_iota(jnp.int32, (8, 128), 1)
+    sub = lax.broadcasted_iota(jnp.int32, (8, 128), 0)
+    back = lanes_of(jnp.broadcast_to(row, (8, 128)), lane + 17 * sub)
+    return jnp.where((lane < 17) & (sub < 6), back, 0.0)
+
+
+def column_row(rows, face, at):
+    lane = lax.broadcasted_iota(jnp.int32, (8, 128), 1)
+    block = jnp.zeros((8, 128), F32)
     for kc in range(6):
-        col = rows[kc][:, lane_from : lane_from + 1]
-        out = jnp.where(lane == kc, jnp.broadcast_to(col, (8, 128)), out)
-    return out
+        block = jnp.where(lane == kc, jnp.broadcast_to(rows[kc][:, at : at + 1], (8, 128)), block)
+    edge = jnp.where(lane == 64, jnp.broadcast_to(face[:, at : at + 1], (8, 128)), 0.0)
+    block = pltpu.roll(block, 0, 1, stride=8, stride_axis=0)
+    edge = pltpu.roll(edge, 0, 1, stride=1, stride_axis=0)
+    return over_sublanes(block + edge)
+
+
+def column_of(row):
+    lane = lax.broadcasted_iota(jnp.int32, (8, 128), 1)
+    sub = lax.broadcasted_iota(jnp.int32, (8, 128), 0)
+    row = jnp.broadcast_to(row, (8, 128))
+    return lanes_of(row, lane + 8 * sub), lanes_of(row, lane + 64 + sub)
 
 
 def sample_kernel(
@@ -132,7 +160,7 @@
             pltpu.store(wgt.at[c, row], jnp.full((8, 128), frac_ref[c, e], F32), mask=mask)
         return carry
 
-    lax.fori_loop(0, 128, element, 0, unroll=4)
+    lax.fori_loop(0, 128, element, 0, unroll=16)
 
     phase = lane & 15
     even = phase < 8
@@ -187,8 +215,9 @@
     node_ref[...] = nodes
     rows = [nodes[kc * 8 : kc * 8 + 8] for kc in range(6)]
     high, low = nodes[48:56], nodes[56:64]
-    col_high = column_block(rows, high, 16)
-    col_low = column_block(rows, high, 0)
+    col_high = column_row(rows, high, 16)
+    col_low = column_row(rows, high, 0)
+    high, low = face_row(high), face_row(low)
     gx, gy = lax.axis_index("gx"), lax.axis_index("gy")
     send_ref[...] = jnp.zeros(send_ref.shape, F32)
     for dx in (-1, 0, 1):
@@ -221,17 +250,17 @@
         return jnp.broadcast_to(x[:, at : at + 1], (8, 128))
 
     def with_corners(dx):
-        mid = block(dx, 0)
-        mid = mid + jnp.where(lane == 0, column(block(dx, -1), 16), 0.0)
-        return mid + jnp.where(lane == 16, column(block(dx, 1), 0), 0.0)
+        mid = face_of(block(dx, 0))
+        mid = mid + jnp.where(lane == 0, column(face_of(block(dx, -1)), 16), 0.0)
+        return mid + jnp.where(lane == 16, column(face_of(block(dx, 1)), 0), 0.0)
 
     keep_x = jnp.where(gx == nx - 1, 0.0, 1.0).astype(F32)
     keep_y = jnp.where(gy == ny - 1, 0.0, 1.0).astype(F32)
     keep_lane = jnp.where(lane == 16, keep_y, 1.0)
     row_low = with_corners(-1)
     row_high = with_corners(1)
-    col_low = block(0, -1)
-    col_high = block(0, 1)
+    col_low, edge_low = column_of(block(0, -1))
+    col_high, edge_high = column_of(block(0, 1))
     grads = []
     square = jnp.zeros((8, 128), F32)
     for kc in range(6):
@@ -245,8 +274,8 @@
         own_g = jnp.where(lane < 16, g, 0.0)
         square = square + own_g * own_g
     face = node_ref[48:56] + row_high
-    face = face + jnp.where(lane == 0, column(col_low, 8), 0.0)
-    face = face + jnp.where(lane == 16, column(col_high, 8), 0.0)
+    face = face + jnp.where(lane == 0, column(edge_low, 0), 0.0)
+    face = face + jnp.where(lane == 16, column(edge_high, 0), 0.0)
     face = jnp.where(sub < 6, face * keep_lane * keep_x, 0.0)
     full = jnp.concatenate(grads + [face, jnp.zeros((8, 128), F32)], axis=0)
     moved = dot_right(expand_ref[...], dot_left(full, wyt_ref[...]))
@@ -279,12 +308,13 @@
     rows = [nodes[kc * 8 : kc * 8 + 8] for kc in range(6)]
     for kc in range(6):
         hess_ref[kc] = rows[kc]
-    high = nodes[48:56]
-    col_high = column_block(rows, high, 16)
-    sums = jnp.where(lane == 32, jnp.sum(sq_ref[...]), 0.0)
-    sums = jnp.where(lane == 33, jnp.sum(square), sums)
-    sums = jnp.where(lane == 34, jnp.sum(curve) * (1.0 / 512.0), sums)
-    tail = lane >= 32
+    col_high = column_row(rows, nodes[48:56], 16)
+    high = face_row(nodes[48:56])
+    spot = lane[:1]
+    sums = jnp.where(spot == 104, jnp.sum(sq_ref[...]), 0.0)
+    sums = jnp.where(spot == 105, jnp.sum(square), sums)
+    sums = jnp.where(spot == 106, jnp.sum(curve) * (1.0 / 512.0), sums)
+    tail = spot >= 104
     send_ref[...] = jnp.broadcast_to(sums[None], send_ref.shape)
     for dx, dy, data in ((1, 0, high), (1, 1, high), (0, 1, col_high)):
         px, py = gx + dx, gy + dy
@@ -310,10 +340,11 @@
         return jnp.broadcast_to(x[:, at : at + 1], (8, 128))
 
     total = jnp.sum(recv_ref[...], axis=0)
-    misfit_ref[...] = total[0:1, 32:33] * (1.0 / voxels)
-    alpha = column(total, 33) / column(total, 34)
-    row_low = block(-1, 0) + jnp.where(lane == 0, column(block(-1, -1), 16), 0.0)
-    col_low = block(0, -1)
+    misfit_ref[...] = total[:, 104:105] * (1.0 / voxels)
+    total = jnp.broadcast_to(total, (8, 128))
+    alpha = column(total, 105) / column(total, 106)
+    row_low = face_of(block(-1, 0)) + jnp.where(lane == 0, column(face_of(block(-1, -1)), 16), 0.0)
+    col_low = column_of(block(0, -1))[0]
     for kc in range(6):
         h = hess_ref[kc]
         h = h + jnp.where(sub == 0, jnp.broadcast_to(row_low[kc : kc + 1], (8, 128)), 0.0)
@@ -359,7 +390,7 @@
             sds((8, 64, 128), BF16),
             sds((3, 8, 8, 8, 128), F32),
             sds((64, 128), F32),
-            sds((peers, 8, 128), F32),
+            sds((peers, 1, 128), F32),
             sds((8, 128), F32),
         ),
         in_specs=[SMEM, SMEM] + [VMEM] * 8,
@@ -377,7 +408,7 @@
     recv = lax.all_to_all(send, ("gx", "gy"), 0, 0, tiled=True)
     grads, hess, send = pl.pallas_call(
         lambda *refs: product_kernel(nx, ny, *refs),
-        out_shape=(sds((6, 8, 128), F32), sds((6, 8, 128), F32), sds((peers, 8, 128), F32)),
+        out_shape=(sds((6, 8, 128), F32), sds((6, 8, 128), F32), sds((peers, 1, 128), F32)),
         in_specs=[VMEM] * 8,
         out_specs=(VMEM,) * 3,
         scratch_shapes=[pltpu.VMEM((6, 8, 8, 128), F32), pltpu.VMEM((6, 8, 8, 128), F32)],

time: 56.6 us -> 53.1 us (0.938)
  blocking collectives: 26.9 us -> 24.6 us
  Pallas kernels: 9.65 us -> 8.31 us
    all_to_all x2, blocking collectives: 26.9 us -> 24.6 us  [on_device(): recv = lax.all_to_all(send, ('gx', 'gy'), 0, 0, tiled=True)]
    pallas_call x1, Pallas kernels: 7.59 us -> 6.03 us  [on_device(): pl.pallas_call(lambda *refs: sample_kernel(nx, ny, *refs), out_shape=(sds...]
where the time goes in v2:
time: 53.1 us; the launch traced here: 52.7 us
  blocking collectives  24.6 us (46%)
  starting transfers between devices  10.2 us (19%)
  Pallas kernels  8.31 us (16%)
  waiting for transfers between devices  5.73 us (11%)
  other arithmetic  2.17 us (4%)
  local copies, waits for them, and re-layouts  0.94 us (2%)
  between operations  0.76 us (1%)
    all_to_all x2, blocking collectives, on_device(): recv = lax.all_to_all(send, ('gx', 'gy'), 0, 0, tiled=True)  24.6 us
    pallas_call x1, Pallas kernels, on_device(): pl.pallas_call(lambda *refs: sample_kernel(nx, ny, *refs), out_shape=(sds...  6.03 us
    ppermute x1, starting transfers between devices, on_device(): below = lax.ppermute(def_image, 'gx', up)  5.51 us
    ppermute x1, waiting for transfers between devices, on_device(): below = lax.ppermute(def_image, 'gx', up)  3.06 us
    ppermute x1, waiting for transfers between devices, on_device(): hi = lax.ppermute(to_left, 'gy', [(j, i) for i, j in up])  2.37 us
    ppermute x1, starting transfers between devices, on_device(): lo = lax.ppermute(to_right, 'gy', up)  1.93 us
    ppermute x1, starting transfers between devices, on_device(): above = lax.ppermute(def_image, 'gx', [(j, i) for i, j in up])  1.42 us
    pallas_call x1, Pallas kernels, on_device(): pl.pallas_call(lambda *refs: product_kernel(nx, ny, *refs), out_shape=(sd...  1.32 us
  transfers between devices with their start and end apart: 4, of which 3 were waited for; matrix products, arithmetic and copies ran while one was open for 4% of the time, Pallas kernels for 0%

profile of v2, /device:TPU:0, one launch (start us, length us, event | category | flops | bytes accessed | tf_op | source)
XLA Modules:
  0.0 52.7 jit_solution(4635275858691578260)
XLA Ops:
  0.6 0.0 copy-start.7
  0.6 0.0 copy-start.8
  0.7 1.4 %collective-permute-start.1 = (bf16[8,64,128]{2,1,0:T(8,128)(2,1)}, bf16[8,64,128]{2,1,0:T(8,128)(2,1)S(1)}, u32[]{:S(2)}, u32[]{:S(2)}) collective-permute-start(bf16[8,64,128]{2,1,0:T(8,128)(2,1)} %refs_3_.1), channel_id=1, source_target_pairs={{4,0},{8,4},{12,8},{16,12},{20,16},{24,20},{28,24},{5,1},{9,5},{13... | collective-permute-start | bytes 393224 | tf_op jit(solution)/shard_map/ppermute | solution.py:362
  2.1 5.5 %collective-permute-start = (bf16[8,64,128]{2,1,0:T(8,128)(2,1)}, bf16[8,64,128]{2,1,0:T(8,128)(2,1)S(1)}, u32[]{:S(2)}, u32[]{:S(2)}) collective-permute-start(bf16[8,64,128]{2,1,0:T(8,128)(2,1)} %refs_3_.1), channel_id=1, source_target_pairs={{0,4},{4,8},{8,12},{12,16},{16,20},{20,24},{24,28},{1,5},{5,9},{9,... | collective-permute-start | bytes 393224 | tf_op jit(solution)/shard_map/ppermute | solution.py:361
  7.6 0.7 %subtract_and_fusion = (s32[1,128]{1,0:T(1,128)S(1)}, s32[1,128]{1,0:T(1,128)S(1)}) fusion(s32[2,128]{1,0:T(2,128)} %param.12, s32[8,128]{1,0:T(8,128)} %param.15), kind=kLoop, calls=%fused_computation.21 | loop fusion | flops 3712 | bytes 2048 | tf_op jit(solution)/shard_map/and | solution.py:382
  8.3 0.0 copy-done.7
  8.3 0.0 copy-done.8
  8.4 0.7 %add_bitcast_fusion = s32[1,128]{1,0:T(1,128)S(1)} fusion(s32[2,128]{1,0:T(2,128)S(1)} %copy-done.7, s32[128]{0:T(128)S(1)} %copy-done.8, s32[8,128]{1,0:T(8,128)} %param.15), kind=kLoop, calls=%fused_computation.22 | loop fusion | flops 5760 | bytes 2560 | tf_op jit(solution)/shard_map/stack | solution.py:384
  9.1 0.3 collective-permute-done.1.down_ref.refs_4_
  9.4 3.1 %collective-permute-done.up_ref.refs_2_ = bf16[8,64,128]{2,1,0:T(8,128)(2,1)S(1)} collective-permute-done((bf16[8,64,128]{2,1,0:T(8,128)(2,1)}, bf16[8,64,128]{2,1,0:T(8,128)(2,1)S(1)}, u32[]{:S(2)}, u32[]{:S(2)}) %collective-permute-start) | collective-permute-done | bytes 131104 | tf_op jit(solution)/shard_map/ppermute | solution.py:361
  12.4 0.0 copy-start
  12.4 0.9 %copy-done = bf16[8,64,128]{2,1,0:T(8,128)(2,1)S(1)} copy-done((bf16[8,64,128]{2,1,0:T(8,128)(2,1)S(1)}, bf16[8,64,128]{2,1,0:T(8,128)(2,1)}, u32[]{:S(2)}) %copy-start) | copy-done | bytes 131096
  13.3 0.0 copy-start.1
  13.3 0.0 copy-start.2
  13.3 0.0 copy-start.3
  13.3 0.2 pack_halo.1
  13.5 1.9 %collective-permute-start.2 = (bf16[4,192,128]{2,1,0:T(8,128)(2,1)S(1)}, bf16[4,192,128]{2,1,0:T(8,128)(2,1)S(1)}, u32[]{:S(2)}, u32[]{:S(2)}) collective-permute-start(bf16[4,192,128]{2,1,0:T(8,128)(2,1)S(1)} %get-tuple-element.17), channel_id=1, source_target_pairs={{0,1},{1,2},{2,3},{4,5},{5,6},{6,7},{8,9},{9,10},{10,11},{12,13},{... | collective-permute-start | bytes 589832 | tf_op jit(solution)/shard_map/ppermute | solution.py:372
  15.5 1.3 %collective-permute-start.3 = (bf16[4,192,128]{2,1,0:T(8,128)(2,1)S(1)}, bf16[4,192,128]{2,1,0:T(8,128)(2,1)S(1)}, u32[]{:S(2)}, u32[]{:S(2)}) collective-permute-start(bf16[4,192,128]{2,1,0:T(8,128)(2,1)S(1)} %get-tuple-element.18), channel_id=1, source_target_pairs={{1,0},{2,1},{3,2},{5,4},{6,5},{7,6},{9,8},{10,9},{11,10},{13,12},{... | collective-permute-start | bytes 589832 | tf_op jit(solution)/shard_map/ppermute | solution.py:373
  16.8 0.7 %fusion.1 = (s32[1,128]{1,0:T(1,128)S(1)}, s32[1,128]{1,0:T(1,128)S(1)}) fusion(s32[1,128]{1,0:T(1,128)S(1)} %get-tuple-element.31, s32[8,128]{1,0:T(8,128)} %param.15), kind=kLoop, calls=%fused_computation.16 | loop fusion | flops 2304 | bytes 2048 | tf_op jit(solution)/shard_map/add | solution.py:383
  17.5 0.0 copy-start.6
  17.5 0.0 collective-permute-done.2.refs_5_
  17.5 2.4 %collective-permute-done.3.refs_6_ = bf16[4,192,128]{2,1,0:T(8,128)(2,1)S(1)} collective-permute-done((bf16[4,192,128]{2,1,0:T(8,128)(2,1)S(1)}, bf16[4,192,128]{2,1,0:T(8,128)(2,1)S(1)}, u32[]{:S(2)}, u32[]{:S(2)}) %collective-permute-start.3) | collective-permute-done | bytes 196640 | tf_op jit(solution)/shard_map/ppermute | solution.py:373
  19.9 0.0 copy-done.1
  19.9 0.0 copy-done.2
  19.9 0.0 copy-done.3
  19.9 0.0 copy-done.6
  19.9 0.0 copy-start.4
  19.9 6.0 %sample_and_gradient.1 = (bf16[8,64,128]{2,1,0:T(8,128)(2,1)}, f32[3,8,8,8,128]{4,3,2,1,0:T(8,128)S(1)}, f32[64,128]{1,0:T(8,128)S(1)}, f32[32,1,128]{2,1,0:T(1,128)S(1)}, f32[8,128]{1,0:T(8,128)S(1)}) custom-call(s32[4,128]{1,0:T(4,128)S(1)} %pad_add_fusion.refs_0_, f32[3,128]{1,0:T(4,128)S(1)} %copy-done.6, ...), custom_call_target="tpu_custom_call" | custom-call | tf_op jit(solution)/shard_map/sample_and_gradient/pallas_call | solution.py:387
  25.9 0.0 copy-start.5
  25.9 15.8 %all_to_all.10.refs_0_ = f32[32,1,128]{2,1,0:T(1,128)S(1)} all-to-all(f32[32,1,128]{2,1,0:T(1,128)S(1)} %get-tuple-element.20), channel_id=1, replica_groups=mesh['gx'=8,'gy'=4] {'gx','gy'}, dimensions={0} | all-to-all | bytes 32768 | tf_op jit(solution)/shard_map/all_to_all | solution.py:408
  41.8 0.0 copy-done.4
  41.8 0.0 copy-done.5
  41.8 1.3 %gauss_newton_product.1 = (f32[6,8,128]{2,1,0:T(8,128)S(1)}, f32[6,8,128]{2,1,0:T(8,128)S(1)}, f32[32,1,128]{2,1,0:T(1,128)S(1)}) custom-call(f32[32,1,128]{2,1,0:T(1,128)S(1)} %all_to_all.10.refs_0_, f32[64,128]{1,0:T(8,128)S(1)} %get-tuple-element.21.refs_1_, f32[3,8,8,8,128]{4,3,2,1,0:T(8,128)S(1)} %get-tuple-element.22.refs_2_, ...), custom_call_target="tpu_custom_call" | custom-call | tf_op jit(solution)/shard_map/gauss_newton_product/pallas_call | solution.py:409
  43.1 8.8 %all_to_all.11.refs_0_ = f32[32,1,128]{2,1,0:T(1,128)S(1)} all-to-all(f32[32,1,128]{2,1,0:T(1,128)S(1)} %get-tuple-element.24), channel_id=1, replica_groups=mesh['gx'=8,'gy'=4] {'gx','gy'}, dimensions={0} | all-to-all | bytes 32768 | tf_op jit(solution)/shard_map/all_to_all | solution.py:418
  51.9 0.8 %finish.1 = (f32[3,2,8,16]{3,2,1,0:T(8,128)}, f32[3,2,8,16]{3,2,1,0:T(8,128)}, f32[1,1]{1,0:T(1,128)}) custom-call(f32[32,1,128]{2,1,0:T(1,128)S(1)} %all_to_all.11.refs_0_, f32[6,8,128]{2,1,0:T(8,128)S(1)} %get-tuple-element.25.refs_1_, f32[6,8,128]{2,1,0:T(8,128)S(1)} %get-tuple-element.26.refs_2_), custom_call_target="tpu_custom_call" | custom-call | tf_op jit(solution)/shard_map/finish/pallas_call | solution.py:420
  (1 shorter events, 0.0 us)
Async XLA Ops:
  0.6 7.7 %copy-start.7 = (s32[2,128]{1,0:T(2,128)S(1)}, s32[2,128]{1,0:T(2,128)}, u32[]{:S(2)}) copy-start(s32[2,128]{1,0:T(2,128)} %param.12) | copy-start | bytes 3076
  0.6 7.7 %copy-start.8 = (s32[128]{0:T(128)S(1)}, s32[128]{0:T(128)}, u32[]{:S(2)}) copy-start(s32[128]{0:T(128)} %param.13) | copy-start | bytes 1540
  0.7 8.7 %collective-permute-start.1 = (bf16[8,64,128]{2,1,0:T(8,128)(2,1)}, bf16[8,64,128]{2,1,0:T(8,128)(2,1)S(1)}, u32[]{:S(2)}, u32[]{:S(2)}) collective-permute-start(bf16[8,64,128]{2,1,0:T(8,128)(2,1)} %refs_3_.1), channel_id=1, source_target_pairs={{4,0},{8,4},{12,8},{16,12},{20,16},{24,20},{28,24},{5,1},{9,5},{13... | collective-permute-start | bytes 393224 | tf_op jit(solution)/shard_map/ppermute | solution.py:362
  2.1 10.3 %collective-permute-start = (bf16[8,64,128]{2,1,0:T(8,128)(2,1)}, bf16[8,64,128]{2,1,0:T(8,128)(2,1)S(1)}, u32[]{:S(2)}, u32[]{:S(2)}) collective-permute-start(bf16[8,64,128]{2,1,0:T(8,128)(2,1)} %refs_3_.1), channel_id=1, source_target_pairs={{0,4},{4,8},{8,12},{12,16},{16,20},{20,24},{24,28},{1,5},{5,9},{9,... | collective-permute-start | bytes 393224 | tf_op jit(solution)/shard_map/ppermute | solution.py:361
  12.4 0.9 %copy-start = (bf16[8,64,128]{2,1,0:T(8,128)(2,1)S(1)}, bf16[8,64,128]{2,1,0:T(8,128)(2,1)}, u32[]{:S(2)}) copy-start(bf16[8,64,128]{2,1,0:T(8,128)(2,1)} %refs_3_.1) | copy-start | bytes 393220
  13.3 6.6 %copy-start.1 = (bf16[64,384]{1,0:T(8,128)(2,1)S(1)}, bf16[64,384]{1,0:T(8,128)(2,1)}, u32[]{:S(2)}) copy-start(bf16[64,384]{1,0:T(8,128)(2,1)} %constant.60.clone.refs_8_.refs_6_) | copy-start | bytes 147460
  13.3 6.6 %copy-start.2 = (bf16[8,64,128]{2,1,0:T(8,128)(2,1)S(1)}, bf16[8,64,128]{2,1,0:T(8,128)(2,1)}, u32[]{:S(2)}) copy-start(bf16[8,64,128]{2,1,0:T(8,128)(2,1)} %refs_7_.2) | copy-start | bytes 393220
  13.3 6.6 %copy-start.3 = (bf16[128,128]{1,0:T(8,128)(2,1)S(1)}, bf16[128,128]{1,0:T(8,128)(2,1)}, u32[]{:S(2)}) copy-start(bf16[128,128]{1,0:T(8,128)(2,1)} %constant.61.clone.refs_9_.refs_7_) | copy-start | bytes 98308
  13.5 4.0 %collective-permute-start.2 = (bf16[4,192,128]{2,1,0:T(8,128)(2,1)S(1)}, bf16[4,192,128]{2,1,0:T(8,128)(2,1)S(1)}, u32[]{:S(2)}, u32[]{:S(2)}) collective-permute-start(bf16[4,192,128]{2,1,0:T(8,128)(2,1)S(1)} %get-tuple-element.17), channel_id=1, source_target_pairs={{0,1},{1,2},{2,3},{4,5},{5,6},{6,7},{8,9},{9,10},{10,11},{12,13},{... | collective-permute-start | bytes 589832 | tf_op jit(solution)/shard_map/ppermute | solution.py:372
  15.5 4.4 %collective-permute-start.3 = (bf16[4,192,128]{2,1,0:T(8,128)(2,1)S(1)}, bf16[4,192,128]{2,1,0:T(8,128)(2,1)S(1)}, u32[]{:S(2)}, u32[]{:S(2)}) collective-permute-start(bf16[4,192,128]{2,1,0:T(8,128)(2,1)S(1)} %get-tuple-element.18), channel_id=1, source_target_pairs={{1,0},{2,1},{3,2},{5,4},{6,5},{7,6},{9,8},{10,9},{11,10},{13,12},{... | collective-permute-start | bytes 589832 | tf_op jit(solution)/shard_map/ppermute | solution.py:373
  17.5 2.4 %copy-start.6 = (f32[3,128]{1,0:T(4,128)S(1)}, f32[3,128]{1,0:T(4,128)}, u32[]{:S(2)}) copy-start(f32[3,128]{1,0:T(4,128)} %refs_1_.1) | copy-start | bytes 4612
  19.9 21.9 %copy-start.4 = (bf16[384,64]{1,0:T(8,128)(2,1)S(1)}, bf16[384,64]{1,0:T(8,128)(2,1)}, u32[]{:S(2)}) copy-start(bf16[384,64]{1,0:T(8,128)(2,1)} %constant.62.clone.refs_4_) | copy-start | bytes 147460
  25.9 15.8 %copy-start.5 = (bf16[128,128]{1,0:T(8,128)(2,1)S(1)}, bf16[128,128]{1,0:T(8,128)(2,1)}, u32[]{:S(2)}) copy-start(bf16[128,128]{1,0:T(8,128)(2,1)} %constant.63.clone.refs_5_) | copy-start | bytes 98308

commit v3 on v2

--- a/solution.py
+++ b/solution.py
@@ -218,18 +218,8 @@
     col_high = column_row(rows, high, 16)
     col_low = column_row(rows, high, 0)
     high, low = face_row(high), face_row(low)
-    gx, gy = lax.axis_index("gx"), lax.axis_index("gy")
-    send_ref[...] = jnp.zeros(send_ref.shape, F32)
-    for dx in (-1, 0, 1):
-        for dy in (-1, 0, 1):
-            if dx == 0 and dy == 0:
-                continue
-            block = high if dx == 1 else low if dx == -1 else col_high if dy == 1 else col_low
-            px, py = gx + dx, gy + dy
-
-            @pl.when((px >= 0) & (px < nx) & (py >= 0) & (py < ny))
-            def _():
-                send_ref[px * ny + py] = block
+    for n, row in enumerate((high, low, col_high, col_low)):
+        send_ref[n : n + 1] = row
 
 
 def product_kernel(
@@ -244,7 +234,8 @@
     def block(dx, dy):
         px, py = gx + dx, gy + dy
         there = (px >= 0) & (px < nx) & (py >= 0) & (py < ny)
-        return recv_ref[jnp.where(there, px * ny + py, own)]
+        n = 0 if dx == -1 else 1 if dx == 1 else 2 if dy == -1 else 3
+        return jnp.where(there, recv_ref[jnp.where(there, px * ny + py, own), n : n + 1], 0.0)
 
     def column(x, at):
         return jnp.broadcast_to(x[:, at : at + 1], (8, 128))
@@ -314,14 +305,8 @@
     sums = jnp.where(spot == 104, jnp.sum(sq_ref[...]), 0.0)
     sums = jnp.where(spot == 105, jnp.sum(square), sums)
     sums = jnp.where(spot == 106, jnp.sum(curve) * (1.0 / 512.0), sums)
-    tail = spot >= 104
-    send_ref[...] = jnp.broadcast_to(sums[None], send_ref.shape)
-    for dx, dy, data in ((1, 0, high), (1, 1, high), (0, 1, col_high)):
-        px, py = gx + dx, gy + dy
-
-        @pl.when((px < nx) & (py < ny))
-        def _():
-            send_ref[px * ny + py] = jnp.where(tail, sums, data)
+    send_ref[0:1] = jnp.where(spot >= 104, sums, high)
+    send_ref[1:2] = col_high
 
 
 def finish_kernel(nx, ny, voxels, recv_ref, grad_ref, hess_ref, step_ref, prod_ref, misfit_ref):
@@ -333,13 +318,14 @@
     def block(dx, dy):
         px, py = gx + dx, gy + dy
         there = (px >= 0) & (py >= 0)
-        data = recv_ref[jnp.where(there, px * ny + py, own)]
+        n = 0 if dx == -1 else 1
+        data = recv_ref[jnp.where(there, px * ny + py, own), n : n + 1]
         return jnp.where(there, data, 0.0)
 
     def column(x, at):
         return jnp.broadcast_to(x[:, at : at + 1], (8, 128))
 
-    total = jnp.sum(recv_ref[...], axis=0)
+    total = jnp.sum(recv_ref[...], axis=0)[0:1]
     misfit_ref[...] = total[:, 104:105] * (1.0 / voxels)
     total = jnp.broadcast_to(total, (8, 128))
     alpha = column(total, 105) / column(total, 106)
@@ -390,7 +376,7 @@
             sds((8, 64, 128), BF16),
             sds((3, 8, 8, 8, 128), F32),
             sds((64, 128), F32),
-            sds((peers, 1, 128), F32),
+            sds((4, 128), F32),
             sds((8, 128), F32),
         ),
         in_specs=[SMEM, SMEM] + [VMEM] * 8,
@@ -405,17 +391,17 @@
         compiler_params=PARAMS,
         name="sample_and_gradient",
     )(idx, frac, below, def_image, above, lo, hi, ref_image, left, wy)
-    recv = lax.all_to_all(send, ("gx", "gy"), 0, 0, tiled=True)
+    recv = lax.all_gather(send, ("gx", "gy"))
     grads, hess, send = pl.pallas_call(
         lambda *refs: product_kernel(nx, ny, *refs),
-        out_shape=(sds((6, 8, 128), F32), sds((6, 8, 128), F32), sds((peers, 1, 128), F32)),
+        out_shape=(sds((6, 8, 128), F32), sds((6, 8, 128), F32), sds((2, 128), F32)),
         in_specs=[VMEM] * 8,
         out_specs=(VMEM,) * 3,
         scratch_shapes=[pltpu.VMEM((6, 8, 8, 128), F32), pltpu.VMEM((6, 8, 8, 128), F32)],
         compiler_params=PARAMS,
         name="gauss_newton_product",
     )(recv, nodes, slopes, square, expand, wyt, left, wy)
-    recv = lax.all_to_all(send, ("gx", "gy"), 0, 0, tiled=True)
+    recv = lax.all_gather(send, ("gx", "gy"))
     voxels = 8 * 64 * 128 * peers
     step, product, misfit = pl.pallas_call(
         lambda *refs: finish_kernel(nx, ny, voxels, *refs),

time: 53.1 us -> 109 us (2.05)
  blocking collectives: 24.6 us -> 80.4 us
    all_gather x0 -> x2, blocking collectives: none -> 80.4 us  [on_device(): recv = lax.all_gather(send, ('gx', 'gy'))]
    all_to_all x2 -> x0, blocking collectives: 24.6 us -> none  [on_device(): recv = lax.all_to_all(send, ('gx', 'gy'), 0, 0, tiled=True)]
  transfers between devices with their start and end apart: 4 -> 4, of which waited for: 3 -> 3; matrix products, arithmetic and copies ran while one was open for 4% -> 2% of each run, Pallas kernels for 0% -> 0%
where the time goes in v3:
time: 109 us; the launch traced here: 108 us
  blocking collectives  80.4 us (74%)
  starting transfers between devices  10.2 us (9%)
  Pallas kernels  8.22 us (8%)
  waiting for transfers between devices  5.73 us (5%)
  other arithmetic  2.17 us (2%)
    all_gather x2, blocking collectives, on_device(): recv = lax.all_gather(send, ('gx', 'gy'))  80.4 us
    pallas_call x1, Pallas kernels, on_device(): pl.pallas_call(lambda *refs: sample_kernel(nx, ny, *refs), out_shape=(sds...  5.95 us
    ppermute x1, starting transfers between devices, on_device(): below = lax.ppermute(def_image, 'gx', up)  5.51 us
    ppermute x1, waiting for transfers between devices, on_device(): below = lax.ppermute(def_image, 'gx', up)  3.06 us
    ppermute x1, waiting for transfers between devices, on_device(): hi = lax.ppermute(to_left, 'gy', [(j, i) for i, j in up])  2.37 us
  transfers between devices with their start and end apart: 4, of which 3 were waited for; matrix products, arithmetic and copies ran while one was open for 2% of the time, Pallas kernels for 0%

profile of v3, /device:TPU:0, one launch (start us, length us, event | category | flops | bytes accessed | tf_op | source)
XLA Modules:
  0.0 108.4 jit_solution(16803115959523854907)
XLA Ops:
  0.6 0.0 copy-start.7
  0.6 0.0 copy-start.8
  0.7 1.4 %collective-permute-start.1 = (bf16[8,64,128]{2,1,0:T(8,128)(2,1)}, bf16[8,64,128]{2,1,0:T(8,128)(2,1)S(1)}, u32[]{:S(2)}, u32[]{:S(2)}) collective-permute-start(bf16[8,64,128]{2,1,0:T(8,128)(2,1)} %refs_3_.1), channel_id=1, source_target_pairs={{4,0},{8,4},{12,8},{16,12},{20,16},{24,20},{28,24},{5,1},{9,5},{13... | collective-permute-start | bytes 393224 | tf_op jit(solution)/shard_map/ppermute | solution.py:348
  2.1 5.5 %collective-permute-start = (bf16[8,64,128]{2,1,0:T(8,128)(2,1)}, bf16[8,64,128]{2,1,0:T(8,128)(2,1)S(1)}, u32[]{:S(2)}, u32[]{:S(2)}) collective-permute-start(bf16[8,64,128]{2,1,0:T(8,128)(2,1)} %refs_3_.1), channel_id=1, source_target_pairs={{0,4},{4,8},{8,12},{12,16},{16,20},{20,24},{24,28},{1,5},{5,9},{9,... | collective-permute-start | bytes 393224 | tf_op jit(solution)/shard_map/ppermute | solution.py:347
  7.6 0.7 subtract_and_fusion
  8.3 0.0 copy-done.7
  8.3 0.0 copy-done.8
  8.4 0.7 add_bitcast_fusion
  9.1 0.3 collective-permute-done.1.down_ref.refs_4_
  9.4 3.1 %collective-permute-done.up_ref.refs_2_ = bf16[8,64,128]{2,1,0:T(8,128)(2,1)S(1)} collective-permute-done((bf16[8,64,128]{2,1,0:T(8,128)(2,1)}, bf16[8,64,128]{2,1,0:T(8,128)(2,1)S(1)}, u32[]{:S(2)}, u32[]{:S(2)}) %collective-permute-start) | collective-permute-done | bytes 131104 | tf_op jit(solution)/shard_map/ppermute | solution.py:347
  12.4 0.0 copy-start
  12.4 0.9 copy-done
  13.3 0.0 copy-start.1
  13.3 0.0 copy-start.2
  13.3 0.0 copy-start.3
  13.3 0.2 pack_halo.1
  13.5 1.9 %collective-permute-start.2 = (bf16[4,192,128]{2,1,0:T(8,128)(2,1)S(1)}, bf16[4,192,128]{2,1,0:T(8,128)(2,1)S(1)}, u32[]{:S(2)}, u32[]{:S(2)}) collective-permute-start(bf16[4,192,128]{2,1,0:T(8,128)(2,1)S(1)} %get-tuple-element.17), channel_id=1, source_target_pairs={{0,1},{1,2},{2,3},{4,5},{5,6},{6,7},{8,9},{9,10},{10,11},{12,13},{... | collective-permute-start | bytes 589832 | tf_op jit(solution)/shard_map/ppermute | solution.py:358
  15.5 1.3 %collective-permute-start.3 = (bf16[4,192,128]{2,1,0:T(8,128)(2,1)S(1)}, bf16[4,192,128]{2,1,0:T(8,128)(2,1)S(1)}, u32[]{:S(2)}, u32[]{:S(2)}) collective-permute-start(bf16[4,192,128]{2,1,0:T(8,128)(2,1)S(1)} %get-tuple-element.18), channel_id=1, source_target_pairs={{1,0},{2,1},{3,2},{5,4},{6,5},{7,6},{9,8},{10,9},{11,10},{13,12},{... | collective-permute-start | bytes 589832 | tf_op jit(solution)/shard_map/ppermute | solution.py:359
  16.8 0.7 fusion.1
  17.5 0.0 copy-start.6
  17.5 0.0 collective-permute-done.2.refs_5_
  17.5 2.4 %collective-permute-done.3.refs_6_ = bf16[4,192,128]{2,1,0:T(8,128)(2,1)S(1)} collective-permute-done((bf16[4,192,128]{2,1,0:T(8,128)(2,1)S(1)}, bf16[4,192,128]{2,1,0:T(8,128)(2,1)S(1)}, u32[]{:S(2)}, u32[]{:S(2)}) %collective-permute-start.3) | collective-permute-done | bytes 196640 | tf_op jit(solution)/shard_map/ppermute | solution.py:359
  19.9 0.0 copy-done.1
  19.9 0.0 copy-done.2
  19.9 0.0 copy-done.3
  19.9 0.0 copy-done.6
  19.9 0.0 copy-start.4
  19.9 6.0 %sample_and_gradient.1 = (bf16[8,64,128]{2,1,0:T(8,128)(2,1)}, f32[3,8,8,8,128]{4,3,2,1,0:T(8,128)S(1)}, f32[64,128]{1,0:T(8,128)S(1)}, f32[4,128]{1,0:T(4,128)S(1)}, f32[8,128]{1,0:T(8,128)S(1)}) custom-call(s32[4,128]{1,0:T(4,128)S(1)} %pad_add_fusion.refs_0_, f32[3,128]{1,0:T(4,128)S(1)} %copy-done.6, ...), custom_call_target="tpu_custom_call" | custom-call | tf_op jit(solution)/shard_map/sample_and_gradient/pallas_call | solution.py:373
  25.9 0.0 copy-start.5
  25.9 43.7 %all-gather.2.refs_0_ = f32[32,4,128]{2,1,0:T(4,128)S(1)} all-gather(f32[1,4,128]{2,1,0:T(4,128)S(1)} %bitcast.30), channel_id=2, replica_groups=mesh['gx'=8,'gy'=4] {'gx','gy'}, dimensions={0}, use_global_device_ids=true | all-gather | bytes 67584 | tf_op jit(solution)/shard_map/all_gather | solution.py:394
  69.6 0.0 copy-done.4
  69.6 0.0 copy-done.5
  69.6 1.3 %gauss_newton_product.1 = (f32[6,8,128]{2,1,0:T(8,128)S(1)}, f32[6,8,128]{2,1,0:T(8,128)S(1)}, f32[2,128]{1,0:T(2,128)S(1)}) custom-call(f32[32,4,128]{2,1,0:T(4,128)S(1)} %all-gather.2.refs_0_, f32[64,128]{1,0:T(8,128)S(1)} %get-tuple-element.21.refs_1_, f32[3,8,8,8,128]{4,3,2,1,0:T(8,128)S(1)} %get-tuple-element.22.refs_2_, ...), custom_call_target="tpu_custom_call" | custom-call | tf_op jit(solution)/shard_map/gauss_newton_product/pallas_call | solution.py:395
  70.9 36.7 %all-gather.3.refs_0_ = f32[32,2,128]{2,1,0:T(2,128)S(1)} all-gather(f32[1,2,128]{2,1,0:T(2,128)S(1)} %bitcast.31), channel_id=3, replica_groups=mesh['gx'=8,'gy'=4] {'gx','gy'}, dimensions={0}, use_global_device_ids=true | all-gather | bytes 33792 | tf_op jit(solution)/shard_map/all_gather | solution.py:404
  107.6 0.8 finish.1
  (1 shorter events, 0.0 us)
Async XLA Ops:
  0.6 7.7 %copy-start.7 = (s32[2,128]{1,0:T(2,128)S(1)}, s32[2,128]{1,0:T(2,128)}, u32[]{:S(2)}) copy-start(s32[2,128]{1,0:T(2,128)} %param.12) | copy-start | bytes 3076
  0.6 7.7 %copy-start.8 = (s32[128]{0:T(128)S(1)}, s32[128]{0:T(128)}, u32[]{:S(2)}) copy-start(s32[128]{0:T(128)} %param.13) | copy-start | bytes 1540
  0.7 8.7 %collective-permute-start.1 = (bf16[8,64,128]{2,1,0:T(8,128)(2,1)}, bf16[8,64,128]{2,1,0:T(8,128)(2,1)S(1)}, u32[]{:S(2)}, u32[]{:S(2)}) collective-permute-start(bf16[8,64,128]{2,1,0:T(8,128)(2,1)} %refs_3_.1), channel_id=1, source_target_pairs={{4,0},{8,4},{12,8},{16,12},{20,16},{24,20},{28,24},{5,1},{9,5},{13... | collective-permute-start | bytes 393224 | tf_op jit(solution)/shard_map/ppermute | solution.py:348
  2.1 10.3 %collective-permute-start = (bf16[8,64,128]{2,1,0:T(8,128)(2,1)}, bf16[8,64,128]{2,1,0:T(8,128)(2,1)S(1)}, u32[]{:S(2)}, u32[]{:S(2)}) collective-permute-start(bf16[8,64,128]{2,1,0:T(8,128)(2,1)} %refs_3_.1), channel_id=1, source_target_pairs={{0,4},{4,8},{8,12},{12,16},{16,20},{20,24},{24,28},{1,5},{5,9},{9,... | collective-permute-start | bytes 393224 | tf_op jit(solution)/shard_map/ppermute | solution.py:347
  12.4 0.9 copy-start
  13.3 6.6 %copy-start.1 = (bf16[64,384]{1,0:T(8,128)(2,1)S(1)}, bf16[64,384]{1,0:T(8,128)(2,1)}, u32[]{:S(2)}) copy-start(bf16[64,384]{1,0:T(8,128)(2,1)} %constant.60.clone.refs_8_.refs_6_) | copy-start | bytes 147460
  13.3 6.6 %copy-start.2 = (bf16[8,64,128]{2,1,0:T(8,128)(2,1)S(1)}, bf16[8,64,128]{2,1,0:T(8,128)(2,1)}, u32[]{:S(2)}) copy-start(bf16[8,64,128]{2,1,0:T(8,128)(2,1)} %refs_7_.2) | copy-start | bytes 393220
  13.3 6.6 %copy-start.3 = (bf16[128,128]{1,0:T(8,128)(2,1)S(1)}, bf16[128,128]{1,0:T(8,128)(2,1)}, u32[]{:S(2)}) copy-start(bf16[128,128]{1,0:T(8,128)(2,1)} %constant.61.clone.refs_9_.refs_7_) | copy-start | bytes 98308
  13.5 4.0 %collective-permute-start.2 = (bf16[4,192,128]{2,1,0:T(8,128)(2,1)S(1)}, bf16[4,192,128]{2,1,0:T(8,128)(2,1)S(1)}, u32[]{:S(2)}, u32[]{:S(2)}) collective-permute-start(bf16[4,192,128]{2,1,0:T(8,128)(2,1)S(1)} %get-tuple-element.17), channel_id=1, source_target_pairs={{0,1},{1,2},{2,3},{4,5},{5,6},{6,7},{8,9},{9,10},{10,11},{12,13},{... | collective-permute-start | bytes 589832 | tf_op jit(solution)/shard_map/ppermute | solution.py:358
  15.5 4.4 %collective-permute-start.3 = (bf16[4,192,128]{2,1,0:T(8,128)(2,1)S(1)}, bf16[4,192,128]{2,1,0:T(8,128)(2,1)S(1)}, u32[]{:S(2)}, u32[]{:S(2)}) collective-permute-start(bf16[4,192,128]{2,1,0:T(8,128)(2,1)S(1)} %get-tuple-element.18), channel_id=1, source_target_pairs={{1,0},{2,1},{3,2},{5,4},{6,5},{7,6},{9,8},{10,9},{11,10},{13,12},{... | collective-permute-start | bytes 589832 | tf_op jit(solution)/shard_map/ppermute | solution.py:359
  17.5 2.4 %copy-start.6 = (f32[3,128]{1,0:T(4,128)S(1)}, f32[3,128]{1,0:T(4,128)}, u32[]{:S(2)}) copy-start(f32[3,128]{1,0:T(4,128)} %refs_1_.1) | copy-start | bytes 4612
  19.9 49.7 %copy-start.4 = (bf16[384,64]{1,0:T(8,128)(2,1)S(1)}, bf16[384,64]{1,0:T(8,128)(2,1)}, u32[]{:S(2)}) copy-start(bf16[384,64]{1,0:T(8,128)(2,1)} %constant.62.clone.refs_4_) | copy-start | bytes 147460
  25.9 43.7 %copy-start.5 = (bf16[128,128]{1,0:T(8,128)(2,1)S(1)}, bf16[128,128]{1,0:T(8,128)(2,1)}, u32[]{:S(2)}) copy-start(bf16[128,128]{1,0:T(8,128)(2,1)} %constant.63.clone.refs_5_) | copy-start | bytes 98308

commit v4 on v2

--- a/solution.py
+++ b/solution.py
@@ -60,17 +60,26 @@
     return dot(hi, w) + dot(lo, w)
 
 
-def pack_kernel(up_ref, own_ref, down_ref, right_ref, left_ref):
+def pack_rows(src, dst_a, dst_b, at, even):
     left = lax.broadcasted_iota(jnp.int32, (64, 128), 1) < 64
     for p in range(4):
-        for s, ref in enumerate((up_ref, own_ref, down_ref)):
-            a = ref[p].astype(F32)
-            c = ref[p + 4].astype(F32)
-            ra = pltpu.roll(a, 64, 1)
-            rc = pltpu.roll(c, 64, 1)
-            rows = pl.ds(s * 64, 64)
-            right_ref[p, rows] = jnp.where(left, ra, c).astype(BF16)
-            left_ref[p, rows] = jnp.where(left, a, rc).astype(BF16)
+        a = src[p].astype(F32)
+        c = src[p + 4].astype(F32)
+        right = jnp.where(left, pltpu.roll(a, 64, 1), c)
+        other = jnp.where(left, a, pltpu.roll(c, 64, 1))
+        dst_a[p, pl.ds(at, 64)] = jnp.where(even, right, other).astype(BF16)
+        dst_b[p, pl.ds(at, 64)] = jnp.where(even, other, right).astype(BF16)
+
+
+def pack_own_kernel(own_ref, a_ref, b_ref):
+    even = lax.axis_index("gy") % 2 == 0
+    pack_rows(own_ref, a_ref, b_ref, 0, even)
+
+
+def pack_corner_kernel(xa_ref, xb_ref, a_ref, b_ref):
+    even = lax.axis_index("gy") % 2 == 0
+    pack_rows(xa_ref, a_ref, b_ref, 0, even)
+    pack_rows(xb_ref, a_ref, b_ref, 64, even)
 
 
 def over_sublanes(x):
@@ -111,7 +120,7 @@
 
 
 def sample_kernel(
-    nx, ny, idx_ref, frac_ref, up_ref, own_ref, down_ref, lo_ref, hi_ref, ref_ref, left_ref, wy_ref,
+    nx, ny, idx_ref, frac_ref, xa_ref, own_ref, xb_ref, ya_ref, yb_ref, ca_ref, cb_ref, ref_ref, left_ref, wy_ref,
     res_ref, slope_ref, node_ref, send_ref, sq_ref, img, arr, wgt, rsc, gsc,
 ):
     half = lax.broadcasted_iota(jnp.int32, (64, 128), 1) < 64
@@ -119,24 +128,33 @@
     for k in range(3):
         img[pl.ds(k * TILE_ROWS, 2 * SPAN)] = zero
         img[pl.ds(k * TILE_ROWS + 10 * SPAN, 2 * SPAN)] = zero
+    odd_x = lax.axis_index("gx") % 2 == 1
+    odd_y = lax.axis_index("gy") % 2 == 1
+    at_a = jnp.where(odd_x, 0, 128)
+    segments = (
+        (xa_ref, ca_ref, cb_ref, 0, pl.multiple_of(at_a, 64)),
+        (own_ref, ya_ref, yb_ref, 0, 64),
+        (xb_ref, ca_ref, cb_ref, 64, pl.multiple_of(128 - at_a, 64)),
+    )
     for p in range(4):
-        for s, ref in enumerate((up_ref, own_ref, down_ref)):
+        for ref, pair_a, pair_b, at, row in segments:
             a = ref[p].astype(F32)
             c = ref[p + 4].astype(F32)
             ra = pltpu.roll(a, 64, 1)
             rc = pltpu.roll(c, 64, 1)
-            rows = pl.ds(s * 64, 64)
-            lo = lo_ref[p, rows].astype(F32)
-            hi = hi_ref[p, rows].astype(F32)
+            from_a = pair_a[p, pl.ds(at, 64)].astype(F32)
+            from_b = pair_b[p, pl.ds(at, 64)].astype(F32)
+            lo = jnp.where(odd_y, from_a, from_b)
+            hi = jnp.where(odd_y, from_b, from_a)
             rlo = pltpu.roll(lo, 64, 1)
             rhi = pltpu.roll(hi, 64, 1)
-            at = lambda k, q: pl.ds(k * TILE_ROWS + (q + 2) * SPAN + s * 64, 64)
-            img[at(0, p)] = jnp.where(half, lo, ra)
-            img[at(1, p)] = a
-            img[at(2, p)] = jnp.where(half, ra, rhi)
-            img[at(0, p + 4)] = jnp.where(half, rlo, rc)
-            img[at(1, p + 4)] = c
-            img[at(2, p + 4)] = jnp.where(half, rc, hi)
+            at_row = lambda k, q: pl.ds(pl.multiple_of(k * TILE_ROWS + (q + 2) * SPAN + row, 8), 64)
+            img[at_row(0, p)] = jnp.where(half, lo, ra)
+            img[at_row(1, p)] = a
+            img[at_row(2, p)] = jnp.where(half, ra, rhi)
+            img[at_row(0, p + 4)] = jnp.where(half, rlo, rc)
+            img[at_row(1, p + 4)] = c
+            img[at_row(2, p + 4)] = jnp.where(half, rc, hi)
     for z in range(8):
         rsc[z] = ref_ref[z].astype(F32).reshape(8, 8, 128)
 
@@ -353,24 +371,41 @@
         step_ref[kc // 2, kc % 2] = (alpha * grad_ref[kc])[:, :16]
 
 
+def swaps(count, first):
+    pairs = [(i, i + 1) for i in range(first, count - 1, 2)]
+    return pairs + [(j, i) for i, j in pairs]
+
+
 def on_device(ref_image, def_image, shift_xy, shift_z, frac, connectivity):
     nx, ny = lax.axis_size("gx"), lax.axis_size("gy")
     peers = nx * ny
     sds = jax.ShapeDtypeStruct
-    up = [(i, i + 1) for i in range(nx - 1)]
-    below = lax.ppermute(def_image, "gx", up)
-    above = lax.ppermute(def_image, "gx", [(j, i) for i, j in up])
-    to_right, to_left = pl.pallas_call(
-        pack_kernel,
-        out_shape=(sds((4, SPAN, 128), BF16), sds((4, SPAN, 128), BF16)),
-        in_specs=[VMEM] * 3,
+    xa = lax.ppermute(def_image, "gx", swaps(nx, 0))
+    xb = lax.ppermute(def_image, "gx", swaps(nx, 1))
+    half = sds((4, 64, 128), BF16)
+    to_a, to_b = pl.pallas_call(
+        pack_own_kernel,
+        out_shape=(half, half),
+        in_specs=[VMEM],
         out_specs=(VMEM, VMEM),
         compiler_params=PARAMS,
-        name="pack_halo",
-    )(below, def_image, above)
-    up = [(i, i + 1) for i in range(ny - 1)]
-    lo = lax.ppermute(to_right, "gy", up)
-    hi = lax.ppermute(to_left, "gy", [(j, i) for i, j in up])
+        cost_estimate=pl.CostEstimate(flops=300000, bytes_accessed=262144, transcendentals=0),
+        name="pack_own_halo",
+    )(def_image)
+    ya = lax.ppermute(to_a, "gy", swaps(ny, 0))
+    yb = lax.ppermute(to_b, "gy", swaps(ny, 1))
+    corner = sds((4, 128, 128), BF16)
+    to_a, to_b = pl.pallas_call(
+        pack_corner_kernel,
+        out_shape=(corner, corner),
+        in_specs=[VMEM] * 2,
+        out_specs=(VMEM, VMEM),
+        compiler_params=PARAMS,
+        cost_estimate=pl.CostEstimate(flops=300000, bytes_accessed=524288, transcendentals=0),
+        name="pack_corner_halo",
+    )(xa, xb)
+    ca = lax.ppermute(to_a, "gy", swaps(ny, 0))
+    cb = lax.ppermute(to_b, "gy", swaps(ny, 1))
 
     first = connectivity[0]
     col_x = first // 17 % 9
@@ -393,7 +428,7 @@
             sds((peers, 1, 128), F32),
             sds((8, 128), F32),
         ),
-        in_specs=[SMEM, SMEM] + [VMEM] * 8,
+        in_specs=[SMEM, SMEM] + [VMEM] * 10,
         out_specs=(VMEM,) * 5,
         scratch_shapes=[
             pltpu.VMEM((3 * TILE_ROWS, 128), F32),
@@ -404,7 +439,7 @@
         ],
         compiler_params=PARAMS,
         name="sample_and_gradient",
-    )(idx, frac, below, def_image, above, lo, hi, ref_image, left, wy)
+    )(idx, frac, xa, def_image, xb, ya, yb, ca, cb, ref_image, left, wy)
     recv = lax.all_to_all(send, ("gx", "gy"), 0, 0, tiled=True)
     grads, hess, send = pl.pallas_call(
         lambda *refs: product_kernel(nx, ny, *refs),

time: 53.1 us -> 49 us (0.923)
  waiting for transfers between devices: 5.73 us -> 1.88 us
  starting transfers between devices: 10.2 us -> 8.94 us
  local copies, waits for them, and re-layouts: 0.94 us -> 1.55 us
    ppermute x4 -> x6, waiting for transfers between devices: 5.73 us -> 1.88 us  [the longest x1 1.86 us: on_device(): xa = lax.ppermute(def_image, 'gx', swaps(nx, 0))]
    ppermute x4 -> x6, starting transfers between devices: 10.2 us -> 8.94 us  [the longest x1 5.79 us: on_device(): xa = lax.ppermute(def_image, 'gx', swaps(nx, 0))]
    unnamed x18 -> x20, local copies, waits for them, and re-layouts: 0.94 us -> 1.55 us
  transfers between devices with their start and end apart: 4 -> 6, of which waited for: 3 -> 1; matrix products, arithmetic and copies ran while one was open for 4% -> 4% of each run, Pallas kernels for 0% -> 1%
where the time goes in v4:
time: 49 us; the launch traced here: 48.6 us
  blocking collectives  24.8 us (51%)
  starting transfers between devices  8.94 us (18%)
  Pallas kernels  8.42 us (17%)
  other arithmetic  2.16 us (4%)
  waiting for transfers between devices  1.88 us (4%)
  local copies, waits for them, and re-layouts  1.55 us (3%)
  between operations  0.81 us (2%)
    all_to_all x2, blocking collectives, on_device(): recv = lax.all_to_all(send, ('gx', 'gy'), 0, 0, tiled=True)  24.8 us
    pallas_call x1, Pallas kernels, on_device(): pl.pallas_call(lambda *refs: sample_kernel(nx, ny, *refs), out_shape=(sds...  6.07 us
    ppermute x1, starting transfers between devices, on_device(): xa = lax.ppermute(def_image, 'gx', swaps(nx, 0))  5.79 us
    ppermute x1, waiting for transfers between devices, on_device(): xa = lax.ppermute(def_image, 'gx', swaps(nx, 0))  1.86 us
    unnamed x20, local copies, waits for them, and re-layouts  1.55 us
    pallas_call x1, Pallas kernels, on_device(): pl.pallas_call(lambda *refs: product_kernel(nx, ny, *refs), out_shape=(sd...  1.33 us
    ppermute x1, starting transfers between devices, on_device(): ca = lax.ppermute(to_a, 'gy', swaps(ny, 0))  1.08 us
  transfers between devices with their start and end apart: 6, of which 1 were waited for; matrix products, arithmetic and copies ran while one was open for 4% of the time, Pallas kernels for 1%

profile of v4, /device:TPU:0, one launch (start us, length us, event | category | flops | bytes accessed | tf_op | source)
XLA Modules:
  0.0 48.6 jit_solution(11743518685081209168)
XLA Ops:
  0.6 0.7 %collective-permute-start.1 = (bf16[8,64,128]{2,1,0:T(8,128)(2,1)}, bf16[8,64,128]{2,1,0:T(8,128)(2,1)S(1)}, u32[]{:S(2)}, u32[]{:S(2)}) collective-permute-start(bf16[8,64,128]{2,1,0:T(8,128)(2,1)} %refs_3_.1), channel_id=1, source_target_pairs={{4,8},{12,16},{20,24},{8,4},{16,12},{24,20},{5,9},{13,17},{21,25},... | collective-permute-start | bytes 393224 | tf_op jit(solution)/shard_map/ppermute | solution.py:384
  1.3 5.8 %collective-permute-start = (bf16[8,64,128]{2,1,0:T(8,128)(2,1)}, bf16[8,64,128]{2,1,0:T(8,128)(2,1)S(1)}, u32[]{:S(2)}, u32[]{:S(2)}) collective-permute-start(bf16[8,64,128]{2,1,0:T(8,128)(2,1)} %refs_3_.1), channel_id=1, source_target_pairs={{0,4},{8,12},{16,20},{24,28},{4,0},{12,8},{20,16},{28,24},{1,5},{9... | collective-permute-start | bytes 393224 | tf_op jit(solution)/shard_map/ppermute | solution.py:383
  7.1 0.0 copy-start
  7.1 0.9 %copy-done = bf16[8,64,128]{2,1,0:T(8,128)(2,1)S(1)} copy-done((bf16[8,64,128]{2,1,0:T(8,128)(2,1)S(1)}, bf16[8,64,128]{2,1,0:T(8,128)(2,1)}, u32[]{:S(2)}) %copy-start) | copy-done | bytes 131096
  8.0 0.0 copy-start.3
  8.0 0.1 pack_own_halo.1
  8.2 0.0 copy-start.8
  8.2 0.1 collective-permute-start.2
  8.2 0.0 copy-start.9
  8.3 0.7 %collective-permute-start.3 = (bf16[4,64,128]{2,1,0:T(8,128)(2,1)S(1)}, bf16[4,64,128]{2,1,0:T(8,128)(2,1)S(1)}, u32[]{:S(2)}, u32[]{:S(2)}) collective-permute-start(bf16[4,64,128]{2,1,0:T(8,128)(2,1)S(1)} %get-tuple-element.20), channel_id=1, source_target_pairs={{1,2},{2,1},{5,6},{6,5},{9,10},{10,9},{13,14},{14,13},{17,18},{18,... | collective-permute-start | bytes 196616 | tf_op jit(solution)/shard_map/ppermute | solution.py:396
  8.9 0.0 copy-done.8
  8.9 0.7 %subtract_and_fusion = (s32[1,128]{1,0:T(1,128)S(1)}, s32[1,128]{1,0:T(1,128)S(1)}) fusion(s32[2,128]{1,0:T(2,128)S(1)} %copy-done.8, s32[8,128]{1,0:T(8,128)} %param.15), kind=kLoop, calls=%fused_computation.21 | loop fusion | flops 3712 | bytes 2048 | tf_op jit(solution)/shard_map/and | solution.py:417
  9.7 0.0 copy-done.9
  9.7 0.7 %add_bitcast_fusion = s32[1,128]{1,0:T(1,128)S(1)} fusion(s32[2,128]{1,0:T(2,128)S(1)} %copy-done.8, s32[128]{0:T(128)S(1)} %copy-done.9, s32[8,128]{1,0:T(8,128)} %param.15), kind=kLoop, calls=%fused_computation.22 | loop fusion | flops 5760 | bytes 2560 | tf_op jit(solution)/shard_map/stack | solution.py:419
  10.4 0.0 copy-start.1
  10.4 0.0 collective-permute-done.1.xb_ref.refs_4_
  10.4 1.9 %collective-permute-done.xa_ref.refs_2_ = bf16[8,64,128]{2,1,0:T(8,128)(2,1)S(1)} collective-permute-done((bf16[8,64,128]{2,1,0:T(8,128)(2,1)}, bf16[8,64,128]{2,1,0:T(8,128)(2,1)S(1)}, u32[]{:S(2)}, u32[]{:S(2)}) %collective-permute-start) | collective-permute-done | bytes 131104 | tf_op jit(solution)/shard_map/ppermute | solution.py:383
  12.3 0.0 copy-start.2
  12.3 0.0 copy-start.4
  12.3 0.1 pack_corner_halo.1
  12.4 1.1 %collective-permute-start.4 = (bf16[4,128,128]{2,1,0:T(8,128)(2,1)S(1)}, bf16[4,128,128]{2,1,0:T(8,128)(2,1)S(1)}, u32[]{:S(2)}, u32[]{:S(2)}) collective-permute-start(bf16[4,128,128]{2,1,0:T(8,128)(2,1)S(1)} %get-tuple-element.21), channel_id=1, source_target_pairs={{0,1},{2,3},{1,0},{3,2},{4,5},{6,7},{5,4},{7,6},{8,9},{10,11},{9,8... | collective-permute-start | bytes 393224 | tf_op jit(solution)/shard_map/ppermute | solution.py:407
  13.5 0.7 %collective-permute-start.5 = (bf16[4,128,128]{2,1,0:T(8,128)(2,1)S(1)}, bf16[4,128,128]{2,1,0:T(8,128)(2,1)S(1)}, u32[]{:S(2)}, u32[]{:S(2)}) collective-permute-start(bf16[4,128,128]{2,1,0:T(8,128)(2,1)S(1)} %get-tuple-element.22), channel_id=1, source_target_pairs={{1,2},{2,1},{5,6},{6,5},{9,10},{10,9},{13,14},{14,13},{17,18},{18,... | collective-permute-start | bytes 393224 | tf_op jit(solution)/shard_map/ppermute | solution.py:408
  14.2 0.7 %fusion.1 = (s32[1,128]{1,0:T(1,128)S(1)}, s32[1,128]{1,0:T(1,128)S(1)}) fusion(s32[1,128]{1,0:T(1,128)S(1)} %get-tuple-element.35, s32[8,128]{1,0:T(8,128)} %param.15), kind=kLoop, calls=%fused_computation.16 | loop fusion | flops 2304 | bytes 2048 | tf_op jit(solution)/shard_map/add | solution.py:418
  14.9 0.0 copy-start.7
  14.9 0.0 collective-permute-done.2.refs_5_
  14.9 0.0 collective-permute-done.3.refs_6_
  14.9 0.0 collective-permute-done.4.refs_7_
  14.9 0.0 collective-permute-done.5.refs_8_
  15.0 0.0 copy-done.3
  15.0 0.0 copy-done.1
  15.0 0.0 copy-done.2
  15.0 0.0 copy-done.4
  15.0 0.6 %copy-done.7 = f32[3,128]{1,0:T(4,128)S(1)} copy-done((f32[3,128]{1,0:T(4,128)S(1)}, f32[3,128]{1,0:T(4,128)}, u32[]{:S(2)}) %copy-start.7) | copy-done | bytes 1560
  15.6 0.0 copy-start.5
  15.6 6.1 %sample_and_gradient.1 = (bf16[8,64,128]{2,1,0:T(8,128)(2,1)}, f32[3,8,8,8,128]{4,3,2,1,0:T(8,128)S(1)}, f32[64,128]{1,0:T(8,128)S(1)}, f32[32,1,128]{2,1,0:T(1,128)S(1)}, f32[8,128]{1,0:T(8,128)S(1)}) custom-call(s32[4,128]{1,0:T(4,128)S(1)} %pad_add_fusion.refs_0_, f32[3,128]{1,0:T(4,128)S(1)} %copy-done.7, ...), custom_call_target="tpu_custom_call" | custom-call | tf_op jit(solution)/shard_map/sample_and_gradient/pallas_call | solution.py:422
  21.6 0.0 copy-start.6
  21.6 16.0 %all_to_all.10.refs_0_ = f32[32,1,128]{2,1,0:T(1,128)S(1)} all-to-all(f32[32,1,128]{2,1,0:T(1,128)S(1)} %get-tuple-element.24), channel_id=1, replica_groups=mesh['gx'=8,'gy'=4] {'gx','gy'}, dimensions={0} | all-to-all | bytes 32768 | tf_op jit(solution)/shard_map/all_to_all | solution.py:443
  37.6 0.0 copy-done.5
  37.7 0.0 copy-done.6
  37.7 1.3 %gauss_newton_product.1 = (f32[6,8,128]{2,1,0:T(8,128)S(1)}, f32[6,8,128]{2,1,0:T(8,128)S(1)}, f32[32,1,128]{2,1,0:T(1,128)S(1)}) custom-call(f32[32,1,128]{2,1,0:T(1,128)S(1)} %all_to_all.10.refs_0_, f32[64,128]{1,0:T(8,128)S(1)} %get-tuple-element.25.refs_1_, f32[3,8,8,8,128]{4,3,2,1,0:T(8,128)S(1)} %get-tuple-element.26.refs_2_, ...), custom_call_target="tpu_custom_call" | custom-call | tf_op jit(solution)/shard_map/gauss_newton_product/pallas_call | solution.py:444
  39.0 8.8 %all_to_all.11.refs_0_ = f32[32,1,128]{2,1,0:T(1,128)S(1)} all-to-all(f32[32,1,128]{2,1,0:T(1,128)S(1)} %get-tuple-element.28), channel_id=1, replica_groups=mesh['gx'=8,'gy'=4] {'gx','gy'}, dimensions={0} | all-to-all | bytes 32768 | tf_op jit(solution)/shard_map/all_to_all | solution.py:453
  47.8 0.8 %finish.1 = (f32[3,2,8,16]{3,2,1,0:T(8,128)}, f32[3,2,8,16]{3,2,1,0:T(8,128)}, f32[1,1]{1,0:T(1,128)}) custom-call(f32[32,1,128]{2,1,0:T(1,128)S(1)} %all_to_all.11.refs_0_, f32[6,8,128]{2,1,0:T(8,128)S(1)} %get-tuple-element.29.refs_1_, f32[6,8,128]{2,1,0:T(8,128)S(1)} %get-tuple-element.30.refs_2_), custom_call_target="tpu_custom_call" | custom-call | tf_op jit(solution)/shard_map/finish/pallas_call | solution.py:455
  (1 shorter events, 0.0 us)
Async XLA Ops:
  0.6 9.8 %collective-permute-start.1 = (bf16[8,64,128]{2,1,0:T(8,128)(2,1)}, bf16[8,64,128]{2,1,0:T(8,128)(2,1)S(1)}, u32[]{:S(2)}, u32[]{:S(2)}) collective-permute-start(bf16[8,64,128]{2,1,0:T(8,128)(2,1)} %refs_3_.1), channel_id=1, source_target_pairs={{4,8},{12,16},{20,24},{8,4},{16,12},{24,20},{5,9},{13,17},{21,25},... | collective-permute-start | bytes 393224 | tf_op jit(solution)/shard_map/ppermute | solution.py:384
  1.3 11.0 %collective-permute-start = (bf16[8,64,128]{2,1,0:T(8,128)(2,1)}, bf16[8,64,128]{2,1,0:T(8,128)(2,1)S(1)}, u32[]{:S(2)}, u32[]{:S(2)}) collective-permute-start(bf16[8,64,128]{2,1,0:T(8,128)(2,1)} %refs_3_.1), channel_id=1, source_target_pairs={{0,4},{8,12},{16,20},{24,28},{4,0},{12,8},{20,16},{28,24},{1,5},{9... | collective-permute-start | bytes 393224 | tf_op jit(solution)/shard_map/ppermute | solution.py:383
  7.1 0.9 %copy-start = (bf16[8,64,128]{2,1,0:T(8,128)(2,1)S(1)}, bf16[8,64,128]{2,1,0:T(8,128)(2,1)}, u32[]{:S(2)}) copy-start(bf16[8,64,128]{2,1,0:T(8,128)(2,1)} %refs_3_.1) | copy-start | bytes 393220
  8.0 6.9 %copy-start.3 = (bf16[8,64,128]{2,1,0:T(8,128)(2,1)S(1)}, bf16[8,64,128]{2,1,0:T(8,128)(2,1)}, u32[]{:S(2)}) copy-start(bf16[8,64,128]{2,1,0:T(8,128)(2,1)} %refs_9_.1) | copy-start | bytes 393220
  8.2 0.8 %copy-start.8 = (s32[2,128]{1,0:T(2,128)S(1)}, s32[2,128]{1,0:T(2,128)}, u32[]{:S(2)}) copy-start(s32[2,128]{1,0:T(2,128)} %param.12) | copy-start | bytes 3076
  8.2 6.8 %collective-permute-start.2 = (bf16[4,64,128]{2,1,0:T(8,128)(2,1)S(1)}, bf16[4,64,128]{2,1,0:T(8,128)(2,1)S(1)}, u32[]{:S(2)}, u32[]{:S(2)}) collective-permute-start(bf16[4,64,128]{2,1,0:T(8,128)(2,1)S(1)} %get-tuple-element.19), channel_id=1, source_target_pairs={{0,1},{2,3},{1,0},{3,2},{4,5},{6,7},{5,4},{7,6},{8,9},{10,11},{9,8... | collective-permute-start | bytes 196616 | tf_op jit(solution)/shard_map/ppermute | solution.py:395
  8.2 1.4 %copy-start.9 = (s32[128]{0:T(128)S(1)}, s32[128]{0:T(128)}, u32[]{:S(2)}) copy-start(s32[128]{0:T(128)} %param.13) | copy-start | bytes 1540
  8.3 6.7 %collective-permute-start.3 = (bf16[4,64,128]{2,1,0:T(8,128)(2,1)S(1)}, bf16[4,64,128]{2,1,0:T(8,128)(2,1)S(1)}, u32[]{:S(2)}, u32[]{:S(2)}) collective-permute-start(bf16[4,64,128]{2,1,0:T(8,128)(2,1)S(1)} %get-tuple-element.20), channel_id=1, source_target_pairs={{1,2},{2,1},{5,6},{6,5},{9,10},{10,9},{13,14},{14,13},{17,18},{18,... | collective-permute-start | bytes 196616 | tf_op jit(solution)/shard_map/ppermute | solution.py:396
  10.4 4.6 %copy-start.1 = (bf16[8,64,128]{2,1,0:T(8,128)(2,1)S(1)}, bf16[8,64,128]{2,1,0:T(8,128)(2,1)}, u32[]{:S(2)}) copy-start(bf16[8,64,128]{2,1,0:T(8,128)(2,1)} %refs_3_.1) | copy-start | bytes 393220
  12.3 2.7 %copy-start.2 = (bf16[64,384]{1,0:T(8,128)(2,1)S(1)}, bf16[64,384]{1,0:T(8,128)(2,1)}, u32[]{:S(2)}) copy-start(bf16[64,384]{1,0:T(8,128)(2,1)} %constant.60.clone.refs_10_.refs_6_) | copy-start | bytes 147460
  12.3 2.7 %copy-start.4 = (bf16[128,128]{1,0:T(8,128)(2,1)S(1)}, bf16[128,128]{1,0:T(8,128)(2,1)}, u32[]{:S(2)}) copy-start(bf16[128,128]{1,0:T(8,128)(2,1)} %constant.61.clone.refs_11_.refs_7_) | copy-start | bytes 98308
  12.4 2.5 %collective-permute-start.4 = (bf16[4,128,128]{2,1,0:T(8,128)(2,1)S(1)}, bf16[4,128,128]{2,1,0:T(8,128)(2,1)S(1)}, u32[]{:S(2)}, u32[]{:S(2)}) collective-permute-start(bf16[4,128,128]{2,1,0:T(8,128)(2,1)S(1)} %get-tuple-element.21), channel_id=1, source_target_pairs={{0,1},{2,3},{1,0},{3,2},{4,5},{6,7},{5,4},{7,6},{8,9},{10,11},{9,8... | collective-permute-start | bytes 393224 | tf_op jit(solution)/shard_map/ppermute | solution.py:407
  13.5 1.4 %collective-permute-start.5 = (bf16[4,128,128]{2,1,0:T(8,128)(2,1)S(1)}, bf16[4,128,128]{2,1,0:T(8,128)(2,1)S(1)}, u32[]{:S(2)}, u32[]{:S(2)}) collective-permute-start(bf16[4,128,128]{2,1,0:T(8,128)(2,1)S(1)} %get-tuple-element.22), channel_id=1, source_target_pairs={{1,2},{2,1},{5,6},{6,5},{9,10},{10,9},{13,14},{14,13},{17,18},{18,... | collective-permute-start | bytes 393224 | tf_op jit(solution)/shard_map/ppermute | solution.py:408
  14.9 0.7 %copy-start.7 = (f32[3,128]{1,0:T(4,128)S(1)}, f32[3,128]{1,0:T(4,128)}, u32[]{:S(2)}) copy-start(f32[3,128]{1,0:T(4,128)} %refs_1_.1) | copy-start | bytes 4612
  15.6 22.1 %copy-start.5 = (bf16[384,64]{1,0:T(8,128)(2,1)S(1)}, bf16[384,64]{1,0:T(8,128)(2,1)}, u32[]{:S(2)}) copy-start(bf16[384,64]{1,0:T(8,128)(2,1)} %constant.62.clone.refs_4_) | copy-start | bytes 147460
  21.6 16.0 %copy-start.6 = (bf16[128,128]{1,0:T(8,128)(2,1)S(1)}, bf16[128,128]{1,0:T(8,128)(2,1)}, u32[]{:S(2)}) copy-start(bf16[128,128]{1,0:T(8,128)(2,1)} %constant.63.clone.refs_5_) | copy-start | bytes 98308

commit v5 on v4

--- a/solution.py
+++ b/solution.py
@@ -11,9 +11,10 @@
 BF16 = jnp.bfloat16
 SPAN = 192
 TILE_ROWS = 12 * SPAN
+CHUNK = 16
 VMEM = pl.BlockSpec(memory_space=pltpu.VMEM)
 SMEM = pl.BlockSpec(memory_space=pltpu.SMEM)
-PARAMS = pltpu.CompilerParams(vmem_limit_bytes=40 * 1024 * 1024)
+PARAMS = pltpu.CompilerParams(vmem_limit_bytes=24 * 1024 * 1024)
 
 
 def node_weights(count):
@@ -71,12 +72,62 @@
         dst_b[p, pl.ds(at, 64)] = jnp.where(even, other, right).astype(BF16)
 
 
-def pack_own_kernel(own_ref, a_ref, b_ref):
-    even = lax.axis_index("gy") % 2 == 0
-    pack_rows(own_ref, a_ref, b_ref, 0, even)
-
-
-def pack_corner_kernel(xa_ref, xb_ref, a_ref, b_ref):
+def dot_rows(a, b):
+    return lax.dot_general(a, b, (((1,), (1,)), ((), ())), preferred_element_type=F32)
+
+
+def as_rows(rows):
+    sub = lax.broadcasted_iota(jnp.int32, (8, 128), 0)
+    out = jnp.zeros((8, 128), F32)
+    for n, row in enumerate(rows):
+        out = jnp.where(sub == n, jnp.broadcast_to(row.astype(F32), (8, 128)), out)
+    return out
+
+
+def prepare_kernel(*refs):
+    sources, (b_ref, a_ref, idx_ref, wgt_ref), scratch, sems = refs[:5], refs[5:9], refs[9:14], refs[14]
+    copies = [pltpu.make_async_copy(sources[n], scratch[n], sems.at[n]) for n in range(5)]
+    for copy in copies:
+        copy.start()
+    for copy in copies:
+        copy.wait()
+    own_ref, conn_ref, xy_ref, z_ref, frac_ref = scratch
+    pack_rows(own_ref, a_ref, b_ref, 0, lax.axis_index("gy") % 2 == 0)
+    first = conn_ref[0:1]
+    col_x = (first * 241) >> 12
+    col_y = first - 17 * col_x
+    start_x = 8 * col_x + xy_ref[0:1] + HALO
+    start_y = 8 * col_y + xy_ref[1:2] + HALO
+    early = (start_y >= 64) & (start_y < 184)
+    below = start_y < 64
+    offset = jnp.where(early, start_y - 64, jnp.where(below, start_y, start_y - 128))
+    base = (z_ref[...] + 2) * SPAN + start_x
+    tile = jnp.where(early | below, 0, TILE_ROWS)
+    shift = (8 * col_y - offset) & 127
+    place = (col_y & 1) * 8 + col_x
+    width = jnp.where(early, 0, 9)
+    flag = early.astype(F32)
+    row = lax.broadcasted_iota(jnp.int32, (128, 128), 0)
+    lane = lax.broadcasted_iota(jnp.int32, (128, 128), 1)
+    upto = dot(as_rows([flag]).astype(BF16), (row <= lane).astype(F32).astype(BF16))[0:1]
+    count = jnp.sum(flag, axis=1, keepdims=True)
+    rank = jnp.where(early, upto - 1.0, count + lane[0:1].astype(F32) - upto)
+    order = (jnp.broadcast_to(rank, (128, 128)) == row.astype(F32)).astype(F32).astype(BF16)
+    hi, lo = split(as_rows([base, shift, place, 8 * col_y, tile, width]))
+    table = dot_rows(hi, order) + dot_rows(lo, order)
+    sub = lax.broadcasted_iota(jnp.int32, (8, 128), 0)
+    table = jnp.where(sub == 6, jnp.broadcast_to(count, (8, 128)), table)
+    idx_ref[...] = table.astype(jnp.int32)
+    value = as_rows([frac_ref[c : c + 1] for c in range(3)])
+    hi, lo = split(value)
+    rest = (value - hi.astype(F32) - lo.astype(F32)).astype(BF16)
+    element = jnp.broadcast_to(col_x * 16 + col_y, (128, 128))
+    for cx in range(8):
+        spread = (element == cx * 16 + (row >> 3)).astype(F32).astype(BF16)
+        wgt_ref[cx] = dot_rows(hi, spread) + dot_rows(lo, spread) + dot_rows(rest, spread)
+
+
+def pack_corner_kernel(xa_ref, xb_ref, own_b_ref, own_a_ref, b_ref, a_ref):
     even = lax.axis_index("gy") % 2 == 0
     pack_rows(xa_ref, a_ref, b_ref, 0, even)
     pack_rows(xb_ref, a_ref, b_ref, 64, even)
@@ -119,73 +170,92 @@
     return lanes_of(row, lane + 8 * sub), lanes_of(row, lane + 64 + sub)
 
 
-def sample_kernel(
-    nx, ny, idx_ref, frac_ref, xa_ref, own_ref, xb_ref, ya_ref, yb_ref, ca_ref, cb_ref, ref_ref, left_ref, wy_ref,
-    res_ref, slope_ref, node_ref, send_ref, sq_ref, img, arr, wgt, rsc, gsc,
+def place_of_a():
+    return pl.multiple_of(jnp.where(lax.axis_index("gx") % 2 == 1, 0, 128), 64)
+
+
+def clear_outside(img, tiles):
+    zero = jnp.zeros((2 * SPAN, 128), F32)
+    for k in range(tiles):
+        img[pl.ds(k * TILE_ROWS, 2 * SPAN)] = zero
+        img[pl.ds(k * TILE_ROWS + 10 * SPAN, 2 * SPAN)] = zero
+
+
+def sample_element(img, arr, base, shift, place, first, width):
+    lane = lax.broadcasted_iota(jnp.int32, (8, 128), 1)
+    mask = ((lane - first) & 127) < width
+    for z in range(9):
+        for q in range(2):
+            v = img[pl.ds(base + (z * SPAN + q), 8), :]
+            pltpu.store(arr.at[place, z * 2 + q], pltpu.roll(v, shift, 1), mask=mask)
+
+
+def early_kernel(idx_ref, xa_ref, own_ref, xb_ref, arr_ref, img):
+    clear_outside(img, 1)
+    at_a = place_of_a()
+    for z in range(8):
+        for ref, row in ((xa_ref, at_a), (own_ref, 64), (xb_ref, 128 - at_a)):
+            img[pl.ds(pl.multiple_of((z + 2) * SPAN + row, 8), 64)] = ref[z].astype(F32)
+
+    def chunk(n, carry):
+        for m in range(CHUNK):
+            e = n * CHUNK + m
+            sample_element(
+                img, arr_ref, idx_ref[0, e], idx_ref[1, e], idx_ref[2, e], idx_ref[3, e], 9
+            )
+        return carry
+
+    lax.fori_loop(0, (idx_ref[6, 0] + (CHUNK - 1)) // CHUNK, chunk, 0)
+
+
+def late_kernel(
+    nx, ny, idx_ref, wgt, xa_ref, own_ref, xb_ref, yb_ref, ya_ref, cb_ref, ca_ref, arr_ref, ref_ref,
+    left_ref, wy_ref, res_ref, slope_ref, node_ref, send_ref, sq_ref, img, arr, rsc, gsc,
 ):
     half = lax.broadcasted_iota(jnp.int32, (64, 128), 1) < 64
-    zero = jnp.zeros((2 * SPAN, 128), F32)
-    for k in range(3):
-        img[pl.ds(k * TILE_ROWS, 2 * SPAN)] = zero
-        img[pl.ds(k * TILE_ROWS + 10 * SPAN, 2 * SPAN)] = zero
-    odd_x = lax.axis_index("gx") % 2 == 1
+    clear_outside(img, 2)
     odd_y = lax.axis_index("gy") % 2 == 1
-    at_a = jnp.where(odd_x, 0, 128)
+    at_a = place_of_a()
     segments = (
-        (xa_ref, ca_ref, cb_ref, 0, pl.multiple_of(at_a, 64)),
+        (xa_ref, ca_ref, cb_ref, 0, at_a),
         (own_ref, ya_ref, yb_ref, 0, 64),
-        (xb_ref, ca_ref, cb_ref, 64, pl.multiple_of(128 - at_a, 64)),
+        (xb_ref, ca_ref, cb_ref, 64, 128 - at_a),
     )
     for p in range(4):
         for ref, pair_a, pair_b, at, row in segments:
-            a = ref[p].astype(F32)
-            c = ref[p + 4].astype(F32)
-            ra = pltpu.roll(a, 64, 1)
-            rc = pltpu.roll(c, 64, 1)
+            ra = pltpu.roll(ref[p].astype(F32), 64, 1)
+            rc = pltpu.roll(ref[p + 4].astype(F32), 64, 1)
             from_a = pair_a[p, pl.ds(at, 64)].astype(F32)
             from_b = pair_b[p, pl.ds(at, 64)].astype(F32)
             lo = jnp.where(odd_y, from_a, from_b)
             hi = jnp.where(odd_y, from_b, from_a)
-            rlo = pltpu.roll(lo, 64, 1)
-            rhi = pltpu.roll(hi, 64, 1)
             at_row = lambda k, q: pl.ds(pl.multiple_of(k * TILE_ROWS + (q + 2) * SPAN + row, 8), 64)
             img[at_row(0, p)] = jnp.where(half, lo, ra)
-            img[at_row(1, p)] = a
-            img[at_row(2, p)] = jnp.where(half, ra, rhi)
-            img[at_row(0, p + 4)] = jnp.where(half, rlo, rc)
-            img[at_row(1, p + 4)] = c
-            img[at_row(2, p + 4)] = jnp.where(half, rc, hi)
+            img[at_row(1, p)] = jnp.where(half, ra, pltpu.roll(hi, 64, 1))
+            img[at_row(0, p + 4)] = jnp.where(half, pltpu.roll(lo, 64, 1), rc)
+            img[at_row(1, p + 4)] = jnp.where(half, rc, hi)
     for z in range(8):
         rsc[z] = ref_ref[z].astype(F32).reshape(8, 8, 128)
-
-    lane = lax.broadcasted_iota(jnp.int32, (8, 128), 1)
-
-    def element(e, carry):
-        base = idx_ref[0, e]
-        shift = idx_ref[1, e]
-        place = idx_ref[2, e]
-        first = idx_ref[3, e]
-        where_to = (lane - first) & 127
-        mask = where_to < 9
-        for z in range(9):
-            for q in range(2):
-                v = img[pl.ds(base + (z * SPAN + q), 8), :]
-                v = pltpu.roll(v, shift, 1)
-                pltpu.store(arr.at[place, z * 2 + q], v, mask=mask)
-        mask = where_to < 8
-        row = place & 7
-        for c in range(3):
-            pltpu.store(wgt.at[c, row], jnp.full((8, 128), frac_ref[c, e], F32), mask=mask)
+    arr[...] = arr_ref[...]
+
+    def chunk(n, carry):
+        for m in range(CHUNK):
+            e = n * CHUNK + m
+            base = idx_ref[0, e] + idx_ref[4, e]
+            sample_element(
+                img, arr, base, idx_ref[1, e], idx_ref[2, e], idx_ref[3, e], idx_ref[5, e]
+            )
         return carry
 
-    lax.fori_loop(0, 128, element, 0, unroll=16)
-
+    lax.fori_loop(idx_ref[6, 0] // CHUNK, 128 // CHUNK, chunk, 0)
+
+    lane = lax.broadcasted_iota(jnp.int32, (8, 128), 1)
     phase = lane & 15
     even = phase < 8
     even_next = (phase >= 1) & (phase <= 8)
 
     def interpolate(cx, square):
-        wz, wx, wy = wgt[0, cx], wgt[1, cx], wgt[2, cx]
+        wz, wx, wy = (jnp.broadcast_to(wgt[cx, c : c + 1], (8, 128)) for c in range(3))
 
         def pair(z, q):
             ev = arr[cx, z * 2 + q]
@@ -383,44 +453,51 @@
     xa = lax.ppermute(def_image, "gx", swaps(nx, 0))
     xb = lax.ppermute(def_image, "gx", swaps(nx, 1))
     half = sds((4, 64, 128), BF16)
-    to_a, to_b = pl.pallas_call(
-        pack_own_kernel,
-        out_shape=(half, half),
-        in_specs=[VMEM],
-        out_specs=(VMEM, VMEM),
+    to_b, to_a, idx, wgt = pl.pallas_call(
+        prepare_kernel,
+        out_shape=(half, half, sds((8, 128), jnp.int32), sds((8, 8, 128), F32)),
+        in_specs=[pl.BlockSpec(memory_space=pltpu.HBM)] * 5,
+        out_specs=(VMEM,) * 4,
+        scratch_shapes=[
+            pltpu.VMEM((8, 64, 128), BF16),
+            pltpu.VMEM((8, 128), jnp.int32),
+            pltpu.VMEM((2, 128), jnp.int32),
+            pltpu.VMEM((1, 128), jnp.int32),
+            pltpu.VMEM((3, 128), F32),
+            pltpu.SemaphoreType.DMA((5,)),
+        ],
         compiler_params=PARAMS,
         cost_estimate=pl.CostEstimate(flops=300000, bytes_accessed=262144, transcendentals=0),
-        name="pack_own_halo",
-    )(def_image)
+        name="prepare",
+    )(def_image, connectivity, shift_xy, shift_z.reshape(1, 128), frac)
+    yb = lax.ppermute(to_b, "gy", swaps(ny, 1))
     ya = lax.ppermute(to_a, "gy", swaps(ny, 0))
-    yb = lax.ppermute(to_b, "gy", swaps(ny, 1))
     corner = sds((4, 128, 128), BF16)
-    to_a, to_b = pl.pallas_call(
+    corner_b, corner_a = pl.pallas_call(
         pack_corner_kernel,
         out_shape=(corner, corner),
-        in_specs=[VMEM] * 2,
+        in_specs=[VMEM, VMEM] + [pl.BlockSpec(memory_space=pl.ANY)] * 2,
         out_specs=(VMEM, VMEM),
         compiler_params=PARAMS,
         cost_estimate=pl.CostEstimate(flops=300000, bytes_accessed=524288, transcendentals=0),
         name="pack_corner_halo",
-    )(xa, xb)
-    ca = lax.ppermute(to_a, "gy", swaps(ny, 0))
-    cb = lax.ppermute(to_b, "gy", swaps(ny, 1))
-
-    first = connectivity[0]
-    col_x = first // 17 % 9
-    col_y = first % 17
-    start_x = 8 * col_x + shift_xy[0] + HALO
-    start_y = 8 * col_y + shift_xy[1] + HALO
-    tile = jnp.minimum(start_y // 64, 2)
-    base = tile * TILE_ROWS + (shift_z + 2) * SPAN + start_x
-    shift = (8 * col_y - (start_y - 64 * tile)) & 127
-    place = (col_y & 1) * 8 + col_x
-    idx = jnp.stack([base, shift, place, 8 * col_y])
+    )(xa, xb, yb, ya)
+    cb = lax.ppermute(corner_b, "gy", swaps(ny, 1))
+    ca = lax.ppermute(corner_a, "gy", swaps(ny, 0))
 
     left, wy, expand, wyt = tables()
+    arr = pl.pallas_call(
+        early_kernel,
+        out_shape=sds((16, 18, 8, 128), F32),
+        in_specs=[SMEM] + [VMEM] * 3,
+        out_specs=VMEM,
+        scratch_shapes=[pltpu.VMEM((TILE_ROWS, 128), F32)],
+        compiler_params=PARAMS,
+        cost_estimate=pl.CostEstimate(flops=4000000, bytes_accessed=2000000, transcendentals=0),
+        name="sample_early",
+    )(idx, xa, def_image, xb)
     residual, slopes, nodes, send, square = pl.pallas_call(
-        lambda *refs: sample_kernel(nx, ny, *refs),
+        lambda *refs: late_kernel(nx, ny, *refs),
         out_shape=(
             sds((8, 64, 128), BF16),
             sds((3, 8, 8, 8, 128), F32),
@@ -428,18 +505,17 @@
             sds((peers, 1, 128), F32),
             sds((8, 128), F32),
         ),
-        in_specs=[SMEM, SMEM] + [VMEM] * 10,
+        in_specs=[SMEM] + [VMEM] * 12,
         out_specs=(VMEM,) * 5,
         scratch_shapes=[
-            pltpu.VMEM((3 * TILE_ROWS, 128), F32),
+            pltpu.VMEM((2 * TILE_ROWS, 128), F32),
             pltpu.VMEM((16, 18, 8, 128), F32),
-            pltpu.VMEM((3, 8, 8, 128), F32),
             pltpu.VMEM((8, 8, 8, 128), F32),
             pltpu.VMEM((6, 8, 8, 128), F32),
         ],
         compiler_params=PARAMS,
         name="sample_and_gradient",
-    )(idx, frac, xa, def_image, xb, ya, yb, ca, cb, ref_image, left, wy)
+    )(idx, wgt, xa, def_image, xb, yb, ya, cb, ca, arr, ref_image, left, wy)
     recv = lax.all_to_all(send, ("gx", "gy"), 0, 0, tiled=True)
     grads, hess, send = pl.pallas_call(
         lambda *refs: product_kernel(nx, ny, *refs),

time: 49 us -> 50.6 us (1.033)
  starting transfers between devices: 8.94 us -> 14.7 us
  blocking collectives: 24.8 us -> 20.3 us
  other arithmetic: 2.16 us -> 0 us
  local copies, waits for them, and re-layouts: 1.55 us -> 3.66 us
  Pallas kernels: 8.42 us -> 10.3 us
  waiting for transfers between devices: 1.88 us -> 0.91 us
    all_to_all x2, blocking collectives: 24.8 us -> 20.3 us  [on_device(): recv = lax.all_to_all(send, ('gx', 'gy'), 0, 0, tiled=True)]
    ppermute x2, starting transfers between devices: 1.74 us -> 4.68 us  [the longest x1 4.01 us: on_device(): ca = lax.ppermute(corner_a, 'gy', swaps(ny, 0))]
    ppermute x1, starting transfers between devices: 0.07 us -> 2.92 us  [on_device(): ya = lax.ppermute(to_a, 'gy', swaps(ny, 0))]
    unnamed x20, local copies, waits for them, and re-layouts: 1.55 us -> 3.66 us
    pallas_call x2 -> x3, Pallas kernels: 6.18 us -> 8.06 us  [the longest x1 4.61 us: on_device(): pl.pallas_call(lambda *refs: late_kernel(nx, ny, *refs), out_shape=(sds((...]
    ppermute x1, waiting for transfers between devices: 1.86 us -> 0.01 us  [on_device(): xa = lax.ppermute(def_image, 'gx', swaps(nx, 0))]
    ppermute x1, waiting for transfers between devices: 0.01 us -> 0.9 us  [on_device(): ya = lax.ppermute(to_a, 'gy', swaps(ny, 0))]
    another operation x2 -> x0, other arithmetic: 0.73 us -> none  [on_device(): idx = jnp.stack([base, shift, place, 8 * col_y])]
  transfers between devices with their start and end apart: 6 -> 6, of which waited for: 1 -> 1; matrix products, arithmetic and copies ran while one was open for 4% -> 0% of each run, Pallas kernels for 1% -> 7%
where the time goes in v5:
time: 50.6 us
  blocking collectives  20.3 us (40%)
  starting transfers between devices  14.7 us (29%)
  Pallas kernels  10.3 us (20%)
  local copies, waits for them, and re-layouts  3.66 us (7%)
  waiting for transfers between devices  0.91 us (2%)
  between operations  0.75 us (1%)
    all_to_all x2, blocking collectives, on_device(): recv = lax.all_to_all(send, ('gx', 'gy'), 0, 0, tiled=True)  20.3 us
    ppermute x1, starting transfers between devices, on_device(): xa = lax.ppermute(def_image, 'gx', swaps(nx, 0))  5.79 us
    pallas_call x1, Pallas kernels, on_device(): pl.pallas_call(lambda *refs: late_kernel(nx, ny, *refs), out_shape=(sds((...  4.61 us
    ppermute x1, starting transfers between devices, on_device(): ca = lax.ppermute(corner_a, 'gy', swaps(ny, 0))  4.01 us
    unnamed x20, local copies, waits for them, and re-layouts  3.66 us
    ppermute x1, starting transfers between devices, on_device(): ya = lax.ppermute(to_a, 'gy', swaps(ny, 0))  2.92 us
    pallas_call x1, Pallas kernels, on_device(): pl.pallas_call(early_kernel, out_shape=sds((16, 18, 8, 128), F32), in_spe...  2.54 us
    pallas_call x1, Pallas kernels, on_device(): pl.pallas_call(lambda *refs: product_kernel(nx, ny, *refs), out_shape=(sd...  1.33 us
  transfers between devices with their start and end apart: 6, of which 1 were waited for; matrix products, arithmetic and copies ran while one was open for 0% of the time, Pallas kernels for 7%

profile of v5, /device:TPU:0, one launch (start us, length us, event | category | flops | bytes accessed | tf_op | source)
XLA Modules:
  0.0 50.6 jit_solution(18120625356493553560)
XLA Ops:
  0.6 0.7 %collective-permute-start.1 = (bf16[8,64,128]{2,1,0:T(8,128)(2,1)}, bf16[8,64,128]{2,1,0:T(8,128)(2,1)S(1)}, u32[]{:S(2)}, u32[]{:S(2)}) collective-permute-start(bf16[8,64,128]{2,1,0:T(8,128)(2,1)} %refs_3_.1), channel_id=1, source_target_pairs={{4,8},{12,16},{20,24},{8,4},{16,12},{24,20},{5,9},{13,17},{21,25},... | collective-permute-start | bytes 393224 | tf_op jit(solution)/shard_map/ppermute | solution.py:454
  1.3 5.8 %collective-permute-start = (bf16[8,64,128]{2,1,0:T(8,128)(2,1)}, bf16[8,64,128]{2,1,0:T(8,128)(2,1)S(1)}, u32[]{:S(2)}, u32[]{:S(2)}) collective-permute-start(bf16[8,64,128]{2,1,0:T(8,128)(2,1)} %refs_3_.1), channel_id=1, source_target_pairs={{0,4},{8,12},{16,20},{24,28},{4,0},{12,8},{20,16},{28,24},{1,5},{9... | collective-permute-start | bytes 393224 | tf_op jit(solution)/shard_map/ppermute | solution.py:453
  7.1 0.0 copy-start
  7.1 0.9 %copy-done = bf16[8,64,128]{2,1,0:T(8,128)(2,1)S(1)} copy-done((bf16[8,64,128]{2,1,0:T(8,128)(2,1)S(1)}, bf16[8,64,128]{2,1,0:T(8,128)(2,1)}, u32[]{:S(2)}) %copy-start) | copy-done | bytes 131096
  8.0 0.0 copy-start.6
  8.0 0.7 %copy-done.6 = s32[8,128]{1,0:T(8,128)S(1)} copy-done((s32[8,128]{1,0:T(8,128)S(1)}, s32[8,128]{1,0:T(8,128)}, u32[]{:S(2)}) %copy-start.6) | copy-done | bytes 4120
  8.7 0.0 copy-start.7
  8.7 0.7 %copy-done.7 = f32[3,128]{1,0:T(4,128)S(1)} copy-done((f32[3,128]{1,0:T(4,128)S(1)}, f32[3,128]{1,0:T(4,128)}, u32[]{:S(2)}) %copy-start.7) | copy-done | bytes 1560
  9.4 0.0 copy-start.8
  9.4 0.7 %copy-done.8 = s32[2,128]{1,0:T(2,128)S(1)} copy-done((s32[2,128]{1,0:T(2,128)S(1)}, s32[2,128]{1,0:T(2,128)}, u32[]{:S(2)}) %copy-start.8) | copy-done | bytes 1048
  10.1 0.0 copy-start.9
  10.1 0.7 %copy-done.9 = s32[128]{0:T(128)S(1)} copy-done((s32[128]{0:T(128)S(1)}, s32[128]{0:T(128)}, u32[]{:S(2)}) %copy-start.9) | copy-done | bytes 536
  10.7 0.0 copy-start.1
  10.7 0.0 copy-start.2
  10.7 0.0 copy-start.3
  10.7 0.9 %prepare.1 = (bf16[4,64,128]{2,1,0:T(8,128)(2,1)S(1)}, bf16[4,64,128]{2,1,0:T(8,128)(2,1)S(1)}, s32[8,128]{1,0:T(8,128)S(1)}, f32[8,8,128]{2,1,0:T(8,128)S(1)}) custom-call(bf16[8,64,128]{2,1,0:T(8,128)(2,1)S(1)} %copy-done, s32[8,128]{1,0:T(8,128)S(1)} %copy-done.6, s32[2,128]{1,0:T(2,128)S(1)} %copy-done.8, s32[1,128]{1,0:T(1,128)S(1)} %bitcast.2, ...), custom_call_target="tpu_custom_call" | custom-call | flops 300000 | bytes 262144 | tf_op jit(solution)/shard_map/prepare/pallas_call | solution.py:456
  11.7 0.7 %collective-permute-start.2 = (bf16[4,64,128]{2,1,0:T(8,128)(2,1)S(1)}, bf16[4,64,128]{2,1,0:T(8,128)(2,1)S(1)}, u32[]{:S(2)}, u32[]{:S(2)}) collective-permute-start(bf16[4,64,128]{2,1,0:T(8,128)(2,1)S(1)} %get-tuple-element.23), channel_id=1, source_target_pairs={{1,2},{2,1},{5,6},{6,5},{9,10},{10,9},{13,14},{14,13},{17,18},{18,... | collective-permute-start | bytes 196616 | tf_op jit(solution)/shard_map/ppermute | solution.py:473
  12.3 2.9 %collective-permute-start.3 = (bf16[4,64,128]{2,1,0:T(8,128)(2,1)S(1)}, bf16[4,64,128]{2,1,0:T(8,128)(2,1)S(1)}, u32[]{:S(2)}, u32[]{:S(2)}) collective-permute-start(bf16[4,64,128]{2,1,0:T(8,128)(2,1)S(1)} %get-tuple-element.24), channel_id=1, source_target_pairs={{0,1},{2,3},{1,0},{3,2},{4,5},{6,7},{5,4},{7,6},{8,9},{10,11},{9,8... | collective-permute-start | bytes 196616 | tf_op jit(solution)/shard_map/ppermute | solution.py:474
  15.3 0.0 collective-permute-done.2.own_b_ref.refs_5_
  15.3 0.9 %collective-permute-done.3.own_a_ref.refs_6_ = bf16[4,64,128]{2,1,0:T(8,128)(2,1)S(1)} collective-permute-done((bf16[4,64,128]{2,1,0:T(8,128)(2,1)S(1)}, bf16[4,64,128]{2,1,0:T(8,128)(2,1)S(1)}, u32[]{:S(2)}, u32[]{:S(2)}) %collective-permute-start.3) | collective-permute-done | bytes 65568 | tf_op jit(solution)/shard_map/ppermute | solution.py:474
  16.2 0.0 collective-permute-done.1.xb_ref.refs_4_
  16.2 0.0 collective-permute-done.xa_ref.refs_2_
  16.2 0.1 pack_corner_halo.1
  16.3 0.7 %collective-permute-start.4 = (bf16[4,128,128]{2,1,0:T(8,128)(2,1)S(1)}, bf16[4,128,128]{2,1,0:T(8,128)(2,1)S(1)}, u32[]{:S(2)}, u32[]{:S(2)}) collective-permute-start(bf16[4,128,128]{2,1,0:T(8,128)(2,1)S(1)} %get-tuple-element.25), channel_id=1, source_target_pairs={{1,2},{2,1},{5,6},{6,5},{9,10},{10,9},{13,14},{14,13},{17,18},{18,... | collective-permute-start | bytes 393224 | tf_op jit(solution)/shard_map/ppermute | solution.py:485
  17.0 4.0 %collective-permute-start.5 = (bf16[4,128,128]{2,1,0:T(8,128)(2,1)S(1)}, bf16[4,128,128]{2,1,0:T(8,128)(2,1)S(1)}, u32[]{:S(2)}, u32[]{:S(2)}) collective-permute-start(bf16[4,128,128]{2,1,0:T(8,128)(2,1)S(1)} %get-tuple-element.26), channel_id=1, source_target_pairs={{0,1},{2,3},{1,0},{3,2},{4,5},{6,7},{5,4},{7,6},{8,9},{10,11},{9,8... | collective-permute-start | bytes 393224 | tf_op jit(solution)/shard_map/ppermute | solution.py:486
  21.0 2.5 %sample_early.1.refs_9_ = f32[16,18,8,128]{3,2,1,0:T(8,128)S(1)} custom-call(s32[8,128]{1,0:T(8,128)S(1)} %get-tuple-element.21.idx_ref.refs_0_, bf16[8,64,128]{2,1,0:T(8,128)(2,1)S(1)} %collective-permute-done.xa_ref.refs_2_, bf16[8,64,128]{2,1,0:T(8,128)(2,1)S(1)} %copy-done, bf16[8,64,128]{2,1,0:T(8,128)(2,1)S(1)} %collective-permute-done.1.xb_ref.refs_4_), custom_call_target="tpu_custom_call" | custom-call | flops 4000000 | bytes 2000000 | tf_op jit(solution)/shard_map/sample_early/pallas_call | solution.py:489
  23.6 0.0 copy-start.4
  23.6 0.0 copy-start.5
  23.6 0.0 collective-permute-done.4.refs_7_
  23.6 0.0 collective-permute-done.5.refs_8_
  23.6 0.0 copy-done.1
  23.6 0.0 copy-done.2
  23.6 0.0 copy-done.3
  23.6 4.6 %sample_and_gradient.1 = (bf16[8,64,128]{2,1,0:T(8,128)(2,1)}, f32[3,8,8,8,128]{4,3,2,1,0:T(8,128)S(1)}, f32[64,128]{1,0:T(8,128)S(1)}, f32[32,1,128]{2,1,0:T(1,128)S(1)}, f32[8,128]{1,0:T(8,128)S(1)}) custom-call(s32[8,128]{1,0:T(8,128)S(1)} %get-tuple-element.21.idx_ref.refs_0_, f32[8,8,128]{2,1,0:T(8,128)S(1)} %get-tuple-element.22.refs_1_, ...), custom_call_target="tpu_custom_call" | custom-call | tf_op jit(solution)/shard_map/sample_and_gradient/pallas_call | solution.py:499
  28.2 11.4 %all_to_all.10.refs_0_ = f32[32,1,128]{2,1,0:T(1,128)S(1)} all-to-all(f32[32,1,128]{2,1,0:T(1,128)S(1)} %get-tuple-element.28), channel_id=1, replica_groups=mesh['gx'=8,'gy'=4] {'gx','gy'}, dimensions={0} | all-to-all | bytes 32768 | tf_op jit(solution)/shard_map/all_to_all | solution.py:519
  39.7 0.0 copy-done.4
  39.7 0.0 copy-done.5
  39.7 1.3 %gauss_newton_product.1 = (f32[6,8,128]{2,1,0:T(8,128)S(1)}, f32[6,8,128]{2,1,0:T(8,128)S(1)}, f32[32,1,128]{2,1,0:T(1,128)S(1)}) custom-call(f32[32,1,128]{2,1,0:T(1,128)S(1)} %all_to_all.10.refs_0_, f32[64,128]{1,0:T(8,128)S(1)} %get-tuple-element.29.refs_1_, f32[3,8,8,8,128]{4,3,2,1,0:T(8,128)S(1)} %get-tuple-element.30.refs_2_, ...), custom_call_target="tpu_custom_call" | custom-call | tf_op jit(solution)/shard_map/gauss_newton_product/pallas_call | solution.py:520
  41.0 8.8 %all_to_all.11.refs_0_ = f32[32,1,128]{2,1,0:T(1,128)S(1)} all-to-all(f32[32,1,128]{2,1,0:T(1,128)S(1)} %get-tuple-element.32), channel_id=1, replica_groups=mesh['gx'=8,'gy'=4] {'gx','gy'}, dimensions={0} | all-to-all | bytes 32768 | tf_op jit(solution)/shard_map/all_to_all | solution.py:529
  49.9 0.8 %finish.1 = (f32[3,2,8,16]{3,2,1,0:T(8,128)}, f32[3,2,8,16]{3,2,1,0:T(8,128)}, f32[1,1]{1,0:T(1,128)}) custom-call(f32[32,1,128]{2,1,0:T(1,128)S(1)} %all_to_all.11.refs_0_, f32[6,8,128]{2,1,0:T(8,128)S(1)} %get-tuple-element.33.refs_1_, f32[6,8,128]{2,1,0:T(8,128)S(1)} %get-tuple-element.34.refs_2_), custom_call_target="tpu_custom_call" | custom-call | tf_op jit(solution)/shard_map/finish/pallas_call | solution.py:531
Async XLA Ops:
  0.6 15.5 %collective-permute-start.1 = (bf16[8,64,128]{2,1,0:T(8,128)(2,1)}, bf16[8,64,128]{2,1,0:T(8,128)(2,1)S(1)}, u32[]{:S(2)}, u32[]{:S(2)}) collective-permute-start(bf16[8,64,128]{2,1,0:T(8,128)(2,1)} %refs_3_.1), channel_id=1, source_target_pairs={{4,8},{12,16},{20,24},{8,4},{16,12},{24,20},{5,9},{13,17},{21,25},... | collective-permute-start | bytes 393224 | tf_op jit(solution)/shard_map/ppermute | solution.py:454
  1.3 14.9 %collective-permute-start = (bf16[8,64,128]{2,1,0:T(8,128)(2,1)}, bf16[8,64,128]{2,1,0:T(8,128)(2,1)S(1)}, u32[]{:S(2)}, u32[]{:S(2)}) collective-permute-start(bf16[8,64,128]{2,1,0:T(8,128)(2,1)} %refs_3_.1), channel_id=1, source_target_pairs={{0,4},{8,12},{16,20},{24,28},{4,0},{12,8},{20,16},{28,24},{1,5},{9... | collective-permute-start | bytes 393224 | tf_op jit(solution)/shard_map/ppermute | solution.py:453
  7.1 0.9 %copy-start = (bf16[8,64,128]{2,1,0:T(8,128)(2,1)S(1)}, bf16[8,64,128]{2,1,0:T(8,128)(2,1)}, u32[]{:S(2)}) copy-start(bf16[8,64,128]{2,1,0:T(8,128)(2,1)} %refs_3_.1) | copy-start | bytes 393220
  8.0 0.7 %copy-start.6 = (s32[8,128]{1,0:T(8,128)S(1)}, s32[8,128]{1,0:T(8,128)}, u32[]{:S(2)}) copy-start(s32[8,128]{1,0:T(8,128)} %refs_1_.1) | copy-start | bytes 12292
  8.7 0.7 %copy-start.7 = (f32[3,128]{1,0:T(4,128)S(1)}, f32[3,128]{1,0:T(4,128)}, u32[]{:S(2)}) copy-start(f32[3,128]{1,0:T(4,128)} %refs_4_.2) | copy-start | bytes 4612
  9.4 0.7 %copy-start.8 = (s32[2,128]{1,0:T(2,128)S(1)}, s32[2,128]{1,0:T(2,128)}, u32[]{:S(2)}) copy-start(s32[2,128]{1,0:T(2,128)} %refs_2_.1) | copy-start | bytes 3076
  10.1 0.7 %copy-start.9 = (s32[128]{0:T(128)S(1)}, s32[128]{0:T(128)}, u32[]{:S(2)}) copy-start(s32[128]{0:T(128)} %param.13) | copy-start | bytes 1540
  10.7 12.9 %copy-start.1 = (bf16[64,384]{1,0:T(8,128)(2,1)S(1)}, bf16[64,384]{1,0:T(8,128)(2,1)}, u32[]{:S(2)}) copy-start(bf16[64,384]{1,0:T(8,128)(2,1)} %constant.8.clone.refs_11_.refs_6_) | copy-start | bytes 147460
  10.7 12.9 %copy-start.2 = (bf16[128,128]{1,0:T(8,128)(2,1)S(1)}, bf16[128,128]{1,0:T(8,128)(2,1)}, u32[]{:S(2)}) copy-start(bf16[128,128]{1,0:T(8,128)(2,1)} %constant.9.clone.refs_12_.refs_7_) | copy-start | bytes 98308
  10.7 12.9 %copy-start.3 = (bf16[8,64,128]{2,1,0:T(8,128)(2,1)S(1)}, bf16[8,64,128]{2,1,0:T(8,128)(2,1)}, u32[]{:S(2)}) copy-start(bf16[8,64,128]{2,1,0:T(8,128)(2,1)} %refs_10_.1) | copy-start | bytes 393220
  11.7 3.6 %collective-permute-start.2 = (bf16[4,64,128]{2,1,0:T(8,128)(2,1)S(1)}, bf16[4,64,128]{2,1,0:T(8,128)(2,1)S(1)}, u32[]{:S(2)}, u32[]{:S(2)}) collective-permute-start(bf16[4,64,128]{2,1,0:T(8,128)(2,1)S(1)} %get-tuple-element.23), channel_id=1, source_target_pairs={{1,2},{2,1},{5,6},{6,5},{9,10},{10,9},{13,14},{14,13},{17,18},{18,... | collective-permute-start | bytes 196616 | tf_op jit(solution)/shard_map/ppermute | solution.py:473
  12.3 3.8 %collective-permute-start.3 = (bf16[4,64,128]{2,1,0:T(8,128)(2,1)S(1)}, bf16[4,64,128]{2,1,0:T(8,128)(2,1)S(1)}, u32[]{:S(2)}, u32[]{:S(2)}) collective-permute-start(bf16[4,64,128]{2,1,0:T(8,128)(2,1)S(1)} %get-tuple-element.24), channel_id=1, source_target_pairs={{0,1},{2,3},{1,0},{3,2},{4,5},{6,7},{5,4},{7,6},{8,9},{10,11},{9,8... | collective-permute-start | bytes 196616 | tf_op jit(solution)/shard_map/ppermute | solution.py:474
  16.3 7.3 %collective-permute-start.4 = (bf16[4,128,128]{2,1,0:T(8,128)(2,1)S(1)}, bf16[4,128,128]{2,1,0:T(8,128)(2,1)S(1)}, u32[]{:S(2)}, u32[]{:S(2)}) collective-permute-start(bf16[4,128,128]{2,1,0:T(8,128)(2,1)S(1)} %get-tuple-element.25), channel_id=1, source_target_pairs={{1,2},{2,1},{5,6},{6,5},{9,10},{10,9},{13,14},{14,13},{17,18},{18,... | collective-permute-start | bytes 393224 | tf_op jit(solution)/shard_map/ppermute | solution.py:485
  17.0 6.6 %collective-permute-start.5 = (bf16[4,128,128]{2,1,0:T(8,128)(2,1)S(1)}, bf16[4,128,128]{2,1,0:T(8,128)(2,1)S(1)}, u32[]{:S(2)}, u32[]{:S(2)}) collective-permute-start(bf16[4,128,128]{2,1,0:T(8,128)(2,1)S(1)} %get-tuple-element.26), channel_id=1, source_target_pairs={{0,1},{2,3},{1,0},{3,2},{4,5},{6,7},{5,4},{7,6},{8,9},{10,11},{9,8... | collective-permute-start | bytes 393224 | tf_op jit(solution)/shard_map/ppermute | solution.py:486
  23.6 16.1 %copy-start.4 = (bf16[384,64]{1,0:T(8,128)(2,1)S(1)}, bf16[384,64]{1,0:T(8,128)(2,1)}, u32[]{:S(2)}) copy-start(bf16[384,64]{1,0:T(8,128)(2,1)} %constant.10.clone.refs_4_) | copy-start | bytes 147460
  23.6 16.1 %copy-start.5 = (bf16[128,128]{1,0:T(8,128)(2,1)S(1)}, bf16[128,128]{1,0:T(8,128)(2,1)}, u32[]{:S(2)}) copy-start(bf16[128,128]{1,0:T(8,128)(2,1)} %constant.11.clone.refs_5_) | copy-start | bytes 98308

commit v6 on v5

--- a/solution.py
+++ b/solution.py
@@ -84,24 +84,21 @@
     return out
 
 
-def prepare_kernel(*refs):
-    sources, (b_ref, a_ref, idx_ref, wgt_ref), scratch, sems = refs[:5], refs[5:9], refs[9:14], refs[14]
-    copies = [pltpu.make_async_copy(sources[n], scratch[n], sems.at[n]) for n in range(5)]
-    for copy in copies:
-        copy.start()
-    for copy in copies:
-        copy.wait()
-    own_ref, conn_ref, xy_ref, z_ref, frac_ref = scratch
+def pack_own_kernel(own_ref, b_ref, a_ref, keep_ref):
+    keep_ref[...] = own_ref[...]
     pack_rows(own_ref, a_ref, b_ref, 0, lax.axis_index("gy") % 2 == 0)
-    first = conn_ref[0:1]
+
+
+def index_kernel(row_ref, idx_ref, wgt_ref):
+    first = row_ref[0:1].astype(jnp.int32)
     col_x = (first * 241) >> 12
     col_y = first - 17 * col_x
-    start_x = 8 * col_x + xy_ref[0:1] + HALO
-    start_y = 8 * col_y + xy_ref[1:2] + HALO
+    start_x = 8 * col_x + row_ref[1:2].astype(jnp.int32) + HALO
+    start_y = 8 * col_y + row_ref[2:3].astype(jnp.int32) + HALO
     early = (start_y >= 64) & (start_y < 184)
     below = start_y < 64
     offset = jnp.where(early, start_y - 64, jnp.where(below, start_y, start_y - 128))
-    base = (z_ref[...] + 2) * SPAN + start_x
+    base = (row_ref[3:4].astype(jnp.int32) + 2) * SPAN + start_x
     tile = jnp.where(early | below, 0, TILE_ROWS)
     shift = (8 * col_y - offset) & 127
     place = (col_y & 1) * 8 + col_x
@@ -118,7 +115,7 @@
     sub = lax.broadcasted_iota(jnp.int32, (8, 128), 0)
     table = jnp.where(sub == 6, jnp.broadcast_to(count, (8, 128)), table)
     idx_ref[...] = table.astype(jnp.int32)
-    value = as_rows([frac_ref[c : c + 1] for c in range(3)])
+    value = as_rows([row_ref[4 + c : 5 + c] for c in range(3)])
     hi, lo = split(value)
     rest = (value - hi.astype(F32) - lo.astype(F32)).astype(BF16)
     element = jnp.broadcast_to(col_x * 16 + col_y, (128, 128))
@@ -127,7 +124,7 @@
         wgt_ref[cx] = dot_rows(hi, spread) + dot_rows(lo, spread) + dot_rows(rest, spread)
 
 
-def pack_corner_kernel(xa_ref, xb_ref, own_b_ref, own_a_ref, b_ref, a_ref):
+def pack_corner_kernel(xa_ref, xb_ref, own_b_ref, own_a_ref, idx_ref, b_ref, a_ref):
     even = lax.axis_index("gy") % 2 == 0
     pack_rows(xa_ref, a_ref, b_ref, 0, even)
     pack_rows(xb_ref, a_ref, b_ref, 64, even)
@@ -321,9 +318,11 @@
 
 
 def product_kernel(
-    nx, ny, recv_ref, node_ref, slope_ref, sq_ref, expand_ref, wyt_ref, left_ref, wy_ref,
-    grad_ref, hess_ref, send_ref, msc, gsc,
+    nx, ny, recv_ref, node_ref, slope_ref, sq_ref, expand_ref, wyt_ref, left_ref, wy_ref, res_ref,
+    grad_ref, hess_ref, send_ref, out_ref, msc, gsc, sem,
 ):
+    copy_out = pltpu.make_async_copy(res_ref, out_ref, sem)
+    copy_out.start()
     gx, gy = lax.axis_index("gx"), lax.axis_index("gy")
     own = gx * ny + gy
     lane = lax.broadcasted_iota(jnp.int32, (8, 128), 1)
@@ -411,6 +410,8 @@
         def _():
             send_ref[px * ny + py] = jnp.where(tail, sums, data)
 
+    copy_out.wait()
+
 
 def finish_kernel(nx, ny, voxels, recv_ref, grad_ref, hess_ref, step_ref, prod_ref, misfit_ref):
     gx, gy = lax.axis_index("gx"), lax.axis_index("gy")
@@ -453,35 +454,38 @@
     xa = lax.ppermute(def_image, "gx", swaps(nx, 0))
     xb = lax.ppermute(def_image, "gx", swaps(nx, 1))
     half = sds((4, 64, 128), BF16)
-    to_b, to_a, idx, wgt = pl.pallas_call(
-        prepare_kernel,
-        out_shape=(half, half, sds((8, 128), jnp.int32), sds((8, 8, 128), F32)),
-        in_specs=[pl.BlockSpec(memory_space=pltpu.HBM)] * 5,
-        out_specs=(VMEM,) * 4,
-        scratch_shapes=[
-            pltpu.VMEM((8, 64, 128), BF16),
-            pltpu.VMEM((8, 128), jnp.int32),
-            pltpu.VMEM((2, 128), jnp.int32),
-            pltpu.VMEM((1, 128), jnp.int32),
-            pltpu.VMEM((3, 128), F32),
-            pltpu.SemaphoreType.DMA((5,)),
-        ],
+    to_b, to_a, own = pl.pallas_call(
+        pack_own_kernel,
+        out_shape=(half, half, sds((8, 64, 128), BF16)),
+        in_specs=[VMEM],
+        out_specs=(VMEM,) * 3,
         compiler_params=PARAMS,
         cost_estimate=pl.CostEstimate(flops=300000, bytes_accessed=262144, transcendentals=0),
-        name="prepare",
-    )(def_image, connectivity, shift_xy, shift_z.reshape(1, 128), frac)
+        name="pack_own_halo",
+    )(def_image)
     yb = lax.ppermute(to_b, "gy", swaps(ny, 1))
     ya = lax.ppermute(to_a, "gy", swaps(ny, 0))
+    table = [connectivity[:1], shift_xy, shift_z[None]]
+    table = [row.astype(F32) for row in table] + [frac, jnp.zeros((1, 128), F32)]
+    idx, wgt = pl.pallas_call(
+        index_kernel,
+        out_shape=(sds((8, 128), jnp.int32), sds((8, 8, 128), F32)),
+        in_specs=[VMEM],
+        out_specs=(VMEM, VMEM),
+        compiler_params=PARAMS,
+        cost_estimate=pl.CostEstimate(flops=300000, bytes_accessed=262144, transcendentals=0),
+        name="order_elements",
+    )(jnp.concatenate(table))
     corner = sds((4, 128, 128), BF16)
     corner_b, corner_a = pl.pallas_call(
         pack_corner_kernel,
         out_shape=(corner, corner),
-        in_specs=[VMEM, VMEM] + [pl.BlockSpec(memory_space=pl.ANY)] * 2,
+        in_specs=[VMEM, VMEM] + [pl.BlockSpec(memory_space=pl.ANY)] * 3,
         out_specs=(VMEM, VMEM),
         compiler_params=PARAMS,
         cost_estimate=pl.CostEstimate(flops=300000, bytes_accessed=524288, transcendentals=0),
         name="pack_corner_halo",
-    )(xa, xb, yb, ya)
+    )(xa, xb, yb, ya, idx)
     cb = lax.ppermute(corner_b, "gy", swaps(ny, 1))
     ca = lax.ppermute(corner_a, "gy", swaps(ny, 0))
 
@@ -495,7 +499,7 @@
         compiler_params=PARAMS,
         cost_estimate=pl.CostEstimate(flops=4000000, bytes_accessed=2000000, transcendentals=0),
         name="sample_early",
-    )(idx, xa, def_image, xb)
+    )(idx, xa, own, xb)
     residual, slopes, nodes, send, square = pl.pallas_call(
         lambda *refs: late_kernel(nx, ny, *refs),
         out_shape=(
@@ -515,17 +519,26 @@
         ],
         compiler_params=PARAMS,
         name="sample_and_gradient",
-    )(idx, wgt, xa, def_image, xb, yb, ya, cb, ca, arr, ref_image, left, wy)
+    )(idx, wgt, xa, own, xb, yb, ya, cb, ca, arr, ref_image, left, wy)
     recv = lax.all_to_all(send, ("gx", "gy"), 0, 0, tiled=True)
-    grads, hess, send = pl.pallas_call(
+    grads, hess, send, residual = pl.pallas_call(
         lambda *refs: product_kernel(nx, ny, *refs),
-        out_shape=(sds((6, 8, 128), F32), sds((6, 8, 128), F32), sds((peers, 1, 128), F32)),
-        in_specs=[VMEM] * 8,
-        out_specs=(VMEM,) * 3,
-        scratch_shapes=[pltpu.VMEM((6, 8, 8, 128), F32), pltpu.VMEM((6, 8, 8, 128), F32)],
+        out_shape=(
+            sds((6, 8, 128), F32),
+            sds((6, 8, 128), F32),
+            sds((peers, 1, 128), F32),
+            sds((8, 64, 128), BF16),
+        ),
+        in_specs=[VMEM] * 9,
+        out_specs=(VMEM,) * 3 + (pl.BlockSpec(memory_space=pl.ANY),),
+        scratch_shapes=[
+            pltpu.VMEM((6, 8, 8, 128), F32),
+            pltpu.VMEM((6, 8, 8, 128), F32),
+            pltpu.SemaphoreType.DMA,
+        ],
         compiler_params=PARAMS,
         name="gauss_newton_product",
-    )(recv, nodes, slopes, square, expand, wyt, left, wy)
+    )(recv, nodes, slopes, square, expand, wyt, left, wy, residual)
     recv = lax.all_to_all(send, ("gx", "gy"), 0, 0, tiled=True)
     voxels = 8 * 64 * 128 * peers
     step, product, misfit = pl.pallas_call(

time: 50.6 us -> 47.3 us (0.935)
  starting transfers between devices: 14.7 us -> 9.41 us
  blocking collectives: 20.3 us -> 23.5 us
  local copies, waits for them, and re-layouts: 3.66 us -> 1.63 us
  other arithmetic: 0 us -> 2.03 us
  waiting for transfers between devices: 0.91 us -> 0.05 us
  Pallas kernels: 10.3 us -> 9.53 us
    all_to_all x2, blocking collectives: 20.3 us -> 23.5 us  [on_device(): recv = lax.all_to_all(send, ('gx', 'gy'), 0, 0, tiled=True)]
    ppermute x1, starting transfers between devices: 5.79 us -> 3.03 us  [on_device(): xa = lax.ppermute(def_image, 'gx', swaps(nx, 0))]
    unnamed x20 -> x12, local copies, waits for them, and re-layouts: 3.66 us -> 0.93 us
    ppermute x1, starting transfers between devices: 4.01 us -> 1.47 us  [on_device(): ca = lax.ppermute(corner_a, 'gy', swaps(ny, 0))]
    convert_element_type x0 -> x3, other arithmetic: none -> 2.03 us  [on_device(): row.astype(F32)]
    pallas_call x1, Pallas kernels: 4.61 us -> 3.21 us  [on_device(): pl.pallas_call(lambda *refs: late_kernel(nx, ny, *refs), out_shape=(sds((...]
    ppermute x1, waiting for transfers between devices: 0.9 us -> 0.01 us  [on_device(): ya = lax.ppermute(to_a, 'gy', swaps(ny, 0))]
    pallas_call x1, Pallas kernels: 2.54 us -> 3.29 us  [on_device(): pl.pallas_call(early_kernel, out_shape=sds((16, 18, 8, 128), F32), in_spe...]
  transfers between devices with their start and end apart: 6 -> 6, of which waited for: 1 -> 0; matrix products, arithmetic and copies ran while one was open for 0% -> 6% of each run, Pallas kernels for 7% -> 9%
where the time goes in v6:
time: 47.3 us; the launch traced here: 47 us
  blocking collectives  23.5 us (50%)
  Pallas kernels  9.53 us (20%)
  starting transfers between devices  9.41 us (20%)
  other arithmetic  2.03 us (4%)
  local copies, waits for them, and re-layouts  1.63 us (3%)
  between operations  0.79 us (2%)
    all_to_all x2, blocking collectives, on_device(): recv = lax.all_to_all(send, ('gx', 'gy'), 0, 0, tiled=True)  23.5 us
    pallas_call x1, Pallas kernels, on_device(): pl.pallas_call(early_kernel, out_shape=sds((16, 18, 8, 128), F32), in_spe...  3.29 us
    pallas_call x1, Pallas kernels, on_device(): pl.pallas_call(lambda *refs: late_kernel(nx, ny, *refs), out_shape=(sds((...  3.21 us
    ppermute x1, starting transfers between devices, on_device(): xa = lax.ppermute(def_image, 'gx', swaps(nx, 0))  3.03 us
    ppermute x1, starting transfers between devices, on_device(): ya = lax.ppermute(to_a, 'gy', swaps(ny, 0))  2.92 us
    convert_element_type x3, other arithmetic, on_device(): row.astype(F32)  2.03 us
    ppermute x1, starting transfers between devices, on_device(): ca = lax.ppermute(corner_a, 'gy', swaps(ny, 0))  1.47 us
    pallas_call x1, Pallas kernels, on_device(): pl.pallas_call(lambda *refs: product_kernel(nx, ny, *refs), out_shape=(sd...  1.33 us
  transfers between devices with their start and end apart: 6, of which 0 were waited for; matrix products, arithmetic and copies ran while one was open for 6% of the time, Pallas kernels for 9%

profile of v6, /device:TPU:0, one launch (start us, length us, event | category | flops | bytes accessed | tf_op | source)
XLA Modules:
  0.0 47.0 jit_solution(4185765828157491575)
XLA Ops:
  0.6 0.0 copy-start.1
  0.6 0.0 copy-start
  0.7 0.0 copy-start.2
  0.7 3.0 %collective-permute-start = (bf16[8,64,128]{2,1,0:T(8,128)(2,1)}, bf16[8,64,128]{2,1,0:T(8,128)(2,1)S(1)}, u32[]{:S(2)}, u32[]{:S(2)}) collective-permute-start(bf16[8,64,128]{2,1,0:T(8,128)(2,1)} %own_ref.1), channel_id=1, source_target_pairs={{0,4},{8,12},{16,20},{24,28},{4,0},{12,8},{20,16},{28,24},{1,5},{9... | collective-permute-start | bytes 393224 | tf_op jit(solution)/shard_map/ppermute | solution.py:454
  3.7 0.7 %collective-permute-start.1 = (bf16[8,64,128]{2,1,0:T(8,128)(2,1)}, bf16[8,64,128]{2,1,0:T(8,128)(2,1)S(1)}, u32[]{:S(2)}, u32[]{:S(2)}) collective-permute-start(bf16[8,64,128]{2,1,0:T(8,128)(2,1)} %own_ref.1), channel_id=1, source_target_pairs={{4,8},{12,16},{20,24},{8,4},{16,12},{24,20},{5,9},{13,17},{21,25},... | collective-permute-start | bytes 393224 | tf_op jit(solution)/shard_map/ppermute | solution.py:455
  4.4 0.0 copy-start.3
  4.4 0.9 %copy-done.3 = bf16[8,64,128]{2,1,0:T(8,128)(2,1)S(1)} copy-done((bf16[8,64,128]{2,1,0:T(8,128)(2,1)S(1)}, bf16[8,64,128]{2,1,0:T(8,128)(2,1)}, u32[]{:S(2)}) %copy-start.3) | copy-done | bytes 131096
  5.3 0.1 pack_own_halo.1
  5.4 0.7 %collective-permute-start.2 = (bf16[4,64,128]{2,1,0:T(8,128)(2,1)S(1)}, bf16[4,64,128]{2,1,0:T(8,128)(2,1)S(1)}, u32[]{:S(2)}, u32[]{:S(2)}) collective-permute-start(bf16[4,64,128]{2,1,0:T(8,128)(2,1)S(1)} %get-tuple-element.26), channel_id=1, source_target_pairs={{1,2},{2,1},{5,6},{6,5},{9,10},{10,9},{13,14},{14,13},{17,18},{18,... | collective-permute-start | bytes 196616 | tf_op jit(solution)/shard_map/ppermute | solution.py:466
  6.1 2.9 %collective-permute-start.3 = (bf16[4,64,128]{2,1,0:T(8,128)(2,1)S(1)}, bf16[4,64,128]{2,1,0:T(8,128)(2,1)S(1)}, u32[]{:S(2)}, u32[]{:S(2)}) collective-permute-start(bf16[4,64,128]{2,1,0:T(8,128)(2,1)S(1)} %get-tuple-element.27), channel_id=1, source_target_pairs={{0,1},{2,3},{1,0},{3,2},{4,5},{6,7},{5,4},{7,6},{8,9},{10,11},{9,8... | collective-permute-start | bytes 196616 | tf_op jit(solution)/shard_map/ppermute | solution.py:467
  9.0 0.7 %slice_convert_fusion = f32[1,128]{1,0:T(1,128)S(1)} fusion(s32[8,128]{1,0:T(8,128)} %param.15), kind=kLoop, calls=%fused_computation.1 | loop fusion | flops 128 | bytes 1024 | tf_op jit(solution)/shard_map/convert_element_type | solution.py:469
  9.7 0.7 %convert_bitcast_fusion = f32[1,128]{1,0:T(1,128)S(1)} fusion(s32[128]{0:T(128)} %param.13), kind=kLoop, calls=%fused_computation | loop fusion | flops 128 | bytes 1024 | tf_op jit(solution)/shard_map/convert_element_type | solution.py:469
  10.3 0.7 %convert_element_type.13 = f32[2,128]{1,0:T(2,128)S(1)} convert(s32[2,128]{1,0:T(2,128)} %param.12) | non-fusion elementwise | flops 256 | bytes 2048 | tf_op jit(solution)/shard_map/convert_element_type | solution.py:469
  11.0 0.7 %concatenate.3.row_ref = f32[8,128]{1,0:T(8,128)S(1)} concatenate(f32[1,128]{1,0:T(1,128)S(1)} %slice_convert_fusion, f32[2,128]{1,0:T(2,128)S(1)} %convert_element_type.13, f32[1,128]{1,0:T(1,128)S(1)} %convert_bitcast_fusion, f32[3,128]{1,0:T(4,128)} %param.14, f32[1,128]{1,0:T(1,128)S(1)} %broadcast_in_dim.4), dimensions={0} | concatenate | bytes 8192 | tf_op jit(solution)/shard_map/concatenate | solution.py:478
  11.7 0.7 %order_elements.1 = (s32[8,128]{1,0:T(8,128)S(1)}, f32[8,8,128]{2,1,0:T(8,128)S(1)}) custom-call(f32[8,128]{1,0:T(8,128)S(1)} %concatenate.3.row_ref), custom_call_target="tpu_custom_call" | custom-call | flops 300000 | bytes 262144 | tf_op jit(solution)/shard_map/order_elements/pallas_call | solution.py:470
  12.4 0.0 collective-permute-done.2.own_b_ref.refs_5_
  12.4 0.0 collective-permute-done.3.own_a_ref.refs_6_
  12.4 0.0 collective-permute-done.xa_ref.refs_2_
  12.4 0.0 collective-permute-done.1.xb_ref.refs_4_
  12.4 0.1 pack_corner_halo.1
  12.6 0.7 %collective-permute-start.4 = (bf16[4,128,128]{2,1,0:T(8,128)(2,1)S(1)}, bf16[4,128,128]{2,1,0:T(8,128)(2,1)S(1)}, u32[]{:S(2)}, u32[]{:S(2)}) collective-permute-start(bf16[4,128,128]{2,1,0:T(8,128)(2,1)S(1)} %get-tuple-element.28), channel_id=1, source_target_pairs={{1,2},{2,1},{5,6},{6,5},{9,10},{10,9},{13,14},{14,13},{17,18},{18,... | collective-permute-start | bytes 393224 | tf_op jit(solution)/shard_map/ppermute | solution.py:489
  13.3 1.5 %collective-permute-start.5 = (bf16[4,128,128]{2,1,0:T(8,128)(2,1)S(1)}, bf16[4,128,128]{2,1,0:T(8,128)(2,1)S(1)}, u32[]{:S(2)}, u32[]{:S(2)}) collective-permute-start(bf16[4,128,128]{2,1,0:T(8,128)(2,1)S(1)} %get-tuple-element.29), channel_id=1, source_target_pairs={{0,1},{2,3},{1,0},{3,2},{4,5},{6,7},{5,4},{7,6},{8,9},{10,11},{9,8... | collective-permute-start | bytes 393224 | tf_op jit(solution)/shard_map/ppermute | solution.py:490
  14.7 3.3 %sample_early.1.refs_9_ = f32[16,18,8,128]{3,2,1,0:T(8,128)S(1)} custom-call(s32[8,128]{1,0:T(8,128)S(1)} %get-tuple-element.23.idx_ref.refs_0_, bf16[8,64,128]{2,1,0:T(8,128)(2,1)S(1)} %collective-permute-done.xa_ref.refs_2_, bf16[8,64,128]{2,1,0:T(8,128)(2,1)S(1)} %get-tuple-element.25.own_ref.refs_3_, ...), custom_call_target="tpu_custom_call" | custom-call | flops 4000000 | bytes 2000000 | tf_op jit(solution)/shard_map/sample_early/pallas_call | solution.py:493
  18.0 0.0 copy-start.4
  18.0 0.0 copy-start.5
  18.0 0.0 collective-permute-done.4.refs_7_
  18.0 0.0 collective-permute-done.5.refs_8_
  18.1 0.0 copy-done.1
  18.1 0.0 copy-done
  18.1 0.0 copy-done.2
  18.1 3.2 %sample_and_gradient.1 = (bf16[8,64,128]{2,1,0:T(8,128)(2,1)S(1)}, f32[3,8,8,8,128]{4,3,2,1,0:T(8,128)S(1)}, f32[64,128]{1,0:T(8,128)S(1)}, f32[32,1,128]{2,1,0:T(1,128)S(1)}, f32[8,128]{1,0:T(8,128)S(1)}) custom-call(s32[8,128]{1,0:T(8,128)S(1)} %get-tuple-element.23.idx_ref.refs_0_, f32[8,8,128]{2,1,0:T(8,128)S(1)} %get-tuple-element.24.refs_1_, ...), custom_call_target="tpu_custom_call" | custom-call | tf_op jit(solution)/shard_map/sample_and_gradient/pallas_call | solution.py:503
  21.3 14.7 %all_to_all.10.refs_0_ = f32[32,1,128]{2,1,0:T(1,128)S(1)} all-to-all(f32[32,1,128]{2,1,0:T(1,128)S(1)} %get-tuple-element.30), channel_id=1, replica_groups=mesh['gx'=8,'gy'=4] {'gx','gy'}, dimensions={0} | all-to-all | bytes 32768 | tf_op jit(solution)/shard_map/all_to_all | solution.py:523
  36.0 0.0 copy-done.4
  36.0 0.0 copy-done.5
  36.0 1.3 %gauss_newton_product.1 = (f32[6,8,128]{2,1,0:T(8,128)S(1)}, f32[6,8,128]{2,1,0:T(8,128)S(1)}, f32[32,1,128]{2,1,0:T(1,128)S(1)}, bf16[8,64,128]{2,1,0:T(8,128)(2,1)}) custom-call(f32[32,1,128]{2,1,0:T(1,128)S(1)} %all_to_all.10.refs_0_, f32[64,128]{1,0:T(8,128)S(1)} %get-tuple-element.31.refs_1_, f32[3,8,8,8,128]{4,3,2,1,0:T(8,128)S(1)} %get-tuple-element.32.refs_2_, ...), custom_call_target="tpu_custom_call" | custom-call | tf_op jit(solution)/shard_map/gauss_newton_product/pallas_call | solution.py:524
  37.3 8.8 %all_to_all.11.refs_0_ = f32[32,1,128]{2,1,0:T(1,128)S(1)} all-to-all(f32[32,1,128]{2,1,0:T(1,128)S(1)} %get-tuple-element.36), channel_id=1, replica_groups=mesh['gx'=8,'gy'=4] {'gx','gy'}, dimensions={0} | all-to-all | bytes 32768 | tf_op jit(solution)/shard_map/all_to_all | solution.py:542
  46.2 0.8 %finish.1 = (f32[3,2,8,16]{3,2,1,0:T(8,128)}, f32[3,2,8,16]{3,2,1,0:T(8,128)}, f32[1,1]{1,0:T(1,128)}) custom-call(f32[32,1,128]{2,1,0:T(1,128)S(1)} %all_to_all.11.refs_0_, f32[6,8,128]{2,1,0:T(8,128)S(1)} %get-tuple-element.37.refs_1_, f32[6,8,128]{2,1,0:T(8,128)S(1)} %get-tuple-element.38.refs_2_), custom_call_target="tpu_custom_call" | custom-call | tf_op jit(solution)/shard_map/finish/pallas_call | solution.py:544
  (1 shorter events, 0.0 us)
Async XLA Ops:
  0.6 17.4 %copy-start.1 = (bf16[128,128]{1,0:T(8,128)(2,1)S(1)}, bf16[128,128]{1,0:T(8,128)(2,1)}, u32[]{:S(2)}) copy-start(bf16[128,128]{1,0:T(8,128)(2,1)} %constant.11.clone.refs_12_.refs_7_) | copy-start | bytes 98308
  0.6 17.4 %copy-start = (bf16[64,384]{1,0:T(8,128)(2,1)S(1)}, bf16[64,384]{1,0:T(8,128)(2,1)}, u32[]{:S(2)}) copy-start(bf16[64,384]{1,0:T(8,128)(2,1)} %constant.10.clone.refs_11_.refs_6_) | copy-start | bytes 147460
  0.7 17.4 %copy-start.2 = (bf16[8,64,128]{2,1,0:T(8,128)(2,1)S(1)}, bf16[8,64,128]{2,1,0:T(8,128)(2,1)}, u32[]{:S(2)}) copy-start(bf16[8,64,128]{2,1,0:T(8,128)(2,1)} %refs_10_.1) | copy-start | bytes 393220
  0.7 11.7 %collective-permute-start = (bf16[8,64,128]{2,1,0:T(8,128)(2,1)}, bf16[8,64,128]{2,1,0:T(8,128)(2,1)S(1)}, u32[]{:S(2)}, u32[]{:S(2)}) collective-permute-start(bf16[8,64,128]{2,1,0:T(8,128)(2,1)} %own_ref.1), channel_id=1, source_target_pairs={{0,4},{8,12},{16,20},{24,28},{4,0},{12,8},{20,16},{28,24},{1,5},{9... | collective-permute-start | bytes 393224 | tf_op jit(solution)/shard_map/ppermute | solution.py:454
  3.7 8.7 %collective-permute-start.1 = (bf16[8,64,128]{2,1,0:T(8,128)(2,1)}, bf16[8,64,128]{2,1,0:T(8,128)(2,1)S(1)}, u32[]{:S(2)}, u32[]{:S(2)}) collective-permute-start(bf16[8,64,128]{2,1,0:T(8,128)(2,1)} %own_ref.1), channel_id=1, source_target_pairs={{4,8},{12,16},{20,24},{8,4},{16,12},{24,20},{5,9},{13,17},{21,25},... | collective-permute-start | bytes 393224 | tf_op jit(solution)/shard_map/ppermute | solution.py:455
  4.4 0.9 %copy-start.3 = (bf16[8,64,128]{2,1,0:T(8,128)(2,1)S(1)}, bf16[8,64,128]{2,1,0:T(8,128)(2,1)}, u32[]{:S(2)}) copy-start(bf16[8,64,128]{2,1,0:T(8,128)(2,1)} %own_ref.1) | copy-start | bytes 393220
  5.4 7.0 %collective-permute-start.2 = (bf16[4,64,128]{2,1,0:T(8,128)(2,1)S(1)}, bf16[4,64,128]{2,1,0:T(8,128)(2,1)S(1)}, u32[]{:S(2)}, u32[]{:S(2)}) collective-permute-start(bf16[4,64,128]{2,1,0:T(8,128)(2,1)S(1)} %get-tuple-element.26), channel_id=1, source_target_pairs={{1,2},{2,1},{5,6},{6,5},{9,10},{10,9},{13,14},{14,13},{17,18},{18,... | collective-permute-start | bytes 196616 | tf_op jit(solution)/shard_map/ppermute | solution.py:466
  6.1 6.3 %collective-permute-start.3 = (bf16[4,64,128]{2,1,0:T(8,128)(2,1)S(1)}, bf16[4,64,128]{2,1,0:T(8,128)(2,1)S(1)}, u32[]{:S(2)}, u32[]{:S(2)}) collective-permute-start(bf16[4,64,128]{2,1,0:T(8,128)(2,1)S(1)} %get-tuple-element.27), channel_id=1, source_target_pairs={{0,1},{2,3},{1,0},{3,2},{4,5},{6,7},{5,4},{7,6},{8,9},{10,11},{9,8... | collective-permute-start | bytes 196616 | tf_op jit(solution)/shard_map/ppermute | solution.py:467
  12.6 5.5 %collective-permute-start.4 = (bf16[4,128,128]{2,1,0:T(8,128)(2,1)S(1)}, bf16[4,128,128]{2,1,0:T(8,128)(2,1)S(1)}, u32[]{:S(2)}, u32[]{:S(2)}) collective-permute-start(bf16[4,128,128]{2,1,0:T(8,128)(2,1)S(1)} %get-tuple-element.28), channel_id=1, source_target_pairs={{1,2},{2,1},{5,6},{6,5},{9,10},{10,9},{13,14},{14,13},{17,18},{18,... | collective-permute-start | bytes 393224 | tf_op jit(solution)/shard_map/ppermute | solution.py:489
  13.3 4.8 %collective-permute-start.5 = (bf16[4,128,128]{2,1,0:T(8,128)(2,1)S(1)}, bf16[4,128,128]{2,1,0:T(8,128)(2,1)S(1)}, u32[]{:S(2)}, u32[]{:S(2)}) collective-permute-start(bf16[4,128,128]{2,1,0:T(8,128)(2,1)S(1)} %get-tuple-element.29), channel_id=1, source_target_pairs={{0,1},{2,3},{1,0},{3,2},{4,5},{6,7},{5,4},{7,6},{8,9},{10,11},{9,8... | collective-permute-start | bytes 393224 | tf_op jit(solution)/shard_map/ppermute | solution.py:490
  18.0 18.0 %copy-start.4 = (bf16[384,64]{1,0:T(8,128)(2,1)S(1)}, bf16[384,64]{1,0:T(8,128)(2,1)}, u32[]{:S(2)}) copy-start(bf16[384,64]{1,0:T(8,128)(2,1)} %constant.12.clone.refs_4_) | copy-start | bytes 147460
  18.0 18.0 %copy-start.5 = (bf16[128,128]{1,0:T(8,128)(2,1)S(1)}, bf16[128,128]{1,0:T(8,128)(2,1)}, u32[]{:S(2)}) copy-start(bf16[128,128]{1,0:T(8,128)(2,1)} %constant.13.clone.refs_5_) | copy-start | bytes 98308

commit v7 on v6

--- a/solution.py
+++ b/solution.py
@@ -93,12 +93,12 @@
     first = row_ref[0:1].astype(jnp.int32)
     col_x = (first * 241) >> 12
     col_y = first - 17 * col_x
-    start_x = 8 * col_x + row_ref[1:2].astype(jnp.int32) + HALO
-    start_y = 8 * col_y + row_ref[2:3].astype(jnp.int32) + HALO
+    start_x = 8 * col_x + row_ref[8:9].astype(jnp.int32) + HALO
+    start_y = 8 * col_y + row_ref[9:10].astype(jnp.int32) + HALO
     early = (start_y >= 64) & (start_y < 184)
     below = start_y < 64
     offset = jnp.where(early, start_y - 64, jnp.where(below, start_y, start_y - 128))
-    base = (row_ref[3:4].astype(jnp.int32) + 2) * SPAN + start_x
+    base = (row_ref[10:11].astype(jnp.int32) + 2) * SPAN + start_x
     tile = jnp.where(early | below, 0, TILE_ROWS)
     shift = (8 * col_y - offset) & 127
     place = (col_y & 1) * 8 + col_x
@@ -115,7 +115,7 @@
     sub = lax.broadcasted_iota(jnp.int32, (8, 128), 0)
     table = jnp.where(sub == 6, jnp.broadcast_to(count, (8, 128)), table)
     idx_ref[...] = table.astype(jnp.int32)
-    value = as_rows([row_ref[4 + c : 5 + c] for c in range(3)])
+    value = as_rows([row_ref[11 + c : 12 + c] for c in range(3)])
     hi, lo = split(value)
     rest = (value - hi.astype(F32) - lo.astype(F32)).astype(BF16)
     element = jnp.broadcast_to(col_x * 16 + col_y, (128, 128))
@@ -294,7 +294,7 @@
             gsc[2 * k + 1, cx] = upper[k]
         return square
 
-    sq_ref[...] = lax.fori_loop(0, 8, interpolate, jnp.zeros((8, 128), F32))
+    sq_ref[...] = lax.fori_loop(0, 8, interpolate, jnp.zeros((8, 128), F32), unroll=4)
     res_ref[...] = rsc[...].reshape(8, 64, 128).astype(BF16)
     nodes = dot_left(dot_right(left_ref[...], gsc[...].reshape(384, 128)), wy_ref[...])
     node_ref[...] = nodes
@@ -390,7 +390,7 @@
             gsc[2 * k + 1, cx] = upper[k]
         return curve
 
-    curve = lax.fori_loop(0, 8, apply, jnp.zeros((8, 128), F32))
+    curve = lax.fori_loop(0, 8, apply, jnp.zeros((8, 128), F32), unroll=4)
     nodes = dot_left(dot_right(left_ref[...], gsc[...].reshape(384, 128)), wy_ref[...])
     rows = [nodes[kc * 8 : kc * 8 + 8] for kc in range(6)]
     for kc in range(6):
@@ -465,8 +465,10 @@
     )(def_image)
     yb = lax.ppermute(to_b, "gy", swaps(ny, 1))
     ya = lax.ppermute(to_a, "gy", swaps(ny, 0))
-    table = [connectivity[:1], shift_xy, shift_z[None]]
-    table = [row.astype(F32) for row in table] + [frac, jnp.zeros((1, 128), F32)]
+    row = lax.broadcasted_iota(jnp.int32, (16, 128), 0)
+    table = jnp.where(row == 10, shift_z[None], 0).astype(F32)
+    for rows, at in ((connectivity, 0), (shift_xy, 8), (frac, 11)):
+        table = table + jnp.pad(rows.astype(F32), ((at, 16 - at - rows.shape[0]), (0, 0)))
     idx, wgt = pl.pallas_call(
         index_kernel,
         out_shape=(sds((8, 128), jnp.int32), sds((8, 8, 128), F32)),
@@ -475,7 +477,7 @@
         compiler_params=PARAMS,
         cost_estimate=pl.CostEstimate(flops=300000, bytes_accessed=262144, transcendentals=0),
         name="order_elements",
-    )(jnp.concatenate(table))
+    )(table)
     corner = sds((4, 128, 128), BF16)
     corner_b, corner_a = pl.pallas_call(
         pack_corner_kernel,

time: 47.3 us -> 46.1 us (0.975)
  local copies, waits for them, and re-layouts: 1.63 us -> 0.93 us
  blocking collectives: 23.5 us -> 22.9 us
  starting transfers between devices: 9.41 us -> 10 us
  Pallas kernels: 9.53 us -> 8.99 us
    add x0 -> x1, other arithmetic: none -> 0.76 us  [on_device(): table + jnp.pad(rows.astype(F32), ((at, 16 - at - rows.shape[0]), (0, 0)))]
    pallas_call x1, Pallas kernels: 3.29 us -> 2.54 us  [on_device(): pl.pallas_call(early_kernel, out_shape=sds((16, 18, 8, 128), F32), in_spe...]
    concatenate x1 -> x0, local copies, waits for them, and re-layouts: 0.7 us -> none  [on_device(): jnp.concatenate(table)]
    convert_element_type x3 -> x2, other arithmetic: 2.03 us -> 1.37 us  [on_device(): rows.astype(F32)]
    ppermute x1, starting transfers between devices: 1.47 us -> 2.07 us  [on_device(): ca = lax.ppermute(corner_a, 'gy', swaps(ny, 0))]
    all_to_all x2, blocking collectives: 23.5 us -> 22.9 us  [on_device(): recv = lax.all_to_all(send, ('gx', 'gy'), 0, 0, tiled=True)]
  transfers between devices with their start and end apart: 6 -> 6, of which waited for: 0 -> 0; matrix products, arithmetic and copies ran while one was open for 6% -> 5% of each run, Pallas kernels for 9% -> 7%
where the time goes in v7:
time: 46.1 us; the launch traced here: 45.8 us
  blocking collectives  22.9 us (50%)
  starting transfers between devices  10 us (22%)
  Pallas kernels  8.99 us (20%)
  other arithmetic  2.13 us (5%)
  local copies, waits for them, and re-layouts  0.93 us (2%)
  between operations  0.79 us (2%)
    all_to_all x2, blocking collectives, on_device(): recv = lax.all_to_all(send, ('gx', 'gy'), 0, 0, tiled=True)  22.9 us
    pallas_call x1, Pallas kernels, on_device(): pl.pallas_call(lambda *refs: late_kernel(nx, ny, *refs), out_shape=(sds((...  3.49 us
    ppermute x1, starting transfers between devices, on_device(): xa = lax.ppermute(def_image, 'gx', swaps(nx, 0))  3.03 us
    ppermute x1, starting transfers between devices, on_device(): ya = lax.ppermute(to_a, 'gy', swaps(ny, 0))  2.92 us
    pallas_call x1, Pallas kernels, on_device(): pl.pallas_call(early_kernel, out_shape=sds((16, 18, 8, 128), F32), in_spe...  2.54 us
    ppermute x1, starting transfers between devices, on_device(): ca = lax.ppermute(corner_a, 'gy', swaps(ny, 0))  2.07 us
    convert_element_type x2, other arithmetic, on_device(): rows.astype(F32)  1.37 us
    pallas_call x1, Pallas kernels, on_device(): pl.pallas_call(lambda *refs: product_kernel(nx, ny, *refs), out_shape=(sd...  1.26 us
  transfers between devices with their start and end apart: 6, of which 0 were waited for; matrix products, arithmetic and copies ran while one was open for 5% of the time, Pallas kernels for 7%

profile of v7, /device:TPU:0, one launch (start us, length us, event | category | flops | bytes accessed | tf_op | source)
XLA Modules:
  0.0 45.8 jit_solution(17759120195592495032)
XLA Ops:
  0.6 0.0 copy-start.1
  0.6 0.0 copy-start
  0.7 0.0 copy-start.2
  0.7 3.0 %collective-permute-start = (bf16[8,64,128]{2,1,0:T(8,128)(2,1)}, bf16[8,64,128]{2,1,0:T(8,128)(2,1)S(1)}, u32[]{:S(2)}, u32[]{:S(2)}) collective-permute-start(bf16[8,64,128]{2,1,0:T(8,128)(2,1)} %own_ref.1), channel_id=1, source_target_pairs={{0,4},{8,12},{16,20},{24,28},{4,0},{12,8},{20,16},{28,24},{1,5},{9... | collective-permute-start | bytes 393224 | tf_op jit(solution)/shard_map/ppermute | solution.py:454
  3.7 0.7 %collective-permute-start.1 = (bf16[8,64,128]{2,1,0:T(8,128)(2,1)}, bf16[8,64,128]{2,1,0:T(8,128)(2,1)S(1)}, u32[]{:S(2)}, u32[]{:S(2)}) collective-permute-start(bf16[8,64,128]{2,1,0:T(8,128)(2,1)} %own_ref.1), channel_id=1, source_target_pairs={{4,8},{12,16},{20,24},{8,4},{16,12},{24,20},{5,9},{13,17},{21,25},... | collective-permute-start | bytes 393224 | tf_op jit(solution)/shard_map/ppermute | solution.py:455
  4.4 0.0 copy-start.3
  4.4 0.9 %copy-done.3 = bf16[8,64,128]{2,1,0:T(8,128)(2,1)S(1)} copy-done((bf16[8,64,128]{2,1,0:T(8,128)(2,1)S(1)}, bf16[8,64,128]{2,1,0:T(8,128)(2,1)}, u32[]{:S(2)}) %copy-start.3) | copy-done | bytes 131096
  5.3 0.1 pack_own_halo.1
  5.4 0.7 %collective-permute-start.2 = (bf16[4,64,128]{2,1,0:T(8,128)(2,1)S(1)}, bf16[4,64,128]{2,1,0:T(8,128)(2,1)S(1)}, u32[]{:S(2)}, u32[]{:S(2)}) collective-permute-start(bf16[4,64,128]{2,1,0:T(8,128)(2,1)S(1)} %get-tuple-element.26), channel_id=1, source_target_pairs={{1,2},{2,1},{5,6},{6,5},{9,10},{10,9},{13,14},{14,13},{17,18},{18,... | collective-permute-start | bytes 196616 | tf_op jit(solution)/shard_map/ppermute | solution.py:466
  6.1 2.9 %collective-permute-start.3 = (bf16[4,64,128]{2,1,0:T(8,128)(2,1)S(1)}, bf16[4,64,128]{2,1,0:T(8,128)(2,1)S(1)}, u32[]{:S(2)}, u32[]{:S(2)}) collective-permute-start(bf16[4,64,128]{2,1,0:T(8,128)(2,1)S(1)} %get-tuple-element.27), channel_id=1, source_target_pairs={{0,1},{2,3},{1,0},{3,2},{4,5},{6,7},{5,4},{7,6},{8,9},{10,11},{9,8... | collective-permute-start | bytes 196616 | tf_op jit(solution)/shard_map/ppermute | solution.py:467
  9.0 0.7 %convert_element_type.17 = f32[2,128]{1,0:T(2,128)S(1)} convert(s32[2,128]{1,0:T(2,128)} %param.12) | non-fusion elementwise | flops 256 | bytes 2048 | tf_op jit(solution)/shard_map/convert_element_type | solution.py:471
  9.7 0.7 %convert_element_type.16 = f32[8,128]{1,0:T(8,128)S(1)} convert(s32[8,128]{1,0:T(8,128)} %param.15) | non-fusion elementwise | flops 1024 | bytes 8192 | tf_op jit(solution)/shard_map/convert_element_type | solution.py:471
  10.3 0.8 %pad_add_fusion.row_ref = f32[16,128]{1,0:T(8,128)S(1)} fusion(f32[3,128]{1,0:T(4,128)} %param.14, f32[2,128]{1,0:T(2,128)S(1)} %convert_element_type.17, f32[8,128]{1,0:T(8,128)S(1)} %convert_element_type.16, s32[128]{0:T(128)} %param.13, pred[16]{0:T(512)(128)(4,1)S(1)} %iota_compare_fusion), kind=kLoop, calls=%fused_computation | loop fusion | flops 10240 | bytes 15376 | tf_op jit(solution)/shard_map/add | solution.py:471
  11.1 0.7 %order_elements.1 = (s32[8,128]{1,0:T(8,128)S(1)}, f32[8,8,128]{2,1,0:T(8,128)S(1)}) custom-call(f32[16,128]{1,0:T(8,128)S(1)} %pad_add_fusion.row_ref), custom_call_target="tpu_custom_call" | custom-call | flops 300000 | bytes 262144 | tf_op jit(solution)/shard_map/order_elements/pallas_call | solution.py:472
  11.8 0.0 collective-permute-done.2.own_b_ref.refs_5_
  11.8 0.0 collective-permute-done.3.own_a_ref.refs_6_
  11.8 0.0 collective-permute-done.xa_ref.refs_2_
  11.8 0.0 collective-permute-done.1.xb_ref.refs_4_
  11.8 0.1 pack_corner_halo.1
  12.0 0.7 %collective-permute-start.4 = (bf16[4,128,128]{2,1,0:T(8,128)(2,1)S(1)}, bf16[4,128,128]{2,1,0:T(8,128)(2,1)S(1)}, u32[]{:S(2)}, u32[]{:S(2)}) collective-permute-start(bf16[4,128,128]{2,1,0:T(8,128)(2,1)S(1)} %get-tuple-element.28), channel_id=1, source_target_pairs={{1,2},{2,1},{5,6},{6,5},{9,10},{10,9},{13,14},{14,13},{17,18},{18,... | collective-permute-start | bytes 393224 | tf_op jit(solution)/shard_map/ppermute | solution.py:491
  12.7 2.1 %collective-permute-start.5 = (bf16[4,128,128]{2,1,0:T(8,128)(2,1)S(1)}, bf16[4,128,128]{2,1,0:T(8,128)(2,1)S(1)}, u32[]{:S(2)}, u32[]{:S(2)}) collective-permute-start(bf16[4,128,128]{2,1,0:T(8,128)(2,1)S(1)} %get-tuple-element.29), channel_id=1, source_target_pairs={{0,1},{2,3},{1,0},{3,2},{4,5},{6,7},{5,4},{7,6},{8,9},{10,11},{9,8... | collective-permute-start | bytes 393224 | tf_op jit(solution)/shard_map/ppermute | solution.py:492
  14.7 2.5 %sample_early.1.refs_9_ = f32[16,18,8,128]{3,2,1,0:T(8,128)S(1)} custom-call(s32[8,128]{1,0:T(8,128)S(1)} %get-tuple-element.23.idx_ref.refs_0_, bf16[8,64,128]{2,1,0:T(8,128)(2,1)S(1)} %collective-permute-done.xa_ref.refs_2_, bf16[8,64,128]{2,1,0:T(8,128)(2,1)S(1)} %get-tuple-element.25.own_ref.refs_3_, ...), custom_call_target="tpu_custom_call" | custom-call | flops 4000000 | bytes 2000000 | tf_op jit(solution)/shard_map/sample_early/pallas_call | solution.py:495
  17.3 0.0 copy-start.4
  17.3 0.0 copy-start.5
  17.3 0.0 collective-permute-done.4.refs_7_
  17.3 0.0 collective-permute-done.5.refs_8_
  17.3 0.0 copy-done.1
  17.3 0.0 copy-done
  17.3 0.0 copy-done.2
  17.3 3.5 %sample_and_gradient.1 = (bf16[8,64,128]{2,1,0:T(8,128)(2,1)S(1)}, f32[3,8,8,8,128]{4,3,2,1,0:T(8,128)S(1)}, f32[64,128]{1,0:T(8,128)S(1)}, f32[32,1,128]{2,1,0:T(1,128)S(1)}, f32[8,128]{1,0:T(8,128)S(1)}) custom-call(s32[8,128]{1,0:T(8,128)S(1)} %get-tuple-element.23.idx_ref.refs_0_, f32[8,8,128]{2,1,0:T(8,128)S(1)} %get-tuple-element.24.refs_1_, ...), custom_call_target="tpu_custom_call" | custom-call | tf_op jit(solution)/shard_map/sample_and_gradient/pallas_call | solution.py:505
  20.8 14.1 %all_to_all.10.refs_0_ = f32[32,1,128]{2,1,0:T(1,128)S(1)} all-to-all(f32[32,1,128]{2,1,0:T(1,128)S(1)} %get-tuple-element.30), channel_id=1, replica_groups=mesh['gx'=8,'gy'=4] {'gx','gy'}, dimensions={0} | all-to-all | bytes 32768 | tf_op jit(solution)/shard_map/all_to_all | solution.py:525
  34.9 0.0 copy-done.4
  34.9 0.0 copy-done.5
  34.9 1.3 %gauss_newton_product.1 = (f32[6,8,128]{2,1,0:T(8,128)S(1)}, f32[6,8,128]{2,1,0:T(8,128)S(1)}, f32[32,1,128]{2,1,0:T(1,128)S(1)}, bf16[8,64,128]{2,1,0:T(8,128)(2,1)}) custom-call(f32[32,1,128]{2,1,0:T(1,128)S(1)} %all_to_all.10.refs_0_, f32[64,128]{1,0:T(8,128)S(1)} %get-tuple-element.31.refs_1_, f32[3,8,8,8,128]{4,3,2,1,0:T(8,128)S(1)} %get-tuple-element.32.refs_2_, ...), custom_call_target="tpu_custom_call" | custom-call | tf_op jit(solution)/shard_map/gauss_newton_product/pallas_call | solution.py:526
  36.2 8.8 %all_to_all.11.refs_0_ = f32[32,1,128]{2,1,0:T(1,128)S(1)} all-to-all(f32[32,1,128]{2,1,0:T(1,128)S(1)} %get-tuple-element.36), channel_id=1, replica_groups=mesh['gx'=8,'gy'=4] {'gx','gy'}, dimensions={0} | all-to-all | bytes 32768 | tf_op jit(solution)/shard_map/all_to_all | solution.py:544
  45.1 0.8 %finish.1 = (f32[3,2,8,16]{3,2,1,0:T(8,128)}, f32[3,2,8,16]{3,2,1,0:T(8,128)}, f32[1,1]{1,0:T(1,128)}) custom-call(f32[32,1,128]{2,1,0:T(1,128)S(1)} %all_to_all.11.refs_0_, f32[6,8,128]{2,1,0:T(8,128)S(1)} %get-tuple-element.37.refs_1_, f32[6,8,128]{2,1,0:T(8,128)S(1)} %get-tuple-element.38.refs_2_), custom_call_target="tpu_custom_call" | custom-call | tf_op jit(solution)/shard_map/finish/pallas_call | solution.py:546
  (1 shorter events, 0.0 us)
Async XLA Ops:
  0.6 16.7 %copy-start.1 = (bf16[128,128]{1,0:T(8,128)(2,1)S(1)}, bf16[128,128]{1,0:T(8,128)(2,1)}, u32[]{:S(2)}) copy-start(bf16[128,128]{1,0:T(8,128)(2,1)} %constant.15.clone.refs_12_.refs_7_) | copy-start | bytes 98308
  0.6 16.7 %copy-start = (bf16[64,384]{1,0:T(8,128)(2,1)S(1)}, bf16[64,384]{1,0:T(8,128)(2,1)}, u32[]{:S(2)}) copy-start(bf16[64,384]{1,0:T(8,128)(2,1)} %constant.14.clone.refs_11_.refs_6_) | copy-start | bytes 147460
  0.7 16.7 %copy-start.2 = (bf16[8,64,128]{2,1,0:T(8,128)(2,1)S(1)}, bf16[8,64,128]{2,1,0:T(8,128)(2,1)}, u32[]{:S(2)}) copy-start(bf16[8,64,128]{2,1,0:T(8,128)(2,1)} %refs_10_.1) | copy-start | bytes 393220
  0.7 11.1 %collective-permute-start = (bf16[8,64,128]{2,1,0:T(8,128)(2,1)}, bf16[8,64,128]{2,1,0:T(8,128)(2,1)S(1)}, u32[]{:S(2)}, u32[]{:S(2)}) collective-permute-start(bf16[8,64,128]{2,1,0:T(8,128)(2,1)} %own_ref.1), channel_id=1, source_target_pairs={{0,4},{8,12},{16,20},{24,28},{4,0},{12,8},{20,16},{28,24},{1,5},{9... | collective-permute-start | bytes 393224 | tf_op jit(solution)/shard_map/ppermute | solution.py:454
  3.7 8.1 %collective-permute-start.1 = (bf16[8,64,128]{2,1,0:T(8,128)(2,1)}, bf16[8,64,128]{2,1,0:T(8,128)(2,1)S(1)}, u32[]{:S(2)}, u32[]{:S(2)}) collective-permute-start(bf16[8,64,128]{2,1,0:T(8,128)(2,1)} %own_ref.1), channel_id=1, source_target_pairs={{4,8},{12,16},{20,24},{8,4},{16,12},{24,20},{5,9},{13,17},{21,25},... | collective-permute-start | bytes 393224 | tf_op jit(solution)/shard_map/ppermute | solution.py:455
  4.4 0.9 %copy-start.3 = (bf16[8,64,128]{2,1,0:T(8,128)(2,1)S(1)}, bf16[8,64,128]{2,1,0:T(8,128)(2,1)}, u32[]{:S(2)}) copy-start(bf16[8,64,128]{2,1,0:T(8,128)(2,1)} %own_ref.1) | copy-start | bytes 393220
  5.4 6.4 %collective-permute-start.2 = (bf16[4,64,128]{2,1,0:T(8,128)(2,1)S(1)}, bf16[4,64,128]{2,1,0:T(8,128)(2,1)S(1)}, u32[]{:S(2)}, u32[]{:S(2)}) collective-permute-start(bf16[4,64,128]{2,1,0:T(8,128)(2,1)S(1)} %get-tuple-element.26), channel_id=1, source_target_pairs={{1,2},{2,1},{5,6},{6,5},{9,10},{10,9},{13,14},{14,13},{17,18},{18,... | collective-permute-start | bytes 196616 | tf_op jit(solution)/shard_map/ppermute | solution.py:466
  6.1 5.7 %collective-permute-start.3 = (bf16[4,64,128]{2,1,0:T(8,128)(2,1)S(1)}, bf16[4,64,128]{2,1,0:T(8,128)(2,1)S(1)}, u32[]{:S(2)}, u32[]{:S(2)}) collective-permute-start(bf16[4,64,128]{2,1,0:T(8,128)(2,1)S(1)} %get-tuple-element.27), channel_id=1, source_target_pairs={{0,1},{2,3},{1,0},{3,2},{4,5},{6,7},{5,4},{7,6},{8,9},{10,11},{9,8... | collective-permute-start | bytes 196616 | tf_op jit(solution)/shard_map/ppermute | solution.py:467
  12.0 5.3 %collective-permute-start.4 = (bf16[4,128,128]{2,1,0:T(8,128)(2,1)S(1)}, bf16[4,128,128]{2,1,0:T(8,128)(2,1)S(1)}, u32[]{:S(2)}, u32[]{:S(2)}) collective-permute-start(bf16[4,128,128]{2,1,0:T(8,128)(2,1)S(1)} %get-tuple-element.28), channel_id=1, source_target_pairs={{1,2},{2,1},{5,6},{6,5},{9,10},{10,9},{13,14},{14,13},{17,18},{18,... | collective-permute-start | bytes 393224 | tf_op jit(solution)/shard_map/ppermute | solution.py:491
  12.7 4.6 %collective-permute-start.5 = (bf16[4,128,128]{2,1,0:T(8,128)(2,1)S(1)}, bf16[4,128,128]{2,1,0:T(8,128)(2,1)S(1)}, u32[]{:S(2)}, u32[]{:S(2)}) collective-permute-start(bf16[4,128,128]{2,1,0:T(8,128)(2,1)S(1)} %get-tuple-element.29), channel_id=1, source_target_pairs={{0,1},{2,3},{1,0},{3,2},{4,5},{6,7},{5,4},{7,6},{8,9},{10,11},{9,8... | collective-permute-start | bytes 393224 | tf_op jit(solution)/shard_map/ppermute | solution.py:492
  17.3 17.7 %copy-start.4 = (bf16[384,64]{1,0:T(8,128)(2,1)S(1)}, bf16[384,64]{1,0:T(8,128)(2,1)}, u32[]{:S(2)}) copy-start(bf16[384,64]{1,0:T(8,128)(2,1)} %constant.16.clone.refs_4_) | copy-start | bytes 147460
  17.3 17.7 %copy-start.5 = (bf16[128,128]{1,0:T(8,128)(2,1)S(1)}, bf16[128,128]{1,0:T(8,128)(2,1)}, u32[]{:S(2)}) copy-start(bf16[128,128]{1,0:T(8,128)(2,1)} %constant.17.clone.refs_5_) | copy-start | bytes 98308

commit v8 on v7

--- a/solution.py
+++ b/solution.py
@@ -84,12 +84,8 @@
     return out
 
 
-def pack_own_kernel(own_ref, b_ref, a_ref, keep_ref):
+def index_kernel(row_ref, own_ref, idx_ref, wgt_ref, keep_ref):
     keep_ref[...] = own_ref[...]
-    pack_rows(own_ref, a_ref, b_ref, 0, lax.axis_index("gy") % 2 == 0)
-
-
-def index_kernel(row_ref, idx_ref, wgt_ref):
     first = row_ref[0:1].astype(jnp.int32)
     col_x = (first * 241) >> 12
     col_y = first - 17 * col_x
@@ -124,10 +120,10 @@
         wgt_ref[cx] = dot_rows(hi, spread) + dot_rows(lo, spread) + dot_rows(rest, spread)
 
 
-def pack_corner_kernel(xa_ref, xb_ref, own_b_ref, own_a_ref, idx_ref, b_ref, a_ref):
+def pack_kernel(xa_ref, own_ref, xb_ref, b_ref, a_ref):
     even = lax.axis_index("gy") % 2 == 0
-    pack_rows(xa_ref, a_ref, b_ref, 0, even)
-    pack_rows(xb_ref, a_ref, b_ref, 64, even)
+    for n, ref in enumerate((xa_ref, own_ref, xb_ref)):
+        pack_rows(ref, a_ref, b_ref, 64 * n, even)
 
 
 def over_sublanes(x):
@@ -206,7 +202,7 @@
 
 
 def late_kernel(
-    nx, ny, idx_ref, wgt, xa_ref, own_ref, xb_ref, yb_ref, ya_ref, cb_ref, ca_ref, arr_ref, ref_ref,
+    nx, ny, idx_ref, wgt, xa_ref, own_ref, xb_ref, yb_ref, ya_ref, arr_ref, ref_ref,
     left_ref, wy_ref, res_ref, slope_ref, node_ref, send_ref, sq_ref, img, arr, rsc, gsc,
 ):
     half = lax.broadcasted_iota(jnp.int32, (64, 128), 1) < 64
@@ -214,16 +210,16 @@
     odd_y = lax.axis_index("gy") % 2 == 1
     at_a = place_of_a()
     segments = (
-        (xa_ref, ca_ref, cb_ref, 0, at_a),
-        (own_ref, ya_ref, yb_ref, 0, 64),
-        (xb_ref, ca_ref, cb_ref, 64, 128 - at_a),
+        (xa_ref, 0, at_a),
+        (own_ref, 64, 64),
+        (xb_ref, 128, 128 - at_a),
     )
     for p in range(4):
-        for ref, pair_a, pair_b, at, row in segments:
+        for ref, at, row in segments:
             ra = pltpu.roll(ref[p].astype(F32), 64, 1)
             rc = pltpu.roll(ref[p + 4].astype(F32), 64, 1)
-            from_a = pair_a[p, pl.ds(at, 64)].astype(F32)
-            from_b = pair_b[p, pl.ds(at, 64)].astype(F32)
+            from_a = ya_ref[p, pl.ds(at, 64)].astype(F32)
+            from_b = yb_ref[p, pl.ds(at, 64)].astype(F32)
             lo = jnp.where(odd_y, from_a, from_b)
             hi = jnp.where(odd_y, from_b, from_a)
             at_row = lambda k, q: pl.ds(pl.multiple_of(k * TILE_ROWS + (q + 2) * SPAN + row, 8), 64)
@@ -453,43 +449,31 @@
     sds = jax.ShapeDtypeStruct
     xa = lax.ppermute(def_image, "gx", swaps(nx, 0))
     xb = lax.ppermute(def_image, "gx", swaps(nx, 1))
-    half = sds((4, 64, 128), BF16)
-    to_b, to_a, own = pl.pallas_call(
-        pack_own_kernel,
-        out_shape=(half, half, sds((8, 64, 128), BF16)),
-        in_specs=[VMEM],
-        out_specs=(VMEM,) * 3,
-        compiler_params=PARAMS,
-        cost_estimate=pl.CostEstimate(flops=300000, bytes_accessed=262144, transcendentals=0),
-        name="pack_own_halo",
-    )(def_image)
-    yb = lax.ppermute(to_b, "gy", swaps(ny, 1))
-    ya = lax.ppermute(to_a, "gy", swaps(ny, 0))
     row = lax.broadcasted_iota(jnp.int32, (16, 128), 0)
     table = jnp.where(row == 10, shift_z[None], 0).astype(F32)
     for rows, at in ((connectivity, 0), (shift_xy, 8), (frac, 11)):
         table = table + jnp.pad(rows.astype(F32), ((at, 16 - at - rows.shape[0]), (0, 0)))
-    idx, wgt = pl.pallas_call(
+    idx, wgt, own = pl.pallas_call(
         index_kernel,
-        out_shape=(sds((8, 128), jnp.int32), sds((8, 8, 128), F32)),
-        in_specs=[VMEM],
-        out_specs=(VMEM, VMEM),
+        out_shape=(sds((8, 128), jnp.int32), sds((8, 8, 128), F32), sds((8, 64, 128), BF16)),
+        in_specs=[VMEM, VMEM],
+        out_specs=(VMEM,) * 3,
         compiler_params=PARAMS,
         cost_estimate=pl.CostEstimate(flops=300000, bytes_accessed=262144, transcendentals=0),
         name="order_elements",
-    )(table)
-    corner = sds((4, 128, 128), BF16)
-    corner_b, corner_a = pl.pallas_call(
-        pack_corner_kernel,
-        out_shape=(corner, corner),
-        in_specs=[VMEM, VMEM] + [pl.BlockSpec(memory_space=pl.ANY)] * 3,
+    )(table, def_image)
+    packed = sds((4, SPAN, 128), BF16)
+    to_b, to_a = pl.pallas_call(
+        pack_kernel,
+        out_shape=(packed, packed),
+        in_specs=[VMEM] * 3,
         out_specs=(VMEM, VMEM),
         compiler_params=PARAMS,
         cost_estimate=pl.CostEstimate(flops=300000, bytes_accessed=524288, transcendentals=0),
-        name="pack_corner_halo",
-    )(xa, xb, yb, ya, idx)
-    cb = lax.ppermute(corner_b, "gy", swaps(ny, 1))
-    ca = lax.ppermute(corner_a, "gy", swaps(ny, 0))
+        name="pack_halo",
+    )(xa, own, xb)
+    yb = lax.ppermute(to_b, "gy", swaps(ny, 1))
+    ya = lax.ppermute(to_a, "gy", swaps(ny, 0))
 
     left, wy, expand, wyt = tables()
     arr = pl.pallas_call(
@@ -511,7 +495,7 @@
             sds((peers, 1, 128), F32),
             sds((8, 128), F32),
         ),
-        in_specs=[SMEM] + [VMEM] * 12,
+        in_specs=[SMEM] + [VMEM] * 10,
         out_specs=(VMEM,) * 5,
         scratch_shapes=[
             pltpu.VMEM((2 * TILE_ROWS, 128), F32),
@@ -521,7 +505,7 @@
         ],
         compiler_params=PARAMS,
         name="sample_and_gradient",
-    )(idx, wgt, xa, own, xb, yb, ya, cb, ca, arr, ref_image, left, wy)
+    )(idx, wgt, xa, own, xb, yb, ya, arr, ref_image, left, wy)
     recv = lax.all_to_all(send, ("gx", "gy"), 0, 0, tiled=True)
     grads, hess, send, residual = pl.pallas_call(
         lambda *refs: product_kernel(nx, ny, *refs),

time: 46.1 us -> 45.9 us (level)
  blocking collectives: 22.9 us -> 20.9 us
  waiting for transfers between devices: 0.05 us -> 1.47 us
    ppermute x1, starting transfers between devices: 3.03 us -> 5.79 us  [on_device(): xa = lax.ppermute(def_image, 'gx', swaps(nx, 0))]
    ppermute x2 -> x0, starting transfers between devices: 2.74 us -> none  [the longest x1 2.07 us: on_device(): ca = lax.ppermute(corner_a, 'gy', swaps(ny, 0))]
    all_to_all x2, blocking collectives: 22.9 us -> 20.9 us  [on_device(): recv = lax.all_to_all(send, ('gx', 'gy'), 0, 0, tiled=True)]
    ppermute x1, waiting for transfers between devices: 0.03 us -> 1.47 us  [on_device(): xa = lax.ppermute(def_image, 'gx', swaps(nx, 0))]
    pallas_call x1, Pallas kernels: 2.54 us -> 3.29 us  [on_device(): pl.pallas_call(early_kernel, out_shape=sds((16, 18, 8, 128), F32), in_spe...]
    pallas_call x1, Pallas kernels: 3.49 us -> 2.74 us  [on_device(): pl.pallas_call(lambda *refs: late_kernel(nx, ny, *refs), out_shape=(sds((...]
  transfers between devices with their start and end apart: 6 -> 4, of which waited for: 0 -> 1; matrix products, arithmetic and copies ran while one was open for 5% -> 5% of each run, Pallas kernels for 7% -> 9%
where the time goes in v8:
time: 45.9 us; the launch traced here: 45.3 us
  blocking collectives  20.9 us (46%)
  starting transfers between devices  10.2 us (22%)
  Pallas kernels  8.92 us (19%)
  other arithmetic  2.13 us (5%)
  waiting for transfers between devices  1.47 us (3%)
  local copies, waits for them, and re-layouts  0.93 us (2%)
  between operations  0.76 us (2%)
    all_to_all x2, blocking collectives, on_device(): recv = lax.all_to_all(send, ('gx', 'gy'), 0, 0, tiled=True)  20.9 us
    ppermute x1, starting transfers between devices, on_device(): xa = lax.ppermute(def_image, 'gx', swaps(nx, 0))  5.79 us
    pallas_call x1, Pallas kernels, on_device(): pl.pallas_call(early_kernel, out_shape=sds((16, 18, 8, 128), F32), in_spe...  3.29 us
    ppermute x1, starting transfers between devices, on_device(): ya = lax.ppermute(to_a, 'gy', swaps(ny, 0))  2.91 us
    pallas_call x1, Pallas kernels, on_device(): pl.pallas_call(lambda *refs: late_kernel(nx, ny, *refs), out_shape=(sds((...  2.74 us
    ppermute x1, waiting for transfers between devices, on_device(): xa = lax.ppermute(def_image, 'gx', swaps(nx, 0))  1.47 us
    convert_element_type x2, other arithmetic, on_device(): rows.astype(F32)  1.37 us
    pallas_call x1, Pallas kernels, on_device(): pl.pallas_call(lambda *refs: product_kernel(nx, ny, *refs), out_shape=(sd...  1.26 us
  transfers between devices with their start and end apart: 4, of which 1 were waited for; matrix products, arithmetic and copies ran while one was open for 5% of the time, Pallas kernels for 9%

profile of v8, /device:TPU:0, one launch (start us, length us, event | category | flops | bytes accessed | tf_op | source)
XLA Modules:
  0.0 45.3 jit_solution(9370454471895337435)
XLA Ops:
  0.6 0.0 copy-start.1
  0.6 0.0 copy-start
  0.7 0.0 copy-start.2
  0.7 0.8 %collective-permute-start.1 = (bf16[8,64,128]{2,1,0:T(8,128)(2,1)}, bf16[8,64,128]{2,1,0:T(8,128)(2,1)S(1)}, u32[]{:S(2)}, u32[]{:S(2)}) collective-permute-start(bf16[8,64,128]{2,1,0:T(8,128)(2,1)} %own_ref.1), channel_id=1, source_target_pairs={{4,8},{12,16},{20,24},{8,4},{16,12},{24,20},{5,9},{13,17},{21,25},... | collective-permute-start | bytes 393224 | tf_op jit(solution)/shard_map/ppermute | solution.py:451
  1.5 5.8 %collective-permute-start = (bf16[8,64,128]{2,1,0:T(8,128)(2,1)}, bf16[8,64,128]{2,1,0:T(8,128)(2,1)S(1)}, u32[]{:S(2)}, u32[]{:S(2)}) collective-permute-start(bf16[8,64,128]{2,1,0:T(8,128)(2,1)} %own_ref.1), channel_id=1, source_target_pairs={{0,4},{8,12},{16,20},{24,28},{4,0},{12,8},{20,16},{28,24},{1,5},{9... | collective-permute-start | bytes 393224 | tf_op jit(solution)/shard_map/ppermute | solution.py:450
  7.3 0.7 %convert_element_type.17 = f32[2,128]{1,0:T(2,128)S(1)} convert(s32[2,128]{1,0:T(2,128)} %param.12) | non-fusion elementwise | flops 256 | bytes 2048 | tf_op jit(solution)/shard_map/convert_element_type | solution.py:455
  8.0 0.7 %convert_element_type.16 = f32[8,128]{1,0:T(8,128)S(1)} convert(s32[8,128]{1,0:T(8,128)} %param.15) | non-fusion elementwise | flops 1024 | bytes 8192 | tf_op jit(solution)/shard_map/convert_element_type | solution.py:455
  8.6 0.8 %pad_add_fusion.row_ref = f32[16,128]{1,0:T(8,128)S(1)} fusion(f32[3,128]{1,0:T(4,128)} %param.14, f32[2,128]{1,0:T(2,128)S(1)} %convert_element_type.17, f32[8,128]{1,0:T(8,128)S(1)} %convert_element_type.16, s32[128]{0:T(128)} %param.13, pred[16]{0:T(512)(128)(4,1)S(1)} %iota_compare_fusion), kind=kLoop, calls=%fused_computation | loop fusion | flops 10240 | bytes 15376 | tf_op jit(solution)/shard_map/add | solution.py:455
  9.4 0.0 copy-start.3
  9.4 0.9 %copy-done.3 = bf16[8,64,128]{2,1,0:T(8,128)(2,1)S(1)} copy-done((bf16[8,64,128]{2,1,0:T(8,128)(2,1)S(1)}, bf16[8,64,128]{2,1,0:T(8,128)(2,1)}, u32[]{:S(2)}) %copy-start.3) | copy-done | bytes 131096
  10.3 0.7 %order_elements.1 = (s32[8,128]{1,0:T(8,128)S(1)}, f32[8,8,128]{2,1,0:T(8,128)S(1)}, bf16[8,64,128]{2,1,0:T(8,128)(2,1)S(1)}) custom-call(f32[16,128]{1,0:T(8,128)S(1)} %pad_add_fusion.row_ref, bf16[8,64,128]{2,1,0:T(8,128)(2,1)S(1)} %copy-done.3), custom_call_target="tpu_custom_call" | custom-call | flops 300000 | bytes 262144 | tf_op jit(solution)/shard_map/order_elements/pallas_call | solution.py:456
  11.0 0.0 collective-permute-done.1.xb_ref.refs_4_
  11.0 1.5 %collective-permute-done.xa_ref.refs_2_ = bf16[8,64,128]{2,1,0:T(8,128)(2,1)S(1)} collective-permute-done((bf16[8,64,128]{2,1,0:T(8,128)(2,1)}, bf16[8,64,128]{2,1,0:T(8,128)(2,1)S(1)}, u32[]{:S(2)}, u32[]{:S(2)}) %collective-permute-start) | collective-permute-done | bytes 131104 | tf_op jit(solution)/shard_map/ppermute | solution.py:450
  12.4 0.2 pack_halo.1
  12.6 0.7 %collective-permute-start.2 = (bf16[4,192,128]{2,1,0:T(8,128)(2,1)S(1)}, bf16[4,192,128]{2,1,0:T(8,128)(2,1)S(1)}, u32[]{:S(2)}, u32[]{:S(2)}) collective-permute-start(bf16[4,192,128]{2,1,0:T(8,128)(2,1)S(1)} %get-tuple-element.24), channel_id=1, source_target_pairs={{1,2},{2,1},{5,6},{6,5},{9,10},{10,9},{13,14},{14,13},{17,18},{18,... | collective-permute-start | bytes 589832 | tf_op jit(solution)/shard_map/ppermute | solution.py:475
  13.3 2.9 %collective-permute-start.3 = (bf16[4,192,128]{2,1,0:T(8,128)(2,1)S(1)}, bf16[4,192,128]{2,1,0:T(8,128)(2,1)S(1)}, u32[]{:S(2)}, u32[]{:S(2)}) collective-permute-start(bf16[4,192,128]{2,1,0:T(8,128)(2,1)S(1)} %get-tuple-element.25), channel_id=1, source_target_pairs={{0,1},{2,3},{1,0},{3,2},{4,5},{6,7},{5,4},{7,6},{8,9},{10,11},{9,8... | collective-permute-start | bytes 589832 | tf_op jit(solution)/shard_map/ppermute | solution.py:476
  16.2 3.3 %sample_early.1.refs_7_ = f32[16,18,8,128]{3,2,1,0:T(8,128)S(1)} custom-call(s32[8,128]{1,0:T(8,128)S(1)} %get-tuple-element.21.idx_ref.refs_0_, bf16[8,64,128]{2,1,0:T(8,128)(2,1)S(1)} %collective-permute-done.xa_ref.refs_2_, bf16[8,64,128]{2,1,0:T(8,128)(2,1)S(1)} %get-tuple-element.23.own_ref.refs_3_, ...), custom_call_target="tpu_custom_call" | custom-call | flops 4000000 | bytes 2000000 | tf_op jit(solution)/shard_map/sample_early/pallas_call | solution.py:479
  19.5 0.0 copy-start.4
  19.5 0.0 copy-start.5
  19.5 0.0 collective-permute-done.2.refs_5_
  19.5 0.0 collective-permute-done.3.refs_6_
  19.6 0.0 copy-done.1
  19.6 0.0 copy-done
  19.6 0.0 copy-done.2
  19.6 2.7 %sample_and_gradient.1 = (bf16[8,64,128]{2,1,0:T(8,128)(2,1)S(1)}, f32[3,8,8,8,128]{4,3,2,1,0:T(8,128)S(1)}, f32[64,128]{1,0:T(8,128)S(1)}, f32[32,1,128]{2,1,0:T(1,128)S(1)}, f32[8,128]{1,0:T(8,128)S(1)}) custom-call(s32[8,128]{1,0:T(8,128)S(1)} %get-tuple-element.21.idx_ref.refs_0_, f32[8,8,128]{2,1,0:T(8,128)S(1)} %get-tuple-element.22.refs_1_, ...), custom_call_target="tpu_custom_call" | custom-call | tf_op jit(solution)/shard_map/sample_and_gradient/pallas_call | solution.py:489
  22.3 12.1 %all_to_all.10.refs_0_ = f32[32,1,128]{2,1,0:T(1,128)S(1)} all-to-all(f32[32,1,128]{2,1,0:T(1,128)S(1)} %get-tuple-element.26), channel_id=1, replica_groups=mesh['gx'=8,'gy'=4] {'gx','gy'}, dimensions={0} | all-to-all | bytes 32768 | tf_op jit(solution)/shard_map/all_to_all | solution.py:509
  34.4 0.0 copy-done.4
  34.4 0.0 copy-done.5
  34.4 1.3 %gauss_newton_product.1 = (f32[6,8,128]{2,1,0:T(8,128)S(1)}, f32[6,8,128]{2,1,0:T(8,128)S(1)}, f32[32,1,128]{2,1,0:T(1,128)S(1)}, bf16[8,64,128]{2,1,0:T(8,128)(2,1)}) custom-call(f32[32,1,128]{2,1,0:T(1,128)S(1)} %all_to_all.10.refs_0_, f32[64,128]{1,0:T(8,128)S(1)} %get-tuple-element.27.refs_1_, f32[3,8,8,8,128]{4,3,2,1,0:T(8,128)S(1)} %get-tuple-element.28.refs_2_, ...), custom_call_target="tpu_custom_call" | custom-call | tf_op jit(solution)/shard_map/gauss_newton_product/pallas_call | solution.py:510
  35.7 8.8 %all_to_all.11.refs_0_ = f32[32,1,128]{2,1,0:T(1,128)S(1)} all-to-all(f32[32,1,128]{2,1,0:T(1,128)S(1)} %get-tuple-element.32), channel_id=1, replica_groups=mesh['gx'=8,'gy'=4] {'gx','gy'}, dimensions={0} | all-to-all | bytes 32768 | tf_op jit(solution)/shard_map/all_to_all | solution.py:528
  44.5 0.8 %finish.1 = (f32[3,2,8,16]{3,2,1,0:T(8,128)}, f32[3,2,8,16]{3,2,1,0:T(8,128)}, f32[1,1]{1,0:T(1,128)}) custom-call(f32[32,1,128]{2,1,0:T(1,128)S(1)} %all_to_all.11.refs_0_, f32[6,8,128]{2,1,0:T(8,128)S(1)} %get-tuple-element.33.refs_1_, f32[6,8,128]{2,1,0:T(8,128)S(1)} %get-tuple-element.34.refs_2_), custom_call_target="tpu_custom_call" | custom-call | tf_op jit(solution)/shard_map/finish/pallas_call | solution.py:530
  (1 shorter events, 0.0 us)
Async XLA Ops:
  0.6 18.9 %copy-start.1 = (bf16[128,128]{1,0:T(8,128)(2,1)S(1)}, bf16[128,128]{1,0:T(8,128)(2,1)}, u32[]{:S(2)}) copy-start(bf16[128,128]{1,0:T(8,128)(2,1)} %constant.15.clone.refs_10_.refs_7_) | copy-start | bytes 98308
  0.6 18.9 %copy-start = (bf16[64,384]{1,0:T(8,128)(2,1)S(1)}, bf16[64,384]{1,0:T(8,128)(2,1)}, u32[]{:S(2)}) copy-start(bf16[64,384]{1,0:T(8,128)(2,1)} %constant.14.clone.refs_9_.refs_6_) | copy-start | bytes 147460
  0.7 18.9 %copy-start.2 = (bf16[8,64,128]{2,1,0:T(8,128)(2,1)S(1)}, bf16[8,64,128]{2,1,0:T(8,128)(2,1)}, u32[]{:S(2)}) copy-start(bf16[8,64,128]{2,1,0:T(8,128)(2,1)} %refs_8_.1) | copy-start | bytes 393220
  0.7 10.3 %collective-permute-start.1 = (bf16[8,64,128]{2,1,0:T(8,128)(2,1)}, bf16[8,64,128]{2,1,0:T(8,128)(2,1)S(1)}, u32[]{:S(2)}, u32[]{:S(2)}) collective-permute-start(bf16[8,64,128]{2,1,0:T(8,128)(2,1)} %own_ref.1), channel_id=1, source_target_pairs={{4,8},{12,16},{20,24},{8,4},{16,12},{24,20},{5,9},{13,17},{21,25},... | collective-permute-start | bytes 393224 | tf_op jit(solution)/shard_map/ppermute | solution.py:451
  1.5 11.0 %collective-permute-start = (bf16[8,64,128]{2,1,0:T(8,128)(2,1)}, bf16[8,64,128]{2,1,0:T(8,128)(2,1)S(1)}, u32[]{:S(2)}, u32[]{:S(2)}) collective-permute-start(bf16[8,64,128]{2,1,0:T(8,128)(2,1)} %own_ref.1), channel_id=1, source_target_pairs={{0,4},{8,12},{16,20},{24,28},{4,0},{12,8},{20,16},{28,24},{1,5},{9... | collective-permute-start | bytes 393224 | tf_op jit(solution)/shard_map/ppermute | solution.py:450
  9.4 0.9 %copy-start.3 = (bf16[8,64,128]{2,1,0:T(8,128)(2,1)S(1)}, bf16[8,64,128]{2,1,0:T(8,128)(2,1)}, u32[]{:S(2)}) copy-start(bf16[8,64,128]{2,1,0:T(8,128)(2,1)} %own_ref.1) | copy-start | bytes 393220
  12.6 6.9 %collective-permute-start.2 = (bf16[4,192,128]{2,1,0:T(8,128)(2,1)S(1)}, bf16[4,192,128]{2,1,0:T(8,128)(2,1)S(1)}, u32[]{:S(2)}, u32[]{:S(2)}) collective-permute-start(bf16[4,192,128]{2,1,0:T(8,128)(2,1)S(1)} %get-tuple-element.24), channel_id=1, source_target_pairs={{1,2},{2,1},{5,6},{6,5},{9,10},{10,9},{13,14},{14,13},{17,18},{18,... | collective-permute-start | bytes 589832 | tf_op jit(solution)/shard_map/ppermute | solution.py:475
  13.3 6.2 %collective-permute-start.3 = (bf16[4,192,128]{2,1,0:T(8,128)(2,1)S(1)}, bf16[4,192,128]{2,1,0:T(8,128)(2,1)S(1)}, u32[]{:S(2)}, u32[]{:S(2)}) collective-permute-start(bf16[4,192,128]{2,1,0:T(8,128)(2,1)S(1)} %get-tuple-element.25), channel_id=1, source_target_pairs={{0,1},{2,3},{1,0},{3,2},{4,5},{6,7},{5,4},{7,6},{8,9},{10,11},{9,8... | collective-permute-start | bytes 589832 | tf_op jit(solution)/shard_map/ppermute | solution.py:476
  19.5 14.9 %copy-start.4 = (bf16[384,64]{1,0:T(8,128)(2,1)S(1)}, bf16[384,64]{1,0:T(8,128)(2,1)}, u32[]{:S(2)}) copy-start(bf16[384,64]{1,0:T(8,128)(2,1)} %constant.16.clone.refs_4_) | copy-start | bytes 147460
  19.5 14.9 %copy-start.5 = (bf16[128,128]{1,0:T(8,128)(2,1)S(1)}, bf16[128,128]{1,0:T(8,128)(2,1)}, u32[]{:S(2)}) copy-start(bf16[128,128]{1,0:T(8,128)(2,1)} %constant.17.clone.refs_5_) | copy-start | bytes 98308

commit v9 on v8

--- a/solution.py
+++ b/solution.py
@@ -120,7 +120,7 @@
         wgt_ref[cx] = dot_rows(hi, spread) + dot_rows(lo, spread) + dot_rows(rest, spread)
 
 
-def pack_kernel(xa_ref, own_ref, xb_ref, b_ref, a_ref):
+def pack_kernel(xb_ref, own_ref, xa_ref, b_ref, a_ref):
     even = lax.axis_index("gy") % 2 == 0
     for n, ref in enumerate((xa_ref, own_ref, xb_ref)):
         pack_rows(ref, a_ref, b_ref, 64 * n, even)
@@ -183,7 +183,7 @@
             pltpu.store(arr.at[place, z * 2 + q], pltpu.roll(v, shift, 1), mask=mask)
 
 
-def early_kernel(idx_ref, xa_ref, own_ref, xb_ref, arr_ref, img):
+def early_kernel(idx_ref, xb_ref, own_ref, xa_ref, arr_ref, img):
     clear_outside(img, 1)
     at_a = place_of_a()
     for z in range(8):
@@ -202,7 +202,7 @@
 
 
 def late_kernel(
-    nx, ny, idx_ref, wgt, xa_ref, own_ref, xb_ref, yb_ref, ya_ref, arr_ref, ref_ref,
+    nx, ny, idx_ref, wgt, xb_ref, own_ref, xa_ref, yb_ref, ya_ref, arr_ref, ref_ref,
     left_ref, wy_ref, res_ref, slope_ref, node_ref, send_ref, sq_ref, img, arr, rsc, gsc,
 ):
     half = lax.broadcasted_iota(jnp.int32, (64, 128), 1) < 64
@@ -471,7 +471,7 @@
         compiler_params=PARAMS,
         cost_estimate=pl.CostEstimate(flops=300000, bytes_accessed=524288, transcendentals=0),
         name="pack_halo",
-    )(xa, own, xb)
+    )(xb, own, xa)
     yb = lax.ppermute(to_b, "gy", swaps(ny, 1))
     ya = lax.ppermute(to_a, "gy", swaps(ny, 0))
 
@@ -485,7 +485,7 @@
         compiler_params=PARAMS,
         cost_estimate=pl.CostEstimate(flops=4000000, bytes_accessed=2000000, transcendentals=0),
         name="sample_early",
-    )(idx, xa, own, xb)
+    )(idx, xb, own, xa)
     residual, slopes, nodes, send, square = pl.pallas_call(
         lambda *refs: late_kernel(nx, ny, *refs),
         out_shape=(
@@ -505,7 +505,7 @@
         ],
         compiler_params=PARAMS,
         name="sample_and_gradient",
-    )(idx, wgt, xa, own, xb, yb, ya, arr, ref_image, left, wy)
+    )(idx, wgt, xb, own, xa, yb, ya, arr, ref_image, left, wy)
     recv = lax.all_to_all(send, ("gx", "gy"), 0, 0, tiled=True)
     grads, hess, send, residual = pl.pallas_call(
         lambda *refs: product_kernel(nx, ny, *refs),

time: 45.9 us -> 44.8 us (0.976)
  blocking collectives: 20.9 us -> 24.3 us
  starting transfers between devices: 10.2 us -> 7.27 us
  waiting for transfers between devices: 1.47 us -> 0.01 us
    all_to_all x2, blocking collectives: 20.9 us -> 24.3 us  [on_device(): recv = lax.all_to_all(send, ('gx', 'gy'), 0, 0, tiled=True)]
    ppermute x1, starting transfers between devices: 5.79 us -> 3.03 us  [on_device(): xa = lax.ppermute(def_image, 'gx', swaps(nx, 0))]
    ppermute x1, waiting for transfers between devices: 1.47 us -> 0.01 us  [on_device(): xa = lax.ppermute(def_image, 'gx', swaps(nx, 0))]
  transfers between devices with their start and end apart: 4 -> 4, of which waited for: 1 -> 0; matrix products, arithmetic and copies ran while one was open for 5% -> 5% of each run, Pallas kernels for 9% -> 9%
where the time goes in v9:
time: 44.8 us; the launch traced here: 44.4 us
  blocking collectives  24.3 us (54%)
  Pallas kernels  8.95 us (20%)
  starting transfers between devices  7.27 us (16%)
  other arithmetic  2.13 us (5%)
  local copies, waits for them, and re-layouts  0.93 us (2%)
  between operations  0.76 us (2%)
    all_to_all x2, blocking collectives, on_device(): recv = lax.all_to_all(send, ('gx', 'gy'), 0, 0, tiled=True)  24.3 us
    pallas_call x1, Pallas kernels, on_device(): pl.pallas_call(early_kernel, out_shape=sds((16, 18, 8, 128), F32), in_spe...  3.29 us
    ppermute x1, starting transfers between devices, on_device(): xa = lax.ppermute(def_image, 'gx', swaps(nx, 0))  3.03 us
    ppermute x1, starting transfers between devices, on_device(): ya = lax.ppermute(to_a, 'gy', swaps(ny, 0))  2.91 us
    pallas_call x1, Pallas kernels, on_device(): pl.pallas_call(lambda *refs: late_kernel(nx, ny, *refs), out_shape=(sds((...  2.74 us
    convert_element_type x2, other arithmetic, on_device(): rows.astype(F32)  1.37 us
    pallas_call x1, Pallas kernels, on_device(): pl.pallas_call(lambda *refs: product_kernel(nx, ny, *refs), out_shape=(sd...  1.26 us
    unnamed x12, local copies, waits for them, and re-layouts  0.93 us
  transfers between devices with their start and end apart: 4, of which 0 were waited for; matrix products, arithmetic and copies ran while one was open for 5% of the time, Pallas kernels for 9%

profile of v9, /device:TPU:0, one launch (start us, length us, event | category | flops | bytes accessed | tf_op | source)
XLA Modules:
  0.0 44.4 jit_solution(6147074584464636603)
XLA Ops:
  0.6 0.0 copy-start.1
  0.6 0.0 copy-start
  0.7 0.0 copy-start.2
  0.7 3.0 %collective-permute-start.1 = (bf16[8,64,128]{2,1,0:T(8,128)(2,1)}, bf16[8,64,128]{2,1,0:T(8,128)(2,1)S(1)}, u32[]{:S(2)}, u32[]{:S(2)}) collective-permute-start(bf16[8,64,128]{2,1,0:T(8,128)(2,1)} %own_ref.1), channel_id=1, source_target_pairs={{0,4},{8,12},{16,20},{24,28},{4,0},{12,8},{20,16},{28,24},{1,5},{9... | collective-permute-start | bytes 393224 | tf_op jit(solution)/shard_map/ppermute | solution.py:450
  3.7 0.7 %collective-permute-start = (bf16[8,64,128]{2,1,0:T(8,128)(2,1)}, bf16[8,64,128]{2,1,0:T(8,128)(2,1)S(1)}, u32[]{:S(2)}, u32[]{:S(2)}) collective-permute-start(bf16[8,64,128]{2,1,0:T(8,128)(2,1)} %own_ref.1), channel_id=1, source_target_pairs={{4,8},{12,16},{20,24},{8,4},{16,12},{24,20},{5,9},{13,17},{21,25},... | collective-permute-start | bytes 393224 | tf_op jit(solution)/shard_map/ppermute | solution.py:451
  4.4 0.7 %convert_element_type.17 = f32[2,128]{1,0:T(2,128)S(1)} convert(s32[2,128]{1,0:T(2,128)} %param.12) | non-fusion elementwise | flops 256 | bytes 2048 | tf_op jit(solution)/shard_map/convert_element_type | solution.py:455
  5.1 0.7 %convert_element_type.16 = f32[8,128]{1,0:T(8,128)S(1)} convert(s32[8,128]{1,0:T(8,128)} %param.15) | non-fusion elementwise | flops 1024 | bytes 8192 | tf_op jit(solution)/shard_map/convert_element_type | solution.py:455
  5.7 0.8 %pad_add_fusion.row_ref = f32[16,128]{1,0:T(8,128)S(1)} fusion(f32[3,128]{1,0:T(4,128)} %param.14, f32[2,128]{1,0:T(2,128)S(1)} %convert_element_type.17, f32[8,128]{1,0:T(8,128)S(1)} %convert_element_type.16, s32[128]{0:T(128)} %param.13, pred[16]{0:T(512)(128)(4,1)S(1)} %iota_compare_fusion), kind=kLoop, calls=%fused_computation | loop fusion | flops 10240 | bytes 15376 | tf_op jit(solution)/shard_map/add | solution.py:455
  6.5 0.0 copy-start.3
  6.5 0.9 %copy-done.3 = bf16[8,64,128]{2,1,0:T(8,128)(2,1)S(1)} copy-done((bf16[8,64,128]{2,1,0:T(8,128)(2,1)S(1)}, bf16[8,64,128]{2,1,0:T(8,128)(2,1)}, u32[]{:S(2)}) %copy-start.3) | copy-done | bytes 131096
  7.4 0.7 %order_elements.1 = (s32[8,128]{1,0:T(8,128)S(1)}, f32[8,8,128]{2,1,0:T(8,128)S(1)}, bf16[8,64,128]{2,1,0:T(8,128)(2,1)S(1)}) custom-call(f32[16,128]{1,0:T(8,128)S(1)} %pad_add_fusion.row_ref, bf16[8,64,128]{2,1,0:T(8,128)(2,1)S(1)} %copy-done.3), custom_call_target="tpu_custom_call" | custom-call | flops 300000 | bytes 262144 | tf_op jit(solution)/shard_map/order_elements/pallas_call | solution.py:456
  8.1 0.0 collective-permute-done.1.xa_ref.refs_4_
  8.1 0.0 collective-permute-done.xb_ref.refs_2_
  8.1 0.2 pack_halo.1
  8.3 0.7 %collective-permute-start.2 = (bf16[4,192,128]{2,1,0:T(8,128)(2,1)S(1)}, bf16[4,192,128]{2,1,0:T(8,128)(2,1)S(1)}, u32[]{:S(2)}, u32[]{:S(2)}) collective-permute-start(bf16[4,192,128]{2,1,0:T(8,128)(2,1)S(1)} %get-tuple-element.24), channel_id=1, source_target_pairs={{1,2},{2,1},{5,6},{6,5},{9,10},{10,9},{13,14},{14,13},{17,18},{18,... | collective-permute-start | bytes 589832 | tf_op jit(solution)/shard_map/ppermute | solution.py:475
  9.0 2.9 %collective-permute-start.3 = (bf16[4,192,128]{2,1,0:T(8,128)(2,1)S(1)}, bf16[4,192,128]{2,1,0:T(8,128)(2,1)S(1)}, u32[]{:S(2)}, u32[]{:S(2)}) collective-permute-start(bf16[4,192,128]{2,1,0:T(8,128)(2,1)S(1)} %get-tuple-element.25), channel_id=1, source_target_pairs={{0,1},{2,3},{1,0},{3,2},{4,5},{6,7},{5,4},{7,6},{8,9},{10,11},{9,8... | collective-permute-start | bytes 589832 | tf_op jit(solution)/shard_map/ppermute | solution.py:476
  11.9 3.3 %sample_early.1.refs_7_ = f32[16,18,8,128]{3,2,1,0:T(8,128)S(1)} custom-call(s32[8,128]{1,0:T(8,128)S(1)} %get-tuple-element.21.idx_ref.refs_0_, bf16[8,64,128]{2,1,0:T(8,128)(2,1)S(1)} %collective-permute-done.xb_ref.refs_2_, bf16[8,64,128]{2,1,0:T(8,128)(2,1)S(1)} %get-tuple-element.23.own_ref.refs_3_, ...), custom_call_target="tpu_custom_call" | custom-call | flops 4000000 | bytes 2000000 | tf_op jit(solution)/shard_map/sample_early/pallas_call | solution.py:479
  15.2 0.0 copy-start.4
  15.2 0.0 copy-start.5
  15.2 0.0 collective-permute-done.2.refs_5_
  15.2 0.0 collective-permute-done.3.refs_6_
  15.2 0.0 copy-done.1
  15.2 0.0 copy-done
  15.3 0.0 copy-done.2
  15.3 2.7 %sample_and_gradient.1 = (bf16[8,64,128]{2,1,0:T(8,128)(2,1)S(1)}, f32[3,8,8,8,128]{4,3,2,1,0:T(8,128)S(1)}, f32[64,128]{1,0:T(8,128)S(1)}, f32[32,1,128]{2,1,0:T(1,128)S(1)}, f32[8,128]{1,0:T(8,128)S(1)}) custom-call(s32[8,128]{1,0:T(8,128)S(1)} %get-tuple-element.21.idx_ref.refs_0_, f32[8,8,128]{2,1,0:T(8,128)S(1)} %get-tuple-element.22.refs_1_, ...), custom_call_target="tpu_custom_call" | custom-call | tf_op jit(solution)/shard_map/sample_and_gradient/pallas_call | solution.py:489
  18.0 15.5 %all_to_all.10.refs_0_ = f32[32,1,128]{2,1,0:T(1,128)S(1)} all-to-all(f32[32,1,128]{2,1,0:T(1,128)S(1)} %get-tuple-element.26), channel_id=1, replica_groups=mesh['gx'=8,'gy'=4] {'gx','gy'}, dimensions={0} | all-to-all | bytes 32768 | tf_op jit(solution)/shard_map/all_to_all | solution.py:509
  33.5 0.0 copy-done.4
  33.5 0.0 copy-done.5
  33.5 1.3 %gauss_newton_product.1 = (f32[6,8,128]{2,1,0:T(8,128)S(1)}, f32[6,8,128]{2,1,0:T(8,128)S(1)}, f32[32,1,128]{2,1,0:T(1,128)S(1)}, bf16[8,64,128]{2,1,0:T(8,128)(2,1)}) custom-call(f32[32,1,128]{2,1,0:T(1,128)S(1)} %all_to_all.10.refs_0_, f32[64,128]{1,0:T(8,128)S(1)} %get-tuple-element.27.refs_1_, f32[3,8,8,8,128]{4,3,2,1,0:T(8,128)S(1)} %get-tuple-element.28.refs_2_, ...), custom_call_target="tpu_custom_call" | custom-call | tf_op jit(solution)/shard_map/gauss_newton_product/pallas_call | solution.py:510
  34.8 8.8 %all_to_all.11.refs_0_ = f32[32,1,128]{2,1,0:T(1,128)S(1)} all-to-all(f32[32,1,128]{2,1,0:T(1,128)S(1)} %get-tuple-element.32), channel_id=1, replica_groups=mesh['gx'=8,'gy'=4] {'gx','gy'}, dimensions={0} | all-to-all | bytes 32768 | tf_op jit(solution)/shard_map/all_to_all | solution.py:528
  43.6 0.8 %finish.1 = (f32[3,2,8,16]{3,2,1,0:T(8,128)}, f32[3,2,8,16]{3,2,1,0:T(8,128)}, f32[1,1]{1,0:T(1,128)}) custom-call(f32[32,1,128]{2,1,0:T(1,128)S(1)} %all_to_all.11.refs_0_, f32[6,8,128]{2,1,0:T(8,128)S(1)} %get-tuple-element.33.refs_1_, f32[6,8,128]{2,1,0:T(8,128)S(1)} %get-tuple-element.34.refs_2_), custom_call_target="tpu_custom_call" | custom-call | tf_op jit(solution)/shard_map/finish/pallas_call | solution.py:530
  (1 shorter events, 0.0 us)
Async XLA Ops:
  0.6 14.6 %copy-start.1 = (bf16[128,128]{1,0:T(8,128)(2,1)S(1)}, bf16[128,128]{1,0:T(8,128)(2,1)}, u32[]{:S(2)}) copy-start(bf16[128,128]{1,0:T(8,128)(2,1)} %constant.15.clone.refs_10_.refs_7_) | copy-start | bytes 98308
  0.6 14.6 %copy-start = (bf16[64,384]{1,0:T(8,128)(2,1)S(1)}, bf16[64,384]{1,0:T(8,128)(2,1)}, u32[]{:S(2)}) copy-start(bf16[64,384]{1,0:T(8,128)(2,1)} %constant.14.clone.refs_9_.refs_6_) | copy-start | bytes 147460
  0.7 14.6 %copy-start.2 = (bf16[8,64,128]{2,1,0:T(8,128)(2,1)S(1)}, bf16[8,64,128]{2,1,0:T(8,128)(2,1)}, u32[]{:S(2)}) copy-start(bf16[8,64,128]{2,1,0:T(8,128)(2,1)} %refs_8_.1) | copy-start | bytes 393220
  0.7 7.4 %collective-permute-start.1 = (bf16[8,64,128]{2,1,0:T(8,128)(2,1)}, bf16[8,64,128]{2,1,0:T(8,128)(2,1)S(1)}, u32[]{:S(2)}, u32[]{:S(2)}) collective-permute-start(bf16[8,64,128]{2,1,0:T(8,128)(2,1)} %own_ref.1), channel_id=1, source_target_pairs={{0,4},{8,12},{16,20},{24,28},{4,0},{12,8},{20,16},{28,24},{1,5},{9... | collective-permute-start | bytes 393224 | tf_op jit(solution)/shard_map/ppermute | solution.py:450
  3.7 4.4 %collective-permute-start = (bf16[8,64,128]{2,1,0:T(8,128)(2,1)}, bf16[8,64,128]{2,1,0:T(8,128)(2,1)S(1)}, u32[]{:S(2)}, u32[]{:S(2)}) collective-permute-start(bf16[8,64,128]{2,1,0:T(8,128)(2,1)} %own_ref.1), channel_id=1, source_target_pairs={{4,8},{12,16},{20,24},{8,4},{16,12},{24,20},{5,9},{13,17},{21,25},... | collective-permute-start | bytes 393224 | tf_op jit(solution)/shard_map/ppermute | solution.py:451
  6.5 0.9 %copy-start.3 = (bf16[8,64,128]{2,1,0:T(8,128)(2,1)S(1)}, bf16[8,64,128]{2,1,0:T(8,128)(2,1)}, u32[]{:S(2)}) copy-start(bf16[8,64,128]{2,1,0:T(8,128)(2,1)} %own_ref.1) | copy-start | bytes 393220
  8.3 6.9 %collective-permute-start.2 = (bf16[4,192,128]{2,1,0:T(8,128)(2,1)S(1)}, bf16[4,192,128]{2,1,0:T(8,128)(2,1)S(1)}, u32[]{:S(2)}, u32[]{:S(2)}) collective-permute-start(bf16[4,192,128]{2,1,0:T(8,128)(2,1)S(1)} %get-tuple-element.24), channel_id=1, source_target_pairs={{1,2},{2,1},{5,6},{6,5},{9,10},{10,9},{13,14},{14,13},{17,18},{18,... | collective-permute-start | bytes 589832 | tf_op jit(solution)/shard_map/ppermute | solution.py:475
  9.0 6.2 %collective-permute-start.3 = (bf16[4,192,128]{2,1,0:T(8,128)(2,1)S(1)}, bf16[4,192,128]{2,1,0:T(8,128)(2,1)S(1)}, u32[]{:S(2)}, u32[]{:S(2)}) collective-permute-start(bf16[4,192,128]{2,1,0:T(8,128)(2,1)S(1)} %get-tuple-element.25), channel_id=1, source_target_pairs={{0,1},{2,3},{1,0},{3,2},{4,5},{6,7},{5,4},{7,6},{8,9},{10,11},{9,8... | collective-permute-start | bytes 589832 | tf_op jit(solution)/shard_map/ppermute | solution.py:476
  15.2 18.3 %copy-start.4 = (bf16[384,64]{1,0:T(8,128)(2,1)S(1)}, bf16[384,64]{1,0:T(8,128)(2,1)}, u32[]{:S(2)}) copy-start(bf16[384,64]{1,0:T(8,128)(2,1)} %constant.16.clone.refs_4_) | copy-start | bytes 147460
  15.2 18.3 %copy-start.5 = (bf16[128,128]{1,0:T(8,128)(2,1)S(1)}, bf16[128,128]{1,0:T(8,128)(2,1)}, u32[]{:S(2)}) copy-start(bf16[128,128]{1,0:T(8,128)(2,1)} %constant.17.clone.refs_5_) | copy-start | bytes 98308

commit v10 on v9

--- a/solution.py
+++ b/solution.py
@@ -84,17 +84,17 @@
     return out
 
 
-def index_kernel(row_ref, own_ref, idx_ref, wgt_ref, keep_ref):
+def index_kernel(row_ref, frac_ref, own_ref, idx_ref, wgt_ref, keep_ref):
     keep_ref[...] = own_ref[...]
-    first = row_ref[0:1].astype(jnp.int32)
+    first = row_ref[0:1]
     col_x = (first * 241) >> 12
     col_y = first - 17 * col_x
-    start_x = 8 * col_x + row_ref[8:9].astype(jnp.int32) + HALO
-    start_y = 8 * col_y + row_ref[9:10].astype(jnp.int32) + HALO
+    start_x = 8 * col_x + row_ref[8:9] + HALO
+    start_y = 8 * col_y + row_ref[9:10] + HALO
     early = (start_y >= 64) & (start_y < 184)
     below = start_y < 64
     offset = jnp.where(early, start_y - 64, jnp.where(below, start_y, start_y - 128))
-    base = (row_ref[10:11].astype(jnp.int32) + 2) * SPAN + start_x
+    base = (row_ref[10:11] + 2) * SPAN + start_x
     tile = jnp.where(early | below, 0, TILE_ROWS)
     shift = (8 * col_y - offset) & 127
     place = (col_y & 1) * 8 + col_x
@@ -111,7 +111,7 @@
     sub = lax.broadcasted_iota(jnp.int32, (8, 128), 0)
     table = jnp.where(sub == 6, jnp.broadcast_to(count, (8, 128)), table)
     idx_ref[...] = table.astype(jnp.int32)
-    value = as_rows([row_ref[11 + c : 12 + c] for c in range(3)])
+    value = as_rows([frac_ref[c : c + 1] for c in range(3)])
     hi, lo = split(value)
     rest = (value - hi.astype(F32) - lo.astype(F32)).astype(BF16)
     element = jnp.broadcast_to(col_x * 16 + col_y, (128, 128))
@@ -294,23 +294,36 @@
     res_ref[...] = rsc[...].reshape(8, 64, 128).astype(BF16)
     nodes = dot_left(dot_right(left_ref[...], gsc[...].reshape(384, 128)), wy_ref[...])
     node_ref[...] = nodes
-    rows = [nodes[kc * 8 : kc * 8 + 8] for kc in range(6)]
-    high, low = nodes[48:56], nodes[56:64]
-    col_high = column_row(rows, high, 16)
-    col_low = column_row(rows, high, 0)
-    high, low = face_row(high), face_row(low)
+    gx = lax.axis_index("gx")
+    send_faces(send_ref, gx, nx, face_row(nodes[48:56]), face_row(nodes[56:64]))
+
+
+def send_faces(send_ref, here, count, after, before):
+    send_ref[...] = jnp.zeros(send_ref.shape, F32)
+
+    @pl.when(here + 1 < count)
+    def _():
+        send_ref[here + 1] = after
+
+    @pl.when(here > 0)
+    def _():
+        send_ref[here - 1] = before
+
+
+def face_kernel(nx, ny, recv_ref, node_ref, sum_ref, send_ref):
     gx, gy = lax.axis_index("gx"), lax.axis_index("gy")
-    send_ref[...] = jnp.zeros(send_ref.shape, F32)
-    for dx in (-1, 0, 1):
-        for dy in (-1, 0, 1):
-            if dx == 0 and dy == 0:
-                continue
-            block = high if dx == 1 else low if dx == -1 else col_high if dy == 1 else col_low
-            px, py = gx + dx, gy + dy
-
-            @pl.when((px >= 0) & (px < nx) & (py >= 0) & (py < ny))
-            def _():
-                send_ref[px * ny + py] = block
+    sub = lax.broadcasted_iota(jnp.int32, (8, 128), 0)
+    row_low = face_of(recv_ref[jnp.where(gx > 0, gx - 1, gx)])
+    row_high = face_of(recv_ref[jnp.where(gx + 1 < nx, gx + 1, gx)])
+    rows = []
+    for kc in range(6):
+        g = node_ref[kc * 8 : kc * 8 + 8]
+        g = g + jnp.where(sub == 0, jnp.broadcast_to(row_low[kc : kc + 1], (8, 128)), 0.0)
+        sum_ref[kc] = g
+        rows.append(g)
+    face = node_ref[48:56] + row_high
+    sum_ref[6] = face
+    send_faces(send_ref, gy, ny, column_row(rows, face, 16), column_row(rows, face, 0))
 
 
 def product_kernel(
@@ -320,35 +333,21 @@
     copy_out = pltpu.make_async_copy(res_ref, out_ref, sem)
     copy_out.start()
     gx, gy = lax.axis_index("gx"), lax.axis_index("gy")
-    own = gx * ny + gy
-    lane = lax.broadcasted_iota(jnp.int32, (8, 128), 1)
-    sub = lax.broadcasted_iota(jnp.int32, (8, 128), 0)
-
-    def block(dx, dy):
-        px, py = gx + dx, gy + dy
-        there = (px >= 0) & (px < nx) & (py >= 0) & (py < ny)
-        return recv_ref[jnp.where(there, px * ny + py, own)]
+    lane = lax.broadcasted_iota(jnp.int32, (8, 128), 1)
+    sub = lax.broadcasted_iota(jnp.int32, (8, 128), 0)
 
     def column(x, at):
         return jnp.broadcast_to(x[:, at : at + 1], (8, 128))
-
-    def with_corners(dx):
-        mid = face_of(block(dx, 0))
-        mid = mid + jnp.where(lane == 0, column(face_of(block(dx, -1)), 16), 0.0)
-        return mid + jnp.where(lane == 16, column(face_of(block(dx, 1)), 0), 0.0)
 
     keep_x = jnp.where(gx == nx - 1, 0.0, 1.0).astype(F32)
     keep_y = jnp.where(gy == ny - 1, 0.0, 1.0).astype(F32)
     keep_lane = jnp.where(lane == 16, keep_y, 1.0)
-    row_low = with_corners(-1)
-    row_high = with_corners(1)
-    col_low, edge_low = column_of(block(0, -1))
-    col_high, edge_high = column_of(block(0, 1))
+    col_low, edge_low = column_of(recv_ref[jnp.where(gy > 0, gy - 1, gy)])
+    col_high, edge_high = column_of(recv_ref[jnp.where(gy + 1 < ny, gy + 1, gy)])
     grads = []
     square = jnp.zeros((8, 128), F32)
     for kc in range(6):
-        g = node_ref[kc * 8 : kc * 8 + 8]
-        g = g + jnp.where(sub == 0, jnp.broadcast_to(row_low[kc : kc + 1], (8, 128)), 0.0)
+        g = node_ref[kc]
         g = g + jnp.where(lane == 0, column(col_low, kc), 0.0)
         g = g + jnp.where(lane == 16, column(col_high, kc), 0.0)
         g = g * keep_lane
@@ -356,7 +355,7 @@
         grad_ref[kc] = g
         own_g = jnp.where(lane < 16, g, 0.0)
         square = square + own_g * own_g
-    face = node_ref[48:56] + row_high
+    face = node_ref[6]
     face = face + jnp.where(lane == 0, column(edge_low, 0), 0.0)
     face = face + jnp.where(lane == 16, column(edge_high, 0), 0.0)
     face = jnp.where(sub < 6, face * keep_lane * keep_x, 0.0)
@@ -391,35 +390,44 @@
     rows = [nodes[kc * 8 : kc * 8 + 8] for kc in range(6)]
     for kc in range(6):
         hess_ref[kc] = rows[kc]
-    col_high = column_row(rows, nodes[48:56], 16)
     high = face_row(nodes[48:56])
     spot = lane[:1]
     sums = jnp.where(spot == 104, jnp.sum(sq_ref[...]), 0.0)
     sums = jnp.where(spot == 105, jnp.sum(square), sums)
     sums = jnp.where(spot == 106, jnp.sum(curve) * (1.0 / 512.0), sums)
-    tail = spot >= 104
     send_ref[...] = jnp.broadcast_to(sums[None], send_ref.shape)
-    for dx, dy, data in ((1, 0, high), (1, 1, high), (0, 1, col_high)):
-        px, py = gx + dx, gy + dy
-
-        @pl.when((px < nx) & (py < ny))
-        def _():
-            send_ref[px * ny + py] = jnp.where(tail, sums, data)
+
+    @pl.when(gx + 1 < nx)
+    def _():
+        send_ref[gx + 1] = jnp.where(spot >= 104, sums, high)
 
     copy_out.wait()
 
 
+def total_kernel(nx, ny, recv_ref, hess_ref, sum_ref, send_ref):
+    gx, gy = lax.axis_index("gx"), lax.axis_index("gy")
+    sub = lax.broadcasted_iota(jnp.int32, (8, 128), 0)
+    spot = lax.broadcasted_iota(jnp.int32, (1, 128), 1)
+    sums = jnp.where(spot >= 104, jnp.sum(recv_ref[...], axis=0), 0.0)
+    row_low = face_of(recv_ref[jnp.where(gx > 0, gx - 1, gx)])
+    row_low = jnp.where(gx > 0, row_low, 0.0)
+    rows = []
+    for kc in range(6):
+        h = hess_ref[kc]
+        h = h + jnp.where(sub == 0, jnp.broadcast_to(row_low[kc : kc + 1], (8, 128)), 0.0)
+        sum_ref[kc] = h
+        rows.append(h)
+    col_high = column_row(rows, jnp.zeros((8, 128), F32), 16)
+    send_ref[...] = jnp.broadcast_to(sums[None], send_ref.shape)
+
+    @pl.when(gy + 1 < ny)
+    def _():
+        send_ref[gy + 1] = jnp.where(spot >= 104, sums, col_high)
+
+
 def finish_kernel(nx, ny, voxels, recv_ref, grad_ref, hess_ref, step_ref, prod_ref, misfit_ref):
-    gx, gy = lax.axis_index("gx"), lax.axis_index("gy")
-    own = gx * ny + gy
-    lane = lax.broadcasted_iota(jnp.int32, (8, 128), 1)
-    sub = lax.broadcasted_iota(jnp.int32, (8, 128), 0)
-
-    def block(dx, dy):
-        px, py = gx + dx, gy + dy
-        there = (px >= 0) & (py >= 0)
-        data = recv_ref[jnp.where(there, px * ny + py, own)]
-        return jnp.where(there, data, 0.0)
+    gy = lax.axis_index("gy")
+    lane = lax.broadcasted_iota(jnp.int32, (8, 128), 1)
 
     def column(x, at):
         return jnp.broadcast_to(x[:, at : at + 1], (8, 128))
@@ -428,12 +436,10 @@
     misfit_ref[...] = total[:, 104:105] * (1.0 / voxels)
     total = jnp.broadcast_to(total, (8, 128))
     alpha = column(total, 105) / column(total, 106)
-    row_low = face_of(block(-1, 0)) + jnp.where(lane == 0, column(face_of(block(-1, -1)), 16), 0.0)
-    col_low = column_of(block(0, -1))[0]
-    for kc in range(6):
-        h = hess_ref[kc]
-        h = h + jnp.where(sub == 0, jnp.broadcast_to(row_low[kc : kc + 1], (8, 128)), 0.0)
-        h = h + jnp.where(lane == 0, column(col_low, kc), 0.0)
+    there = gy > 0
+    col_low = column_of(recv_ref[jnp.where(there, gy - 1, gy)])[0]
+    for kc in range(6):
+        h = hess_ref[kc] + jnp.where(there & (lane == 0), column(col_low, kc), 0.0)
         prod_ref[kc // 2, kc % 2] = h[:, :16]
         step_ref[kc // 2, kc % 2] = (alpha * grad_ref[kc])[:, :16]
 
@@ -450,18 +456,17 @@
     xa = lax.ppermute(def_image, "gx", swaps(nx, 0))
     xb = lax.ppermute(def_image, "gx", swaps(nx, 1))
     row = lax.broadcasted_iota(jnp.int32, (16, 128), 0)
-    table = jnp.where(row == 10, shift_z[None], 0).astype(F32)
-    for rows, at in ((connectivity, 0), (shift_xy, 8), (frac, 11)):
-        table = table + jnp.pad(rows.astype(F32), ((at, 16 - at - rows.shape[0]), (0, 0)))
+    table = jnp.where(row == 10, shift_z[None], 0)
+    table = table + jnp.pad(connectivity, ((0, 8), (0, 0))) + jnp.pad(shift_xy, ((8, 6), (0, 0)))
     idx, wgt, own = pl.pallas_call(
         index_kernel,
         out_shape=(sds((8, 128), jnp.int32), sds((8, 8, 128), F32), sds((8, 64, 128), BF16)),
-        in_specs=[VMEM, VMEM],
+        in_specs=[VMEM] * 3,
         out_specs=(VMEM,) * 3,
         compiler_params=PARAMS,
         cost_estimate=pl.CostEstimate(flops=300000, bytes_accessed=262144, transcendentals=0),
         name="order_elements",
-    )(table, def_image)
+    )(table, frac, def_image)
     packed = sds((4, SPAN, 128), BF16)
     to_b, to_a = pl.pallas_call(
         pack_kernel,
@@ -492,7 +497,7 @@
             sds((8, 64, 128), BF16),
             sds((3, 8, 8, 8, 128), F32),
             sds((64, 128), F32),
-            sds((peers, 1, 128), F32),
+            sds((nx, 1, 128), F32),
             sds((8, 128), F32),
         ),
         in_specs=[SMEM] + [VMEM] * 10,
@@ -506,13 +511,22 @@
         compiler_params=PARAMS,
         name="sample_and_gradient",
     )(idx, wgt, xb, own, xa, yb, ya, arr, ref_image, left, wy)
-    recv = lax.all_to_all(send, ("gx", "gy"), 0, 0, tiled=True)
+    recv = lax.all_to_all(send, "gx", 0, 0, tiled=True)
+    nodes, send = pl.pallas_call(
+        lambda *refs: face_kernel(nx, ny, *refs),
+        out_shape=(sds((7, 8, 128), F32), sds((ny, 1, 128), F32)),
+        in_specs=[VMEM] * 2,
+        out_specs=(VMEM,) * 2,
+        compiler_params=PARAMS,
+        name="add_faces",
+    )(recv, nodes)
+    recv = lax.all_to_all(send, "gy", 0, 0, tiled=True)
     grads, hess, send, residual = pl.pallas_call(
         lambda *refs: product_kernel(nx, ny, *refs),
         out_shape=(
             sds((6, 8, 128), F32),
             sds((6, 8, 128), F32),
-            sds((peers, 1, 128), F32),
+            sds((nx, 1, 128), F32),
             sds((8, 64, 128), BF16),
         ),
         in_specs=[VMEM] * 9,
@@ -525,7 +539,16 @@
         compiler_params=PARAMS,
         name="gauss_newton_product",
     )(recv, nodes, slopes, square, expand, wyt, left, wy, residual)
-    recv = lax.all_to_all(send, ("gx", "gy"), 0, 0, tiled=True)
+    recv = lax.all_to_all(send, "gx", 0, 0, tiled=True)
+    hess, send = pl.pallas_call(
+        lambda *refs: total_kernel(nx, ny, *refs),
+        out_shape=(sds((6, 8, 128), F32), sds((ny, 1, 128), F32)),
+        in_specs=[VMEM] * 2,
+        out_specs=(VMEM,) * 2,
+        compiler_params=PARAMS,
+        name="add_faces_and_sums",
+    )(recv, hess)
+    recv = lax.all_to_all(send, "gy", 0, 0, tiled=True)
     voxels = 8 * 64 * 128 * peers
     step, product, misfit = pl.pallas_call(
         lambda *refs: finish_kernel(nx, ny, voxels, *refs),

time: 44.8 us -> 56.8 us (1.27)
  blocking collectives: 24.3 us -> 36.9 us
  other arithmetic: 2.13 us -> 0.78 us
  local copies, waits for them, and re-layouts: 0.93 us -> 1.61 us
    all_to_all x2 -> x4, blocking collectives: 24.3 us -> 36.9 us  [the longest x2 24 us: on_device(): recv = lax.all_to_all(send, 'gx', 0, 0, tiled=True)]
    convert_element_type x2 -> x0, other arithmetic: 1.37 us -> none  [on_device(): rows.astype(F32)]
    pallas_call x1, Pallas kernels: 3.29 us -> 2.54 us  [on_device(): pl.pallas_call(early_kernel, out_shape=sds((16, 18, 8, 128), F32), in_spe...]
    unnamed x12 -> x14, local copies, waits for them, and re-layouts: 0.93 us -> 1.61 us
    pallas_call x1, Pallas kernels: 2.74 us -> 3.38 us  [on_device(): pl.pallas_call(lambda *refs: late_kernel(nx, ny, *refs), out_shape=(sds((...]
  transfers between devices with their start and end apart: 4 -> 4, of which waited for: 0 -> 0; matrix products, arithmetic and copies ran while one was open for 5% -> 1% of each run, Pallas kernels for 9% -> 6%
where the time goes in v10:
time: 56.8 us; the launch traced here: 56.7 us
  blocking collectives  36.9 us (65%)
  Pallas kernels  9.18 us (16%)
  starting transfers between devices  7.46 us (13%)
  local copies, waits for them, and re-layouts  1.61 us (3%)
  other arithmetic  0.78 us (1%)
  between operations  0.76 us (1%)
    all_to_all x2, blocking collectives, on_device(): recv = lax.all_to_all(send, 'gx', 0, 0, tiled=True)  24 us
    all_to_all x2, blocking collectives, on_device(): recv = lax.all_to_all(send, 'gy', 0, 0, tiled=True)  12.8 us
    pallas_call x1, Pallas kernels, on_device(): pl.pallas_call(lambda *refs: late_kernel(nx, ny, *refs), out_shape=(sds((...  3.38 us
    ppermute x1, starting transfers between devices, on_device(): ya = lax.ppermute(to_a, 'gy', swaps(ny, 0))  3.09 us
    ppermute x1, starting transfers between devices, on_device(): xa = lax.ppermute(def_image, 'gx', swaps(nx, 0))  3.03 us
    pallas_call x1, Pallas kernels, on_device(): pl.pallas_call(early_kernel, out_shape=sds((16, 18, 8, 128), F32), in_spe...  2.54 us
    unnamed x14, local copies, waits for them, and re-layouts  1.61 us
    pallas_call x1, Pallas kernels, on_device(): pl.pallas_call(lambda *refs: product_kernel(nx, ny, *refs), out_shape=(sd...  1.17 us
  transfers between devices with their start and end apart: 4, of which 0 were waited for; matrix products, arithmetic and copies ran while one was open for 1% of the time, Pallas kernels for 6%

profile of v10, /device:TPU:0, one launch (start us, length us, event | category | flops | bytes accessed | tf_op | source)
XLA Modules:
  0.0 56.7 jit_solution(4982662069546603971)
XLA Ops:
  0.6 0.0 copy-start.1
  0.6 0.0 copy-start
  0.7 0.0 copy-start.2
  0.7 3.0 %collective-permute-start.1 = (bf16[8,64,128]{2,1,0:T(8,128)(2,1)}, bf16[8,64,128]{2,1,0:T(8,128)(2,1)S(1)}, u32[]{:S(2)}, u32[]{:S(2)}) collective-permute-start(bf16[8,64,128]{2,1,0:T(8,128)(2,1)} %own_ref.1), channel_id=1, source_target_pairs={{0,4},{8,12},{16,20},{24,28},{4,0},{12,8},{20,16},{28,24},{1,5},{9... | collective-permute-start | bytes 393224 | tf_op jit(solution)/shard_map/ppermute | solution.py:456
  3.7 0.7 %collective-permute-start = (bf16[8,64,128]{2,1,0:T(8,128)(2,1)}, bf16[8,64,128]{2,1,0:T(8,128)(2,1)S(1)}, u32[]{:S(2)}, u32[]{:S(2)}) collective-permute-start(bf16[8,64,128]{2,1,0:T(8,128)(2,1)} %own_ref.1), channel_id=1, source_target_pairs={{4,8},{12,16},{20,24},{8,4},{16,12},{24,20},{5,9},{13,17},{21,25},... | collective-permute-start | bytes 393224 | tf_op jit(solution)/shard_map/ppermute | solution.py:457
  4.4 0.8 %pad_add_fusion.row_ref = s32[16,128]{1,0:T(8,128)S(1)} fusion(s32[2,128]{1,0:T(2,128)} %param.12, s32[8,128]{1,0:T(8,128)} %param.15, s32[128]{0:T(128)} %param.13, pred[16]{0:T(512)(128)(4,1)S(1)} %iota_compare_fusion), kind=kLoop, calls=%fused_computation | loop fusion | flops 6144 | bytes 13840 | tf_op jit(solution)/shard_map/add | solution.py:460
  5.1 0.0 copy-start.3
  5.2 0.9 %copy-done.3 = bf16[8,64,128]{2,1,0:T(8,128)(2,1)S(1)} copy-done((bf16[8,64,128]{2,1,0:T(8,128)(2,1)S(1)}, bf16[8,64,128]{2,1,0:T(8,128)(2,1)}, u32[]{:S(2)}) %copy-start.3) | copy-done | bytes 131096
  6.1 0.0 copy-start.6
  6.1 0.7 %copy-done.6 = f32[3,128]{1,0:T(4,128)S(1)} copy-done((f32[3,128]{1,0:T(4,128)S(1)}, f32[3,128]{1,0:T(4,128)}, u32[]{:S(2)}) %copy-start.6) | copy-done | bytes 1560
  6.7 0.7 %order_elements.1 = (s32[8,128]{1,0:T(8,128)S(1)}, f32[8,8,128]{2,1,0:T(8,128)S(1)}, bf16[8,64,128]{2,1,0:T(8,128)(2,1)S(1)}) custom-call(s32[16,128]{1,0:T(8,128)S(1)} %pad_add_fusion.row_ref, f32[3,128]{1,0:T(4,128)S(1)} %copy-done.6, bf16[8,64,128]{2,1,0:T(8,128)(2,1)S(1)} %copy-done.3), custom_call_target="tpu_custom_call" | custom-call | flops 300000 | bytes 262144 | tf_op jit(solution)/shard_map/order_elements/pallas_call | solution.py:461
  7.4 0.0 collective-permute-done.1.xa_ref.refs_4_
  7.4 0.0 collective-permute-done.xb_ref.refs_2_
  7.4 0.2 pack_halo.1
  7.6 0.7 %collective-permute-start.2 = (bf16[4,192,128]{2,1,0:T(8,128)(2,1)S(1)}, bf16[4,192,128]{2,1,0:T(8,128)(2,1)S(1)}, u32[]{:S(2)}, u32[]{:S(2)}) collective-permute-start(bf16[4,192,128]{2,1,0:T(8,128)(2,1)S(1)} %get-tuple-element.28), channel_id=1, source_target_pairs={{1,2},{2,1},{5,6},{6,5},{9,10},{10,9},{13,14},{14,13},{17,18},{18,... | collective-permute-start | bytes 589832 | tf_op jit(solution)/shard_map/ppermute | solution.py:480
  8.3 3.1 %collective-permute-start.3 = (bf16[4,192,128]{2,1,0:T(8,128)(2,1)S(1)}, bf16[4,192,128]{2,1,0:T(8,128)(2,1)S(1)}, u32[]{:S(2)}, u32[]{:S(2)}) collective-permute-start(bf16[4,192,128]{2,1,0:T(8,128)(2,1)S(1)} %get-tuple-element.29), channel_id=1, source_target_pairs={{0,1},{2,3},{1,0},{3,2},{4,5},{6,7},{5,4},{7,6},{8,9},{10,11},{9,8... | collective-permute-start | bytes 589832 | tf_op jit(solution)/shard_map/ppermute | solution.py:481
  11.4 2.5 %sample_early.1.refs_7_ = f32[16,18,8,128]{3,2,1,0:T(8,128)S(1)} custom-call(s32[8,128]{1,0:T(8,128)S(1)} %get-tuple-element.25.idx_ref.refs_0_, bf16[8,64,128]{2,1,0:T(8,128)(2,1)S(1)} %collective-permute-done.xb_ref.refs_2_, bf16[8,64,128]{2,1,0:T(8,128)(2,1)S(1)} %get-tuple-element.27.own_ref.refs_3_, ...), custom_call_target="tpu_custom_call" | custom-call | flops 4000000 | bytes 2000000 | tf_op jit(solution)/shard_map/sample_early/pallas_call | solution.py:484
  14.0 0.0 copy-start.4
  14.0 0.0 copy-start.5
  14.0 0.0 collective-permute-done.2.refs_5_
  14.0 0.0 collective-permute-done.3.refs_6_
  14.0 0.0 copy-done.1
  14.0 0.0 copy-done
  14.0 0.0 copy-done.2
  14.0 3.4 %sample_and_gradient.1 = (bf16[8,64,128]{2,1,0:T(8,128)(2,1)S(1)}, f32[3,8,8,8,128]{4,3,2,1,0:T(8,128)S(1)}, f32[64,128]{1,0:T(8,128)S(1)}, f32[8,1,128]{2,1,0:T(1,128)S(1)}, f32[8,128]{1,0:T(8,128)S(1)}) custom-call(s32[8,128]{1,0:T(8,128)S(1)} %get-tuple-element.25.idx_ref.refs_0_, f32[8,8,128]{2,1,0:T(8,128)S(1)} %get-tuple-element.26.refs_1_, ...), custom_call_target="tpu_custom_call" | custom-call | tf_op jit(solution)/shard_map/sample_and_gradient/pallas_call | solution.py:494
  17.4 15.2 %all_to_all.20.refs_0_ = f32[8,1,128]{2,1,0:T(1,128)S(1)} all-to-all(f32[8,1,128]{2,1,0:T(1,128)S(1)} %get-tuple-element.30), channel_id=1, replica_groups=mesh['gx'=8,'gy'=4] {'gx'}, dimensions={0} | all-to-all | bytes 8192 | tf_op jit(solution)/shard_map/all_to_all | solution.py:514
  32.6 0.2 add_faces.1
  32.8 6.8 %all_to_all.21.refs_0_ = f32[4,1,128]{2,1,0:T(1,128)S(1)} all-to-all(f32[4,1,128]{2,1,0:T(1,128)S(1)} %get-tuple-element.32), channel_id=1, replica_groups=mesh['gx'=8,'gy'=4] {'gy'}, dimensions={0} | all-to-all | bytes 4096 | tf_op jit(solution)/shard_map/all_to_all | solution.py:523
  39.6 0.0 copy-done.4
  39.6 0.0 copy-done.5
  39.6 1.2 %gauss_newton_product.1 = (f32[6,8,128]{2,1,0:T(8,128)S(1)}, f32[6,8,128]{2,1,0:T(8,128)S(1)}, f32[8,1,128]{2,1,0:T(1,128)S(1)}, bf16[8,64,128]{2,1,0:T(8,128)(2,1)}) custom-call(f32[4,1,128]{2,1,0:T(1,128)S(1)} %all_to_all.21.refs_0_, f32[7,8,128]{2,1,0:T(8,128)S(1)} %get-tuple-element.33.refs_1_, f32[3,8,8,8,128]{4,3,2,1,0:T(8,128)S(1)} %get-tuple-element.34.refs_2_, ...), custom_call_target="tpu_custom_call" | custom-call | tf_op jit(solution)/shard_map/gauss_newton_product/pallas_call | solution.py:524
  40.7 8.8 %all_to_all.22.refs_0_ = f32[8,1,128]{2,1,0:T(1,128)S(1)} all-to-all(f32[8,1,128]{2,1,0:T(1,128)S(1)} %get-tuple-element.38), channel_id=1, replica_groups=mesh['gx'=8,'gy'=4] {'gx'}, dimensions={0} | all-to-all | bytes 8192 | tf_op jit(solution)/shard_map/all_to_all | solution.py:542
  49.6 0.2 add_faces_and_sums.1
  49.8 6.1 %all_to_all.23.refs_0_ = f32[4,1,128]{2,1,0:T(1,128)S(1)} all-to-all(f32[4,1,128]{2,1,0:T(1,128)S(1)} %get-tuple-element.40), channel_id=1, replica_groups=mesh['gx'=8,'gy'=4] {'gy'}, dimensions={0} | all-to-all | bytes 4096 | tf_op jit(solution)/shard_map/all_to_all | solution.py:551
  55.9 0.8 %finish.1 = (f32[3,2,8,16]{3,2,1,0:T(8,128)}, f32[3,2,8,16]{3,2,1,0:T(8,128)}, f32[1,1]{1,0:T(1,128)}) custom-call(f32[4,1,128]{2,1,0:T(1,128)S(1)} %all_to_all.23.refs_0_, f32[6,8,128]{2,1,0:T(8,128)S(1)} %get-tuple-element.41.refs_1_, f32[6,8,128]{2,1,0:T(8,128)S(1)} %get-tuple-element.42.refs_2_), custom_call_target="tpu_custom_call" | custom-call | tf_op jit(solution)/shard_map/finish/pallas_call | solution.py:553
  (1 shorter events, 0.0 us)
Async XLA Ops:
  0.6 13.4 %copy-start.1 = (bf16[128,128]{1,0:T(8,128)(2,1)S(1)}, bf16[128,128]{1,0:T(8,128)(2,1)}, u32[]{:S(2)}) copy-start(bf16[128,128]{1,0:T(8,128)(2,1)} %constant.13.clone.refs_10_.refs_7_) | copy-start | bytes 98308
  0.6 13.4 %copy-start = (bf16[64,384]{1,0:T(8,128)(2,1)S(1)}, bf16[64,384]{1,0:T(8,128)(2,1)}, u32[]{:S(2)}) copy-start(bf16[64,384]{1,0:T(8,128)(2,1)} %constant.12.clone.refs_9_.refs_6_) | copy-start | bytes 147460
  0.7 13.4 %copy-start.2 = (bf16[8,64,128]{2,1,0:T(8,128)(2,1)S(1)}, bf16[8,64,128]{2,1,0:T(8,128)(2,1)}, u32[]{:S(2)}) copy-start(bf16[8,64,128]{2,1,0:T(8,128)(2,1)} %refs_8_.1) | copy-start | bytes 393220
  0.7 6.7 %collective-permute-start.1 = (bf16[8,64,128]{2,1,0:T(8,128)(2,1)}, bf16[8,64,128]{2,1,0:T(8,128)(2,1)S(1)}, u32[]{:S(2)}, u32[]{:S(2)}) collective-permute-start(bf16[8,64,128]{2,1,0:T(8,128)(2,1)} %own_ref.1), channel_id=1, source_target_pairs={{0,4},{8,12},{16,20},{24,28},{4,0},{12,8},{20,16},{28,24},{1,5},{9... | collective-permute-start | bytes 393224 | tf_op jit(solution)/shard_map/ppermute | solution.py:456
  3.7 3.7 %collective-permute-start = (bf16[8,64,128]{2,1,0:T(8,128)(2,1)}, bf16[8,64,128]{2,1,0:T(8,128)(2,1)S(1)}, u32[]{:S(2)}, u32[]{:S(2)}) collective-permute-start(bf16[8,64,128]{2,1,0:T(8,128)(2,1)} %own_ref.1), channel_id=1, source_target_pairs={{4,8},{12,16},{20,24},{8,4},{16,12},{24,20},{5,9},{13,17},{21,25},... | collective-permute-start | bytes 393224 | tf_op jit(solution)/shard_map/ppermute | solution.py:457
  5.1 0.9 %copy-start.3 = (bf16[8,64,128]{2,1,0:T(8,128)(2,1)S(1)}, bf16[8,64,128]{2,1,0:T(8,128)(2,1)}, u32[]{:S(2)}) copy-start(bf16[8,64,128]{2,1,0:T(8,128)(2,1)} %own_ref.1) | copy-start | bytes 393220
  6.1 0.7 %copy-start.6 = (f32[3,128]{1,0:T(4,128)S(1)}, f32[3,128]{1,0:T(4,128)}, u32[]{:S(2)}) copy-start(f32[3,128]{1,0:T(4,128)} %frac_ref.1) | copy-start | bytes 4612
  7.6 6.3 %collective-permute-start.2 = (bf16[4,192,128]{2,1,0:T(8,128)(2,1)S(1)}, bf16[4,192,128]{2,1,0:T(8,128)(2,1)S(1)}, u32[]{:S(2)}, u32[]{:S(2)}) collective-permute-start(bf16[4,192,128]{2,1,0:T(8,128)(2,1)S(1)} %get-tuple-element.28), channel_id=1, source_target_pairs={{1,2},{2,1},{5,6},{6,5},{9,10},{10,9},{13,14},{14,13},{17,18},{18,... | collective-permute-start | bytes 589832 | tf_op jit(solution)/shard_map/ppermute | solution.py:480
  8.3 5.7 %collective-permute-start.3 = (bf16[4,192,128]{2,1,0:T(8,128)(2,1)S(1)}, bf16[4,192,128]{2,1,0:T(8,128)(2,1)S(1)}, u32[]{:S(2)}, u32[]{:S(2)}) collective-permute-start(bf16[4,192,128]{2,1,0:T(8,128)(2,1)S(1)} %get-tuple-element.29), channel_id=1, source_target_pairs={{0,1},{2,3},{1,0},{3,2},{4,5},{6,7},{5,4},{7,6},{8,9},{10,11},{9,8... | collective-permute-start | bytes 589832 | tf_op jit(solution)/shard_map/ppermute | solution.py:481
  14.0 25.6 %copy-start.4 = (bf16[384,64]{1,0:T(8,128)(2,1)S(1)}, bf16[384,64]{1,0:T(8,128)(2,1)}, u32[]{:S(2)}) copy-start(bf16[384,64]{1,0:T(8,128)(2,1)} %constant.14.clone.refs_4_) | copy-start | bytes 147460
  14.0 25.6 %copy-start.5 = (bf16[128,128]{1,0:T(8,128)(2,1)S(1)}, bf16[128,128]{1,0:T(8,128)(2,1)}, u32[]{:S(2)}) copy-start(bf16[128,128]{1,0:T(8,128)(2,1)} %constant.15.clone.refs_5_) | copy-start | bytes 98308

commit v11 on v9

--- a/solution.py
+++ b/solution.py
@@ -84,17 +84,17 @@
     return out
 
 
-def index_kernel(row_ref, own_ref, idx_ref, wgt_ref, keep_ref):
+def index_kernel(row_ref, frac_ref, own_ref, idx_ref, wgt_ref, keep_ref):
     keep_ref[...] = own_ref[...]
-    first = row_ref[0:1].astype(jnp.int32)
+    first = row_ref[0:1]
     col_x = (first * 241) >> 12
     col_y = first - 17 * col_x
-    start_x = 8 * col_x + row_ref[8:9].astype(jnp.int32) + HALO
-    start_y = 8 * col_y + row_ref[9:10].astype(jnp.int32) + HALO
+    start_x = 8 * col_x + row_ref[8:9] + HALO
+    start_y = 8 * col_y + row_ref[9:10] + HALO
     early = (start_y >= 64) & (start_y < 184)
     below = start_y < 64
     offset = jnp.where(early, start_y - 64, jnp.where(below, start_y, start_y - 128))
-    base = (row_ref[10:11].astype(jnp.int32) + 2) * SPAN + start_x
+    base = (row_ref[10:11] + 2) * SPAN + start_x
     tile = jnp.where(early | below, 0, TILE_ROWS)
     shift = (8 * col_y - offset) & 127
     place = (col_y & 1) * 8 + col_x
@@ -111,7 +111,7 @@
     sub = lax.broadcasted_iota(jnp.int32, (8, 128), 0)
     table = jnp.where(sub == 6, jnp.broadcast_to(count, (8, 128)), table)
     idx_ref[...] = table.astype(jnp.int32)
-    value = as_rows([row_ref[11 + c : 12 + c] for c in range(3)])
+    value = as_rows([frac_ref[c : c + 1] for c in range(3)])
     hi, lo = split(value)
     rest = (value - hi.astype(F32) - lo.astype(F32)).astype(BF16)
     element = jnp.broadcast_to(col_x * 16 + col_y, (128, 128))
@@ -203,7 +203,7 @@
 
 def late_kernel(
     nx, ny, idx_ref, wgt, xb_ref, own_ref, xa_ref, yb_ref, ya_ref, arr_ref, ref_ref,
-    left_ref, wy_ref, res_ref, slope_ref, node_ref, send_ref, sq_ref, img, arr, rsc, gsc,
+    left_ref, wy_ref, res_ref, slope_ref, node_ref, b_ref, a_ref, sq_ref, img, arr, rsc, gsc,
 ):
     half = lax.broadcasted_iota(jnp.int32, (64, 128), 1) < 64
     clear_outside(img, 2)
@@ -294,61 +294,58 @@
     res_ref[...] = rsc[...].reshape(8, 64, 128).astype(BF16)
     nodes = dot_left(dot_right(left_ref[...], gsc[...].reshape(384, 128)), wy_ref[...])
     node_ref[...] = nodes
-    rows = [nodes[kc * 8 : kc * 8 + 8] for kc in range(6)]
-    high, low = nodes[48:56], nodes[56:64]
-    col_high = column_row(rows, high, 16)
-    col_low = column_row(rows, high, 0)
-    high, low = face_row(high), face_row(low)
-    gx, gy = lax.axis_index("gx"), lax.axis_index("gy")
-    send_ref[...] = jnp.zeros(send_ref.shape, F32)
-    for dx in (-1, 0, 1):
-        for dy in (-1, 0, 1):
-            if dx == 0 and dy == 0:
-                continue
-            block = high if dx == 1 else low if dx == -1 else col_high if dy == 1 else col_low
-            px, py = gx + dx, gy + dy
-
-            @pl.when((px >= 0) & (px < nx) & (py >= 0) & (py < ny))
-            def _():
-                send_ref[px * ny + py] = block
+    send_pairs(a_ref, b_ref, "gx", face_row(nodes[48:56]), face_row(nodes[56:64]))
+
+
+def send_pairs(a_ref, b_ref, axis, after, before):
+    even = lax.axis_index(axis) % 2 == 0
+    a_ref[...] = jnp.where(even, after, before)
+    b_ref[...] = jnp.where(even, before, after)
+
+
+def from_pairs(a_ref, b_ref, axis):
+    even = lax.axis_index(axis) % 2 == 0
+    a, b = a_ref[...], b_ref[...]
+    return jnp.where(even, b, a), jnp.where(even, a, b)
+
+
+def face_kernel(xb_ref, xa_ref, node_ref, sum_ref, b_ref, a_ref):
+    sub = lax.broadcasted_iota(jnp.int32, (8, 128), 0)
+    row_low, row_high = (face_of(row) for row in from_pairs(xa_ref, xb_ref, "gx"))
+    rows = []
+    for kc in range(6):
+        g = node_ref[kc * 8 : kc * 8 + 8]
+        g = g + jnp.where(sub == 0, jnp.broadcast_to(row_low[kc : kc + 1], (8, 128)), 0.0)
+        sum_ref[kc] = g
+        rows.append(g)
+    face = node_ref[48:56] + row_high
+    sum_ref[6] = face
+    send_pairs(a_ref, b_ref, "gy", column_row(rows, face, 16), column_row(rows, face, 0))
 
 
 def product_kernel(
-    nx, ny, recv_ref, node_ref, slope_ref, sq_ref, expand_ref, wyt_ref, left_ref, wy_ref, res_ref,
+    nx, ny, yb_ref, ya_ref, node_ref, slope_ref, sq_ref, expand_ref, wyt_ref, left_ref, wy_ref, res_ref,
     grad_ref, hess_ref, send_ref, out_ref, msc, gsc, sem,
 ):
     copy_out = pltpu.make_async_copy(res_ref, out_ref, sem)
     copy_out.start()
     gx, gy = lax.axis_index("gx"), lax.axis_index("gy")
-    own = gx * ny + gy
-    lane = lax.broadcasted_iota(jnp.int32, (8, 128), 1)
-    sub = lax.broadcasted_iota(jnp.int32, (8, 128), 0)
-
-    def block(dx, dy):
-        px, py = gx + dx, gy + dy
-        there = (px >= 0) & (px < nx) & (py >= 0) & (py < ny)
-        return recv_ref[jnp.where(there, px * ny + py, own)]
+    lane = lax.broadcasted_iota(jnp.int32, (8, 128), 1)
+    sub = lax.broadcasted_iota(jnp.int32, (8, 128), 0)
 
     def column(x, at):
         return jnp.broadcast_to(x[:, at : at + 1], (8, 128))
-
-    def with_corners(dx):
-        mid = face_of(block(dx, 0))
-        mid = mid + jnp.where(lane == 0, column(face_of(block(dx, -1)), 16), 0.0)
-        return mid + jnp.where(lane == 16, column(face_of(block(dx, 1)), 0), 0.0)
 
     keep_x = jnp.where(gx == nx - 1, 0.0, 1.0).astype(F32)
     keep_y = jnp.where(gy == ny - 1, 0.0, 1.0).astype(F32)
     keep_lane = jnp.where(lane == 16, keep_y, 1.0)
-    row_low = with_corners(-1)
-    row_high = with_corners(1)
-    col_low, edge_low = column_of(block(0, -1))
-    col_high, edge_high = column_of(block(0, 1))
+    before, after = from_pairs(ya_ref, yb_ref, "gy")
+    col_low, edge_low = column_of(before)
+    col_high, edge_high = column_of(after)
     grads = []
     square = jnp.zeros((8, 128), F32)
     for kc in range(6):
-        g = node_ref[kc * 8 : kc * 8 + 8]
-        g = g + jnp.where(sub == 0, jnp.broadcast_to(row_low[kc : kc + 1], (8, 128)), 0.0)
+        g = node_ref[kc]
         g = g + jnp.where(lane == 0, column(col_low, kc), 0.0)
         g = g + jnp.where(lane == 16, column(col_high, kc), 0.0)
         g = g * keep_lane
@@ -356,7 +353,7 @@
         grad_ref[kc] = g
         own_g = jnp.where(lane < 16, g, 0.0)
         square = square + own_g * own_g
-    face = node_ref[48:56] + row_high
+    face = node_ref[6]
     face = face + jnp.where(lane == 0, column(edge_low, 0), 0.0)
     face = face + jnp.where(lane == 16, column(edge_high, 0), 0.0)
     face = jnp.where(sub < 6, face * keep_lane * keep_x, 0.0)
@@ -450,18 +447,17 @@
     xa = lax.ppermute(def_image, "gx", swaps(nx, 0))
     xb = lax.ppermute(def_image, "gx", swaps(nx, 1))
     row = lax.broadcasted_iota(jnp.int32, (16, 128), 0)
-    table = jnp.where(row == 10, shift_z[None], 0).astype(F32)
-    for rows, at in ((connectivity, 0), (shift_xy, 8), (frac, 11)):
-        table = table + jnp.pad(rows.astype(F32), ((at, 16 - at - rows.shape[0]), (0, 0)))
+    table = jnp.where(row == 10, shift_z[None], 0)
+    table = table + jnp.pad(connectivity, ((0, 8), (0, 0))) + jnp.pad(shift_xy, ((8, 6), (0, 0)))
     idx, wgt, own = pl.pallas_call(
         index_kernel,
         out_shape=(sds((8, 128), jnp.int32), sds((8, 8, 128), F32), sds((8, 64, 128), BF16)),
-        in_specs=[VMEM, VMEM],
+        in_specs=[VMEM] * 3,
         out_specs=(VMEM,) * 3,
         compiler_params=PARAMS,
         cost_estimate=pl.CostEstimate(flops=300000, bytes_accessed=262144, transcendentals=0),
         name="order_elements",
-    )(table, def_image)
+    )(table, frac, def_image)
     packed = sds((4, SPAN, 128), BF16)
     to_b, to_a = pl.pallas_call(
         pack_kernel,
@@ -486,17 +482,18 @@
         cost_estimate=pl.CostEstimate(flops=4000000, bytes_accessed=2000000, transcendentals=0),
         name="sample_early",
     )(idx, xb, own, xa)
-    residual, slopes, nodes, send, square = pl.pallas_call(
+    residual, slopes, nodes, to_b, to_a, square = pl.pallas_call(
         lambda *refs: late_kernel(nx, ny, *refs),
         out_shape=(
             sds((8, 64, 128), BF16),
             sds((3, 8, 8, 8, 128), F32),
             sds((64, 128), F32),
-            sds((peers, 1, 128), F32),
+            sds((1, 128), F32),
+            sds((1, 128), F32),
             sds((8, 128), F32),
         ),
         in_specs=[SMEM] + [VMEM] * 10,
-        out_specs=(VMEM,) * 5,
+        out_specs=(VMEM,) * 6,
         scratch_shapes=[
             pltpu.VMEM((2 * TILE_ROWS, 128), F32),
             pltpu.VMEM((16, 18, 8, 128), F32),
@@ -506,7 +503,19 @@
         compiler_params=PARAMS,
         name="sample_and_gradient",
     )(idx, wgt, xb, own, xa, yb, ya, arr, ref_image, left, wy)
-    recv = lax.all_to_all(send, ("gx", "gy"), 0, 0, tiled=True)
+    xa = lax.ppermute(to_a, "gx", swaps(nx, 0))
+    xb = lax.ppermute(to_b, "gx", swaps(nx, 1))
+    line = sds((1, 128), F32)
+    nodes, to_b, to_a = pl.pallas_call(
+        face_kernel,
+        out_shape=(sds((7, 8, 128), F32), line, line),
+        in_specs=[VMEM] * 3,
+        out_specs=(VMEM,) * 3,
+        compiler_params=PARAMS,
+        name="add_faces",
+    )(xb, xa, nodes)
+    yb = lax.ppermute(to_b, "gy", swaps(ny, 1))
+    ya = lax.ppermute(to_a, "gy", swaps(ny, 0))
     grads, hess, send, residual = pl.pallas_call(
         lambda *refs: product_kernel(nx, ny, *refs),
         out_shape=(
@@ -515,7 +524,7 @@
             sds((peers, 1, 128), F32),
             sds((8, 64, 128), BF16),
         ),
-        in_specs=[VMEM] * 9,
+        in_specs=[VMEM] * 10,
         out_specs=(VMEM,) * 3 + (pl.BlockSpec(memory_space=pl.ANY),),
         scratch_shapes=[
             pltpu.VMEM((6, 8, 8, 128), F32),
@@ -524,7 +533,7 @@
         ],
         compiler_params=PARAMS,
         name="gauss_newton_product",
-    )(recv, nodes, slopes, square, expand, wyt, left, wy, residual)
+    )(yb, ya, nodes, slopes, square, expand, wyt, left, wy, residual)
     recv = lax.all_to_all(send, ("gx", "gy"), 0, 0, tiled=True)
     voxels = 8 * 64 * 128 * peers
     step, product, misfit = pl.pallas_call(

time: 44.8 us -> 47.6 us (1.062)
  starting transfers between devices: 7.27 us -> 19.4 us
  blocking collectives: 24.3 us -> 13.5 us
  waiting for transfers between devices: 0.01 us -> 2.35 us
  other arithmetic: 2.13 us -> 0.78 us
  local copies, waits for them, and re-layouts: 0.93 us -> 1.61 us
    all_to_all x2 -> x1, blocking collectives: 24.3 us -> 13.5 us  [on_device(): recv = lax.all_to_all(send, ('gx', 'gy'), 0, 0, tiled=True)]
    ppermute x0 -> x2, starting transfers between devices: none -> 9.04 us  [the longest x1 8.38 us: on_device(): xa = lax.ppermute(to_a, 'gx', swaps(nx, 0))]
    ppermute x1 -> x2, starting transfers between devices: 2.91 us -> 5.33 us  [on_device(): ya = lax.ppermute(to_a, 'gy', swaps(ny, 0))]
    ppermute x0 -> x2, waiting for transfers between devices: none -> 1.52 us  [the longest x1 1.52 us: on_device(): xa = lax.ppermute(to_a, 'gx', swaps(nx, 0))]
    convert_element_type x2 -> x0, other arithmetic: 1.37 us -> none  [on_device(): rows.astype(F32)]
    ppermute x1 -> x2, waiting for transfers between devices: 0.01 us -> 0.82 us  [on_device(): ya = lax.ppermute(to_a, 'gy', swaps(ny, 0))]
    pallas_call x1, Pallas kernels: 3.29 us -> 2.54 us  [on_device(): pl.pallas_call(early_kernel, out_shape=sds((16, 18, 8, 128), F32), in_spe...]
    unnamed x12 -> x14, local copies, waits for them, and re-layouts: 0.93 us -> 1.61 us
  transfers between devices with their start and end apart: 4 -> 8, of which waited for: 0 -> 2; matrix products, arithmetic and copies ran while one was open for 5% -> 2% of each run, Pallas kernels for 9% -> 7%
where the time goes in v11:
time: 47.6 us; the launch traced here: 47.5 us
  starting transfers between devices  19.4 us (41%)
  blocking collectives  13.5 us (28%)
  Pallas kernels  9.07 us (19%)
  waiting for transfers between devices  2.35 us (5%)
  local copies, waits for them, and re-layouts  1.61 us (3%)
  between operations  0.79 us (2%)
  other arithmetic  0.78 us (2%)
    all_to_all x1, blocking collectives, on_device(): recv = lax.all_to_all(send, ('gx', 'gy'), 0, 0, tiled=True)  13.5 us
    ppermute x1, starting transfers between devices, on_device(): xa = lax.ppermute(to_a, 'gx', swaps(nx, 0))  8.38 us
    ppermute x2, starting transfers between devices, on_device(): ya = lax.ppermute(to_a, 'gy', swaps(ny, 0))  5.33 us
    pallas_call x1, Pallas kernels, on_device(): pl.pallas_call(lambda *refs: late_kernel(nx, ny, *refs), out_shape=(sds((...  3.39 us
    ppermute x1, starting transfers between devices, on_device(): xa = lax.ppermute(def_image, 'gx', swaps(nx, 0))  3.03 us
    pallas_call x1, Pallas kernels, on_device(): pl.pallas_call(early_kernel, out_shape=sds((16, 18, 8, 128), F32), in_spe...  2.54 us
    unnamed x14, local copies, waits for them, and re-layouts  1.61 us
    ppermute x1, waiting for transfers between devices, on_device(): xa = lax.ppermute(to_a, 'gx', swaps(nx, 0))  1.52 us
  transfers between devices with their start and end apart: 8, of which 2 were waited for; matrix products, arithmetic and copies ran while one was open for 2% of the time, Pallas kernels for 7%

profile of v11, /device:TPU:0, one launch (start us, length us, event | category | flops | bytes accessed | tf_op | source)
XLA Modules:
  0.0 47.5 jit_solution(7537015745420984673)
XLA Ops:
  0.6 0.0 copy-start.2
  0.6 0.0 copy-start
  0.7 0.0 copy-start.1
  0.7 3.0 %collective-permute-start.1 = (bf16[8,64,128]{2,1,0:T(8,128)(2,1)}, bf16[8,64,128]{2,1,0:T(8,128)(2,1)S(1)}, u32[]{:S(2)}, u32[]{:S(2)}) collective-permute-start(bf16[8,64,128]{2,1,0:T(8,128)(2,1)} %own_ref.1), channel_id=1, source_target_pairs={{0,4},{8,12},{16,20},{24,28},{4,0},{12,8},{20,16},{28,24},{1,5},{9... | collective-permute-start | bytes 393224 | tf_op jit(solution)/shard_map/ppermute | solution.py:447
  3.7 0.7 %collective-permute-start = (bf16[8,64,128]{2,1,0:T(8,128)(2,1)}, bf16[8,64,128]{2,1,0:T(8,128)(2,1)S(1)}, u32[]{:S(2)}, u32[]{:S(2)}) collective-permute-start(bf16[8,64,128]{2,1,0:T(8,128)(2,1)} %own_ref.1), channel_id=1, source_target_pairs={{4,8},{12,16},{20,24},{8,4},{16,12},{24,20},{5,9},{13,17},{21,25},... | collective-permute-start | bytes 393224 | tf_op jit(solution)/shard_map/ppermute | solution.py:448
  4.4 0.8 %pad_add_fusion.row_ref = s32[16,128]{1,0:T(8,128)S(1)} fusion(s32[2,128]{1,0:T(2,128)} %param.12, s32[8,128]{1,0:T(8,128)} %param.15, s32[128]{0:T(128)} %param.13, pred[16]{0:T(512)(128)(4,1)S(1)} %iota_compare_fusion), kind=kLoop, calls=%fused_computation | loop fusion | flops 6144 | bytes 13840 | tf_op jit(solution)/shard_map/add | solution.py:451
  5.1 0.0 copy-start.3
  5.2 0.9 %copy-done.3 = bf16[8,64,128]{2,1,0:T(8,128)(2,1)S(1)} copy-done((bf16[8,64,128]{2,1,0:T(8,128)(2,1)S(1)}, bf16[8,64,128]{2,1,0:T(8,128)(2,1)}, u32[]{:S(2)}) %copy-start.3) | copy-done | bytes 131096
  6.1 0.0 copy-start.6
  6.1 0.7 %copy-done.6 = f32[3,128]{1,0:T(4,128)S(1)} copy-done((f32[3,128]{1,0:T(4,128)S(1)}, f32[3,128]{1,0:T(4,128)}, u32[]{:S(2)}) %copy-start.6) | copy-done | bytes 1560
  6.7 0.7 %order_elements.1 = (s32[8,128]{1,0:T(8,128)S(1)}, f32[8,8,128]{2,1,0:T(8,128)S(1)}, bf16[8,64,128]{2,1,0:T(8,128)(2,1)S(1)}) custom-call(s32[16,128]{1,0:T(8,128)S(1)} %pad_add_fusion.row_ref, f32[3,128]{1,0:T(4,128)S(1)} %copy-done.6, bf16[8,64,128]{2,1,0:T(8,128)(2,1)S(1)} %copy-done.3), custom_call_target="tpu_custom_call" | custom-call | flops 300000 | bytes 262144 | tf_op jit(solution)/shard_map/order_elements/pallas_call | solution.py:452
  7.4 0.0 collective-permute-done.1.xa_ref.refs_4_
  7.4 0.0 collective-permute-done.xb_ref.refs_2_
  7.4 0.2 pack_halo.1
  7.6 0.7 %collective-permute-start.2 = (bf16[4,192,128]{2,1,0:T(8,128)(2,1)S(1)}, bf16[4,192,128]{2,1,0:T(8,128)(2,1)S(1)}, u32[]{:S(2)}, u32[]{:S(2)}) collective-permute-start(bf16[4,192,128]{2,1,0:T(8,128)(2,1)S(1)} %get-tuple-element.28), channel_id=1, source_target_pairs={{1,2},{2,1},{5,6},{6,5},{9,10},{10,9},{13,14},{14,13},{17,18},{18,... | collective-permute-start | bytes 589832 | tf_op jit(solution)/shard_map/ppermute | solution.py:471
  8.3 3.1 %collective-permute-start.3 = (bf16[4,192,128]{2,1,0:T(8,128)(2,1)S(1)}, bf16[4,192,128]{2,1,0:T(8,128)(2,1)S(1)}, u32[]{:S(2)}, u32[]{:S(2)}) collective-permute-start(bf16[4,192,128]{2,1,0:T(8,128)(2,1)S(1)} %get-tuple-element.29), channel_id=1, source_target_pairs={{0,1},{2,3},{1,0},{3,2},{4,5},{6,7},{5,4},{7,6},{8,9},{10,11},{9,8... | collective-permute-start | bytes 589832 | tf_op jit(solution)/shard_map/ppermute | solution.py:472
  11.4 2.5 %sample_early.1.refs_7_ = f32[16,18,8,128]{3,2,1,0:T(8,128)S(1)} custom-call(s32[8,128]{1,0:T(8,128)S(1)} %get-tuple-element.25.idx_ref.refs_0_, bf16[8,64,128]{2,1,0:T(8,128)(2,1)S(1)} %collective-permute-done.xb_ref.refs_2_, bf16[8,64,128]{2,1,0:T(8,128)(2,1)S(1)} %get-tuple-element.27.own_ref.refs_3_, ...), custom_call_target="tpu_custom_call" | custom-call | flops 4000000 | bytes 2000000 | tf_op jit(solution)/shard_map/sample_early/pallas_call | solution.py:475
  14.0 0.0 copy-start.4
  14.0 0.0 copy-start.5
  14.0 0.0 collective-permute-done.2.refs_5_
  14.0 0.0 collective-permute-done.3.refs_6_
  14.0 0.0 copy-done.2
  14.0 0.0 copy-done
  14.0 0.0 copy-done.1
  14.0 3.4 %sample_and_gradient.1 = (bf16[8,64,128]{2,1,0:T(8,128)(2,1)S(1)}, f32[3,8,8,8,128]{4,3,2,1,0:T(8,128)S(1)}, f32[64,128]{1,0:T(8,128)S(1)}, f32[1,128]{1,0:T(1,1...) custom-call(s32[8,128]{1,0:T(8,128)S(1)} %get-tuple-element.25.idx_ref.refs_0_, ...), custom_call_target="tpu_custom_call" | custom-call | tf_op jit(solution)/shard_map/sample_and_gradient/pallas_call | solution.py:485
  17.4 0.7 %collective-permute-start.4 = (f32[1,128]{1,0:T(1,128)S(1)}, f32[1,128]{1,0:T(1,128)S(1)}, u32[]{:S(2)}, u32[]{:S(2)}) collective-permute-start(f32[1,128]{1,0:T(1,128)S(1)} %get-tuple-element.30), channel_id=1, source_target_pairs={{4,8},{12,16},{20,24},{8,4},{16,12},{24,20},{5,9},{13,17},{21,25},... | collective-permute-start | bytes 1544 | tf_op jit(solution)/shard_map/ppermute | solution.py:507
  18.1 8.4 %collective-permute-start.5 = (f32[1,128]{1,0:T(1,128)S(1)}, f32[1,128]{1,0:T(1,128)S(1)}, u32[]{:S(2)}, u32[]{:S(2)}) collective-permute-start(f32[1,128]{1,0:T(1,128)S(1)} %get-tuple-element.31), channel_id=1, source_target_pairs={{0,4},{8,12},{16,20},{24,28},{4,0},{12,8},{20,16},{28,24},{1,5},{9... | collective-permute-start | bytes 1544 | tf_op jit(solution)/shard_map/ppermute | solution.py:506
  26.5 0.0 collective-permute-done.4.xb_ref
  26.5 1.5 %collective-permute-done.5.xa_ref = f32[1,128]{1,0:T(1,128)S(1)} collective-permute-done((f32[1,128]{1,0:T(1,128)S(1)}, f32[1,128]{1,0:T(1,128)S(1)}, u32[]{:S(2)}, u32[]{:S(2)}) %collective-permute-start.5) | collective-permute-done | bytes 544 | tf_op jit(solution)/shard_map/ppermute | solution.py:506
  28.0 0.2 add_faces.1
  28.2 0.7 %collective-permute-start.6 = (f32[1,128]{1,0:T(1,128)S(1)}, f32[1,128]{1,0:T(1,128)S(1)}, u32[]{:S(2)}, u32[]{:S(2)}) collective-permute-start(f32[1,128]{1,0:T(1,128)S(1)} %get-tuple-element.33), channel_id=1, source_target_pairs={{1,2},{2,1},{5,6},{6,5},{9,10},{10,9},{13,14},{14,13},{17,18},{18,... | collective-permute-start | bytes 1544 | tf_op jit(solution)/shard_map/ppermute | solution.py:517
  28.9 2.2 %collective-permute-start.7 = (f32[1,128]{1,0:T(1,128)S(1)}, f32[1,128]{1,0:T(1,128)S(1)}, u32[]{:S(2)}, u32[]{:S(2)}) collective-permute-start(f32[1,128]{1,0:T(1,128)S(1)} %get-tuple-element.34), channel_id=1, source_target_pairs={{0,1},{2,3},{1,0},{3,2},{4,5},{6,7},{5,4},{7,6},{8,9},{10,11},{9,8... | collective-permute-start | bytes 1544 | tf_op jit(solution)/shard_map/ppermute | solution.py:518
  31.1 0.0 collective-permute-done.6.refs_0_
  31.1 0.8 %collective-permute-done.7.refs_1_ = f32[1,128]{1,0:T(1,128)S(1)} collective-permute-done((f32[1,128]{1,0:T(1,128)S(1)}, f32[1,128]{1,0:T(1,128)S(1)}, u32[]{:S(2)}, u32[]{:S(2)}) %collective-permute-start.7) | collective-permute-done | bytes 544 | tf_op jit(solution)/shard_map/ppermute | solution.py:518
  32.0 0.0 copy-done.4
  32.0 0.0 copy-done.5
  32.0 1.3 %gauss_newton_product.1 = (f32[6,8,128]{2,1,0:T(8,128)S(1)}, f32[6,8,128]{2,1,0:T(8,128)S(1)}, f32[32,1,128]{2,1,0:T(1,128)S(1)}, bf16[8,64,128]{2,1,0:T(8,128)(2,1)}) custom-call(f32[1,128]{1,0:T(1,128)S(1)} %collective-permute-done.6.refs_0_, f32[1,128]{1,0:T(1,128)S(1)} %collective-permute-done.7.refs_1_, f32[7,8,128]{2,1,0:T(8,128)S(1)} %get-tuple-element.35.refs_2_, ...), custom_call_target="tpu_custom_call" | custom-call | tf_op jit(solution)/shard_map/gauss_newton_product/pallas_call | solution.py:519
  33.2 13.5 %all_to_all.5.refs_0_ = f32[32,1,128]{2,1,0:T(1,128)S(1)} all-to-all(f32[32,1,128]{2,1,0:T(1,128)S(1)} %get-tuple-element.40), channel_id=1, replica_groups=mesh['gx'=8,'gy'=4] {'gx','gy'}, dimensions={0} | all-to-all | bytes 32768 | tf_op jit(solution)/shard_map/all_to_all | solution.py:537
  46.7 0.8 %finish.1 = (f32[3,2,8,16]{3,2,1,0:T(8,128)}, f32[3,2,8,16]{3,2,1,0:T(8,128)}, f32[1,1]{1,0:T(1,128)}) custom-call(f32[32,1,128]{2,1,0:T(1,128)S(1)} %all_to_all.5.refs_0_, f32[6,8,128]{2,1,0:T(8,128)S(1)} %get-tuple-element.41.refs_1_, f32[6,8,128]{2,1,0:T(8,128)S(1)} %get-tuple-element.42.refs_2_), custom_call_target="tpu_custom_call" | custom-call | tf_op jit(solution)/shard_map/finish/pallas_call | solution.py:539
  (1 shorter events, 0.0 us)
Async XLA Ops:
  0.6 13.4 %copy-start.2 = (bf16[128,128]{1,0:T(8,128)(2,1)S(1)}, bf16[128,128]{1,0:T(8,128)(2,1)}, u32[]{:S(2)}) copy-start(bf16[128,128]{1,0:T(8,128)(2,1)} %constant.13.clone.refs_10_.refs_8_) | copy-start | bytes 98308
  0.6 13.4 %copy-start = (bf16[64,384]{1,0:T(8,128)(2,1)S(1)}, bf16[64,384]{1,0:T(8,128)(2,1)}, u32[]{:S(2)}) copy-start(bf16[64,384]{1,0:T(8,128)(2,1)} %constant.12.clone.refs_9_.refs_7_) | copy-start | bytes 147460
  0.7 13.4 %copy-start.1 = (bf16[8,64,128]{2,1,0:T(8,128)(2,1)S(1)}, bf16[8,64,128]{2,1,0:T(8,128)(2,1)}, u32[]{:S(2)}) copy-start(bf16[8,64,128]{2,1,0:T(8,128)(2,1)} %refs_8_.2) | copy-start | bytes 393220
  0.7 6.7 %collective-permute-start.1 = (bf16[8,64,128]{2,1,0:T(8,128)(2,1)}, bf16[8,64,128]{2,1,0:T(8,128)(2,1)S(1)}, u32[]{:S(2)}, u32[]{:S(2)}) collective-permute-start(bf16[8,64,128]{2,1,0:T(8,128)(2,1)} %own_ref.1), channel_id=1, source_target_pairs={{0,4},{8,12},{16,20},{24,28},{4,0},{12,8},{20,16},{28,24},{1,5},{9... | collective-permute-start | bytes 393224 | tf_op jit(solution)/shard_map/ppermute | solution.py:447
  3.7 3.7 %collective-permute-start = (bf16[8,64,128]{2,1,0:T(8,128)(2,1)}, bf16[8,64,128]{2,1,0:T(8,128)(2,1)S(1)}, u32[]{:S(2)}, u32[]{:S(2)}) collective-permute-start(bf16[8,64,128]{2,1,0:T(8,128)(2,1)} %own_ref.1), channel_id=1, source_target_pairs={{4,8},{12,16},{20,24},{8,4},{16,12},{24,20},{5,9},{13,17},{21,25},... | collective-permute-start | bytes 393224 | tf_op jit(solution)/shard_map/ppermute | solution.py:448
  5.1 0.9 %copy-start.3 = (bf16[8,64,128]{2,1,0:T(8,128)(2,1)S(1)}, bf16[8,64,128]{2,1,0:T(8,128)(2,1)}, u32[]{:S(2)}) copy-start(bf16[8,64,128]{2,1,0:T(8,128)(2,1)} %own_ref.1) | copy-start | bytes 393220
  6.1 0.7 %copy-start.6 = (f32[3,128]{1,0:T(4,128)S(1)}, f32[3,128]{1,0:T(4,128)}, u32[]{:S(2)}) copy-start(f32[3,128]{1,0:T(4,128)} %frac_ref.1) | copy-start | bytes 4612
  7.6 6.3 %collective-permute-start.2 = (bf16[4,192,128]{2,1,0:T(8,128)(2,1)S(1)}, bf16[4,192,128]{2,1,0:T(8,128)(2,1)S(1)}, u32[]{:S(2)}, u32[]{:S(2)}) collective-permute-start(bf16[4,192,128]{2,1,0:T(8,128)(2,1)S(1)} %get-tuple-element.28), channel_id=1, source_target_pairs={{1,2},{2,1},{5,6},{6,5},{9,10},{10,9},{13,14},{14,13},{17,18},{18,... | collective-permute-start | bytes 589832 | tf_op jit(solution)/shard_map/ppermute | solution.py:471
  8.3 5.7 %collective-permute-start.3 = (bf16[4,192,128]{2,1,0:T(8,128)(2,1)S(1)}, bf16[4,192,128]{2,1,0:T(8,128)(2,1)S(1)}, u32[]{:S(2)}, u32[]{:S(2)}) collective-permute-start(bf16[4,192,128]{2,1,0:T(8,128)(2,1)S(1)} %get-tuple-element.29), channel_id=1, source_target_pairs={{0,1},{2,3},{1,0},{3,2},{4,5},{6,7},{5,4},{7,6},{8,9},{10,11},{9,8... | collective-permute-start | bytes 589832 | tf_op jit(solution)/shard_map/ppermute | solution.py:472
  14.0 18.0 %copy-start.4 = (bf16[384,64]{1,0:T(8,128)(2,1)S(1)}, bf16[384,64]{1,0:T(8,128)(2,1)}, u32[]{:S(2)}) copy-start(bf16[384,64]{1,0:T(8,128)(2,1)} %constant.14.clone.refs_5_) | copy-start | bytes 147460
  14.0 18.0 %copy-start.5 = (bf16[128,128]{1,0:T(8,128)(2,1)S(1)}, bf16[128,128]{1,0:T(8,128)(2,1)}, u32[]{:S(2)}) copy-start(bf16[128,128]{1,0:T(8,128)(2,1)} %constant.15.clone.refs_6_) | copy-start | bytes 98308
  17.4 9.1 %collective-permute-start.4 = (f32[1,128]{1,0:T(1,128)S(1)}, f32[1,128]{1,0:T(1,128)S(1)}, u32[]{:S(2)}, u32[]{:S(2)}) collective-permute-start(f32[1,128]{1,0:T(1,128)S(1)} %get-tuple-element.30), channel_id=1, source_target_pairs={{4,8},{12,16},{20,24},{8,4},{16,12},{24,20},{5,9},{13,17},{21,25},... | collective-permute-start | bytes 1544 | tf_op jit(solution)/shard_map/ppermute | solution.py:507
  18.1 9.9 %collective-permute-start.5 = (f32[1,128]{1,0:T(1,128)S(1)}, f32[1,128]{1,0:T(1,128)S(1)}, u32[]{:S(2)}, u32[]{:S(2)}) collective-permute-start(f32[1,128]{1,0:T(1,128)S(1)} %get-tuple-element.31), channel_id=1, source_target_pairs={{0,4},{8,12},{16,20},{24,28},{4,0},{12,8},{20,16},{28,24},{1,5},{9... | collective-permute-start | bytes 1544 | tf_op jit(solution)/shard_map/ppermute | solution.py:506
  28.2 2.9 %collective-permute-start.6 = (f32[1,128]{1,0:T(1,128)S(1)}, f32[1,128]{1,0:T(1,128)S(1)}, u32[]{:S(2)}, u32[]{:S(2)}) collective-permute-start(f32[1,128]{1,0:T(1,128)S(1)} %get-tuple-element.33), channel_id=1, source_target_pairs={{1,2},{2,1},{5,6},{6,5},{9,10},{10,9},{13,14},{14,13},{17,18},{18,... | collective-permute-start | bytes 1544 | tf_op jit(solution)/shard_map/ppermute | solution.py:517
  28.9 3.1 %collective-permute-start.7 = (f32[1,128]{1,0:T(1,128)S(1)}, f32[1,128]{1,0:T(1,128)S(1)}, u32[]{:S(2)}, u32[]{:S(2)}) collective-permute-start(f32[1,128]{1,0:T(1,128)S(1)} %get-tuple-element.34), channel_id=1, source_target_pairs={{0,1},{2,3},{1,0},{3,2},{4,5},{6,7},{5,4},{7,6},{8,9},{10,11},{9,8... | collective-permute-start | bytes 1544 | tf_op jit(solution)/shard_map/ppermute | solution.py:518

commit v12 on v9

--- a/solution.py
+++ b/solution.py
@@ -84,17 +84,17 @@
     return out
 
 
-def index_kernel(row_ref, own_ref, idx_ref, wgt_ref, keep_ref):
+def index_kernel(row_ref, frac_ref, own_ref, idx_ref, wgt_ref, keep_ref):
     keep_ref[...] = own_ref[...]
-    first = row_ref[0:1].astype(jnp.int32)
+    first = row_ref[0:1]
     col_x = (first * 241) >> 12
     col_y = first - 17 * col_x
-    start_x = 8 * col_x + row_ref[8:9].astype(jnp.int32) + HALO
-    start_y = 8 * col_y + row_ref[9:10].astype(jnp.int32) + HALO
+    start_x = 8 * col_x + row_ref[8:9] + HALO
+    start_y = 8 * col_y + row_ref[9:10] + HALO
     early = (start_y >= 64) & (start_y < 184)
     below = start_y < 64
     offset = jnp.where(early, start_y - 64, jnp.where(below, start_y, start_y - 128))
-    base = (row_ref[10:11].astype(jnp.int32) + 2) * SPAN + start_x
+    base = (row_ref[10:11] + 2) * SPAN + start_x
     tile = jnp.where(early | below, 0, TILE_ROWS)
     shift = (8 * col_y - offset) & 127
     place = (col_y & 1) * 8 + col_x
@@ -111,7 +111,7 @@
     sub = lax.broadcasted_iota(jnp.int32, (8, 128), 0)
     table = jnp.where(sub == 6, jnp.broadcast_to(count, (8, 128)), table)
     idx_ref[...] = table.astype(jnp.int32)
-    value = as_rows([row_ref[11 + c : 12 + c] for c in range(3)])
+    value = as_rows([frac_ref[c : c + 1] for c in range(3)])
     hi, lo = split(value)
     rest = (value - hi.astype(F32) - lo.astype(F32)).astype(BF16)
     element = jnp.broadcast_to(col_x * 16 + col_y, (128, 128))
@@ -177,10 +177,10 @@
 def sample_element(img, arr, base, shift, place, first, width):
     lane = lax.broadcasted_iota(jnp.int32, (8, 128), 1)
     mask = ((lane - first) & 127) < width
-    for z in range(9):
-        for q in range(2):
-            v = img[pl.ds(base + (z * SPAN + q), 8), :]
-            pltpu.store(arr.at[place, z * 2 + q], pltpu.roll(v, shift, 1), mask=mask)
+    starts = [pl.ds(base + z * SPAN, 8) for z in range(9)]
+    starts += [pl.ds(base + 8, 8, stride=SPAN), pl.ds(base + (8 * SPAN + 8), 8)]
+    for n, start in enumerate(starts):
+        pltpu.store(arr.at[place, n], pltpu.roll(img[start, :], shift, 1), mask=mask)
 
 
 def early_kernel(idx_ref, xb_ref, own_ref, xa_ref, arr_ref, img):
@@ -243,6 +243,7 @@
     lax.fori_loop(idx_ref[6, 0] // CHUNK, 128 // CHUNK, chunk, 0)
 
     lane = lax.broadcasted_iota(jnp.int32, (8, 128), 1)
+    sub = lax.broadcasted_iota(jnp.int32, (8, 128), 0)
     phase = lane & 15
     even = phase < 8
     even_next = (phase >= 1) & (phase <= 8)
@@ -250,18 +251,28 @@
     def interpolate(cx, square):
         wz, wx, wy = (jnp.broadcast_to(wgt[cx, c : c + 1], (8, 128)) for c in range(3))
 
-        def pair(z, q):
-            ev = arr[cx, z * 2 + q]
-            od = arr[cx + 8, z * 2 + q]
+        def pair(n):
+            ev = arr[cx, n]
+            od = arr[cx + 8, n]
             near = jnp.where(even, ev, od)
-            far = pltpu.roll(jnp.where(even_next, ev, od), 127, 1)
-            return near, far
+            return near, pltpu.roll(jnp.where(even_next, ev, od), 127, 1)
+
+        edge, corner = pair(9), pair(10)
+
+        def both_rows(z):
+            here = pair(z)
+            last = [corner[y][0:1] if z == 8 else edge[y][z : z + 1] for y in range(2)]
+            after = [
+                jnp.where(sub == 7, jnp.broadcast_to(last[y], (8, 128)), pltpu.roll(here[y], 7, 0))
+                for y in range(2)
+            ]
+            return here, after
 
         total = [None] * 3
         upper = [None] * 3
-        prev = [pair(0, 0), pair(0, 1)]
+        prev = both_rows(0)
         for z in range(8):
-            cur = [pair(z + 1, 0), pair(z + 1, 1)]
+            cur = both_rows(z + 1)
             low, dzx, dx = [], [], []
             for y in range(2):
                 d0 = cur[0][y] - prev[0][y]
@@ -450,18 +461,17 @@
     xa = lax.ppermute(def_image, "gx", swaps(nx, 0))
     xb = lax.ppermute(def_image, "gx", swaps(nx, 1))
     row = lax.broadcasted_iota(jnp.int32, (16, 128), 0)
-    table = jnp.where(row == 10, shift_z[None], 0).astype(F32)
-    for rows, at in ((connectivity, 0), (shift_xy, 8), (frac, 11)):
-        table = table + jnp.pad(rows.astype(F32), ((at, 16 - at - rows.shape[0]), (0, 0)))
+    table = jnp.where(row == 10, shift_z[None], 0)
+    table = table + jnp.pad(connectivity, ((0, 8), (0, 0))) + jnp.pad(shift_xy, ((8, 6), (0, 0)))
     idx, wgt, own = pl.pallas_call(
         index_kernel,
         out_shape=(sds((8, 128), jnp.int32), sds((8, 8, 128), F32), sds((8, 64, 128), BF16)),
-        in_specs=[VMEM, VMEM],
+        in_specs=[VMEM] * 3,
         out_specs=(VMEM,) * 3,
         compiler_params=PARAMS,
         cost_estimate=pl.CostEstimate(flops=300000, bytes_accessed=262144, transcendentals=0),
         name="order_elements",
-    )(table, def_image)
+    )(table, frac, def_image)
     packed = sds((4, SPAN, 128), BF16)
     to_b, to_a = pl.pallas_call(
         pack_kernel,
@@ -478,10 +488,10 @@
     left, wy, expand, wyt = tables()
     arr = pl.pallas_call(
         early_kernel,
-        out_shape=sds((16, 18, 8, 128), F32),
+        out_shape=sds((16, 11, 8, 128), F32),
         in_specs=[SMEM] + [VMEM] * 3,
         out_specs=VMEM,
-        scratch_shapes=[pltpu.VMEM((TILE_ROWS, 128), F32)],
+        scratch_shapes=[pltpu.VMEM((TILE_ROWS + 8, 128), F32)],
         compiler_params=PARAMS,
         cost_estimate=pl.CostEstimate(flops=4000000, bytes_accessed=2000000, transcendentals=0),
         name="sample_early",
@@ -498,8 +508,8 @@
         in_specs=[SMEM] + [VMEM] * 10,
         out_specs=(VMEM,) * 5,
         scratch_shapes=[
-            pltpu.VMEM((2 * TILE_ROWS, 128), F32),
-            pltpu.VMEM((16, 18, 8, 128), F32),
+            pltpu.VMEM((2 * TILE_ROWS + 8, 128), F32),
+            pltpu.VMEM((16, 11, 8, 128), F32),
             pltpu.VMEM((8, 8, 8, 128), F32),
             pltpu.VMEM((6, 8, 8, 128), F32),
         ],

time: 44.8 us -> 44.5 us (level)
  blocking collectives: 24.3 us -> 25.7 us
  other arithmetic: 2.13 us -> 0.77 us
  Pallas kernels: 8.95 us -> 7.87 us
  waiting for transfers between devices: 0.01 us -> 0.67 us
    convert_element_type x2 -> x0, other arithmetic: 1.37 us -> none  [on_device(): rows.astype(F32)]
    pallas_call x1, Pallas kernels: 3.29 us -> 1.96 us  [on_device(): pl.pallas_call(early_kernel, out_shape=sds((16, 11, 8, 128), F32), in_spe...]
    all_to_all x2, blocking collectives: 24.3 us -> 25.7 us  [on_device(): recv = lax.all_to_all(send, ('gx', 'gy'), 0, 0, tiled=True)]
    ppermute x1, waiting for transfers between devices: 0.01 us -> 0.66 us  [on_device(): xa = lax.ppermute(def_image, 'gx', swaps(nx, 0))]
    unnamed x12 -> x18, local copies, waits for them, and re-layouts: 0.93 us -> 0.94 us
  transfers between devices with their start and end apart: 4 -> 4, of which waited for: 0 -> 1; matrix products, arithmetic and copies ran while one was open for 5% -> 2% of each run, Pallas kernels for 9% -> 6%
where the time goes in v12:
time: 44.5 us; the launch traced here: 44.2 us
  blocking collectives  25.7 us (58%)
  Pallas kernels  7.87 us (18%)
  starting transfers between devices  7.49 us (17%)
  local copies, waits for them, and re-layouts  0.94 us (2%)
  between operations  0.78 us (2%)
  other arithmetic  0.77 us (2%)
  waiting for transfers between devices  0.67 us (2%)
    all_to_all x2, blocking collectives, on_device(): recv = lax.all_to_all(send, ('gx', 'gy'), 0, 0, tiled=True)  25.7 us
    ppermute x1, starting transfers between devices, on_device(): ya = lax.ppermute(to_a, 'gy', swaps(ny, 0))  3.13 us
    ppermute x1, starting transfers between devices, on_device(): xa = lax.ppermute(def_image, 'gx', swaps(nx, 0))  3.03 us
    pallas_call x1, Pallas kernels, on_device(): pl.pallas_call(lambda *refs: late_kernel(nx, ny, *refs), out_shape=(sds((...  3.03 us
    pallas_call x1, Pallas kernels, on_device(): pl.pallas_call(early_kernel, out_shape=sds((16, 11, 8, 128), F32), in_spe...  1.96 us
    pallas_call x1, Pallas kernels, on_device(): pl.pallas_call(lambda *refs: product_kernel(nx, ny, *refs), out_shape=(sd...  1.26 us
    unnamed x18, local copies, waits for them, and re-layouts  0.94 us
  transfers between devices with their start and end apart: 4, of which 1 were waited for; matrix products, arithmetic and copies ran while one was open for 2% of the time, Pallas kernels for 6%

profile of v12, /device:TPU:0, one launch (start us, length us, event | category | flops | bytes accessed | tf_op | source)
XLA Modules:
  0.0 44.2 jit_solution(7905701263521096794)
XLA Ops:
  0.6 0.0 copy-start.8
  0.6 0.0 copy-start.7
  0.7 3.0 %collective-permute-start.1 = (bf16[8,64,128]{2,1,0:T(8,128)(2,1)}, bf16[8,64,128]{2,1,0:T(8,128)(2,1)S(1)}, u32[]{:S(2)}, u32[]{:S(2)}) collective-permute-start(bf16[8,64,128]{2,1,0:T(8,128)(2,1)} %own_ref.1), channel_id=1, source_target_pairs={{0,4},{8,12},{16,20},{24,28},{4,0},{12,8},{20,16},{28,24},{1,5},{9... | collective-permute-start | bytes 393224 | tf_op jit(solution)/shard_map/ppermute | solution.py:461
  3.7 0.7 %collective-permute-start = (bf16[8,64,128]{2,1,0:T(8,128)(2,1)}, bf16[8,64,128]{2,1,0:T(8,128)(2,1)S(1)}, u32[]{:S(2)}, u32[]{:S(2)}) collective-permute-start(bf16[8,64,128]{2,1,0:T(8,128)(2,1)} %own_ref.1), channel_id=1, source_target_pairs={{4,8},{12,16},{20,24},{8,4},{16,12},{24,20},{5,9},{13,17},{21,25},... | collective-permute-start | bytes 393224 | tf_op jit(solution)/shard_map/ppermute | solution.py:462
  4.4 0.0 copy-done.8
  4.4 0.0 copy-done.7
  4.4 0.0 copy-start.6
  4.4 0.8 %pad_add_fusion.row_ref = s32[16,128]{1,0:T(8,128)S(1)} fusion(s32[2,128]{1,0:T(2,128)S(1)} %copy-done.7, s32[8,128]{1,0:T(8,128)} %param.15, s32[128]{0:T(128)S(1)} %copy-done.8, pred[16]{0:T(512)(128)(4,1)S(1)} %iota_compare_fusion), kind=kLoop, calls=%fused_computation | loop fusion | flops 6144 | bytes 13840 | tf_op jit(solution)/shard_map/add | solution.py:465
  5.2 0.0 copy-done.6
  5.2 0.0 copy-start.2
  5.2 0.9 %copy-done.2 = bf16[8,64,128]{2,1,0:T(8,128)(2,1)S(1)} copy-done((bf16[8,64,128]{2,1,0:T(8,128)(2,1)S(1)}, bf16[8,64,128]{2,1,0:T(8,128)(2,1)}, u32[]{:S(2)}) %copy-start.2) | copy-done | bytes 131096
  6.1 0.7 %order_elements.1 = (s32[8,128]{1,0:T(8,128)S(1)}, f32[8,8,128]{2,1,0:T(8,128)S(1)}, bf16[8,64,128]{2,1,0:T(8,128)(2,1)S(1)}) custom-call(s32[16,128]{1,0:T(8,128)S(1)} %pad_add_fusion.row_ref, f32[3,128]{1,0:T(4,128)S(1)} %copy-done.6, bf16[8,64,128]{2,1,0:T(8,128)(2,1)S(1)} %copy-done.2), custom_call_target="tpu_custom_call" | custom-call | flops 300000 | bytes 262144 | tf_op jit(solution)/shard_map/order_elements/pallas_call | solution.py:466
  6.7 0.7 %collective-permute-done.1.xa_ref.refs_4_ = bf16[8,64,128]{2,1,0:T(8,128)(2,1)S(1)} collective-permute-done((bf16[8,64,128]{2,1,0:T(8,128)(2,1)}, bf16[8,64,128]{2,1,0:T(8,128)(2,1)S(1)}, u32[]{:S(2)}, u32[]{:S(2)}) %collective-permute-start.1) | collective-permute-done | bytes 131104 | tf_op jit(solution)/shard_map/ppermute | solution.py:461
  7.4 0.0 collective-permute-done.xb_ref.refs_2_
  7.4 0.2 pack_halo.1
  7.6 0.7 %collective-permute-start.2 = (bf16[4,192,128]{2,1,0:T(8,128)(2,1)S(1)}, bf16[4,192,128]{2,1,0:T(8,128)(2,1)S(1)}, u32[]{:S(2)}, u32[]{:S(2)}) collective-permute-start(bf16[4,192,128]{2,1,0:T(8,128)(2,1)S(1)} %get-tuple-element.24), channel_id=1, source_target_pairs={{1,2},{2,1},{5,6},{6,5},{9,10},{10,9},{13,14},{14,13},{17,18},{18,... | collective-permute-start | bytes 589832 | tf_op jit(solution)/shard_map/ppermute | solution.py:485
  8.3 3.1 %collective-permute-start.3 = (bf16[4,192,128]{2,1,0:T(8,128)(2,1)S(1)}, bf16[4,192,128]{2,1,0:T(8,128)(2,1)S(1)}, u32[]{:S(2)}, u32[]{:S(2)}) collective-permute-start(bf16[4,192,128]{2,1,0:T(8,128)(2,1)S(1)} %get-tuple-element.25), channel_id=1, source_target_pairs={{0,1},{2,3},{1,0},{3,2},{4,5},{6,7},{5,4},{7,6},{8,9},{10,11},{9,8... | collective-permute-start | bytes 589832 | tf_op jit(solution)/shard_map/ppermute | solution.py:486
  11.4 0.0 copy-start
  11.4 0.0 copy-start.1
  11.4 0.0 copy-start.3
  11.4 2.0 %sample_early.1.refs_7_ = f32[16,11,8,128]{3,2,1,0:T(8,128)S(1)} custom-call(s32[8,128]{1,0:T(8,128)S(1)} %get-tuple-element.21.idx_ref.refs_0_, bf16[8,64,128]{2,1,0:T(8,128)(2,1)S(1)} %collective-permute-done.xb_ref.refs_2_, bf16[8,64,128]{2,1,0:T(8,128)(2,1)S(1)} %get-tuple-element.23.own_ref.refs_3_, ...), custom_call_target="tpu_custom_call" | custom-call | flops 4000000 | bytes 2000000 | tf_op jit(solution)/shard_map/sample_early/pallas_call | solution.py:489
  13.4 0.0 collective-permute-done.2.refs_5_
  13.4 0.0 collective-permute-done.3.refs_6_
  13.4 0.0 copy-done
  13.4 0.0 copy-done.1
  13.4 0.0 copy-done.3
  13.4 0.0 copy-start.4
  13.4 3.0 %sample_and_gradient.1 = (bf16[8,64,128]{2,1,0:T(8,128)(2,1)S(1)}, f32[3,8,8,8,128]{4,3,2,1,0:T(8,128)S(1)}, f32[64,128]{1,0:T(8,128)S(1)}, f32[32,1,128]{2,1,0:T(1,128)S(1)}, f32[8,128]{1,0:T(8,128)S(1)}) custom-call(s32[8,128]{1,0:T(8,128)S(1)} %get-tuple-element.21.idx_ref.refs_0_, f32[8,8,128]{2,1,0:T(8,128)S(1)} %get-tuple-element.22.refs_1_, ...), custom_call_target="tpu_custom_call" | custom-call | tf_op jit(solution)/shard_map/sample_and_gradient/pallas_call | solution.py:499
  16.5 0.0 copy-start.5
  16.5 16.8 %all_to_all.10.refs_0_ = f32[32,1,128]{2,1,0:T(1,128)S(1)} all-to-all(f32[32,1,128]{2,1,0:T(1,128)S(1)} %get-tuple-element.26), channel_id=1, replica_groups=mesh['gx'=8,'gy'=4] {'gx','gy'}, dimensions={0} | all-to-all | bytes 32768 | tf_op jit(solution)/shard_map/all_to_all | solution.py:519
  33.3 0.0 copy-done.4
  33.3 0.0 copy-done.5
  33.3 1.3 %gauss_newton_product.1 = (f32[6,8,128]{2,1,0:T(8,128)S(1)}, f32[6,8,128]{2,1,0:T(8,128)S(1)}, f32[32,1,128]{2,1,0:T(1,128)S(1)}, bf16[8,64,128]{2,1,0:T(8,128)(2,1)}) custom-call(f32[32,1,128]{2,1,0:T(1,128)S(1)} %all_to_all.10.refs_0_, f32[64,128]{1,0:T(8,128)S(1)} %get-tuple-element.27.refs_1_, f32[3,8,8,8,128]{4,3,2,1,0:T(8,128)S(1)} %get-tuple-element.28.refs_2_, ...), custom_call_target="tpu_custom_call" | custom-call | tf_op jit(solution)/shard_map/gauss_newton_product/pallas_call | solution.py:520
  34.6 8.8 %all_to_all.11.refs_0_ = f32[32,1,128]{2,1,0:T(1,128)S(1)} all-to-all(f32[32,1,128]{2,1,0:T(1,128)S(1)} %get-tuple-element.32), channel_id=1, replica_groups=mesh['gx'=8,'gy'=4] {'gx','gy'}, dimensions={0} | all-to-all | bytes 32768 | tf_op jit(solution)/shard_map/all_to_all | solution.py:538
  43.4 0.8 %finish.1 = (f32[3,2,8,16]{3,2,1,0:T(8,128)}, f32[3,2,8,16]{3,2,1,0:T(8,128)}, f32[1,1]{1,0:T(1,128)}) custom-call(f32[32,1,128]{2,1,0:T(1,128)S(1)} %all_to_all.11.refs_0_, f32[6,8,128]{2,1,0:T(8,128)S(1)} %get-tuple-element.33.refs_1_, f32[6,8,128]{2,1,0:T(8,128)S(1)} %get-tuple-element.34.refs_2_), custom_call_target="tpu_custom_call" | custom-call | tf_op jit(solution)/shard_map/finish/pallas_call | solution.py:540
  (1 shorter events, 0.0 us)
Async XLA Ops:
  0.6 3.7 %copy-start.8 = (s32[128]{0:T(128)S(1)}, s32[128]{0:T(128)}, u32[]{:S(2)}) copy-start(s32[128]{0:T(128)} %param.13) | copy-start | bytes 1540
  0.6 3.7 %copy-start.7 = (s32[2,128]{1,0:T(2,128)S(1)}, s32[2,128]{1,0:T(2,128)}, u32[]{:S(2)}) copy-start(s32[2,128]{1,0:T(2,128)} %param.12) | copy-start | bytes 3076
  0.7 6.7 %collective-permute-start.1 = (bf16[8,64,128]{2,1,0:T(8,128)(2,1)}, bf16[8,64,128]{2,1,0:T(8,128)(2,1)S(1)}, u32[]{:S(2)}, u32[]{:S(2)}) collective-permute-start(bf16[8,64,128]{2,1,0:T(8,128)(2,1)} %own_ref.1), channel_id=1, source_target_pairs={{0,4},{8,12},{16,20},{24,28},{4,0},{12,8},{20,16},{28,24},{1,5},{9... | collective-permute-start | bytes 393224 | tf_op jit(solution)/shard_map/ppermute | solution.py:461
  3.7 3.7 %collective-permute-start = (bf16[8,64,128]{2,1,0:T(8,128)(2,1)}, bf16[8,64,128]{2,1,0:T(8,128)(2,1)S(1)}, u32[]{:S(2)}, u32[]{:S(2)}) collective-permute-start(bf16[8,64,128]{2,1,0:T(8,128)(2,1)} %own_ref.1), channel_id=1, source_target_pairs={{4,8},{12,16},{20,24},{8,4},{16,12},{24,20},{5,9},{13,17},{21,25},... | collective-permute-start | bytes 393224 | tf_op jit(solution)/shard_map/ppermute | solution.py:462
  4.4 0.8 %copy-start.6 = (f32[3,128]{1,0:T(4,128)S(1)}, f32[3,128]{1,0:T(4,128)}, u32[]{:S(2)}) copy-start(f32[3,128]{1,0:T(4,128)} %frac_ref.1) | copy-start | bytes 4612
  5.2 0.9 %copy-start.2 = (bf16[8,64,128]{2,1,0:T(8,128)(2,1)S(1)}, bf16[8,64,128]{2,1,0:T(8,128)(2,1)}, u32[]{:S(2)}) copy-start(bf16[8,64,128]{2,1,0:T(8,128)(2,1)} %own_ref.1) | copy-start | bytes 393220
  7.6 5.8 %collective-permute-start.2 = (bf16[4,192,128]{2,1,0:T(8,128)(2,1)S(1)}, bf16[4,192,128]{2,1,0:T(8,128)(2,1)S(1)}, u32[]{:S(2)}, u32[]{:S(2)}) collective-permute-start(bf16[4,192,128]{2,1,0:T(8,128)(2,1)S(1)} %get-tuple-element.24), channel_id=1, source_target_pairs={{1,2},{2,1},{5,6},{6,5},{9,10},{10,9},{13,14},{14,13},{17,18},{18,... | collective-permute-start | bytes 589832 | tf_op jit(solution)/shard_map/ppermute | solution.py:485
  8.3 5.1 %collective-permute-start.3 = (bf16[4,192,128]{2,1,0:T(8,128)(2,1)S(1)}, bf16[4,192,128]{2,1,0:T(8,128)(2,1)S(1)}, u32[]{:S(2)}, u32[]{:S(2)}) collective-permute-start(bf16[4,192,128]{2,1,0:T(8,128)(2,1)S(1)} %get-tuple-element.25), channel_id=1, source_target_pairs={{0,1},{2,3},{1,0},{3,2},{4,5},{6,7},{5,4},{7,6},{8,9},{10,11},{9,8... | collective-permute-start | bytes 589832 | tf_op jit(solution)/shard_map/ppermute | solution.py:486
  11.4 2.0 %copy-start = (bf16[64,384]{1,0:T(8,128)(2,1)S(1)}, bf16[64,384]{1,0:T(8,128)(2,1)}, u32[]{:S(2)}) copy-start(bf16[64,384]{1,0:T(8,128)(2,1)} %constant.12.clone.refs_9_.refs_6_) | copy-start | bytes 147460
  11.4 2.0 %copy-start.1 = (bf16[128,128]{1,0:T(8,128)(2,1)S(1)}, bf16[128,128]{1,0:T(8,128)(2,1)}, u32[]{:S(2)}) copy-start(bf16[128,128]{1,0:T(8,128)(2,1)} %constant.13.clone.refs_10_.refs_7_) | copy-start | bytes 98308
  11.4 2.0 %copy-start.3 = (bf16[8,64,128]{2,1,0:T(8,128)(2,1)S(1)}, bf16[8,64,128]{2,1,0:T(8,128)(2,1)}, u32[]{:S(2)}) copy-start(bf16[8,64,128]{2,1,0:T(8,128)(2,1)} %refs_8_.1) | copy-start | bytes 393220
  13.4 19.9 %copy-start.4 = (bf16[384,64]{1,0:T(8,128)(2,1)S(1)}, bf16[384,64]{1,0:T(8,128)(2,1)}, u32[]{:S(2)}) copy-start(bf16[384,64]{1,0:T(8,128)(2,1)} %constant.14.clone.refs_4_) | copy-start | bytes 147460
  16.5 16.8 %copy-start.5 = (bf16[128,128]{1,0:T(8,128)(2,1)S(1)}, bf16[128,128]{1,0:T(8,128)(2,1)}, u32[]{:S(2)}) copy-start(bf16[128,128]{1,0:T(8,128)(2,1)} %constant.15.clone.refs_5_) | copy-start | bytes 98308

commit v13 on v12

--- a/solution.py
+++ b/solution.py
@@ -34,12 +34,10 @@
         left[48 + kc, kc] = wx[8]
         left[56 + kc, kc] = wx[0]
     left = left.reshape(64, 384)
-    expand = left.T.copy()
-    expand[:, 56:] = 0.0
     wy = np.zeros((128, 128), np.float32)
     wy[:, :17] = node_weights(16).T
     as_bf = lambda a: jnp.asarray(a, BF16)
-    return as_bf(left / 512.0), as_bf(wy), as_bf(expand), as_bf(wy.T)
+    return as_bf(left / 512.0), as_bf(wy), as_bf(wy.T)
 
 
 def split(x):
@@ -301,7 +299,10 @@
             gsc[2 * k + 1, cx] = upper[k]
         return square
 
-    sq_ref[...] = lax.fori_loop(0, 8, interpolate, jnp.zeros((8, 128), F32), unroll=4)
+    square = jnp.zeros((8, 128), F32)
+    for cx in range(8):
+        square = interpolate(cx, square)
+    sq_ref[...] = square
     res_ref[...] = rsc[...].reshape(8, 64, 128).astype(BF16)
     nodes = dot_left(dot_right(left_ref[...], gsc[...].reshape(384, 128)), wy_ref[...])
     node_ref[...] = nodes
@@ -325,7 +326,7 @@
 
 
 def product_kernel(
-    nx, ny, recv_ref, node_ref, slope_ref, sq_ref, expand_ref, wyt_ref, left_ref, wy_ref, res_ref,
+    nx, ny, recv_ref, node_ref, slope_ref, sq_ref, wyt_ref, left_ref, wy_ref, res_ref,
     grad_ref, hess_ref, send_ref, out_ref, msc, gsc, sem,
 ):
     copy_out = pltpu.make_async_copy(res_ref, out_ref, sem)
@@ -372,12 +373,20 @@
     face = face + jnp.where(lane == 16, column(edge_high, 0), 0.0)
     face = jnp.where(sub < 6, face * keep_lane * keep_x, 0.0)
     full = jnp.concatenate(grads + [face, jnp.zeros((8, 128), F32)], axis=0)
-    moved = dot_right(expand_ref[...], dot_left(full, wyt_ref[...]))
-    msc[...] = moved.reshape(6, 8, 8, 128)
+    along_y = dot_left(full, wyt_ref[...])
+    for kc in range(6):
+        msc[kc, 0:8] = along_y[kc * 8 : kc * 8 + 8]
+        msc[kc, 8:9] = along_y[48 + kc : 49 + kc]
+    weight_x = (sub.astype(F32) + 0.5) / 8.0
+
+    def along_x(kc, cx):
+        low = jnp.broadcast_to(msc[kc, cx : cx + 1], (8, 128))
+        high = jnp.broadcast_to(msc[kc, cx + 1 : cx + 2], (8, 128))
+        return low + weight_x * (high - low)
 
     def apply(cx, curve):
-        m0 = [msc[2 * k, cx] for k in range(3)]
-        dm = [msc[2 * k + 1, cx] - m0[k] for k in range(3)]
+        m0 = [along_x(2 * k, cx) for k in range(3)]
+        dm = [along_x(2 * k + 1, cx) - m0[k] for k in range(3)]
         total = [None] * 3
         upper = [None] * 3
         for z in range(8):
@@ -397,7 +406,9 @@
             gsc[2 * k + 1, cx] = upper[k]
         return curve
 
-    curve = lax.fori_loop(0, 8, apply, jnp.zeros((8, 128), F32), unroll=4)
+    curve = jnp.zeros((8, 128), F32)
+    for cx in range(8):
+        curve = apply(cx, curve)
     nodes = dot_left(dot_right(left_ref[...], gsc[...].reshape(384, 128)), wy_ref[...])
     rows = [nodes[kc * 8 : kc * 8 + 8] for kc in range(6)]
     for kc in range(6):
@@ -485,7 +496,7 @@
     yb = lax.ppermute(to_b, "gy", swaps(ny, 1))
     ya = lax.ppermute(to_a, "gy", swaps(ny, 0))
 
-    left, wy, expand, wyt = tables()
+    left, wy, wyt = tables()
     arr = pl.pallas_call(
         early_kernel,
         out_shape=sds((16, 11, 8, 128), F32),
@@ -525,16 +536,16 @@
             sds((peers, 1, 128), F32),
             sds((8, 64, 128), BF16),
         ),
-        in_specs=[VMEM] * 9,
+        in_specs=[VMEM] * 8,
         out_specs=(VMEM,) * 3 + (pl.BlockSpec(memory_space=pl.ANY),),
         scratch_shapes=[
-            pltpu.VMEM((6, 8, 8, 128), F32),
+            pltpu.VMEM((6, 16, 128), F32),
             pltpu.VMEM((6, 8, 8, 128), F32),
             pltpu.SemaphoreType.DMA,
         ],
         compiler_params=PARAMS,
         name="gauss_newton_product",
-    )(recv, nodes, slopes, square, expand, wyt, left, wy, residual)
+    )(recv, nodes, slopes, square, wyt, left, wy, residual)
     recv = lax.all_to_all(send, ("gx", "gy"), 0, 0, tiled=True)
     voxels = 8 * 64 * 128 * peers
     step, product, misfit = pl.pallas_call(

time: 44.5 us -> 44.8 us (level)
    unnamed x18 -> x16, local copies, waits for them, and re-layouts: 0.94 us -> 0.93 us
where the time goes in v13:
time: 44.8 us; the launch traced here: 44.5 us
  blocking collectives  25.9 us (58%)
  Pallas kernels  7.98 us (18%)
  starting transfers between devices  7.49 us (17%)
  local copies, waits for them, and re-layouts  0.93 us (2%)
  other arithmetic  0.77 us (2%)
  between operations  0.77 us (2%)
  waiting for transfers between devices  0.67 us (1%)
    all_to_all x2, blocking collectives, on_device(): recv = lax.all_to_all(send, ('gx', 'gy'), 0, 0, tiled=True)  25.9 us
    ppermute x1, starting transfers between devices, on_device(): ya = lax.ppermute(to_a, 'gy', swaps(ny, 0))  3.13 us
    pallas_call x1, Pallas kernels, on_device(): pl.pallas_call(lambda *refs: late_kernel(nx, ny, *refs), out_shape=(sds((...  3.09 us
    ppermute x1, starting transfers between devices, on_device(): xa = lax.ppermute(def_image, 'gx', swaps(nx, 0))  3.03 us
    pallas_call x1, Pallas kernels, on_device(): pl.pallas_call(early_kernel, out_shape=sds((16, 11, 8, 128), F32), in_spe...  1.96 us
    pallas_call x1, Pallas kernels, on_device(): pl.pallas_call(lambda *refs: product_kernel(nx, ny, *refs), out_shape=(sd...  1.31 us
    unnamed x16, local copies, waits for them, and re-layouts  0.93 us
  transfers between devices with their start and end apart: 4, of which 1 were waited for; matrix products, arithmetic and copies ran while one was open for 2% of the time, Pallas kernels for 6%

profile of v13, /device:TPU:0, one launch (start us, length us, event | category | flops | bytes accessed | tf_op | source)
XLA Modules:
  0.0 44.5 jit_solution(8848870569923271367)
XLA Ops:
  0.6 0.0 copy-start.7
  0.6 0.0 copy-start.6
  0.7 3.0 %collective-permute-start.1 = (bf16[8,64,128]{2,1,0:T(8,128)(2,1)}, bf16[8,64,128]{2,1,0:T(8,128)(2,1)S(1)}, u32[]{:S(2)}, u32[]{:S(2)}) collective-permute-start(bf16[8,64,128]{2,1,0:T(8,128)(2,1)} %own_ref.1), channel_id=1, source_target_pairs={{0,4},{8,12},{16,20},{24,28},{4,0},{12,8},{20,16},{28,24},{1,5},{9... | collective-permute-start | bytes 393224 | tf_op jit(solution)/shard_map/ppermute | solution.py:472
  3.7 0.7 %collective-permute-start = (bf16[8,64,128]{2,1,0:T(8,128)(2,1)}, bf16[8,64,128]{2,1,0:T(8,128)(2,1)S(1)}, u32[]{:S(2)}, u32[]{:S(2)}) collective-permute-start(bf16[8,64,128]{2,1,0:T(8,128)(2,1)} %own_ref.1), channel_id=1, source_target_pairs={{4,8},{12,16},{20,24},{8,4},{16,12},{24,20},{5,9},{13,17},{21,25},... | collective-permute-start | bytes 393224 | tf_op jit(solution)/shard_map/ppermute | solution.py:473
  4.4 0.0 copy-done.7
  4.4 0.0 copy-done.6
  4.4 0.0 copy-start.5
  4.4 0.8 %pad_add_fusion.row_ref = s32[16,128]{1,0:T(8,128)S(1)} fusion(s32[2,128]{1,0:T(2,128)S(1)} %copy-done.6, s32[8,128]{1,0:T(8,128)} %param.14, s32[128]{0:T(128)S(1)} %copy-done.7, pred[16]{0:T(512)(128)(4,1)S(1)} %iota_compare_fusion), kind=kLoop, calls=%fused_computation | loop fusion | flops 6144 | bytes 13840 | tf_op jit(solution)/shard_map/add | solution.py:476
  5.2 0.0 copy-done.5
  5.2 0.0 copy-start.2
  5.2 0.9 %copy-done.2 = bf16[8,64,128]{2,1,0:T(8,128)(2,1)S(1)} copy-done((bf16[8,64,128]{2,1,0:T(8,128)(2,1)S(1)}, bf16[8,64,128]{2,1,0:T(8,128)(2,1)}, u32[]{:S(2)}) %copy-start.2) | copy-done | bytes 131096
  6.1 0.7 %order_elements.1 = (s32[8,128]{1,0:T(8,128)S(1)}, f32[8,8,128]{2,1,0:T(8,128)S(1)}, bf16[8,64,128]{2,1,0:T(8,128)(2,1)S(1)}) custom-call(s32[16,128]{1,0:T(8,128)S(1)} %pad_add_fusion.row_ref, f32[3,128]{1,0:T(4,128)S(1)} %copy-done.5, bf16[8,64,128]{2,1,0:T(8,128)(2,1)S(1)} %copy-done.2), custom_call_target="tpu_custom_call" | custom-call | flops 300000 | bytes 262144 | tf_op jit(solution)/shard_map/order_elements/pallas_call | solution.py:477
  6.7 0.7 %collective-permute-done.1.xa_ref.refs_4_ = bf16[8,64,128]{2,1,0:T(8,128)(2,1)S(1)} collective-permute-done((bf16[8,64,128]{2,1,0:T(8,128)(2,1)}, bf16[8,64,128]{2,1,0:T(8,128)(2,1)S(1)}, u32[]{:S(2)}, u32[]{:S(2)}) %collective-permute-start.1) | collective-permute-done | bytes 131104 | tf_op jit(solution)/shard_map/ppermute | solution.py:472
  7.4 0.0 collective-permute-done.xb_ref.refs_2_
  7.4 0.2 pack_halo.1
  7.6 0.7 %collective-permute-start.2 = (bf16[4,192,128]{2,1,0:T(8,128)(2,1)S(1)}, bf16[4,192,128]{2,1,0:T(8,128)(2,1)S(1)}, u32[]{:S(2)}, u32[]{:S(2)}) collective-permute-start(bf16[4,192,128]{2,1,0:T(8,128)(2,1)S(1)} %get-tuple-element.24), channel_id=1, source_target_pairs={{1,2},{2,1},{5,6},{6,5},{9,10},{10,9},{13,14},{14,13},{17,18},{18,... | collective-permute-start | bytes 589832 | tf_op jit(solution)/shard_map/ppermute | solution.py:496
  8.3 3.1 %collective-permute-start.3 = (bf16[4,192,128]{2,1,0:T(8,128)(2,1)S(1)}, bf16[4,192,128]{2,1,0:T(8,128)(2,1)S(1)}, u32[]{:S(2)}, u32[]{:S(2)}) collective-permute-start(bf16[4,192,128]{2,1,0:T(8,128)(2,1)S(1)} %get-tuple-element.25), channel_id=1, source_target_pairs={{0,1},{2,3},{1,0},{3,2},{4,5},{6,7},{5,4},{7,6},{8,9},{10,11},{9,8... | collective-permute-start | bytes 589832 | tf_op jit(solution)/shard_map/ppermute | solution.py:497
  11.4 0.0 copy-start
  11.4 0.0 copy-start.1
  11.4 0.0 copy-start.3
  11.4 2.0 %sample_early.1.refs_7_ = f32[16,11,8,128]{3,2,1,0:T(8,128)S(1)} custom-call(s32[8,128]{1,0:T(8,128)S(1)} %get-tuple-element.21.idx_ref.refs_0_, bf16[8,64,128]{2,1,0:T(8,128)(2,1)S(1)} %collective-permute-done.xb_ref.refs_2_, bf16[8,64,128]{2,1,0:T(8,128)(2,1)S(1)} %get-tuple-element.23.own_ref.refs_3_, ...), custom_call_target="tpu_custom_call" | custom-call | flops 4000000 | bytes 2000000 | tf_op jit(solution)/shard_map/sample_early/pallas_call | solution.py:500
  13.4 0.0 collective-permute-done.2.refs_5_
  13.4 0.0 collective-permute-done.3.refs_6_
  13.4 0.0 copy-done
  13.4 0.0 copy-done.1
  13.4 0.0 copy-done.3
  13.4 3.1 %sample_and_gradient.1 = (bf16[8,64,128]{2,1,0:T(8,128)(2,1)S(1)}, f32[3,8,8,8,128]{4,3,2,1,0:T(8,128)S(1)}, f32[64,128]{1,0:T(8,128)S(1)}, f32[32,1,128]{2,1,0:T(1,128)S(1)}, f32[8,128]{1,0:T(8,128)S(1)}) custom-call(s32[8,128]{1,0:T(8,128)S(1)} %get-tuple-element.21.idx_ref.refs_0_, f32[8,8,128]{2,1,0:T(8,128)S(1)} %get-tuple-element.22.refs_1_, ...), custom_call_target="tpu_custom_call" | custom-call | tf_op jit(solution)/shard_map/sample_and_gradient/pallas_call | solution.py:510
  16.5 0.0 copy-start.4
  16.5 17.0 %all_to_all.10.refs_0_ = f32[32,1,128]{2,1,0:T(1,128)S(1)} all-to-all(f32[32,1,128]{2,1,0:T(1,128)S(1)} %get-tuple-element.26), channel_id=1, replica_groups=mesh['gx'=8,'gy'=4] {'gx','gy'}, dimensions={0} | all-to-all | bytes 32768 | tf_op jit(solution)/shard_map/all_to_all | solution.py:530
  33.6 0.0 copy-done.4
  33.6 1.3 %gauss_newton_product.1 = (f32[6,8,128]{2,1,0:T(8,128)S(1)}, f32[6,8,128]{2,1,0:T(8,128)S(1)}, f32[32,1,128]{2,1,0:T(1,128)S(1)}, bf16[8,64,128]{2,1,0:T(8,128)(2,1)}) custom-call(f32[32,1,128]{2,1,0:T(1,128)S(1)} %all_to_all.10.refs_0_, f32[64,128]{1,0:T(8,128)S(1)} %get-tuple-element.27.refs_1_, f32[3,8,8,8,128]{4,3,2,1,0:T(8,128)S(1)} %get-tuple-element.28.refs_2_, ...), custom_call_target="tpu_custom_call" | custom-call | tf_op jit(solution)/shard_map/gauss_newton_product/pallas_call | solution.py:531
  34.9 8.8 %all_to_all.11.refs_0_ = f32[32,1,128]{2,1,0:T(1,128)S(1)} all-to-all(f32[32,1,128]{2,1,0:T(1,128)S(1)} %get-tuple-element.32), channel_id=1, replica_groups=mesh['gx'=8,'gy'=4] {'gx','gy'}, dimensions={0} | all-to-all | bytes 32768 | tf_op jit(solution)/shard_map/all_to_all | solution.py:549
  43.7 0.8 %finish.1 = (f32[3,2,8,16]{3,2,1,0:T(8,128)}, f32[3,2,8,16]{3,2,1,0:T(8,128)}, f32[1,1]{1,0:T(1,128)}) custom-call(f32[32,1,128]{2,1,0:T(1,128)S(1)} %all_to_all.11.refs_0_, f32[6,8,128]{2,1,0:T(8,128)S(1)} %get-tuple-element.33.refs_1_, f32[6,8,128]{2,1,0:T(8,128)S(1)} %get-tuple-element.34.refs_2_), custom_call_target="tpu_custom_call" | custom-call | tf_op jit(solution)/shard_map/finish/pallas_call | solution.py:551
  (1 shorter events, 0.0 us)
Async XLA Ops:
  0.6 3.7 %copy-start.7 = (s32[128]{0:T(128)S(1)}, s32[128]{0:T(128)}, u32[]{:S(2)}) copy-start(s32[128]{0:T(128)} %param.12) | copy-start | bytes 1540
  0.6 3.7 %copy-start.6 = (s32[2,128]{1,0:T(2,128)S(1)}, s32[2,128]{1,0:T(2,128)}, u32[]{:S(2)}) copy-start(s32[2,128]{1,0:T(2,128)} %param.11) | copy-start | bytes 3076
  0.7 6.7 %collective-permute-start.1 = (bf16[8,64,128]{2,1,0:T(8,128)(2,1)}, bf16[8,64,128]{2,1,0:T(8,128)(2,1)S(1)}, u32[]{:S(2)}, u32[]{:S(2)}) collective-permute-start(bf16[8,64,128]{2,1,0:T(8,128)(2,1)} %own_ref.1), channel_id=1, source_target_pairs={{0,4},{8,12},{16,20},{24,28},{4,0},{12,8},{20,16},{28,24},{1,5},{9... | collective-permute-start | bytes 393224 | tf_op jit(solution)/shard_map/ppermute | solution.py:472
  3.7 3.7 %collective-permute-start = (bf16[8,64,128]{2,1,0:T(8,128)(2,1)}, bf16[8,64,128]{2,1,0:T(8,128)(2,1)S(1)}, u32[]{:S(2)}, u32[]{:S(2)}) collective-permute-start(bf16[8,64,128]{2,1,0:T(8,128)(2,1)} %own_ref.1), channel_id=1, source_target_pairs={{4,8},{12,16},{20,24},{8,4},{16,12},{24,20},{5,9},{13,17},{21,25},... | collective-permute-start | bytes 393224 | tf_op jit(solution)/shard_map/ppermute | solution.py:473
  4.4 0.8 %copy-start.5 = (f32[3,128]{1,0:T(4,128)S(1)}, f32[3,128]{1,0:T(4,128)}, u32[]{:S(2)}) copy-start(f32[3,128]{1,0:T(4,128)} %frac_ref.1) | copy-start | bytes 4612
  5.2 0.9 %copy-start.2 = (bf16[8,64,128]{2,1,0:T(8,128)(2,1)S(1)}, bf16[8,64,128]{2,1,0:T(8,128)(2,1)}, u32[]{:S(2)}) copy-start(bf16[8,64,128]{2,1,0:T(8,128)(2,1)} %own_ref.1) | copy-start | bytes 393220
  7.6 5.8 %collective-permute-start.2 = (bf16[4,192,128]{2,1,0:T(8,128)(2,1)S(1)}, bf16[4,192,128]{2,1,0:T(8,128)(2,1)S(1)}, u32[]{:S(2)}, u32[]{:S(2)}) collective-permute-start(bf16[4,192,128]{2,1,0:T(8,128)(2,1)S(1)} %get-tuple-element.24), channel_id=1, source_target_pairs={{1,2},{2,1},{5,6},{6,5},{9,10},{10,9},{13,14},{14,13},{17,18},{18,... | collective-permute-start | bytes 589832 | tf_op jit(solution)/shard_map/ppermute | solution.py:496
  8.3 5.1 %collective-permute-start.3 = (bf16[4,192,128]{2,1,0:T(8,128)(2,1)S(1)}, bf16[4,192,128]{2,1,0:T(8,128)(2,1)S(1)}, u32[]{:S(2)}, u32[]{:S(2)}) collective-permute-start(bf16[4,192,128]{2,1,0:T(8,128)(2,1)S(1)} %get-tuple-element.25), channel_id=1, source_target_pairs={{0,1},{2,3},{1,0},{3,2},{4,5},{6,7},{5,4},{7,6},{8,9},{10,11},{9,8... | collective-permute-start | bytes 589832 | tf_op jit(solution)/shard_map/ppermute | solution.py:497
  11.4 2.0 %copy-start = (bf16[64,384]{1,0:T(8,128)(2,1)S(1)}, bf16[64,384]{1,0:T(8,128)(2,1)}, u32[]{:S(2)}) copy-start(bf16[64,384]{1,0:T(8,128)(2,1)} %constant.10.clone.refs_9_.refs_5_) | copy-start | bytes 147460
  11.4 2.0 %copy-start.1 = (bf16[128,128]{1,0:T(8,128)(2,1)S(1)}, bf16[128,128]{1,0:T(8,128)(2,1)}, u32[]{:S(2)}) copy-start(bf16[128,128]{1,0:T(8,128)(2,1)} %constant.11.clone.refs_10_.refs_6_) | copy-start | bytes 98308
  11.4 2.0 %copy-start.3 = (bf16[8,64,128]{2,1,0:T(8,128)(2,1)S(1)}, bf16[8,64,128]{2,1,0:T(8,128)(2,1)}, u32[]{:S(2)}) copy-start(bf16[8,64,128]{2,1,0:T(8,128)(2,1)} %refs_8_.1) | copy-start | bytes 393220
  16.5 17.1 %copy-start.4 = (bf16[128,128]{1,0:T(8,128)(2,1)S(1)}, bf16[128,128]{1,0:T(8,128)(2,1)}, u32[]{:S(2)}) copy-start(bf16[128,128]{1,0:T(8,128)(2,1)} %constant.12.clone.refs_4_) | copy-start | bytes 98308

commit v14 on v12

--- a/solution.py
+++ b/solution.py
@@ -120,10 +120,14 @@
         wgt_ref[cx] = dot_rows(hi, spread) + dot_rows(lo, spread) + dot_rows(rest, spread)
 
 
-def pack_kernel(xb_ref, own_ref, xa_ref, b_ref, a_ref):
+def pack_first_kernel(xa_ref, own_ref, b_ref, a_ref):
     even = lax.axis_index("gy") % 2 == 0
-    for n, ref in enumerate((xa_ref, own_ref, xb_ref)):
-        pack_rows(ref, a_ref, b_ref, 64 * n, even)
+    pack_rows(xa_ref, a_ref, b_ref, 0, even)
+    pack_rows(own_ref, a_ref, b_ref, 64, even)
+
+
+def pack_second_kernel(xb_ref, after_ref, b_ref, a_ref):
+    pack_rows(xb_ref, a_ref, b_ref, 0, lax.axis_index("gy") % 2 == 0)
 
 
 def over_sublanes(x):
@@ -202,7 +206,7 @@
 
 
 def late_kernel(
-    nx, ny, idx_ref, wgt, xb_ref, own_ref, xa_ref, yb_ref, ya_ref, arr_ref, ref_ref,
+    nx, ny, idx_ref, wgt, xb_ref, own_ref, xa_ref, yb_ref, ya_ref, yd_ref, yc_ref, arr_ref, ref_ref,
     left_ref, wy_ref, res_ref, slope_ref, node_ref, send_ref, sq_ref, img, arr, rsc, gsc,
 ):
     half = lax.broadcasted_iota(jnp.int32, (64, 128), 1) < 64
@@ -210,16 +214,16 @@
     odd_y = lax.axis_index("gy") % 2 == 1
     at_a = place_of_a()
     segments = (
-        (xa_ref, 0, at_a),
-        (own_ref, 64, 64),
-        (xb_ref, 128, 128 - at_a),
+        (xa_ref, ya_ref, yb_ref, 0, at_a),
+        (own_ref, ya_ref, yb_ref, 64, 64),
+        (xb_ref, yc_ref, yd_ref, 0, 128 - at_a),
     )
     for p in range(4):
-        for ref, at, row in segments:
+        for ref, pair_a, pair_b, at, row in segments:
             ra = pltpu.roll(ref[p].astype(F32), 64, 1)
             rc = pltpu.roll(ref[p + 4].astype(F32), 64, 1)
-            from_a = ya_ref[p, pl.ds(at, 64)].astype(F32)
-            from_b = yb_ref[p, pl.ds(at, 64)].astype(F32)
+            from_a = pair_a[p, pl.ds(at, 64)].astype(F32)
+            from_b = pair_b[p, pl.ds(at, 64)].astype(F32)
             lo = jnp.where(odd_y, from_a, from_b)
             hi = jnp.where(odd_y, from_b, from_a)
             at_row = lambda k, q: pl.ds(pl.multiple_of(k * TILE_ROWS + (q + 2) * SPAN + row, 8), 64)
@@ -472,18 +476,30 @@
         cost_estimate=pl.CostEstimate(flops=300000, bytes_accessed=262144, transcendentals=0),
         name="order_elements",
     )(table, frac, def_image)
-    packed = sds((4, SPAN, 128), BF16)
+    packed = sds((4, 128, 128), BF16)
     to_b, to_a = pl.pallas_call(
-        pack_kernel,
+        pack_first_kernel,
         out_shape=(packed, packed),
-        in_specs=[VMEM] * 3,
+        in_specs=[VMEM] * 2,
         out_specs=(VMEM, VMEM),
         compiler_params=PARAMS,
         cost_estimate=pl.CostEstimate(flops=300000, bytes_accessed=524288, transcendentals=0),
-        name="pack_halo",
-    )(xb, own, xa)
+        name="pack_first_halo",
+    )(xa, own)
     yb = lax.ppermute(to_b, "gy", swaps(ny, 1))
     ya = lax.ppermute(to_a, "gy", swaps(ny, 0))
+    packed = sds((4, 64, 128), BF16)
+    to_d, to_c = pl.pallas_call(
+        pack_second_kernel,
+        out_shape=(packed, packed),
+        in_specs=[VMEM, pl.BlockSpec(memory_space=pl.ANY)],
+        out_specs=(VMEM, VMEM),
+        compiler_params=PARAMS,
+        cost_estimate=pl.CostEstimate(flops=300000, bytes_accessed=524288, transcendentals=0),
+        name="pack_second_halo",
+    )(xb, to_a)
+    yd = lax.ppermute(to_d, "gy", swaps(ny, 1))
+    yc = lax.ppermute(to_c, "gy", swaps(ny, 0))
 
     left, wy, expand, wyt = tables()
     arr = pl.pallas_call(
@@ -505,7 +521,7 @@
             sds((peers, 1, 128), F32),
             sds((8, 128), F32),
         ),
-        in_specs=[SMEM] + [VMEM] * 10,
+        in_specs=[SMEM] + [VMEM] * 12,
         out_specs=(VMEM,) * 5,
         scratch_shapes=[
             pltpu.VMEM((2 * TILE_ROWS + 8, 128), F32),
@@ -515,7 +531,7 @@
         ],
         compiler_params=PARAMS,
         name="sample_and_gradient",
-    )(idx, wgt, xb, own, xa, yb, ya, arr, ref_image, left, wy)
+    )(idx, wgt, xb, own, xa, yb, ya, yd, yc, arr, ref_image, left, wy)
     recv = lax.all_to_all(send, ("gx", "gy"), 0, 0, tiled=True)
     grads, hess, send, residual = pl.pallas_call(
         lambda *refs: product_kernel(nx, ny, *refs),

time: 44.5 us -> 43.8 us (0.984)
  blocking collectives: 25.7 us -> 22.8 us
  starting transfers between devices: 7.49 us -> 9.49 us
    all_to_all x2, blocking collectives: 25.7 us -> 22.8 us  [on_device(): recv = lax.all_to_all(send, ('gx', 'gy'), 0, 0, tiled=True)]
    ppermute x0 -> x2, starting transfers between devices: none -> 2.01 us  [the longest x1 1.34 us: on_device(): yc = lax.ppermute(to_c, 'gy', swaps(ny, 0))]
  transfers between devices with their start and end apart: 4 -> 6, of which waited for: 1 -> 1; matrix products, arithmetic and copies ran while one was open for 2% -> 2% of each run, Pallas kernels for 6% -> 7%
where the time goes in v14:
time: 43.8 us; the launch traced here: 43.5 us
  blocking collectives  22.8 us (52%)
  starting transfers between devices  9.49 us (22%)
  Pallas kernels  7.95 us (18%)
  local copies, waits for them, and re-layouts  0.94 us (2%)
  between operations  0.81 us (2%)
  other arithmetic  0.77 us (2%)
  waiting for transfers between devices  0.68 us (2%)
    all_to_all x2, blocking collectives, on_device(): recv = lax.all_to_all(send, ('gx', 'gy'), 0, 0, tiled=True)  22.8 us
    ppermute x1, starting transfers between devices, on_device(): ya = lax.ppermute(to_a, 'gy', swaps(ny, 0))  3.13 us
    pallas_call x1, Pallas kernels, on_device(): pl.pallas_call(lambda *refs: late_kernel(nx, ny, *refs), out_shape=(sds((...  3.03 us
    ppermute x1, starting transfers between devices, on_device(): xa = lax.ppermute(def_image, 'gx', swaps(nx, 0))  3.03 us
    pallas_call x1, Pallas kernels, on_device(): pl.pallas_call(early_kernel, out_shape=sds((16, 11, 8, 128), F32), in_spe...  1.96 us
    ppermute x1, starting transfers between devices, on_device(): yc = lax.ppermute(to_c, 'gy', swaps(ny, 0))  1.34 us
    pallas_call x1, Pallas kernels, on_device(): pl.pallas_call(lambda *refs: product_kernel(nx, ny, *refs), out_shape=(sd...  1.26 us
    unnamed x18, local copies, waits for them, and re-layouts  0.94 us
  transfers between devices with their start and end apart: 6, of which 1 were waited for; matrix products, arithmetic and copies ran while one was open for 2% of the time, Pallas kernels for 7%

profile of v14, /device:TPU:0, one launch (start us, length us, event | category | flops | bytes accessed | tf_op | source)
XLA Modules:
  0.0 43.5 jit_solution(11875520451266559336)
XLA Ops:
  0.6 0.0 copy-start.8
  0.6 0.0 copy-start.7
  0.7 3.0 %collective-permute-start.1 = (bf16[8,64,128]{2,1,0:T(8,128)(2,1)}, bf16[8,64,128]{2,1,0:T(8,128)(2,1)S(1)}, u32[]{:S(2)}, u32[]{:S(2)}) collective-permute-start(bf16[8,64,128]{2,1,0:T(8,128)(2,1)} %own_ref.1), channel_id=1, source_target_pairs={{0,4},{8,12},{16,20},{24,28},{4,0},{12,8},{20,16},{28,24},{1,5},{9... | collective-permute-start | bytes 393224 | tf_op jit(solution)/shard_map/ppermute | solution.py:465
  3.7 0.7 %collective-permute-start = (bf16[8,64,128]{2,1,0:T(8,128)(2,1)}, bf16[8,64,128]{2,1,0:T(8,128)(2,1)S(1)}, u32[]{:S(2)}, u32[]{:S(2)}) collective-permute-start(bf16[8,64,128]{2,1,0:T(8,128)(2,1)} %own_ref.1), channel_id=1, source_target_pairs={{4,8},{12,16},{20,24},{8,4},{16,12},{24,20},{5,9},{13,17},{21,25},... | collective-permute-start | bytes 393224 | tf_op jit(solution)/shard_map/ppermute | solution.py:466
  4.4 0.0 copy-done.8
  4.4 0.0 copy-done.7
  4.4 0.0 copy-start.6
  4.4 0.8 %pad_add_fusion.row_ref = s32[16,128]{1,0:T(8,128)S(1)} fusion(s32[2,128]{1,0:T(2,128)S(1)} %copy-done.7, s32[8,128]{1,0:T(8,128)} %param.15, s32[128]{0:T(128)S(1)} %copy-done.8, pred[16]{0:T(512)(128)(4,1)S(1)} %iota_compare_fusion), kind=kLoop, calls=%fused_computation | loop fusion | flops 6144 | bytes 13840 | tf_op jit(solution)/shard_map/add | solution.py:469
  5.2 0.0 copy-done.6
  5.2 0.0 copy-start.2
  5.2 0.9 %copy-done.2 = bf16[8,64,128]{2,1,0:T(8,128)(2,1)S(1)} copy-done((bf16[8,64,128]{2,1,0:T(8,128)(2,1)S(1)}, bf16[8,64,128]{2,1,0:T(8,128)(2,1)}, u32[]{:S(2)}) %copy-start.2) | copy-done | bytes 131096
  6.1 0.7 %order_elements.1 = (s32[8,128]{1,0:T(8,128)S(1)}, f32[8,8,128]{2,1,0:T(8,128)S(1)}, bf16[8,64,128]{2,1,0:T(8,128)(2,1)S(1)}) custom-call(s32[16,128]{1,0:T(8,128)S(1)} %pad_add_fusion.row_ref, f32[3,128]{1,0:T(4,128)S(1)} %copy-done.6, bf16[8,64,128]{2,1,0:T(8,128)(2,1)S(1)} %copy-done.2), custom_call_target="tpu_custom_call" | custom-call | flops 300000 | bytes 262144 | tf_op jit(solution)/shard_map/order_elements/pallas_call | solution.py:470
  6.7 0.7 %collective-permute-done.1.xa_ref.refs_4_ = bf16[8,64,128]{2,1,0:T(8,128)(2,1)S(1)} collective-permute-done((bf16[8,64,128]{2,1,0:T(8,128)(2,1)}, bf16[8,64,128]{2,1,0:T(8,128)(2,1)S(1)}, u32[]{:S(2)}, u32[]{:S(2)}) %collective-permute-start.1) | collective-permute-done | bytes 131104 | tf_op jit(solution)/shard_map/ppermute | solution.py:465
  7.4 0.1 pack_first_halo.1
  7.5 0.7 %collective-permute-start.2 = (bf16[4,128,128]{2,1,0:T(8,128)(2,1)S(1)}, bf16[4,128,128]{2,1,0:T(8,128)(2,1)S(1)}, u32[]{:S(2)}, u32[]{:S(2)}) collective-permute-start(bf16[4,128,128]{2,1,0:T(8,128)(2,1)S(1)} %get-tuple-element.26), channel_id=1, source_target_pairs={{1,2},{2,1},{5,6},{6,5},{9,10},{10,9},{13,14},{14,13},{17,18},{18,... | collective-permute-start | bytes 393224 | tf_op jit(solution)/shard_map/ppermute | solution.py:489
  8.2 3.1 %collective-permute-start.3 = (bf16[4,128,128]{2,1,0:T(8,128)(2,1)S(1)}, bf16[4,128,128]{2,1,0:T(8,128)(2,1)S(1)}, u32[]{:S(2)}, u32[]{:S(2)}) collective-permute-start(bf16[4,128,128]{2,1,0:T(8,128)(2,1)S(1)} %get-tuple-element.27.after_ref), channel_id=1, source_target_pairs={{0,1},{2,3},{1,0},{3,2},{4,5},{6,7},{5,4},{7,6},{8,9},{10,11},{9,8... | collective-permute-start | bytes 393224 | tf_op jit(solution)/shard_map/ppermute | solution.py:490
  11.4 0.0 collective-permute-done.xb_ref.refs_2_
  11.4 0.1 pack_second_halo.1
  11.5 0.7 %collective-permute-start.4 = (bf16[4,64,128]{2,1,0:T(8,128)(2,1)S(1)}, bf16[4,64,128]{2,1,0:T(8,128)(2,1)S(1)}, u32[]{:S(2)}, u32[]{:S(2)}) collective-permute-start(bf16[4,64,128]{2,1,0:T(8,128)(2,1)S(1)} %get-tuple-element.28), channel_id=1, source_target_pairs={{1,2},{2,1},{5,6},{6,5},{9,10},{10,9},{13,14},{14,13},{17,18},{18,... | collective-permute-start | bytes 196616 | tf_op jit(solution)/shard_map/ppermute | solution.py:501
  12.1 1.3 %collective-permute-start.5 = (bf16[4,64,128]{2,1,0:T(8,128)(2,1)S(1)}, bf16[4,64,128]{2,1,0:T(8,128)(2,1)S(1)}, u32[]{:S(2)}, u32[]{:S(2)}) collective-permute-start(bf16[4,64,128]{2,1,0:T(8,128)(2,1)S(1)} %get-tuple-element.29), channel_id=1, source_target_pairs={{0,1},{2,3},{1,0},{3,2},{4,5},{6,7},{5,4},{7,6},{8,9},{10,11},{9,8... | collective-permute-start | bytes 196616 | tf_op jit(solution)/shard_map/ppermute | solution.py:502
  13.5 0.0 copy-start
  13.5 0.0 copy-start.1
  13.5 0.0 copy-start.3
  13.5 2.0 %sample_early.1.refs_9_ = f32[16,11,8,128]{3,2,1,0:T(8,128)S(1)} custom-call(s32[8,128]{1,0:T(8,128)S(1)} %get-tuple-element.23.idx_ref.refs_0_, bf16[8,64,128]{2,1,0:T(8,128)(2,1)S(1)} %collective-permute-done.xb_ref.refs_2_, bf16[8,64,128]{2,1,0:T(8,128)(2,1)S(1)} %get-tuple-element.25.own_ref.refs_3_, ...), custom_call_target="tpu_custom_call" | custom-call | flops 4000000 | bytes 2000000 | tf_op jit(solution)/shard_map/sample_early/pallas_call | solution.py:505
  15.5 0.0 collective-permute-done.4.refs_7_
  15.5 0.0 collective-permute-done.5.refs_8_
  15.5 0.0 collective-permute-done.2.refs_5_
  15.5 0.0 collective-permute-done.3.refs_6_
  15.5 0.0 copy-done
  15.5 0.0 copy-done.1
  15.5 0.0 copy-done.3
  15.5 0.0 copy-start.4
  15.5 3.0 %sample_and_gradient.1 = (bf16[8,64,128]{2,1,0:T(8,128)(2,1)S(1)}, f32[3,8,8,8,128]{4,3,2,1,0:T(8,128)S(1)}, f32[64,128]{1,0:T(8,128)S(1)}, f32[32,1,128]{2,1,0:T(1,128)S(1)}, f32[8,128]{1,0:T(8,128)S(1)}) custom-call(s32[8,128]{1,0:T(8,128)S(1)} %get-tuple-element.23.idx_ref.refs_0_, f32[8,8,128]{2,1,0:T(8,128)S(1)} %get-tuple-element.24.refs_1_, ...), custom_call_target="tpu_custom_call" | custom-call | tf_op jit(solution)/shard_map/sample_and_gradient/pallas_call | solution.py:515
  18.6 0.0 copy-start.5
  18.6 14.0 %all_to_all.10.refs_0_ = f32[32,1,128]{2,1,0:T(1,128)S(1)} all-to-all(f32[32,1,128]{2,1,0:T(1,128)S(1)} %get-tuple-element.30), channel_id=1, replica_groups=mesh['gx'=8,'gy'=4] {'gx','gy'}, dimensions={0} | all-to-all | bytes 32768 | tf_op jit(solution)/shard_map/all_to_all | solution.py:535
  32.6 0.0 copy-done.4
  32.6 0.0 copy-done.5
  32.6 1.3 %gauss_newton_product.1 = (f32[6,8,128]{2,1,0:T(8,128)S(1)}, f32[6,8,128]{2,1,0:T(8,128)S(1)}, f32[32,1,128]{2,1,0:T(1,128)S(1)}, bf16[8,64,128]{2,1,0:T(8,128)(2,1)}) custom-call(f32[32,1,128]{2,1,0:T(1,128)S(1)} %all_to_all.10.refs_0_, f32[64,128]{1,0:T(8,128)S(1)} %get-tuple-element.31.refs_1_, f32[3,8,8,8,128]{4,3,2,1,0:T(8,128)S(1)} %get-tuple-element.32.refs_2_, ...), custom_call_target="tpu_custom_call" | custom-call | tf_op jit(solution)/shard_map/gauss_newton_product/pallas_call | solution.py:536
  33.8 8.8 %all_to_all.11.refs_0_ = f32[32,1,128]{2,1,0:T(1,128)S(1)} all-to-all(f32[32,1,128]{2,1,0:T(1,128)S(1)} %get-tuple-element.36), channel_id=1, replica_groups=mesh['gx'=8,'gy'=4] {'gx','gy'}, dimensions={0} | all-to-all | bytes 32768 | tf_op jit(solution)/shard_map/all_to_all | solution.py:554
  42.7 0.8 %finish.1 = (f32[3,2,8,16]{3,2,1,0:T(8,128)}, f32[3,2,8,16]{3,2,1,0:T(8,128)}, f32[1,1]{1,0:T(1,128)}) custom-call(f32[32,1,128]{2,1,0:T(1,128)S(1)} %all_to_all.11.refs_0_, f32[6,8,128]{2,1,0:T(8,128)S(1)} %get-tuple-element.37.refs_1_, f32[6,8,128]{2,1,0:T(8,128)S(1)} %get-tuple-element.38.refs_2_), custom_call_target="tpu_custom_call" | custom-call | tf_op jit(solution)/shard_map/finish/pallas_call | solution.py:556
  (1 shorter events, 0.0 us)
Async XLA Ops:
  0.6 3.7 %copy-start.8 = (s32[128]{0:T(128)S(1)}, s32[128]{0:T(128)}, u32[]{:S(2)}) copy-start(s32[128]{0:T(128)} %param.13) | copy-start | bytes 1540
  0.6 3.7 %copy-start.7 = (s32[2,128]{1,0:T(2,128)S(1)}, s32[2,128]{1,0:T(2,128)}, u32[]{:S(2)}) copy-start(s32[2,128]{1,0:T(2,128)} %param.12) | copy-start | bytes 3076
  0.7 6.7 %collective-permute-start.1 = (bf16[8,64,128]{2,1,0:T(8,128)(2,1)}, bf16[8,64,128]{2,1,0:T(8,128)(2,1)S(1)}, u32[]{:S(2)}, u32[]{:S(2)}) collective-permute-start(bf16[8,64,128]{2,1,0:T(8,128)(2,1)} %own_ref.1), channel_id=1, source_target_pairs={{0,4},{8,12},{16,20},{24,28},{4,0},{12,8},{20,16},{28,24},{1,5},{9... | collective-permute-start | bytes 393224 | tf_op jit(solution)/shard_map/ppermute | solution.py:465
  3.7 7.7 %collective-permute-start = (bf16[8,64,128]{2,1,0:T(8,128)(2,1)}, bf16[8,64,128]{2,1,0:T(8,128)(2,1)S(1)}, u32[]{:S(2)}, u32[]{:S(2)}) collective-permute-start(bf16[8,64,128]{2,1,0:T(8,128)(2,1)} %own_ref.1), channel_id=1, source_target_pairs={{4,8},{12,16},{20,24},{8,4},{16,12},{24,20},{5,9},{13,17},{21,25},... | collective-permute-start | bytes 393224 | tf_op jit(solution)/shard_map/ppermute | solution.py:466
  4.4 0.8 %copy-start.6 = (f32[3,128]{1,0:T(4,128)S(1)}, f32[3,128]{1,0:T(4,128)}, u32[]{:S(2)}) copy-start(f32[3,128]{1,0:T(4,128)} %frac_ref.1) | copy-start | bytes 4612
  5.2 0.9 %copy-start.2 = (bf16[8,64,128]{2,1,0:T(8,128)(2,1)S(1)}, bf16[8,64,128]{2,1,0:T(8,128)(2,1)}, u32[]{:S(2)}) copy-start(bf16[8,64,128]{2,1,0:T(8,128)(2,1)} %own_ref.1) | copy-start | bytes 393220
  7.5 7.9 %collective-permute-start.2 = (bf16[4,128,128]{2,1,0:T(8,128)(2,1)S(1)}, bf16[4,128,128]{2,1,0:T(8,128)(2,1)S(1)}, u32[]{:S(2)}, u32[]{:S(2)}) collective-permute-start(bf16[4,128,128]{2,1,0:T(8,128)(2,1)S(1)} %get-tuple-element.26), channel_id=1, source_target_pairs={{1,2},{2,1},{5,6},{6,5},{9,10},{10,9},{13,14},{14,13},{17,18},{18,... | collective-permute-start | bytes 393224 | tf_op jit(solution)/shard_map/ppermute | solution.py:489
  8.2 7.3 %collective-permute-start.3 = (bf16[4,128,128]{2,1,0:T(8,128)(2,1)S(1)}, bf16[4,128,128]{2,1,0:T(8,128)(2,1)S(1)}, u32[]{:S(2)}, u32[]{:S(2)}) collective-permute-start(bf16[4,128,128]{2,1,0:T(8,128)(2,1)S(1)} %get-tuple-element.27.after_ref), channel_id=1, source_target_pairs={{0,1},{2,3},{1,0},{3,2},{4,5},{6,7},{5,4},{7,6},{8,9},{10,11},{9,8... | collective-permute-start | bytes 393224 | tf_op jit(solution)/shard_map/ppermute | solution.py:490
  11.5 4.0 %collective-permute-start.4 = (bf16[4,64,128]{2,1,0:T(8,128)(2,1)S(1)}, bf16[4,64,128]{2,1,0:T(8,128)(2,1)S(1)}, u32[]{:S(2)}, u32[]{:S(2)}) collective-permute-start(bf16[4,64,128]{2,1,0:T(8,128)(2,1)S(1)} %get-tuple-element.28), channel_id=1, source_target_pairs={{1,2},{2,1},{5,6},{6,5},{9,10},{10,9},{13,14},{14,13},{17,18},{18,... | collective-permute-start | bytes 196616 | tf_op jit(solution)/shard_map/ppermute | solution.py:501
  12.1 3.3 %collective-permute-start.5 = (bf16[4,64,128]{2,1,0:T(8,128)(2,1)S(1)}, bf16[4,64,128]{2,1,0:T(8,128)(2,1)S(1)}, u32[]{:S(2)}, u32[]{:S(2)}) collective-permute-start(bf16[4,64,128]{2,1,0:T(8,128)(2,1)S(1)} %get-tuple-element.29), channel_id=1, source_target_pairs={{0,1},{2,3},{1,0},{3,2},{4,5},{6,7},{5,4},{7,6},{8,9},{10,11},{9,8... | collective-permute-start | bytes 196616 | tf_op jit(solution)/shard_map/ppermute | solution.py:502
  13.5 2.0 %copy-start = (bf16[64,384]{1,0:T(8,128)(2,1)S(1)}, bf16[64,384]{1,0:T(8,128)(2,1)}, u32[]{:S(2)}) copy-start(bf16[64,384]{1,0:T(8,128)(2,1)} %constant.12.clone.refs_11_.refs_6_) | copy-start | bytes 147460
  13.5 2.0 %copy-start.1 = (bf16[128,128]{1,0:T(8,128)(2,1)S(1)}, bf16[128,128]{1,0:T(8,128)(2,1)}, u32[]{:S(2)}) copy-start(bf16[128,128]{1,0:T(8,128)(2,1)} %constant.13.clone.refs_12_.refs_7_) | copy-start | bytes 98308
  13.5 2.0 %copy-start.3 = (bf16[8,64,128]{2,1,0:T(8,128)(2,1)S(1)}, bf16[8,64,128]{2,1,0:T(8,128)(2,1)}, u32[]{:S(2)}) copy-start(bf16[8,64,128]{2,1,0:T(8,128)(2,1)} %refs_10_.1) | copy-start | bytes 393220
  15.5 17.0 %copy-start.4 = (bf16[384,64]{1,0:T(8,128)(2,1)S(1)}, bf16[384,64]{1,0:T(8,128)(2,1)}, u32[]{:S(2)}) copy-start(bf16[384,64]{1,0:T(8,128)(2,1)} %constant.14.clone.refs_4_) | copy-start | bytes 147460
  18.6 14.0 %copy-start.5 = (bf16[128,128]{1,0:T(8,128)(2,1)S(1)}, bf16[128,128]{1,0:T(8,128)(2,1)}, u32[]{:S(2)}) copy-start(bf16[128,128]{1,0:T(8,128)(2,1)} %constant.15.clone.refs_5_) | copy-start | bytes 98308

commit v15 on v14

--- a/solution.py
+++ b/solution.py
@@ -84,8 +84,7 @@
     return out
 
 
-def index_kernel(row_ref, frac_ref, own_ref, idx_ref, wgt_ref, keep_ref):
-    keep_ref[...] = own_ref[...]
+def index_kernel(row_ref, frac_ref, after_ref, idx_ref, wgt_ref):
     first = row_ref[0:1]
     col_x = (first * 241) >> 12
     col_y = first - 17 * col_x
@@ -120,7 +119,8 @@
         wgt_ref[cx] = dot_rows(hi, spread) + dot_rows(lo, spread) + dot_rows(rest, spread)
 
 
-def pack_first_kernel(xa_ref, own_ref, b_ref, a_ref):
+def pack_first_kernel(xa_ref, own_ref, b_ref, a_ref, keep_ref):
+    keep_ref[...] = own_ref[...]
     even = lax.axis_index("gy") % 2 == 0
     pack_rows(xa_ref, a_ref, b_ref, 0, even)
     pack_rows(own_ref, a_ref, b_ref, 64, even)
@@ -305,7 +305,10 @@
             gsc[2 * k + 1, cx] = upper[k]
         return square
 
-    sq_ref[...] = lax.fori_loop(0, 8, interpolate, jnp.zeros((8, 128), F32), unroll=4)
+    square = jnp.zeros((8, 128), F32)
+    for cx in range(8):
+        square = interpolate(cx, square)
+    sq_ref[...] = square
     res_ref[...] = rsc[...].reshape(8, 64, 128).astype(BF16)
     nodes = dot_left(dot_right(left_ref[...], gsc[...].reshape(384, 128)), wy_ref[...])
     node_ref[...] = nodes
@@ -464,30 +467,30 @@
     sds = jax.ShapeDtypeStruct
     xa = lax.ppermute(def_image, "gx", swaps(nx, 0))
     xb = lax.ppermute(def_image, "gx", swaps(nx, 1))
+    packed = sds((4, 128, 128), BF16)
+    to_b, to_a, own = pl.pallas_call(
+        pack_first_kernel,
+        out_shape=(packed, packed, sds((8, 64, 128), BF16)),
+        in_specs=[VMEM] * 2,
+        out_specs=(VMEM,) * 3,
+        compiler_params=PARAMS,
+        cost_estimate=pl.CostEstimate(flops=300000, bytes_accessed=524288, transcendentals=0),
+        name="pack_first_halo",
+    )(xa, def_image)
+    yb = lax.ppermute(to_b, "gy", swaps(ny, 1))
+    ya = lax.ppermute(to_a, "gy", swaps(ny, 0))
     row = lax.broadcasted_iota(jnp.int32, (16, 128), 0)
     table = jnp.where(row == 10, shift_z[None], 0)
     table = table + jnp.pad(connectivity, ((0, 8), (0, 0))) + jnp.pad(shift_xy, ((8, 6), (0, 0)))
-    idx, wgt, own = pl.pallas_call(
+    idx, wgt = pl.pallas_call(
         index_kernel,
-        out_shape=(sds((8, 128), jnp.int32), sds((8, 8, 128), F32), sds((8, 64, 128), BF16)),
-        in_specs=[VMEM] * 3,
-        out_specs=(VMEM,) * 3,
+        out_shape=(sds((8, 128), jnp.int32), sds((8, 8, 128), F32)),
+        in_specs=[VMEM, VMEM, pl.BlockSpec(memory_space=pl.ANY)],
+        out_specs=(VMEM, VMEM),
         compiler_params=PARAMS,
         cost_estimate=pl.CostEstimate(flops=300000, bytes_accessed=262144, transcendentals=0),
         name="order_elements",
-    )(table, frac, def_image)
-    packed = sds((4, 128, 128), BF16)
-    to_b, to_a = pl.pallas_call(
-        pack_first_kernel,
-        out_shape=(packed, packed),
-        in_specs=[VMEM] * 2,
-        out_specs=(VMEM, VMEM),
-        compiler_params=PARAMS,
-        cost_estimate=pl.CostEstimate(flops=300000, bytes_accessed=524288, transcendentals=0),
-        name="pack_first_halo",
-    )(xa, own)
-    yb = lax.ppermute(to_b, "gy", swaps(ny, 1))
-    ya = lax.ppermute(to_a, "gy", swaps(ny, 0))
+    )(table, frac, to_b)
     packed = sds((4, 64, 128), BF16)
     to_d, to_c = pl.pallas_call(
         pack_second_kernel,
@@ -497,7 +500,7 @@
         compiler_params=PARAMS,
         cost_estimate=pl.CostEstimate(flops=300000, bytes_accessed=524288, transcendentals=0),
         name="pack_second_halo",
-    )(xb, to_a)
+    )(xb, idx)
     yd = lax.ppermute(to_d, "gy", swaps(ny, 1))
     yc = lax.ppermute(to_c, "gy", swaps(ny, 0))
 

time: 43.8 us -> 44.6 us (1.018)
  waiting for transfers between devices: 0.68 us -> 3.05 us
  blocking collectives: 22.8 us -> 21.4 us
  other arithmetic: 0.77 us -> 0.08 us
  starting transfers between devices: 9.49 us -> 9.99 us
    ppermute x1, starting transfers between devices: 1.34 us -> 4.9 us  [on_device(): yc = lax.ppermute(to_c, 'gy', swaps(ny, 0))]
    ppermute x1, starting transfers between devices: 3.13 us -> 0.07 us  [on_device(): ya = lax.ppermute(to_a, 'gy', swaps(ny, 0))]
    ppermute x1, waiting for transfers between devices: 0.66 us -> 3.03 us  [on_device(): xa = lax.ppermute(def_image, 'gx', swaps(nx, 0))]
    all_to_all x2, blocking collectives: 22.8 us -> 21.4 us  [on_device(): recv = lax.all_to_all(send, ('gx', 'gy'), 0, 0, tiled=True)]
    add x1, other arithmetic: 0.77 us -> 0.08 us  [on_device(): table + jnp.pad(connectivity, ((0, 8), (0, 0)))]
    unnamed x18 -> x20, local copies, waits for them, and re-layouts: 0.94 us -> 0.95 us
  transfers between devices with their start and end apart: 6 -> 6, of which waited for: 1 -> 1; matrix products, arithmetic and copies ran while one was open for 2% -> 0% of each run, Pallas kernels for 7% -> 7%
where the time goes in v15:
time: 44.6 us; the launch traced here: 44.3 us
  blocking collectives  21.4 us (48%)
  starting transfers between devices  9.99 us (22%)
  Pallas kernels  8.04 us (18%)
  waiting for transfers between devices  3.05 us (7%)
  local copies, waits for them, and re-layouts  0.95 us (2%)
  between operations  0.82 us (2%)
    all_to_all x2, blocking collectives, on_device(): recv = lax.all_to_all(send, ('gx', 'gy'), 0, 0, tiled=True)  21.4 us
    ppermute x1, starting transfers between devices, on_device(): yc = lax.ppermute(to_c, 'gy', swaps(ny, 0))  4.9 us
    pallas_call x1, Pallas kernels, on_device(): pl.pallas_call(lambda *refs: late_kernel(nx, ny, *refs), out_shape=(sds((...  3.09 us
    ppermute x1, starting transfers between devices, on_device(): xa = lax.ppermute(def_image, 'gx', swaps(nx, 0))  3.03 us
    ppermute x1, waiting for transfers between devices, on_device(): xa = lax.ppermute(def_image, 'gx', swaps(nx, 0))  3.03 us
    pallas_call x1, Pallas kernels, on_device(): pl.pallas_call(early_kernel, out_shape=sds((16, 11, 8, 128), F32), in_spe...  1.96 us
    pallas_call x1, Pallas kernels, on_device(): pl.pallas_call(lambda *refs: product_kernel(nx, ny, *refs), out_shape=(sd...  1.26 us
    unnamed x20, local copies, waits for them, and re-layouts  0.95 us
  transfers between devices with their start and end apart: 6, of which 1 were waited for; matrix products, arithmetic and copies ran while one was open for 0% of the time, Pallas kernels for 7%

profile of v15, /device:TPU:0, one launch (start us, length us, event | category | flops | bytes accessed | tf_op | source)
XLA Modules:
  0.0 44.3 jit_solution(14446080850220973114)
XLA Ops:
  0.6 3.0 %collective-permute-start = (bf16[8,64,128]{2,1,0:T(8,128)(2,1)}, bf16[8,64,128]{2,1,0:T(8,128)(2,1)S(1)}, u32[]{:S(2)}, u32[]{:S(2)}) collective-permute-start(bf16[8,64,128]{2,1,0:T(8,128)(2,1)} %own_ref.1), channel_id=1, source_target_pairs={{0,4},{8,12},{16,20},{24,28},{4,0},{12,8},{20,16},{28,24},{1,5},{9... | collective-permute-start | bytes 393224 | tf_op jit(solution)/shard_map/ppermute | solution.py:468
  3.7 0.7 %collective-permute-start.1 = (bf16[8,64,128]{2,1,0:T(8,128)(2,1)}, bf16[8,64,128]{2,1,0:T(8,128)(2,1)S(1)}, u32[]{:S(2)}, u32[]{:S(2)}) collective-permute-start(bf16[8,64,128]{2,1,0:T(8,128)(2,1)} %own_ref.1), channel_id=1, source_target_pairs={{4,8},{12,16},{20,24},{8,4},{16,12},{24,20},{5,9},{13,17},{21,25},... | collective-permute-start | bytes 393224 | tf_op jit(solution)/shard_map/ppermute | solution.py:469
  4.3 3.0 %collective-permute-done.xa_ref.refs_4_ = bf16[8,64,128]{2,1,0:T(8,128)(2,1)S(1)} collective-permute-done((bf16[8,64,128]{2,1,0:T(8,128)(2,1)}, bf16[8,64,128]{2,1,0:T(8,128)(2,1)S(1)}, u32[]{:S(2)}, u32[]{:S(2)}) %collective-permute-start) | collective-permute-done | bytes 131104 | tf_op jit(solution)/shard_map/ppermute | solution.py:468
  7.4 0.0 copy-start.2
  7.4 0.9 %copy-done.2 = bf16[8,64,128]{2,1,0:T(8,128)(2,1)S(1)} copy-done((bf16[8,64,128]{2,1,0:T(8,128)(2,1)S(1)}, bf16[8,64,128]{2,1,0:T(8,128)(2,1)}, u32[]{:S(2)}) %copy-start.2) | copy-done | bytes 131096
  8.3 0.0 copy-start.7
  8.3 0.1 pack_first_halo.1
  8.4 0.0 copy-start.8
  8.4 0.0 copy-start.9
  8.5 0.1 collective-permute-start.3
  8.5 0.0 copy-start.6
  8.5 0.7 %collective-permute-start.2 = (bf16[4,128,128]{2,1,0:T(8,128)(2,1)S(1)}, bf16[4,128,128]{2,1,0:T(8,128)(2,1)S(1)}, u32[]{:S(2)}, u32[]{:S(2)}) collective-permute-start(bf16[4,128,128]{2,1,0:T(8,128)(2,1)S(1)} %get-tuple-element.23.after_ref), channel_id=1, source_target_pairs={{1,2},{2,1},{5,6},{6,5},{9,10},{10,9},{13,14},{14,13},{17,18},{18,... | collective-permute-start | bytes 393224 | tf_op jit(solution)/shard_map/ppermute | solution.py:480
  9.2 0.0 copy-done.7
  9.2 0.0 copy-done.8
  9.2 0.0 copy-done.9
  9.3 0.1 pad_add_fusion.row_ref
  9.3 0.0 copy-done.6
  9.3 0.7 %order_elements.1 = (s32[8,128]{1,0:T(8,128)S(1)}, f32[8,8,128]{2,1,0:T(8,128)S(1)}) custom-call(s32[16,128]{1,0:T(8,128)S(1)} %pad_add_fusion.row_ref, f32[3,128]{1,0:T(4,128)S(1)} %copy-done.6, bf16[4,128,128]{2,1,0:T(8,128)(2,1)S(1)} %get-tuple-element.23.after_ref), custom_call_target="tpu_custom_call" | custom-call | flops 300000 | bytes 262144 | tf_op jit(solution)/shard_map/order_elements/pallas_call | solution.py:485
  10.0 0.0 collective-permute-done.1.xb_ref.refs_2_
  10.0 0.1 pack_second_halo.1
  10.1 0.7 %collective-permute-start.4 = (bf16[4,64,128]{2,1,0:T(8,128)(2,1)S(1)}, bf16[4,64,128]{2,1,0:T(8,128)(2,1)S(1)}, u32[]{:S(2)}, u32[]{:S(2)}) collective-permute-start(bf16[4,64,128]{2,1,0:T(8,128)(2,1)S(1)} %get-tuple-element.28), channel_id=1, source_target_pairs={{1,2},{2,1},{5,6},{6,5},{9,10},{10,9},{13,14},{14,13},{17,18},{18,... | collective-permute-start | bytes 196616 | tf_op jit(solution)/shard_map/ppermute | solution.py:504
  10.8 4.9 %collective-permute-start.5 = (bf16[4,64,128]{2,1,0:T(8,128)(2,1)S(1)}, bf16[4,64,128]{2,1,0:T(8,128)(2,1)S(1)}, u32[]{:S(2)}, u32[]{:S(2)}) collective-permute-start(bf16[4,64,128]{2,1,0:T(8,128)(2,1)S(1)} %get-tuple-element.29), channel_id=1, source_target_pairs={{0,1},{2,3},{1,0},{3,2},{4,5},{6,7},{5,4},{7,6},{8,9},{10,11},{9,8... | collective-permute-start | bytes 196616 | tf_op jit(solution)/shard_map/ppermute | solution.py:505
  15.7 0.0 copy-start
  15.7 0.0 copy-start.1
  15.7 0.0 copy-start.3
  15.7 2.0 %sample_early.1.refs_9_ = f32[16,11,8,128]{3,2,1,0:T(8,128)S(1)} custom-call(s32[8,128]{1,0:T(8,128)S(1)} %get-tuple-element.24.after_ref.idx_ref.refs_0_, bf16[8,64,128]{2,1,0:T(8,128)(2,1)S(1)} %collective-permute-done.1.xb_ref.refs_2_, bf16[8,64,128]{2,1,0:T(8,128)(2,1)S(1)} %get-tuple-element.26.own_ref.refs_3_, ...), custom_call_target="tpu_custom_call" | custom-call | flops 4000000 | bytes 2000000 | tf_op jit(solution)/shard_map/sample_early/pallas_call | solution.py:508
  17.7 0.0 collective-permute-done.4.refs_7_
  17.7 0.0 collective-permute-done.5.refs_8_
  17.7 0.0 collective-permute-done.3.refs_6_
  17.7 0.0 collective-permute-done.2.refs_5_
  17.7 0.0 copy-done
  17.7 0.0 copy-done.1
  17.7 0.0 copy-done.3
  17.8 0.0 copy-start.4
  17.8 3.1 %sample_and_gradient.1 = (bf16[8,64,128]{2,1,0:T(8,128)(2,1)S(1)}, f32[3,8,8,8,128]{4,3,2,1,0:T(8,128)S(1)}, f32[64,128]{1,0:T(8,128)S(1)}, f32[32,1,128]{2,1,0:T(1,128)S(1)}, f32[8,128]{1,0:T(8,128)S(1)}) custom-call(s32[8,128]{1,0:T(8,128)S(1)} %get-tuple-element.24.after_ref.idx_ref.refs_0_, f32[8,8,128]{2,1,0:T(8,128)S(1)} %get-tuple-element.25.refs_1_, ...), custom_call_target="tpu_custom_call" | custom-call | tf_op jit(solution)/shard_map/sample_and_gradient/pallas_call | solution.py:518
  20.9 0.0 copy-start.5
  20.9 12.6 %all_to_all.10.refs_0_ = f32[32,1,128]{2,1,0:T(1,128)S(1)} all-to-all(f32[32,1,128]{2,1,0:T(1,128)S(1)} %get-tuple-element.30), channel_id=1, replica_groups=mesh['gx'=8,'gy'=4] {'gx','gy'}, dimensions={0} | all-to-all | bytes 32768 | tf_op jit(solution)/shard_map/all_to_all | solution.py:538
  33.4 0.0 copy-done.4
  33.4 0.0 copy-done.5
  33.4 1.3 %gauss_newton_product.1 = (f32[6,8,128]{2,1,0:T(8,128)S(1)}, f32[6,8,128]{2,1,0:T(8,128)S(1)}, f32[32,1,128]{2,1,0:T(1,128)S(1)}, bf16[8,64,128]{2,1,0:T(8,128)(2,1)}) custom-call(f32[32,1,128]{2,1,0:T(1,128)S(1)} %all_to_all.10.refs_0_, f32[64,128]{1,0:T(8,128)S(1)} %get-tuple-element.31.refs_1_, f32[3,8,8,8,128]{4,3,2,1,0:T(8,128)S(1)} %get-tuple-element.32.refs_2_, ...), custom_call_target="tpu_custom_call" | custom-call | tf_op jit(solution)/shard_map/gauss_newton_product/pallas_call | solution.py:539
  34.7 8.8 %all_to_all.11.refs_0_ = f32[32,1,128]{2,1,0:T(1,128)S(1)} all-to-all(f32[32,1,128]{2,1,0:T(1,128)S(1)} %get-tuple-element.36), channel_id=1, replica_groups=mesh['gx'=8,'gy'=4] {'gx','gy'}, dimensions={0} | all-to-all | bytes 32768 | tf_op jit(solution)/shard_map/all_to_all | solution.py:557
  43.6 0.8 %finish.1 = (f32[3,2,8,16]{3,2,1,0:T(8,128)}, f32[3,2,8,16]{3,2,1,0:T(8,128)}, f32[1,1]{1,0:T(1,128)}) custom-call(f32[32,1,128]{2,1,0:T(1,128)S(1)} %all_to_all.11.refs_0_, f32[6,8,128]{2,1,0:T(8,128)S(1)} %get-tuple-element.37.refs_1_, f32[6,8,128]{2,1,0:T(8,128)S(1)} %get-tuple-element.38.refs_2_), custom_call_target="tpu_custom_call" | custom-call | tf_op jit(solution)/shard_map/finish/pallas_call | solution.py:559
  (1 shorter events, 0.0 us)
Async XLA Ops:
  0.6 6.7 %collective-permute-start = (bf16[8,64,128]{2,1,0:T(8,128)(2,1)}, bf16[8,64,128]{2,1,0:T(8,128)(2,1)S(1)}, u32[]{:S(2)}, u32[]{:S(2)}) collective-permute-start(bf16[8,64,128]{2,1,0:T(8,128)(2,1)} %own_ref.1), channel_id=1, source_target_pairs={{0,4},{8,12},{16,20},{24,28},{4,0},{12,8},{20,16},{28,24},{1,5},{9... | collective-permute-start | bytes 393224 | tf_op jit(solution)/shard_map/ppermute | solution.py:468
  3.7 6.3 %collective-permute-start.1 = (bf16[8,64,128]{2,1,0:T(8,128)(2,1)}, bf16[8,64,128]{2,1,0:T(8,128)(2,1)S(1)}, u32[]{:S(2)}, u32[]{:S(2)}) collective-permute-start(bf16[8,64,128]{2,1,0:T(8,128)(2,1)} %own_ref.1), channel_id=1, source_target_pairs={{4,8},{12,16},{20,24},{8,4},{16,12},{24,20},{5,9},{13,17},{21,25},... | collective-permute-start | bytes 393224 | tf_op jit(solution)/shard_map/ppermute | solution.py:469
  7.4 0.9 %copy-start.2 = (bf16[8,64,128]{2,1,0:T(8,128)(2,1)S(1)}, bf16[8,64,128]{2,1,0:T(8,128)(2,1)}, u32[]{:S(2)}) copy-start(bf16[8,64,128]{2,1,0:T(8,128)(2,1)} %own_ref.1) | copy-start | bytes 393220
  8.3 1.0 %copy-start.7 = (s32[8,128]{1,0:T(8,128)S(1)}, s32[8,128]{1,0:T(8,128)}, u32[]{:S(2)}) copy-start(s32[8,128]{1,0:T(8,128)} %param.15) | copy-start | bytes 12292
  8.4 0.8 %copy-start.8 = (s32[2,128]{1,0:T(2,128)S(1)}, s32[2,128]{1,0:T(2,128)}, u32[]{:S(2)}) copy-start(s32[2,128]{1,0:T(2,128)} %param.12) | copy-start | bytes 3076
  8.4 0.8 %copy-start.9 = (s32[128]{0:T(128)S(1)}, s32[128]{0:T(128)}, u32[]{:S(2)}) copy-start(s32[128]{0:T(128)} %param.13) | copy-start | bytes 1540
  8.5 9.2 %collective-permute-start.3 = (bf16[4,128,128]{2,1,0:T(8,128)(2,1)S(1)}, bf16[4,128,128]{2,1,0:T(8,128)(2,1)S(1)}, u32[]{:S(2)}, u32[]{:S(2)}) collective-permute-start(bf16[4,128,128]{2,1,0:T(8,128)(2,1)S(1)} %get-tuple-element.27), channel_id=1, source_target_pairs={{0,1},{2,3},{1,0},{3,2},{4,5},{6,7},{5,4},{7,6},{8,9},{10,11},{9,8... | collective-permute-start | bytes 393224 | tf_op jit(solution)/shard_map/ppermute | solution.py:481
  8.5 0.8 %copy-start.6 = (f32[3,128]{1,0:T(4,128)S(1)}, f32[3,128]{1,0:T(4,128)}, u32[]{:S(2)}) copy-start(f32[3,128]{1,0:T(4,128)} %frac_ref.1) | copy-start | bytes 4612
  8.5 9.2 %collective-permute-start.2 = (bf16[4,128,128]{2,1,0:T(8,128)(2,1)S(1)}, bf16[4,128,128]{2,1,0:T(8,128)(2,1)S(1)}, u32[]{:S(2)}, u32[]{:S(2)}) collective-permute-start(bf16[4,128,128]{2,1,0:T(8,128)(2,1)S(1)} %get-tuple-element.23.after_ref), channel_id=1, source_target_pairs={{1,2},{2,1},{5,6},{6,5},{9,10},{10,9},{13,14},{14,13},{17,18},{18,... | collective-permute-start | bytes 393224 | tf_op jit(solution)/shard_map/ppermute | solution.py:480
  10.1 7.5 %collective-permute-start.4 = (bf16[4,64,128]{2,1,0:T(8,128)(2,1)S(1)}, bf16[4,64,128]{2,1,0:T(8,128)(2,1)S(1)}, u32[]{:S(2)}, u32[]{:S(2)}) collective-permute-start(bf16[4,64,128]{2,1,0:T(8,128)(2,1)S(1)} %get-tuple-element.28), channel_id=1, source_target_pairs={{1,2},{2,1},{5,6},{6,5},{9,10},{10,9},{13,14},{14,13},{17,18},{18,... | collective-permute-start | bytes 196616 | tf_op jit(solution)/shard_map/ppermute | solution.py:504
  10.8 6.9 %collective-permute-start.5 = (bf16[4,64,128]{2,1,0:T(8,128)(2,1)S(1)}, bf16[4,64,128]{2,1,0:T(8,128)(2,1)S(1)}, u32[]{:S(2)}, u32[]{:S(2)}) collective-permute-start(bf16[4,64,128]{2,1,0:T(8,128)(2,1)S(1)} %get-tuple-element.29), channel_id=1, source_target_pairs={{0,1},{2,3},{1,0},{3,2},{4,5},{6,7},{5,4},{7,6},{8,9},{10,11},{9,8... | collective-permute-start | bytes 196616 | tf_op jit(solution)/shard_map/ppermute | solution.py:505
  15.7 2.0 %copy-start = (bf16[64,384]{1,0:T(8,128)(2,1)S(1)}, bf16[64,384]{1,0:T(8,128)(2,1)}, u32[]{:S(2)}) copy-start(bf16[64,384]{1,0:T(8,128)(2,1)} %constant.12.clone.refs_11_.refs_6_) | copy-start | bytes 147460
  15.7 2.0 %copy-start.1 = (bf16[128,128]{1,0:T(8,128)(2,1)S(1)}, bf16[128,128]{1,0:T(8,128)(2,1)}, u32[]{:S(2)}) copy-start(bf16[128,128]{1,0:T(8,128)(2,1)} %constant.13.clone.refs_12_.refs_7_) | copy-start | bytes 98308
  15.7 2.0 %copy-start.3 = (bf16[8,64,128]{2,1,0:T(8,128)(2,1)S(1)}, bf16[8,64,128]{2,1,0:T(8,128)(2,1)}, u32[]{:S(2)}) copy-start(bf16[8,64,128]{2,1,0:T(8,128)(2,1)} %refs_10_.1) | copy-start | bytes 393220
  17.8 15.7 %copy-start.4 = (bf16[384,64]{1,0:T(8,128)(2,1)S(1)}, bf16[384,64]{1,0:T(8,128)(2,1)}, u32[]{:S(2)}) copy-start(bf16[384,64]{1,0:T(8,128)(2,1)} %constant.14.clone.refs_4_) | copy-start | bytes 147460
  20.9 12.6 %copy-start.5 = (bf16[128,128]{1,0:T(8,128)(2,1)S(1)}, bf16[128,128]{1,0:T(8,128)(2,1)}, u32[]{:S(2)}) copy-start(bf16[128,128]{1,0:T(8,128)(2,1)} %constant.15.clone.refs_5_) | copy-start | bytes 98308

commit v16 on v14

--- a/solution.py
+++ b/solution.py
@@ -305,7 +305,10 @@
             gsc[2 * k + 1, cx] = upper[k]
         return square
 
-    sq_ref[...] = lax.fori_loop(0, 8, interpolate, jnp.zeros((8, 128), F32), unroll=4)
+    square = jnp.zeros((8, 128), F32)
+    for cx in range(8):
+        square = interpolate(cx, square)
+    sq_ref[...] = square
     res_ref[...] = rsc[...].reshape(8, 64, 128).astype(BF16)
     nodes = dot_left(dot_right(left_ref[...], gsc[...].reshape(384, 128)), wy_ref[...])
     node_ref[...] = nodes

time: 43.8 us -> 43.8 us (level)
  no operation moved by 1% of the time
where the time goes in v16:
time: 43.8 us; the launch traced here: 43.5 us
  blocking collectives  22.8 us (52%)
  starting transfers between devices  9.49 us (22%)
  Pallas kernels  8 us (18%)
  local copies, waits for them, and re-layouts  0.94 us (2%)
  between operations  0.81 us (2%)
  other arithmetic  0.77 us (2%)
  waiting for transfers between devices  0.68 us (2%)
    all_to_all x2, blocking collectives, on_device(): recv = lax.all_to_all(send, ('gx', 'gy'), 0, 0, tiled=True)  22.8 us
    ppermute x1, starting transfers between devices, on_device(): ya = lax.ppermute(to_a, 'gy', swaps(ny, 0))  3.13 us
    pallas_call x1, Pallas kernels, on_device(): pl.pallas_call(lambda *refs: late_kernel(nx, ny, *refs), out_shape=(sds((...  3.09 us
    ppermute x1, starting transfers between devices, on_device(): xa = lax.ppermute(def_image, 'gx', swaps(nx, 0))  3.03 us
    pallas_call x1, Pallas kernels, on_device(): pl.pallas_call(early_kernel, out_shape=sds((16, 11, 8, 128), F32), in_spe...  1.96 us
    ppermute x1, starting transfers between devices, on_device(): yc = lax.ppermute(to_c, 'gy', swaps(ny, 0))  1.34 us
    pallas_call x1, Pallas kernels, on_device(): pl.pallas_call(lambda *refs: product_kernel(nx, ny, *refs), out_shape=(sd...  1.26 us
    unnamed x18, local copies, waits for them, and re-layouts  0.94 us
  transfers between devices with their start and end apart: 6, of which 1 were waited for; matrix products, arithmetic and copies ran while one was open for 2% of the time, Pallas kernels for 7%

profile of v16, /device:TPU:0, one launch (start us, length us, event | category | flops | bytes accessed | tf_op | source)
XLA Modules:
  0.0 43.5 jit_solution(2002384273266853836)
XLA Ops:
  0.6 0.0 copy-start.8
  0.6 0.0 copy-start.7
  0.7 3.0 %collective-permute-start.1 = (bf16[8,64,128]{2,1,0:T(8,128)(2,1)}, bf16[8,64,128]{2,1,0:T(8,128)(2,1)S(1)}, u32[]{:S(2)}, u32[]{:S(2)}) collective-permute-start(bf16[8,64,128]{2,1,0:T(8,128)(2,1)} %own_ref.1), channel_id=1, source_target_pairs={{0,4},{8,12},{16,20},{24,28},{4,0},{12,8},{20,16},{28,24},{1,5},{9... | collective-permute-start | bytes 393224 | tf_op jit(solution)/shard_map/ppermute | solution.py:468
  3.7 0.7 %collective-permute-start = (bf16[8,64,128]{2,1,0:T(8,128)(2,1)}, bf16[8,64,128]{2,1,0:T(8,128)(2,1)S(1)}, u32[]{:S(2)}, u32[]{:S(2)}) collective-permute-start(bf16[8,64,128]{2,1,0:T(8,128)(2,1)} %own_ref.1), channel_id=1, source_target_pairs={{4,8},{12,16},{20,24},{8,4},{16,12},{24,20},{5,9},{13,17},{21,25},... | collective-permute-start | bytes 393224 | tf_op jit(solution)/shard_map/ppermute | solution.py:469
  4.4 0.0 copy-done.8
  4.4 0.0 copy-done.7
  4.4 0.0 copy-start.6
  4.4 0.8 %pad_add_fusion.row_ref = s32[16,128]{1,0:T(8,128)S(1)} fusion(s32[2,128]{1,0:T(2,128)S(1)} %copy-done.7, s32[8,128]{1,0:T(8,128)} %param.15, s32[128]{0:T(128)S(1)} %copy-done.8, pred[16]{0:T(512)(128)(4,1)S(1)} %iota_compare_fusion), kind=kLoop, calls=%fused_computation | loop fusion | flops 6144 | bytes 13840 | tf_op jit(solution)/shard_map/add | solution.py:472
  5.2 0.0 copy-done.6
  5.2 0.0 copy-start.2
  5.2 0.9 %copy-done.2 = bf16[8,64,128]{2,1,0:T(8,128)(2,1)S(1)} copy-done((bf16[8,64,128]{2,1,0:T(8,128)(2,1)S(1)}, bf16[8,64,128]{2,1,0:T(8,128)(2,1)}, u32[]{:S(2)}) %copy-start.2) | copy-done | bytes 131096
  6.1 0.7 %order_elements.1 = (s32[8,128]{1,0:T(8,128)S(1)}, f32[8,8,128]{2,1,0:T(8,128)S(1)}, bf16[8,64,128]{2,1,0:T(8,128)(2,1)S(1)}) custom-call(s32[16,128]{1,0:T(8,128)S(1)} %pad_add_fusion.row_ref, f32[3,128]{1,0:T(4,128)S(1)} %copy-done.6, bf16[8,64,128]{2,1,0:T(8,128)(2,1)S(1)} %copy-done.2), custom_call_target="tpu_custom_call" | custom-call | flops 300000 | bytes 262144 | tf_op jit(solution)/shard_map/order_elements/pallas_call | solution.py:473
  6.7 0.7 %collective-permute-done.1.xa_ref.refs_4_ = bf16[8,64,128]{2,1,0:T(8,128)(2,1)S(1)} collective-permute-done((bf16[8,64,128]{2,1,0:T(8,128)(2,1)}, bf16[8,64,128]{2,1,0:T(8,128)(2,1)S(1)}, u32[]{:S(2)}, u32[]{:S(2)}) %collective-permute-start.1) | collective-permute-done | bytes 131104 | tf_op jit(solution)/shard_map/ppermute | solution.py:468
  7.4 0.1 pack_first_halo.1
  7.5 0.7 %collective-permute-start.2 = (bf16[4,128,128]{2,1,0:T(8,128)(2,1)S(1)}, bf16[4,128,128]{2,1,0:T(8,128)(2,1)S(1)}, u32[]{:S(2)}, u32[]{:S(2)}) collective-permute-start(bf16[4,128,128]{2,1,0:T(8,128)(2,1)S(1)} %get-tuple-element.26), channel_id=1, source_target_pairs={{1,2},{2,1},{5,6},{6,5},{9,10},{10,9},{13,14},{14,13},{17,18},{18,... | collective-permute-start | bytes 393224 | tf_op jit(solution)/shard_map/ppermute | solution.py:492
  8.2 3.1 %collective-permute-start.3 = (bf16[4,128,128]{2,1,0:T(8,128)(2,1)S(1)}, bf16[4,128,128]{2,1,0:T(8,128)(2,1)S(1)}, u32[]{:S(2)}, u32[]{:S(2)}) collective-permute-start(bf16[4,128,128]{2,1,0:T(8,128)(2,1)S(1)} %get-tuple-element.27.after_ref), channel_id=1, source_target_pairs={{0,1},{2,3},{1,0},{3,2},{4,5},{6,7},{5,4},{7,6},{8,9},{10,11},{9,8... | collective-permute-start | bytes 393224 | tf_op jit(solution)/shard_map/ppermute | solution.py:493
  11.4 0.0 collective-permute-done.xb_ref.refs_2_
  11.4 0.1 pack_second_halo.1
  11.5 0.7 %collective-permute-start.4 = (bf16[4,64,128]{2,1,0:T(8,128)(2,1)S(1)}, bf16[4,64,128]{2,1,0:T(8,128)(2,1)S(1)}, u32[]{:S(2)}, u32[]{:S(2)}) collective-permute-start(bf16[4,64,128]{2,1,0:T(8,128)(2,1)S(1)} %get-tuple-element.28), channel_id=1, source_target_pairs={{1,2},{2,1},{5,6},{6,5},{9,10},{10,9},{13,14},{14,13},{17,18},{18,... | collective-permute-start | bytes 196616 | tf_op jit(solution)/shard_map/ppermute | solution.py:504
  12.1 1.3 %collective-permute-start.5 = (bf16[4,64,128]{2,1,0:T(8,128)(2,1)S(1)}, bf16[4,64,128]{2,1,0:T(8,128)(2,1)S(1)}, u32[]{:S(2)}, u32[]{:S(2)}) collective-permute-start(bf16[4,64,128]{2,1,0:T(8,128)(2,1)S(1)} %get-tuple-element.29), channel_id=1, source_target_pairs={{0,1},{2,3},{1,0},{3,2},{4,5},{6,7},{5,4},{7,6},{8,9},{10,11},{9,8... | collective-permute-start | bytes 196616 | tf_op jit(solution)/shard_map/ppermute | solution.py:505
  13.5 0.0 copy-start
  13.5 0.0 copy-start.1
  13.5 0.0 copy-start.3
  13.5 2.0 %sample_early.1.refs_9_ = f32[16,11,8,128]{3,2,1,0:T(8,128)S(1)} custom-call(s32[8,128]{1,0:T(8,128)S(1)} %get-tuple-element.23.idx_ref.refs_0_, bf16[8,64,128]{2,1,0:T(8,128)(2,1)S(1)} %collective-permute-done.xb_ref.refs_2_, bf16[8,64,128]{2,1,0:T(8,128)(2,1)S(1)} %get-tuple-element.25.own_ref.refs_3_, ...), custom_call_target="tpu_custom_call" | custom-call | flops 4000000 | bytes 2000000 | tf_op jit(solution)/shard_map/sample_early/pallas_call | solution.py:508
  15.5 0.0 collective-permute-done.4.refs_7_
  15.5 0.0 collective-permute-done.5.refs_8_
  15.5 0.0 collective-permute-done.2.refs_5_
  15.5 0.0 collective-permute-done.3.refs_6_
  15.5 0.0 copy-done
  15.5 0.0 copy-done.1
  15.5 0.0 copy-done.3
  15.5 0.0 copy-start.4
  15.5 3.1 %sample_and_gradient.1 = (bf16[8,64,128]{2,1,0:T(8,128)(2,1)S(1)}, f32[3,8,8,8,128]{4,3,2,1,0:T(8,128)S(1)}, f32[64,128]{1,0:T(8,128)S(1)}, f32[32,1,128]{2,1,0:T(1,128)S(1)}, f32[8,128]{1,0:T(8,128)S(1)}) custom-call(s32[8,128]{1,0:T(8,128)S(1)} %get-tuple-element.23.idx_ref.refs_0_, f32[8,8,128]{2,1,0:T(8,128)S(1)} %get-tuple-element.24.refs_1_, ...), custom_call_target="tpu_custom_call" | custom-call | tf_op jit(solution)/shard_map/sample_and_gradient/pallas_call | solution.py:518
  18.6 0.0 copy-start.5
  18.6 14.0 %all_to_all.10.refs_0_ = f32[32,1,128]{2,1,0:T(1,128)S(1)} all-to-all(f32[32,1,128]{2,1,0:T(1,128)S(1)} %get-tuple-element.30), channel_id=1, replica_groups=mesh['gx'=8,'gy'=4] {'gx','gy'}, dimensions={0} | all-to-all | bytes 32768 | tf_op jit(solution)/shard_map/all_to_all | solution.py:538
  32.6 0.0 copy-done.4
  32.6 0.0 copy-done.5
  32.6 1.3 %gauss_newton_product.1 = (f32[6,8,128]{2,1,0:T(8,128)S(1)}, f32[6,8,128]{2,1,0:T(8,128)S(1)}, f32[32,1,128]{2,1,0:T(1,128)S(1)}, bf16[8,64,128]{2,1,0:T(8,128)(2,1)}) custom-call(f32[32,1,128]{2,1,0:T(1,128)S(1)} %all_to_all.10.refs_0_, f32[64,128]{1,0:T(8,128)S(1)} %get-tuple-element.31.refs_1_, f32[3,8,8,8,128]{4,3,2,1,0:T(8,128)S(1)} %get-tuple-element.32.refs_2_, ...), custom_call_target="tpu_custom_call" | custom-call | tf_op jit(solution)/shard_map/gauss_newton_product/pallas_call | solution.py:539
  33.9 8.8 %all_to_all.11.refs_0_ = f32[32,1,128]{2,1,0:T(1,128)S(1)} all-to-all(f32[32,1,128]{2,1,0:T(1,128)S(1)} %get-tuple-element.36), channel_id=1, replica_groups=mesh['gx'=8,'gy'=4] {'gx','gy'}, dimensions={0} | all-to-all | bytes 32768 | tf_op jit(solution)/shard_map/all_to_all | solution.py:557
  42.7 0.8 %finish.1 = (f32[3,2,8,16]{3,2,1,0:T(8,128)}, f32[3,2,8,16]{3,2,1,0:T(8,128)}, f32[1,1]{1,0:T(1,128)}) custom-call(f32[32,1,128]{2,1,0:T(1,128)S(1)} %all_to_all.11.refs_0_, f32[6,8,128]{2,1,0:T(8,128)S(1)} %get-tuple-element.37.refs_1_, f32[6,8,128]{2,1,0:T(8,128)S(1)} %get-tuple-element.38.refs_2_), custom_call_target="tpu_custom_call" | custom-call | tf_op jit(solution)/shard_map/finish/pallas_call | solution.py:559
  (1 shorter events, 0.0 us)
Async XLA Ops:
  0.6 3.7 %copy-start.8 = (s32[128]{0:T(128)S(1)}, s32[128]{0:T(128)}, u32[]{:S(2)}) copy-start(s32[128]{0:T(128)} %param.13) | copy-start | bytes 1540
  0.6 3.7 %copy-start.7 = (s32[2,128]{1,0:T(2,128)S(1)}, s32[2,128]{1,0:T(2,128)}, u32[]{:S(2)}) copy-start(s32[2,128]{1,0:T(2,128)} %param.12) | copy-start | bytes 3076
  0.7 6.7 %collective-permute-start.1 = (bf16[8,64,128]{2,1,0:T(8,128)(2,1)}, bf16[8,64,128]{2,1,0:T(8,128)(2,1)S(1)}, u32[]{:S(2)}, u32[]{:S(2)}) collective-permute-start(bf16[8,64,128]{2,1,0:T(8,128)(2,1)} %own_ref.1), channel_id=1, source_target_pairs={{0,4},{8,12},{16,20},{24,28},{4,0},{12,8},{20,16},{28,24},{1,5},{9... | collective-permute-start | bytes 393224 | tf_op jit(solution)/shard_map/ppermute | solution.py:468
  3.7 7.7 %collective-permute-start = (bf16[8,64,128]{2,1,0:T(8,128)(2,1)}, bf16[8,64,128]{2,1,0:T(8,128)(2,1)S(1)}, u32[]{:S(2)}, u32[]{:S(2)}) collective-permute-start(bf16[8,64,128]{2,1,0:T(8,128)(2,1)} %own_ref.1), channel_id=1, source_target_pairs={{4,8},{12,16},{20,24},{8,4},{16,12},{24,20},{5,9},{13,17},{21,25},... | collective-permute-start | bytes 393224 | tf_op jit(solution)/shard_map/ppermute | solution.py:469
  4.4 0.8 %copy-start.6 = (f32[3,128]{1,0:T(4,128)S(1)}, f32[3,128]{1,0:T(4,128)}, u32[]{:S(2)}) copy-start(f32[3,128]{1,0:T(4,128)} %frac_ref.1) | copy-start | bytes 4612
  5.2 0.9 %copy-start.2 = (bf16[8,64,128]{2,1,0:T(8,128)(2,1)S(1)}, bf16[8,64,128]{2,1,0:T(8,128)(2,1)}, u32[]{:S(2)}) copy-start(bf16[8,64,128]{2,1,0:T(8,128)(2,1)} %own_ref.1) | copy-start | bytes 393220
  7.5 7.9 %collective-permute-start.2 = (bf16[4,128,128]{2,1,0:T(8,128)(2,1)S(1)}, bf16[4,128,128]{2,1,0:T(8,128)(2,1)S(1)}, u32[]{:S(2)}, u32[]{:S(2)}) collective-permute-start(bf16[4,128,128]{2,1,0:T(8,128)(2,1)S(1)} %get-tuple-element.26), channel_id=1, source_target_pairs={{1,2},{2,1},{5,6},{6,5},{9,10},{10,9},{13,14},{14,13},{17,18},{18,... | collective-permute-start | bytes 393224 | tf_op jit(solution)/shard_map/ppermute | solution.py:492
  8.2 7.3 %collective-permute-start.3 = (bf16[4,128,128]{2,1,0:T(8,128)(2,1)S(1)}, bf16[4,128,128]{2,1,0:T(8,128)(2,1)S(1)}, u32[]{:S(2)}, u32[]{:S(2)}) collective-permute-start(bf16[4,128,128]{2,1,0:T(8,128)(2,1)S(1)} %get-tuple-element.27.after_ref), channel_id=1, source_target_pairs={{0,1},{2,3},{1,0},{3,2},{4,5},{6,7},{5,4},{7,6},{8,9},{10,11},{9,8... | collective-permute-start | bytes 393224 | tf_op jit(solution)/shard_map/ppermute | solution.py:493
  11.5 4.0 %collective-permute-start.4 = (bf16[4,64,128]{2,1,0:T(8,128)(2,1)S(1)}, bf16[4,64,128]{2,1,0:T(8,128)(2,1)S(1)}, u32[]{:S(2)}, u32[]{:S(2)}) collective-permute-start(bf16[4,64,128]{2,1,0:T(8,128)(2,1)S(1)} %get-tuple-element.28), channel_id=1, source_target_pairs={{1,2},{2,1},{5,6},{6,5},{9,10},{10,9},{13,14},{14,13},{17,18},{18,... | collective-permute-start | bytes 196616 | tf_op jit(solution)/shard_map/ppermute | solution.py:504
  12.1 3.3 %collective-permute-start.5 = (bf16[4,64,128]{2,1,0:T(8,128)(2,1)S(1)}, bf16[4,64,128]{2,1,0:T(8,128)(2,1)S(1)}, u32[]{:S(2)}, u32[]{:S(2)}) collective-permute-start(bf16[4,64,128]{2,1,0:T(8,128)(2,1)S(1)} %get-tuple-element.29), channel_id=1, source_target_pairs={{0,1},{2,3},{1,0},{3,2},{4,5},{6,7},{5,4},{7,6},{8,9},{10,11},{9,8... | collective-permute-start | bytes 196616 | tf_op jit(solution)/shard_map/ppermute | solution.py:505
  13.5 2.0 %copy-start = (bf16[64,384]{1,0:T(8,128)(2,1)S(1)}, bf16[64,384]{1,0:T(8,128)(2,1)}, u32[]{:S(2)}) copy-start(bf16[64,384]{1,0:T(8,128)(2,1)} %constant.12.clone.refs_11_.refs_6_) | copy-start | bytes 147460
  13.5 2.0 %copy-start.1 = (bf16[128,128]{1,0:T(8,128)(2,1)S(1)}, bf16[128,128]{1,0:T(8,128)(2,1)}, u32[]{:S(2)}) copy-start(bf16[128,128]{1,0:T(8,128)(2,1)} %constant.13.clone.refs_12_.refs_7_) | copy-start | bytes 98308
  13.5 2.0 %copy-start.3 = (bf16[8,64,128]{2,1,0:T(8,128)(2,1)S(1)}, bf16[8,64,128]{2,1,0:T(8,128)(2,1)}, u32[]{:S(2)}) copy-start(bf16[8,64,128]{2,1,0:T(8,128)(2,1)} %refs_10_.1) | copy-start | bytes 393220
  15.5 17.1 %copy-start.4 = (bf16[384,64]{1,0:T(8,128)(2,1)S(1)}, bf16[384,64]{1,0:T(8,128)(2,1)}, u32[]{:S(2)}) copy-start(bf16[384,64]{1,0:T(8,128)(2,1)} %constant.14.clone.refs_4_) | copy-start | bytes 147460
  18.6 14.0 %copy-start.5 = (bf16[128,128]{1,0:T(8,128)(2,1)S(1)}, bf16[128,128]{1,0:T(8,128)(2,1)}, u32[]{:S(2)}) copy-start(bf16[128,128]{1,0:T(8,128)(2,1)} %constant.15.clone.refs_5_) | copy-start | bytes 98308

commit v17 on v14

--- a/solution.py
+++ b/solution.py
@@ -151,13 +151,12 @@
 
 def column_row(rows, face, at):
     lane = lax.broadcasted_iota(jnp.int32, (8, 128), 1)
-    block = jnp.zeros((8, 128), F32)
+    sub = lax.broadcasted_iota(jnp.int32, (8, 128), 0)
+    out = jnp.where(lane == 64 + sub, jnp.broadcast_to(face[:, at : at + 1], (8, 128)), 0.0)
     for kc in range(6):
-        block = jnp.where(lane == kc, jnp.broadcast_to(rows[kc][:, at : at + 1], (8, 128)), block)
-    edge = jnp.where(lane == 64, jnp.broadcast_to(face[:, at : at + 1], (8, 128)), 0.0)
-    block = pltpu.roll(block, 0, 1, stride=8, stride_axis=0)
-    edge = pltpu.roll(edge, 0, 1, stride=1, stride_axis=0)
-    return over_sublanes(block + edge)
+        col = jnp.broadcast_to(rows[kc][:, at : at + 1], (8, 128))
+        out = jnp.where(lane == 8 * sub + kc, col, out)
+    return over_sublanes(out)
 
 
 def column_of(row):

time: 43.8 us -> 43.6 us (level)
    pallas_call x1, Pallas kernels: 3.03 us -> 2.5 us  [on_device(): pl.pallas_call(lambda *refs: late_kernel(nx, ny, *refs), out_shape=(sds((...]
    pallas_call x1, Pallas kernels: 1.96 us -> 2.46 us  [on_device(): pl.pallas_call(early_kernel, out_shape=sds((16, 11, 8, 128), F32), in_spe...]
  transfers between devices with their start and end apart: 6 -> 6, of which waited for: 1 -> 1; matrix products, arithmetic and copies ran while one was open for 2% -> 2% of each run, Pallas kernels for 7% -> 8%
where the time goes in v17:
time: 43.6 us; the launch traced here: 43.3 us
  blocking collectives  22.7 us (52%)
  starting transfers between devices  9.49 us (22%)
  Pallas kernels  7.84 us (18%)
  local copies, waits for them, and re-layouts  0.94 us (2%)
  between operations  0.81 us (2%)
  other arithmetic  0.77 us (2%)
  waiting for transfers between devices  0.68 us (2%)
    all_to_all x2, blocking collectives, on_device(): recv = lax.all_to_all(send, ('gx', 'gy'), 0, 0, tiled=True)  22.7 us
    ppermute x1, starting transfers between devices, on_device(): ya = lax.ppermute(to_a, 'gy', swaps(ny, 0))  3.13 us
    ppermute x1, starting transfers between devices, on_device(): xa = lax.ppermute(def_image, 'gx', swaps(nx, 0))  3.03 us
    pallas_call x1, Pallas kernels, on_device(): pl.pallas_call(lambda *refs: late_kernel(nx, ny, *refs), out_shape=(sds((...  2.5 us
    pallas_call x1, Pallas kernels, on_device(): pl.pallas_call(early_kernel, out_shape=sds((16, 11, 8, 128), F32), in_spe...  2.46 us
    ppermute x1, starting transfers between devices, on_device(): yc = lax.ppermute(to_c, 'gy', swaps(ny, 0))  1.34 us
    pallas_call x1, Pallas kernels, on_device(): pl.pallas_call(lambda *refs: product_kernel(nx, ny, *refs), out_shape=(sd...  1.19 us
    unnamed x18, local copies, waits for them, and re-layouts  0.94 us
  transfers between devices with their start and end apart: 6, of which 1 were waited for; matrix products, arithmetic and copies ran while one was open for 2% of the time, Pallas kernels for 8%

profile of v17, /device:TPU:0, one launch (start us, length us, event | category | flops | bytes accessed | tf_op | source)
XLA Modules:
  0.0 43.3 jit_solution(8075964847347089386)
XLA Ops:
  0.6 0.0 copy-start.8
  0.6 0.0 copy-start.7
  0.7 3.0 %collective-permute-start.1 = (bf16[8,64,128]{2,1,0:T(8,128)(2,1)}, bf16[8,64,128]{2,1,0:T(8,128)(2,1)S(1)}, u32[]{:S(2)}, u32[]{:S(2)}) collective-permute-start(bf16[8,64,128]{2,1,0:T(8,128)(2,1)} %own_ref.1), channel_id=1, source_target_pairs={{0,4},{8,12},{16,20},{24,28},{4,0},{12,8},{20,16},{28,24},{1,5},{9... | collective-permute-start | bytes 393224 | tf_op jit(solution)/shard_map/ppermute | solution.py:464
  3.7 0.7 %collective-permute-start = (bf16[8,64,128]{2,1,0:T(8,128)(2,1)}, bf16[8,64,128]{2,1,0:T(8,128)(2,1)S(1)}, u32[]{:S(2)}, u32[]{:S(2)}) collective-permute-start(bf16[8,64,128]{2,1,0:T(8,128)(2,1)} %own_ref.1), channel_id=1, source_target_pairs={{4,8},{12,16},{20,24},{8,4},{16,12},{24,20},{5,9},{13,17},{21,25},... | collective-permute-start | bytes 393224 | tf_op jit(solution)/shard_map/ppermute | solution.py:465
  4.4 0.0 copy-done.8
  4.4 0.0 copy-done.7
  4.4 0.0 copy-start.6
  4.4 0.8 %pad_add_fusion.row_ref = s32[16,128]{1,0:T(8,128)S(1)} fusion(s32[2,128]{1,0:T(2,128)S(1)} %copy-done.7, s32[8,128]{1,0:T(8,128)} %param.15, s32[128]{0:T(128)S(1)} %copy-done.8, pred[16]{0:T(512)(128)(4,1)S(1)} %iota_compare_fusion), kind=kLoop, calls=%fused_computation | loop fusion | flops 6144 | bytes 13840 | tf_op jit(solution)/shard_map/add | solution.py:468
  5.2 0.0 copy-done.6
  5.2 0.0 copy-start.2
  5.2 0.9 %copy-done.2 = bf16[8,64,128]{2,1,0:T(8,128)(2,1)S(1)} copy-done((bf16[8,64,128]{2,1,0:T(8,128)(2,1)S(1)}, bf16[8,64,128]{2,1,0:T(8,128)(2,1)}, u32[]{:S(2)}) %copy-start.2) | copy-done | bytes 131096
  6.1 0.7 %order_elements.1 = (s32[8,128]{1,0:T(8,128)S(1)}, f32[8,8,128]{2,1,0:T(8,128)S(1)}, bf16[8,64,128]{2,1,0:T(8,128)(2,1)S(1)}) custom-call(s32[16,128]{1,0:T(8,128)S(1)} %pad_add_fusion.row_ref, f32[3,128]{1,0:T(4,128)S(1)} %copy-done.6, bf16[8,64,128]{2,1,0:T(8,128)(2,1)S(1)} %copy-done.2), custom_call_target="tpu_custom_call" | custom-call | flops 300000 | bytes 262144 | tf_op jit(solution)/shard_map/order_elements/pallas_call | solution.py:469
  6.7 0.7 %collective-permute-done.1.xa_ref.refs_4_ = bf16[8,64,128]{2,1,0:T(8,128)(2,1)S(1)} collective-permute-done((bf16[8,64,128]{2,1,0:T(8,128)(2,1)}, bf16[8,64,128]{2,1,0:T(8,128)(2,1)S(1)}, u32[]{:S(2)}, u32[]{:S(2)}) %collective-permute-start.1) | collective-permute-done | bytes 131104 | tf_op jit(solution)/shard_map/ppermute | solution.py:464
  7.4 0.1 pack_first_halo.1
  7.5 0.7 %collective-permute-start.2 = (bf16[4,128,128]{2,1,0:T(8,128)(2,1)S(1)}, bf16[4,128,128]{2,1,0:T(8,128)(2,1)S(1)}, u32[]{:S(2)}, u32[]{:S(2)}) collective-permute-start(bf16[4,128,128]{2,1,0:T(8,128)(2,1)S(1)} %get-tuple-element.26), channel_id=1, source_target_pairs={{1,2},{2,1},{5,6},{6,5},{9,10},{10,9},{13,14},{14,13},{17,18},{18,... | collective-permute-start | bytes 393224 | tf_op jit(solution)/shard_map/ppermute | solution.py:488
  8.2 3.1 %collective-permute-start.3 = (bf16[4,128,128]{2,1,0:T(8,128)(2,1)S(1)}, bf16[4,128,128]{2,1,0:T(8,128)(2,1)S(1)}, u32[]{:S(2)}, u32[]{:S(2)}) collective-permute-start(bf16[4,128,128]{2,1,0:T(8,128)(2,1)S(1)} %get-tuple-element.27.after_ref), channel_id=1, source_target_pairs={{0,1},{2,3},{1,0},{3,2},{4,5},{6,7},{5,4},{7,6},{8,9},{10,11},{9,8... | collective-permute-start | bytes 393224 | tf_op jit(solution)/shard_map/ppermute | solution.py:489
  11.4 0.0 collective-permute-done.xb_ref.refs_2_
  11.4 0.1 pack_second_halo.1
  11.5 0.7 %collective-permute-start.4 = (bf16[4,64,128]{2,1,0:T(8,128)(2,1)S(1)}, bf16[4,64,128]{2,1,0:T(8,128)(2,1)S(1)}, u32[]{:S(2)}, u32[]{:S(2)}) collective-permute-start(bf16[4,64,128]{2,1,0:T(8,128)(2,1)S(1)} %get-tuple-element.28), channel_id=1, source_target_pairs={{1,2},{2,1},{5,6},{6,5},{9,10},{10,9},{13,14},{14,13},{17,18},{18,... | collective-permute-start | bytes 196616 | tf_op jit(solution)/shard_map/ppermute | solution.py:500
  12.1 1.3 %collective-permute-start.5 = (bf16[4,64,128]{2,1,0:T(8,128)(2,1)S(1)}, bf16[4,64,128]{2,1,0:T(8,128)(2,1)S(1)}, u32[]{:S(2)}, u32[]{:S(2)}) collective-permute-start(bf16[4,64,128]{2,1,0:T(8,128)(2,1)S(1)} %get-tuple-element.29), channel_id=1, source_target_pairs={{0,1},{2,3},{1,0},{3,2},{4,5},{6,7},{5,4},{7,6},{8,9},{10,11},{9,8... | collective-permute-start | bytes 196616 | tf_op jit(solution)/shard_map/ppermute | solution.py:501
  13.5 0.0 copy-start
  13.5 0.0 copy-start.1
  13.5 0.0 copy-start.3
  13.5 2.5 %sample_early.1.refs_9_ = f32[16,11,8,128]{3,2,1,0:T(8,128)S(1)} custom-call(s32[8,128]{1,0:T(8,128)S(1)} %get-tuple-element.23.idx_ref.refs_0_, bf16[8,64,128]{2,1,0:T(8,128)(2,1)S(1)} %collective-permute-done.xb_ref.refs_2_, bf16[8,64,128]{2,1,0:T(8,128)(2,1)S(1)} %get-tuple-element.25.own_ref.refs_3_, ...), custom_call_target="tpu_custom_call" | custom-call | flops 4000000 | bytes 2000000 | tf_op jit(solution)/shard_map/sample_early/pallas_call | solution.py:504
  16.0 0.0 collective-permute-done.4.refs_7_
  16.0 0.0 collective-permute-done.5.refs_8_
  16.0 0.0 collective-permute-done.2.refs_5_
  16.0 0.0 collective-permute-done.3.refs_6_
  16.0 0.0 copy-done
  16.0 0.0 copy-done.1
  16.0 0.0 copy-done.3
  16.0 0.0 copy-start.4
  16.0 2.5 %sample_and_gradient.1 = (bf16[8,64,128]{2,1,0:T(8,128)(2,1)S(1)}, f32[3,8,8,8,128]{4,3,2,1,0:T(8,128)S(1)}, f32[64,128]{1,0:T(8,128)S(1)}, f32[32,1,128]{2,1,0:T(1,128)S(1)}, f32[8,128]{1,0:T(8,128)S(1)}) custom-call(s32[8,128]{1,0:T(8,128)S(1)} %get-tuple-element.23.idx_ref.refs_0_, f32[8,8,128]{2,1,0:T(8,128)S(1)} %get-tuple-element.24.refs_1_, ...), custom_call_target="tpu_custom_call" | custom-call | tf_op jit(solution)/shard_map/sample_and_gradient/pallas_call | solution.py:514
  18.6 0.0 copy-start.5
  18.6 13.9 %all_to_all.10.refs_0_ = f32[32,1,128]{2,1,0:T(1,128)S(1)} all-to-all(f32[32,1,128]{2,1,0:T(1,128)S(1)} %get-tuple-element.30), channel_id=1, replica_groups=mesh['gx'=8,'gy'=4] {'gx','gy'}, dimensions={0} | all-to-all | bytes 32768 | tf_op jit(solution)/shard_map/all_to_all | solution.py:534
  32.5 0.0 copy-done.4
  32.5 0.0 copy-done.5
  32.5 1.2 %gauss_newton_product.1 = (f32[6,8,128]{2,1,0:T(8,128)S(1)}, f32[6,8,128]{2,1,0:T(8,128)S(1)}, f32[32,1,128]{2,1,0:T(1,128)S(1)}, bf16[8,64,128]{2,1,0:T(8,128)(2,1)}) custom-call(f32[32,1,128]{2,1,0:T(1,128)S(1)} %all_to_all.10.refs_0_, f32[64,128]{1,0:T(8,128)S(1)} %get-tuple-element.31.refs_1_, f32[3,8,8,8,128]{4,3,2,1,0:T(8,128)S(1)} %get-tuple-element.32.refs_2_, ...), custom_call_target="tpu_custom_call" | custom-call | tf_op jit(solution)/shard_map/gauss_newton_product/pallas_call | solution.py:535
  33.7 8.8 %all_to_all.11.refs_0_ = f32[32,1,128]{2,1,0:T(1,128)S(1)} all-to-all(f32[32,1,128]{2,1,0:T(1,128)S(1)} %get-tuple-element.36), channel_id=1, replica_groups=mesh['gx'=8,'gy'=4] {'gx','gy'}, dimensions={0} | all-to-all | bytes 32768 | tf_op jit(solution)/shard_map/all_to_all | solution.py:553
  42.5 0.8 %finish.1 = (f32[3,2,8,16]{3,2,1,0:T(8,128)}, f32[3,2,8,16]{3,2,1,0:T(8,128)}, f32[1,1]{1,0:T(1,128)}) custom-call(f32[32,1,128]{2,1,0:T(1,128)S(1)} %all_to_all.11.refs_0_, f32[6,8,128]{2,1,0:T(8,128)S(1)} %get-tuple-element.37.refs_1_, f32[6,8,128]{2,1,0:T(8,128)S(1)} %get-tuple-element.38.refs_2_), custom_call_target="tpu_custom_call" | custom-call | tf_op jit(solution)/shard_map/finish/pallas_call | solution.py:555
  (1 shorter events, 0.0 us)
Async XLA Ops:
  0.6 3.7 %copy-start.8 = (s32[128]{0:T(128)S(1)}, s32[128]{0:T(128)}, u32[]{:S(2)}) copy-start(s32[128]{0:T(128)} %param.13) | copy-start | bytes 1540
  0.6 3.7 %copy-start.7 = (s32[2,128]{1,0:T(2,128)S(1)}, s32[2,128]{1,0:T(2,128)}, u32[]{:S(2)}) copy-start(s32[2,128]{1,0:T(2,128)} %param.12) | copy-start | bytes 3076
  0.7 6.7 %collective-permute-start.1 = (bf16[8,64,128]{2,1,0:T(8,128)(2,1)}, bf16[8,64,128]{2,1,0:T(8,128)(2,1)S(1)}, u32[]{:S(2)}, u32[]{:S(2)}) collective-permute-start(bf16[8,64,128]{2,1,0:T(8,128)(2,1)} %own_ref.1), channel_id=1, source_target_pairs={{0,4},{8,12},{16,20},{24,28},{4,0},{12,8},{20,16},{28,24},{1,5},{9... | collective-permute-start | bytes 393224 | tf_op jit(solution)/shard_map/ppermute | solution.py:464
  3.7 7.7 %collective-permute-start = (bf16[8,64,128]{2,1,0:T(8,128)(2,1)}, bf16[8,64,128]{2,1,0:T(8,128)(2,1)S(1)}, u32[]{:S(2)}, u32[]{:S(2)}) collective-permute-start(bf16[8,64,128]{2,1,0:T(8,128)(2,1)} %own_ref.1), channel_id=1, source_target_pairs={{4,8},{12,16},{20,24},{8,4},{16,12},{24,20},{5,9},{13,17},{21,25},... | collective-permute-start | bytes 393224 | tf_op jit(solution)/shard_map/ppermute | solution.py:465
  4.4 0.8 %copy-start.6 = (f32[3,128]{1,0:T(4,128)S(1)}, f32[3,128]{1,0:T(4,128)}, u32[]{:S(2)}) copy-start(f32[3,128]{1,0:T(4,128)} %frac_ref.1) | copy-start | bytes 4612
  5.2 0.9 %copy-start.2 = (bf16[8,64,128]{2,1,0:T(8,128)(2,1)S(1)}, bf16[8,64,128]{2,1,0:T(8,128)(2,1)}, u32[]{:S(2)}) copy-start(bf16[8,64,128]{2,1,0:T(8,128)(2,1)} %own_ref.1) | copy-start | bytes 393220
  7.5 8.4 %collective-permute-start.2 = (bf16[4,128,128]{2,1,0:T(8,128)(2,1)S(1)}, bf16[4,128,128]{2,1,0:T(8,128)(2,1)S(1)}, u32[]{:S(2)}, u32[]{:S(2)}) collective-permute-start(bf16[4,128,128]{2,1,0:T(8,128)(2,1)S(1)} %get-tuple-element.26), channel_id=1, source_target_pairs={{1,2},{2,1},{5,6},{6,5},{9,10},{10,9},{13,14},{14,13},{17,18},{18,... | collective-permute-start | bytes 393224 | tf_op jit(solution)/shard_map/ppermute | solution.py:488
  8.2 7.8 %collective-permute-start.3 = (bf16[4,128,128]{2,1,0:T(8,128)(2,1)S(1)}, bf16[4,128,128]{2,1,0:T(8,128)(2,1)S(1)}, u32[]{:S(2)}, u32[]{:S(2)}) collective-permute-start(bf16[4,128,128]{2,1,0:T(8,128)(2,1)S(1)} %get-tuple-element.27.after_ref), channel_id=1, source_target_pairs={{0,1},{2,3},{1,0},{3,2},{4,5},{6,7},{5,4},{7,6},{8,9},{10,11},{9,8... | collective-permute-start | bytes 393224 | tf_op jit(solution)/shard_map/ppermute | solution.py:489
  11.5 4.5 %collective-permute-start.4 = (bf16[4,64,128]{2,1,0:T(8,128)(2,1)S(1)}, bf16[4,64,128]{2,1,0:T(8,128)(2,1)S(1)}, u32[]{:S(2)}, u32[]{:S(2)}) collective-permute-start(bf16[4,64,128]{2,1,0:T(8,128)(2,1)S(1)} %get-tuple-element.28), channel_id=1, source_target_pairs={{1,2},{2,1},{5,6},{6,5},{9,10},{10,9},{13,14},{14,13},{17,18},{18,... | collective-permute-start | bytes 196616 | tf_op jit(solution)/shard_map/ppermute | solution.py:500
  12.1 3.8 %collective-permute-start.5 = (bf16[4,64,128]{2,1,0:T(8,128)(2,1)S(1)}, bf16[4,64,128]{2,1,0:T(8,128)(2,1)S(1)}, u32[]{:S(2)}, u32[]{:S(2)}) collective-permute-start(bf16[4,64,128]{2,1,0:T(8,128)(2,1)S(1)} %get-tuple-element.29), channel_id=1, source_target_pairs={{0,1},{2,3},{1,0},{3,2},{4,5},{6,7},{5,4},{7,6},{8,9},{10,11},{9,8... | collective-permute-start | bytes 196616 | tf_op jit(solution)/shard_map/ppermute | solution.py:501
  13.5 2.5 %copy-start = (bf16[64,384]{1,0:T(8,128)(2,1)S(1)}, bf16[64,384]{1,0:T(8,128)(2,1)}, u32[]{:S(2)}) copy-start(bf16[64,384]{1,0:T(8,128)(2,1)} %constant.12.clone.refs_11_.refs_6_) | copy-start | bytes 147460
  13.5 2.5 %copy-start.1 = (bf16[128,128]{1,0:T(8,128)(2,1)S(1)}, bf16[128,128]{1,0:T(8,128)(2,1)}, u32[]{:S(2)}) copy-start(bf16[128,128]{1,0:T(8,128)(2,1)} %constant.13.clone.refs_12_.refs_7_) | copy-start | bytes 98308
  13.5 2.5 %copy-start.3 = (bf16[8,64,128]{2,1,0:T(8,128)(2,1)S(1)}, bf16[8,64,128]{2,1,0:T(8,128)(2,1)}, u32[]{:S(2)}) copy-start(bf16[8,64,128]{2,1,0:T(8,128)(2,1)} %refs_10_.1) | copy-start | bytes 393220
  16.0 16.4 %copy-start.4 = (bf16[384,64]{1,0:T(8,128)(2,1)S(1)}, bf16[384,64]{1,0:T(8,128)(2,1)}, u32[]{:S(2)}) copy-start(bf16[384,64]{1,0:T(8,128)(2,1)} %constant.14.clone.refs_4_) | copy-start | bytes 147460
  18.6 13.9 %copy-start.5 = (bf16[128,128]{1,0:T(8,128)(2,1)S(1)}, bf16[128,128]{1,0:T(8,128)(2,1)}, u32[]{:S(2)}) copy-start(bf16[128,128]{1,0:T(8,128)(2,1)} %constant.15.clone.refs_5_) | copy-start | bytes 98308

commit v18 on v14

--- a/solution.py
+++ b/solution.py
@@ -12,6 +12,7 @@
 SPAN = 192
 TILE_ROWS = 12 * SPAN
 CHUNK = 16
+EARLY_CHUNK = 32
 VMEM = pl.BlockSpec(memory_space=pltpu.VMEM)
 SMEM = pl.BlockSpec(memory_space=pltpu.SMEM)
 PARAMS = pltpu.CompilerParams(vmem_limit_bytes=24 * 1024 * 1024)
@@ -195,14 +196,14 @@
             img[pl.ds(pl.multiple_of((z + 2) * SPAN + row, 8), 64)] = ref[z].astype(F32)
 
     def chunk(n, carry):
-        for m in range(CHUNK):
-            e = n * CHUNK + m
+        for m in range(EARLY_CHUNK):
+            e = n * EARLY_CHUNK + m
             sample_element(
                 img, arr_ref, idx_ref[0, e], idx_ref[1, e], idx_ref[2, e], idx_ref[3, e], 9
             )
         return carry
 
-    lax.fori_loop(0, (idx_ref[6, 0] + (CHUNK - 1)) // CHUNK, chunk, 0)
+    lax.fori_loop(0, (idx_ref[6, 0] + (EARLY_CHUNK - 1)) // EARLY_CHUNK, chunk, 0)
 
 
 def late_kernel(

time: 43.8 us -> 43.6 us (level)
    pallas_call x1, Pallas kernels: 3.03 us -> 2.53 us  [on_device(): pl.pallas_call(lambda *refs: late_kernel(nx, ny, *refs), out_shape=(sds((...]
    pallas_call x1, Pallas kernels: 1.96 us -> 2.45 us  [on_device(): pl.pallas_call(early_kernel, out_shape=sds((16, 11, 8, 128), F32), in_spe...]
  transfers between devices with their start and end apart: 6 -> 6, of which waited for: 1 -> 1; matrix products, arithmetic and copies ran while one was open for 2% -> 2% of each run, Pallas kernels for 7% -> 8%
where the time goes in v18:
time: 43.6 us; the launch traced here: 43.4 us
  blocking collectives  22.8 us (52%)
  starting transfers between devices  9.49 us (22%)
  Pallas kernels  7.93 us (18%)
  local copies, waits for them, and re-layouts  0.94 us (2%)
  between operations  0.81 us (2%)
  other arithmetic  0.77 us (2%)
  waiting for transfers between devices  0.68 us (2%)
    all_to_all x2, blocking collectives, on_device(): recv = lax.all_to_all(send, ('gx', 'gy'), 0, 0, tiled=True)  22.8 us
    ppermute x1, starting transfers between devices, on_device(): ya = lax.ppermute(to_a, 'gy', swaps(ny, 0))  3.13 us
    ppermute x1, starting transfers between devices, on_device(): xa = lax.ppermute(def_image, 'gx', swaps(nx, 0))  3.03 us
    pallas_call x1, Pallas kernels, on_device(): pl.pallas_call(lambda *refs: late_kernel(nx, ny, *refs), out_shape=(sds((...  2.53 us
    pallas_call x1, Pallas kernels, on_device(): pl.pallas_call(early_kernel, out_shape=sds((16, 11, 8, 128), F32), in_spe...  2.45 us
    ppermute x1, starting transfers between devices, on_device(): yc = lax.ppermute(to_c, 'gy', swaps(ny, 0))  1.34 us
    pallas_call x1, Pallas kernels, on_device(): pl.pallas_call(lambda *refs: product_kernel(nx, ny, *refs), out_shape=(sd...  1.26 us
    unnamed x18, local copies, waits for them, and re-layouts  0.94 us
  transfers between devices with their start and end apart: 6, of which 1 were waited for; matrix products, arithmetic and copies ran while one was open for 2% of the time, Pallas kernels for 8%

profile of v18, /device:TPU:0, one launch (start us, length us, event | category | flops | bytes accessed | tf_op | source)
XLA Modules:
  0.0 43.4 jit_solution(18270410171128469147)
XLA Ops:
  0.6 0.0 copy-start.8
  0.6 0.0 copy-start.7
  0.7 3.0 %collective-permute-start.1 = (bf16[8,64,128]{2,1,0:T(8,128)(2,1)}, bf16[8,64,128]{2,1,0:T(8,128)(2,1)S(1)}, u32[]{:S(2)}, u32[]{:S(2)}) collective-permute-start(bf16[8,64,128]{2,1,0:T(8,128)(2,1)} %own_ref.1), channel_id=1, source_target_pairs={{0,4},{8,12},{16,20},{24,28},{4,0},{12,8},{20,16},{28,24},{1,5},{9... | collective-permute-start | bytes 393224 | tf_op jit(solution)/shard_map/ppermute | solution.py:466
  3.7 0.7 %collective-permute-start = (bf16[8,64,128]{2,1,0:T(8,128)(2,1)}, bf16[8,64,128]{2,1,0:T(8,128)(2,1)S(1)}, u32[]{:S(2)}, u32[]{:S(2)}) collective-permute-start(bf16[8,64,128]{2,1,0:T(8,128)(2,1)} %own_ref.1), channel_id=1, source_target_pairs={{4,8},{12,16},{20,24},{8,4},{16,12},{24,20},{5,9},{13,17},{21,25},... | collective-permute-start | bytes 393224 | tf_op jit(solution)/shard_map/ppermute | solution.py:467
  4.4 0.0 copy-done.8
  4.4 0.0 copy-done.7
  4.4 0.0 copy-start.6
  4.4 0.8 %pad_add_fusion.row_ref = s32[16,128]{1,0:T(8,128)S(1)} fusion(s32[2,128]{1,0:T(2,128)S(1)} %copy-done.7, s32[8,128]{1,0:T(8,128)} %param.15, s32[128]{0:T(128)S(1)} %copy-done.8, pred[16]{0:T(512)(128)(4,1)S(1)} %iota_compare_fusion), kind=kLoop, calls=%fused_computation | loop fusion | flops 6144 | bytes 13840 | tf_op jit(solution)/shard_map/add | solution.py:470
  5.2 0.0 copy-done.6
  5.2 0.0 copy-start.2
  5.2 0.9 %copy-done.2 = bf16[8,64,128]{2,1,0:T(8,128)(2,1)S(1)} copy-done((bf16[8,64,128]{2,1,0:T(8,128)(2,1)S(1)}, bf16[8,64,128]{2,1,0:T(8,128)(2,1)}, u32[]{:S(2)}) %copy-start.2) | copy-done | bytes 131096
  6.1 0.7 %order_elements.1 = (s32[8,128]{1,0:T(8,128)S(1)}, f32[8,8,128]{2,1,0:T(8,128)S(1)}, bf16[8,64,128]{2,1,0:T(8,128)(2,1)S(1)}) custom-call(s32[16,128]{1,0:T(8,128)S(1)} %pad_add_fusion.row_ref, f32[3,128]{1,0:T(4,128)S(1)} %copy-done.6, bf16[8,64,128]{2,1,0:T(8,128)(2,1)S(1)} %copy-done.2), custom_call_target="tpu_custom_call" | custom-call | flops 300000 | bytes 262144 | tf_op jit(solution)/shard_map/order_elements/pallas_call | solution.py:471
  6.7 0.7 %collective-permute-done.1.xa_ref.refs_4_ = bf16[8,64,128]{2,1,0:T(8,128)(2,1)S(1)} collective-permute-done((bf16[8,64,128]{2,1,0:T(8,128)(2,1)}, bf16[8,64,128]{2,1,0:T(8,128)(2,1)S(1)}, u32[]{:S(2)}, u32[]{:S(2)}) %collective-permute-start.1) | collective-permute-done | bytes 131104 | tf_op jit(solution)/shard_map/ppermute | solution.py:466
  7.4 0.1 pack_first_halo.1
  7.5 0.7 %collective-permute-start.2 = (bf16[4,128,128]{2,1,0:T(8,128)(2,1)S(1)}, bf16[4,128,128]{2,1,0:T(8,128)(2,1)S(1)}, u32[]{:S(2)}, u32[]{:S(2)}) collective-permute-start(bf16[4,128,128]{2,1,0:T(8,128)(2,1)S(1)} %get-tuple-element.26), channel_id=1, source_target_pairs={{1,2},{2,1},{5,6},{6,5},{9,10},{10,9},{13,14},{14,13},{17,18},{18,... | collective-permute-start | bytes 393224 | tf_op jit(solution)/shard_map/ppermute | solution.py:490
  8.2 3.1 %collective-permute-start.3 = (bf16[4,128,128]{2,1,0:T(8,128)(2,1)S(1)}, bf16[4,128,128]{2,1,0:T(8,128)(2,1)S(1)}, u32[]{:S(2)}, u32[]{:S(2)}) collective-permute-start(bf16[4,128,128]{2,1,0:T(8,128)(2,1)S(1)} %get-tuple-element.27.after_ref), channel_id=1, source_target_pairs={{0,1},{2,3},{1,0},{3,2},{4,5},{6,7},{5,4},{7,6},{8,9},{10,11},{9,8... | collective-permute-start | bytes 393224 | tf_op jit(solution)/shard_map/ppermute | solution.py:491
  11.4 0.0 collective-permute-done.xb_ref.refs_2_
  11.4 0.1 pack_second_halo.1
  11.5 0.7 %collective-permute-start.4 = (bf16[4,64,128]{2,1,0:T(8,128)(2,1)S(1)}, bf16[4,64,128]{2,1,0:T(8,128)(2,1)S(1)}, u32[]{:S(2)}, u32[]{:S(2)}) collective-permute-start(bf16[4,64,128]{2,1,0:T(8,128)(2,1)S(1)} %get-tuple-element.28), channel_id=1, source_target_pairs={{1,2},{2,1},{5,6},{6,5},{9,10},{10,9},{13,14},{14,13},{17,18},{18,... | collective-permute-start | bytes 196616 | tf_op jit(solution)/shard_map/ppermute | solution.py:502
  12.1 1.3 %collective-permute-start.5 = (bf16[4,64,128]{2,1,0:T(8,128)(2,1)S(1)}, bf16[4,64,128]{2,1,0:T(8,128)(2,1)S(1)}, u32[]{:S(2)}, u32[]{:S(2)}) collective-permute-start(bf16[4,64,128]{2,1,0:T(8,128)(2,1)S(1)} %get-tuple-element.29), channel_id=1, source_target_pairs={{0,1},{2,3},{1,0},{3,2},{4,5},{6,7},{5,4},{7,6},{8,9},{10,11},{9,8... | collective-permute-start | bytes 196616 | tf_op jit(solution)/shard_map/ppermute | solution.py:503
  13.5 0.0 copy-start
  13.5 0.0 copy-start.1
  13.5 0.0 copy-start.3
  13.5 2.5 %sample_early.1.refs_9_ = f32[16,11,8,128]{3,2,1,0:T(8,128)S(1)} custom-call(s32[8,128]{1,0:T(8,128)S(1)} %get-tuple-element.23.idx_ref.refs_0_, bf16[8,64,128]{2,1,0:T(8,128)(2,1)S(1)} %collective-permute-done.xb_ref.refs_2_, bf16[8,64,128]{2,1,0:T(8,128)(2,1)S(1)} %get-tuple-element.25.own_ref.refs_3_, ...), custom_call_target="tpu_custom_call" | custom-call | flops 4000000 | bytes 2000000 | tf_op jit(solution)/shard_map/sample_early/pallas_call | solution.py:506
  16.0 0.0 collective-permute-done.4.refs_7_
  16.0 0.0 collective-permute-done.5.refs_8_
  16.0 0.0 collective-permute-done.2.refs_5_
  16.0 0.0 collective-permute-done.3.refs_6_
  16.0 0.0 copy-done
  16.0 0.0 copy-done.1
  16.0 0.0 copy-done.3
  16.0 0.0 copy-start.4
  16.0 2.5 %sample_and_gradient.1 = (bf16[8,64,128]{2,1,0:T(8,128)(2,1)S(1)}, f32[3,8,8,8,128]{4,3,2,1,0:T(8,128)S(1)}, f32[64,128]{1,0:T(8,128)S(1)}, f32[32,1,128]{2,1,0:T(1,128)S(1)}, f32[8,128]{1,0:T(8,128)S(1)}) custom-call(s32[8,128]{1,0:T(8,128)S(1)} %get-tuple-element.23.idx_ref.refs_0_, f32[8,8,128]{2,1,0:T(8,128)S(1)} %get-tuple-element.24.refs_1_, ...), custom_call_target="tpu_custom_call" | custom-call | tf_op jit(solution)/shard_map/sample_and_gradient/pallas_call | solution.py:516
  18.6 0.0 copy-start.5
  18.6 14.0 %all_to_all.10.refs_0_ = f32[32,1,128]{2,1,0:T(1,128)S(1)} all-to-all(f32[32,1,128]{2,1,0:T(1,128)S(1)} %get-tuple-element.30), channel_id=1, replica_groups=mesh['gx'=8,'gy'=4] {'gx','gy'}, dimensions={0} | all-to-all | bytes 32768 | tf_op jit(solution)/shard_map/all_to_all | solution.py:536
  32.6 0.0 copy-done.4
  32.6 0.0 copy-done.5
  32.6 1.3 %gauss_newton_product.1 = (f32[6,8,128]{2,1,0:T(8,128)S(1)}, f32[6,8,128]{2,1,0:T(8,128)S(1)}, f32[32,1,128]{2,1,0:T(1,128)S(1)}, bf16[8,64,128]{2,1,0:T(8,128)(2,1)}) custom-call(f32[32,1,128]{2,1,0:T(1,128)S(1)} %all_to_all.10.refs_0_, f32[64,128]{1,0:T(8,128)S(1)} %get-tuple-element.31.refs_1_, f32[3,8,8,8,128]{4,3,2,1,0:T(8,128)S(1)} %get-tuple-element.32.refs_2_, ...), custom_call_target="tpu_custom_call" | custom-call | tf_op jit(solution)/shard_map/gauss_newton_product/pallas_call | solution.py:537
  33.8 8.8 %all_to_all.11.refs_0_ = f32[32,1,128]{2,1,0:T(1,128)S(1)} all-to-all(f32[32,1,128]{2,1,0:T(1,128)S(1)} %get-tuple-element.36), channel_id=1, replica_groups=mesh['gx'=8,'gy'=4] {'gx','gy'}, dimensions={0} | all-to-all | bytes 32768 | tf_op jit(solution)/shard_map/all_to_all | solution.py:555
  42.7 0.8 %finish.1 = (f32[3,2,8,16]{3,2,1,0:T(8,128)}, f32[3,2,8,16]{3,2,1,0:T(8,128)}, f32[1,1]{1,0:T(1,128)}) custom-call(f32[32,1,128]{2,1,0:T(1,128)S(1)} %all_to_all.11.refs_0_, f32[6,8,128]{2,1,0:T(8,128)S(1)} %get-tuple-element.37.refs_1_, f32[6,8,128]{2,1,0:T(8,128)S(1)} %get-tuple-element.38.refs_2_), custom_call_target="tpu_custom_call" | custom-call | tf_op jit(solution)/shard_map/finish/pallas_call | solution.py:557
  (1 shorter events, 0.0 us)
Async XLA Ops:
  0.6 3.7 %copy-start.8 = (s32[128]{0:T(128)S(1)}, s32[128]{0:T(128)}, u32[]{:S(2)}) copy-start(s32[128]{0:T(128)} %param.13) | copy-start | bytes 1540
  0.6 3.7 %copy-start.7 = (s32[2,128]{1,0:T(2,128)S(1)}, s32[2,128]{1,0:T(2,128)}, u32[]{:S(2)}) copy-start(s32[2,128]{1,0:T(2,128)} %param.12) | copy-start | bytes 3076
  0.7 6.7 %collective-permute-start.1 = (bf16[8,64,128]{2,1,0:T(8,128)(2,1)}, bf16[8,64,128]{2,1,0:T(8,128)(2,1)S(1)}, u32[]{:S(2)}, u32[]{:S(2)}) collective-permute-start(bf16[8,64,128]{2,1,0:T(8,128)(2,1)} %own_ref.1), channel_id=1, source_target_pairs={{0,4},{8,12},{16,20},{24,28},{4,0},{12,8},{20,16},{28,24},{1,5},{9... | collective-permute-start | bytes 393224 | tf_op jit(solution)/shard_map/ppermute | solution.py:466
  3.7 7.7 %collective-permute-start = (bf16[8,64,128]{2,1,0:T(8,128)(2,1)}, bf16[8,64,128]{2,1,0:T(8,128)(2,1)S(1)}, u32[]{:S(2)}, u32[]{:S(2)}) collective-permute-start(bf16[8,64,128]{2,1,0:T(8,128)(2,1)} %own_ref.1), channel_id=1, source_target_pairs={{4,8},{12,16},{20,24},{8,4},{16,12},{24,20},{5,9},{13,17},{21,25},... | collective-permute-start | bytes 393224 | tf_op jit(solution)/shard_map/ppermute | solution.py:467
  4.4 0.8 %copy-start.6 = (f32[3,128]{1,0:T(4,128)S(1)}, f32[3,128]{1,0:T(4,128)}, u32[]{:S(2)}) copy-start(f32[3,128]{1,0:T(4,128)} %frac_ref.1) | copy-start | bytes 4612
  5.2 0.9 %copy-start.2 = (bf16[8,64,128]{2,1,0:T(8,128)(2,1)S(1)}, bf16[8,64,128]{2,1,0:T(8,128)(2,1)}, u32[]{:S(2)}) copy-start(bf16[8,64,128]{2,1,0:T(8,128)(2,1)} %own_ref.1) | copy-start | bytes 393220
  7.5 8.4 %collective-permute-start.2 = (bf16[4,128,128]{2,1,0:T(8,128)(2,1)S(1)}, bf16[4,128,128]{2,1,0:T(8,128)(2,1)S(1)}, u32[]{:S(2)}, u32[]{:S(2)}) collective-permute-start(bf16[4,128,128]{2,1,0:T(8,128)(2,1)S(1)} %get-tuple-element.26), channel_id=1, source_target_pairs={{1,2},{2,1},{5,6},{6,5},{9,10},{10,9},{13,14},{14,13},{17,18},{18,... | collective-permute-start | bytes 393224 | tf_op jit(solution)/shard_map/ppermute | solution.py:490
  8.2 7.8 %collective-permute-start.3 = (bf16[4,128,128]{2,1,0:T(8,128)(2,1)S(1)}, bf16[4,128,128]{2,1,0:T(8,128)(2,1)S(1)}, u32[]{:S(2)}, u32[]{:S(2)}) collective-permute-start(bf16[4,128,128]{2,1,0:T(8,128)(2,1)S(1)} %get-tuple-element.27.after_ref), channel_id=1, source_target_pairs={{0,1},{2,3},{1,0},{3,2},{4,5},{6,7},{5,4},{7,6},{8,9},{10,11},{9,8... | collective-permute-start | bytes 393224 | tf_op jit(solution)/shard_map/ppermute | solution.py:491
  11.5 4.5 %collective-permute-start.4 = (bf16[4,64,128]{2,1,0:T(8,128)(2,1)S(1)}, bf16[4,64,128]{2,1,0:T(8,128)(2,1)S(1)}, u32[]{:S(2)}, u32[]{:S(2)}) collective-permute-start(bf16[4,64,128]{2,1,0:T(8,128)(2,1)S(1)} %get-tuple-element.28), channel_id=1, source_target_pairs={{1,2},{2,1},{5,6},{6,5},{9,10},{10,9},{13,14},{14,13},{17,18},{18,... | collective-permute-start | bytes 196616 | tf_op jit(solution)/shard_map/ppermute | solution.py:502
  12.1 3.8 %collective-permute-start.5 = (bf16[4,64,128]{2,1,0:T(8,128)(2,1)S(1)}, bf16[4,64,128]{2,1,0:T(8,128)(2,1)S(1)}, u32[]{:S(2)}, u32[]{:S(2)}) collective-permute-start(bf16[4,64,128]{2,1,0:T(8,128)(2,1)S(1)} %get-tuple-element.29), channel_id=1, source_target_pairs={{0,1},{2,3},{1,0},{3,2},{4,5},{6,7},{5,4},{7,6},{8,9},{10,11},{9,8... | collective-permute-start | bytes 196616 | tf_op jit(solution)/shard_map/ppermute | solution.py:503
  13.5 2.5 %copy-start = (bf16[64,384]{1,0:T(8,128)(2,1)S(1)}, bf16[64,384]{1,0:T(8,128)(2,1)}, u32[]{:S(2)}) copy-start(bf16[64,384]{1,0:T(8,128)(2,1)} %constant.12.clone.refs_11_.refs_6_) | copy-start | bytes 147460
  13.5 2.5 %copy-start.1 = (bf16[128,128]{1,0:T(8,128)(2,1)S(1)}, bf16[128,128]{1,0:T(8,128)(2,1)}, u32[]{:S(2)}) copy-start(bf16[128,128]{1,0:T(8,128)(2,1)} %constant.13.clone.refs_12_.refs_7_) | copy-start | bytes 98308
  13.5 2.5 %copy-start.3 = (bf16[8,64,128]{2,1,0:T(8,128)(2,1)S(1)}, bf16[8,64,128]{2,1,0:T(8,128)(2,1)}, u32[]{:S(2)}) copy-start(bf16[8,64,128]{2,1,0:T(8,128)(2,1)} %refs_10_.1) | copy-start | bytes 393220
  16.0 16.5 %copy-start.4 = (bf16[384,64]{1,0:T(8,128)(2,1)S(1)}, bf16[384,64]{1,0:T(8,128)(2,1)}, u32[]{:S(2)}) copy-start(bf16[384,64]{1,0:T(8,128)(2,1)} %constant.14.clone.refs_4_) | copy-start | bytes 147460
  18.6 14.0 %copy-start.5 = (bf16[128,128]{1,0:T(8,128)(2,1)S(1)}, bf16[128,128]{1,0:T(8,128)(2,1)}, u32[]{:S(2)}) copy-start(bf16[128,128]{1,0:T(8,128)(2,1)} %constant.15.clone.refs_5_) | copy-start | bytes 98308
